TPU v7x, 256 devices: a whole 4x4x8 slice. The times are simulated.
256 devices in a mesh: tm: 32 (over x, y, core), patch: 8 (over z).
Axes of the slice: x: 4, y: 4, z: 8, core: 2. Of those that a mesh axis runs over, the one named last changes fastest.
Arguments:
- stream: bfloat16 [256, 128, 2048], P('patch', 'tm'), may hold values from -6 to 6
- spatial_gain: float32 [2048], replicated, may hold values from 0.1 to 1.9
- spatial_qkv: bfloat16 [2048, 3, 2048], P(None, None, 'patch')
- spatial_out: bfloat16 [2048, 2048], P('patch'), may hold values from -1 to 1
- temporal_gain: float32 [2048], replicated, may hold values from 0.1 to 1.9
- temporal_qkv: bfloat16 [2048, 3, 2048], P(None, None, 'patch')
- temporal_out: bfloat16 [2048, 2048], P('patch'), may hold values from -0.125 to 0.125
- starts: int32 [2], replicated, may hold values from 1 to 63
Outputs:
- block_out: bfloat16 [256, 128, 2048], P('patch', 'tm')
All inputs are finite; a program needn't handle non-finite values.
Results may differ from a plain program's by a relative error of at most 0.02.
Values may be sent and summed in bfloat16 or wider, within the bound.
No kernel may reach another device: no remote copies, remote signals or barrier semaphores. Data moves between devices by JAX's collectives and lax.ppermute only.
A program may use at most 128 MiB of HBM per device.

v0:
```python
import math

import jax
import jax.numpy as jnp
from jax import lax
from jax.sharding import PartitionSpec as P

E = 128
SEQ = 64


def passed_along(value, axis, steps):
    count = lax.axis_size(axis)
    first, last = (max(0, -steps), min(count, count - steps))
    return lax.ppermute(value, axis, [(source, source + steps) for source in range(first, last)])


def rms_norm(stream, gain):
    values = stream.astype(jnp.float32)
    scaled = values * lax.rsqrt(jnp.mean(values * values, axis=-1, keepdims=True) + 1e-05)
    return (scaled * gain).astype(jnp.bfloat16)


def masked_softmax(scores, allowed):
    scores = jnp.where(allowed, scores, -1e30)
    row_max = jnp.max(scores, axis=-1, keepdims=True)
    shifted = jnp.exp(scores - row_max)
    return (shifted / jnp.sum(shifted, axis=-1, keepdims=True)).astype(jnp.bfloat16)


def projector(weight, frames, heads_here, shard_piece):
    model_width = weight.shape[0]
    flat_weight = weight.reshape(model_width, -1)
    row_block = shard_piece.reshape(-1, model_width)
    output = jnp.dot(row_block, flat_weight, preferred_element_type=jnp.float32).astype(
        jnp.bfloat16
    )
    return output.reshape(shard_piece.shape[0], frames, 3, heads_here, E)


def out_terms(mixed, weight, row_count):
    frames = mixed.shape[1]
    model_width = weight.shape[1]
    flat_rows = mixed.reshape(-1, mixed.shape[-1])
    return jnp.dot(flat_rows, weight, preferred_element_type=jnp.float32).reshape(
        row_count, frames, model_width
    )


def spatial_attend(rows_all):
    query_rows = rows_all[:, :, 0]
    key_rows = rows_all[:, :, 1]
    value_rows = rows_all[:, :, 2]
    scores = jnp.einsum(
        "pfhe,qfhe->fhpq", query_rows, key_rows, preferred_element_type=jnp.float32
    ) * (1.0 / math.sqrt(E))
    attn_weights = masked_softmax(scores, True)
    mixed = jnp.einsum(
        "fhpq,qfhe->pfhe", attn_weights, value_rows, preferred_element_type=jnp.float32
    ).astype(jnp.bfloat16)
    return mixed.reshape(mixed.shape[0], mixed.shape[1], -1)


def window_attend(query_rows, window, starts):
    frames = query_rows.shape[1]
    reach_span = window.shape[1] // frames
    position = lax.axis_index("tm")
    episodes = starts.shape[0]
    query_frame = position * frames + jnp.arange(frames, dtype=jnp.int32)
    key_frame = (position - reach_span + 1) * frames + jnp.arange(
        reach_span * frames, dtype=jnp.int32
    )
    query_episode = query_frame // SEQ
    key_episode = key_frame // SEQ
    episode_ids = jnp.arange(episodes, dtype=jnp.int32)
    query_start = jnp.sum(
        jnp.where(query_episode[:, None] == episode_ids[None, :], starts[None, :], 0), axis=1
    )
    query_pos = query_frame - query_episode * SEQ
    key_pos = key_frame[None, :] - query_episode[:, None] * SEQ
    allowed = (key_episode[None, :] == query_episode[:, None]) & (
        key_frame[None, :] <= query_frame[:, None]
    )
    allowed = allowed & ((key_pos >= query_start[:, None]) == (query_pos >= query_start)[:, None])
    key_rows = window[:, :, 0]
    value_rows = window[:, :, 1]
    scores = jnp.einsum(
        "pfhe,pkhe->phfk", query_rows, key_rows, preferred_element_type=jnp.float32
    ) * (1.0 / math.sqrt(E))
    attn_weights = masked_softmax(scores, allowed[None, None])
    return jnp.einsum(
        "phfk,pkhe->pfhe", attn_weights, value_rows, preferred_element_type=jnp.float32
    ).astype(jnp.bfloat16)


def local(
    stream,
    spatial_gain,
    spatial_qkv,
    spatial_out,
    temporal_gain,
    temporal_qkv,
    temporal_out,
    starts,
):
    local_patches, frames, model_width = stream.shape
    heads_here = spatial_qkv.shape[2] // E
    all_patches = local_patches * lax.axis_size("patch")
    spatial_normed = rms_norm(stream, spatial_gain)
    spatial_rows = projector(
        spatial_qkv, frames, heads_here, lax.all_gather(spatial_normed, "patch", axis=0, tiled=True)
    )
    spatial_mix = spatial_attend(spatial_rows)
    summed = lax.psum_scatter(
        out_terms(spatial_mix, spatial_out, local_patches * lax.axis_size("patch")).astype(
            jnp.bfloat16
        ),
        "patch",
        scatter_dimension=0,
        tiled=True,
    ).astype(jnp.float32)
    middle = (stream.astype(jnp.float32) + summed).astype(jnp.bfloat16)
    temporal_normed = rms_norm(middle, temporal_gain)
    temporal_rows = projector(
        temporal_qkv,
        frames,
        heads_here,
        lax.all_gather(temporal_normed, "patch", axis=0, tiled=True),
    )
    query_rows = temporal_rows[:, :, 0]
    reach_span = SEQ // frames
    own_pairs = temporal_rows[:, :, 1:]
    collected = []
    for offset in range(reach_span - 1, 0, -1):
        collected.append(passed_along(own_pairs, "tm", offset))
    window = jnp.concatenate(collected + [own_pairs], axis=1)
    temporal_mix = window_attend(query_rows, window, starts)
    temporal_mix = temporal_mix.reshape(all_patches, frames, -1)
    summed_time = lax.psum_scatter(
        out_terms(temporal_mix, temporal_out, local_patches * lax.axis_size("patch")).astype(
            jnp.bfloat16
        ),
        "patch",
        scatter_dimension=0,
        tiled=True,
    ).astype(jnp.float32)
    return (middle.astype(jnp.float32) + summed_time).astype(jnp.bfloat16)


def solution(mesh):
    placed = (
        P("patch", "tm", None),
        P(),
        P(None, None, "patch"),
        P("patch", None),
        P(),
        P(None, None, "patch"),
        P("patch", None),
        P(),
    )
    return jax.shard_map(
        local, mesh=mesh, in_specs=placed, out_specs=P("patch", "tm", None), check_vma=False
    )
```

profile of v0, /device:TPU:1, one launch (start us, length us, event | category | flops | bytes accessed | tf_op | source)
XLA Modules:
  0.0 887.6 jit_solution(2150005623111132847)
XLA Ops:
  10.4 4.7 copy.35
  15.1 54.0 %all-gather.3.cloned.1.call-done = bf16[256,4,2048]{2,0,1:T(8,128)(2,1)} async-done(((bf16[32,4,2048]{2,0,1:T(8,128)(2,1)}), bf16[256,4,2048]{2,0,1:T(8,128)(2,1)}) %all-gather.3.cloned.1.call-update) | async-done | bytes 4194320 | tf_op jit(solution)/shard_map/all_gather | solution.py:111
  69.1 7.4 copy.34
  76.5 6.9 reshape.207
  83.4 7.8 convolution_convert_fusion.3
  105.8 53.9 %reduce-scatter.3.cloned.1.call-done = bf16[32,4,2048]{2,0,1:T(8,128)(2,1)} async-done(((bf16[256,4,2048]{2,0,1:T(8,128)(2,1)}), bf16[32,4,2048]{2,0,1:T(8,128)(2,1)}) %reduce-scatter.3.cloned.1.call-update) | async-done | bytes 524304 | tf_op jit(solution)/shard_map/reduce_scatter | solution.py:114
  163.5 4.7 copy.42
  168.2 48.8 %all-gather.5.cloned.1.call-done = bf16[256,4,2048]{2,0,1:T(8,128)(2,1)} async-done(((bf16[32,4,2048]{2,0,1:T(8,128)(2,1)}), bf16[256,4,2048]{2,0,1:T(8,128)(2,1)}) %all-gather.5.cloned.1.call-update) | async-done | bytes 4194320 | tf_op jit(solution)/shard_map/all_gather | solution.py:128
  217.0 7.4 copy.41
  224.4 6.9 reshape.210
  231.3 7.8 convolution_convert_fusion.2
  239.1 3.4 reshape.212
  243.7 3.7 collective-permute-start.14
  250.6 3.4 collective-permute-start.12
  257.4 4.8 collective-permute-start.10
  262.2 5.6 collective-permute-done.14
  267.8 20.5 %collective-permute-start.9 = (bf16[256,4,2,2,128]{4,1,3,0,2:T(4,128)(2,1)S(1)}, bf16[256,4,2,2,128]{4,1,3,0,2:T(4,128)(2,1)S(1)}, u32[]{:S(2)}, u32[]{:S(2)}) collective-permute-start(bf16[256,4,2,2,128]{4,1,3,0,2:T(4,128)(2,1)S(1)} %copy.54), channel_id=1, source_target_pairs={{0,48},{8,56},{16,64},{24,72},{32,80},{40,88},{48,96},{56,104},{64... | collective-permute-start | bytes 3145736 | tf_op jit(solution)/shard_map/ppermute | solution.py:15
  290.3 13.0 %collective-permute-start.8 = (bf16[256,4,2,2,128]{4,1,3,0,2:T(4,128)(2,1)S(1)}, bf16[256,4,2,2,128]{4,1,3,0,2:T(4,128)(2,1)S(1)}, u32[]{:S(2)}, u32[]{:S(2)}) collective-permute-start(bf16[256,4,2,2,128]{4,1,3,0,2:T(4,128)(2,1)S(1)} %copy.54), channel_id=1, source_target_pairs={{0,56},{8,64},{16,72},{24,80},{32,88},{40,96},{48,104},{56,112},{6... | collective-permute-start | bytes 3145736 | tf_op jit(solution)/shard_map/ppermute | solution.py:15
  303.3 9.5 %collective-permute-done.12 = bf16[256,4,2,2,128]{4,1,3,0,2:T(4,128)(2,1)S(1)} collective-permute-done((bf16[256,4,2,2,128]{4,1,3,0,2:T(4,128)(2,1)S(1)}, bf16[256,4,2,2,128]{4,1,3,0,2:T(4,128)(2,1)S(1)}, u32[]{:S(2)}, u32[]{:S(2)}) %collective-permute-start.12) | collective-permute-done | bytes 1048608 | tf_op jit(solution)/shard_map/ppermute | solution.py:15
  312.7 32.5 %collective-permute-start.7 = (bf16[256,4,2,2,128]{4,1,3,0,2:T(4,128)(2,1)S(1)}, bf16[256,4,2,2,128]{4,1,3,0,2:T(4,128)(2,1)S(1)}, u32[]{:S(2)}, u32[]{:S(2)}) collective-permute-start(bf16[256,4,2,2,128]{4,1,3,0,2:T(4,128)(2,1)S(1)} %copy.54), channel_id=1, source_target_pairs={{0,64},{8,72},{16,80},{24,88},{32,96},{40,104},{48,112},{56,120},{... | collective-permute-start | bytes 3145736 | tf_op jit(solution)/shard_map/ppermute | solution.py:15
  345.3 42.3 %collective-permute-start.6 = (bf16[256,4,2,2,128]{4,1,3,0,2:T(4,128)(2,1)S(1)}, bf16[256,4,2,2,128]{4,1,3,0,2:T(4,128)(2,1)S(1)}, u32[]{:S(2)}, u32[]{:S(2)}) collective-permute-start(bf16[256,4,2,2,128]{4,1,3,0,2:T(4,128)(2,1)S(1)} %copy.54), channel_id=1, source_target_pairs={{0,72},{8,80},{16,88},{24,96},{32,104},{40,112},{48,120},{56,128},... | collective-permute-start | bytes 3145736 | tf_op jit(solution)/shard_map/ppermute | solution.py:15
  387.6 36.2 %collective-permute-start.5 = (bf16[256,4,2,2,128]{4,1,3,0,2:T(4,128)(2,1)S(1)}, bf16[256,4,2,2,128]{4,1,3,0,2:T(4,128)(2,1)S(1)}, u32[]{:S(2)}, u32[]{:S(2)}) collective-permute-start(bf16[256,4,2,2,128]{4,1,3,0,2:T(4,128)(2,1)S(1)} %copy.54), channel_id=1, source_target_pairs={{0,80},{8,88},{16,96},{24,104},{32,112},{40,120},{48,128},{56,136}... | collective-permute-start | bytes 3145736 | tf_op jit(solution)/shard_map/ppermute | solution.py:15
  423.8 23.4 %collective-permute-start.4 = (bf16[256,4,2,2,128]{4,1,3,0,2:T(4,128)(2,1)S(1)}, bf16[256,4,2,2,128]{4,1,3,0,2:T(4,128)(2,1)}, u32[]{:S(2)}, u32[]{:S(2)}) collective-permute-start(bf16[256,4,2,2,128]{4,1,3,0,2:T(4,128)(2,1)S(1)} %copy.54), channel_id=1, source_target_pairs={{0,88},{8,96},{16,104},{24,112},{32,120},{40,128},{48,136},{56,144... | collective-permute-start | bytes 3145736 | tf_op jit(solution)/shard_map/ppermute | solution.py:15
  447.2 22.2 %collective-permute-start.3 = (bf16[256,4,2,2,128]{4,1,3,0,2:T(4,128)(2,1)S(1)}, bf16[256,4,2,2,128]{4,1,3,0,2:T(4,128)(2,1)}, u32[]{:S(2)}, u32[]{:S(2)}) collective-permute-start(bf16[256,4,2,2,128]{4,1,3,0,2:T(4,128)(2,1)S(1)} %copy.54), channel_id=1, source_target_pairs={{0,96},{8,104},{16,112},{24,120},{32,128},{40,136},{48,144},{56,15... | collective-permute-start | bytes 3145736 | tf_op jit(solution)/shard_map/ppermute | solution.py:15
  469.4 21.8 %collective-permute-start.2 = (bf16[256,4,2,2,128]{4,1,3,0,2:T(4,128)(2,1)S(1)}, bf16[256,4,2,2,128]{4,1,3,0,2:T(4,128)(2,1)}, u32[]{:S(2)}, u32[]{:S(2)}) collective-permute-start(bf16[256,4,2,2,128]{4,1,3,0,2:T(4,128)(2,1)S(1)} %copy.54), channel_id=1, source_target_pairs={{0,104},{8,112},{16,120},{24,128},{32,136},{40,144},{48,152},{56,1... | collective-permute-start | bytes 3145736 | tf_op jit(solution)/shard_map/ppermute | solution.py:15
  491.2 22.3 %collective-permute-start.1 = (bf16[256,4,2,2,128]{4,1,3,0,2:T(4,128)(2,1)S(1)}, bf16[256,4,2,2,128]{4,1,3,0,2:T(4,128)(2,1)}, u32[]{:S(2)}, u32[]{:S(2)}) collective-permute-start(bf16[256,4,2,2,128]{4,1,3,0,2:T(4,128)(2,1)S(1)} %copy.54), channel_id=1, source_target_pairs={{0,112},{8,120},{16,128},{24,136},{32,144},{40,152},{48,160},{56,1... | collective-permute-start | bytes 3145736 | tf_op jit(solution)/shard_map/ppermute | solution.py:15
  513.5 48.5 %collective-permute-start = (bf16[256,4,2,2,128]{4,1,3,0,2:T(4,128)(2,1)S(1)}, bf16[256,4,2,2,128]{4,1,3,0,2:T(4,128)(2,1)}, u32[]{:S(2)}, u32[]{:S(2)}) collective-permute-start(bf16[256,4,2,2,128]{4,1,3,0,2:T(4,128)(2,1)S(1)} %copy.54), channel_id=1, source_target_pairs={{0,120},{8,128},{16,136},{24,144},{32,152},{40,160},{48,168},{56,1... | collective-permute-start | bytes 3145736 | tf_op jit(solution)/shard_map/ppermute | solution.py:15
  563.4 12.1 %collective-permute-done = bf16[256,4,2,2,128]{4,1,3,0,2:T(4,128)(2,1)} collective-permute-done((bf16[256,4,2,2,128]{4,1,3,0,2:T(4,128)(2,1)S(1)}, bf16[256,4,2,2,128]{4,1,3,0,2:T(4,128)(2,1)}, u32[]{:S(2)}, u32[]{:S(2)}) %collective-permute-start) | collective-permute-done | bytes 1048608 | tf_op jit(solution)/shard_map/ppermute | solution.py:15
  575.6 78.2 %concatenate.3 = bf16[256,64,2,2,128]{4,1,3,0,2:T(8,128)(2,1)} concatenate(bf16[256,4,2,2,128]{4,1,3,0,2:T(4,128)(2,1)} %collective-permute-done, bf16[256,4,2,2,128]{4,1,3,0,2:T(4,128)(2,1)} %collective-permute-done.1, bf16[256,4,2,2,128]{4,1,3,0,2:T(4,128)(2,1)} %collective-permute-done.2, bf16[256,4,2,2,128]{4,1,3,0,2:T(4,128)(2,1)} %collective-permute-done.3, ...), dimensions={1} | concatenate | bytes 33554432 | tf_op jit(solution)/shard_map/concatenate | solution.py:136
  653.8 9.1 %fusion.31 = (f32[256,2,4]{2,1,0:T(2,128)S(1)}, f32[256,2,4,64]{3,2,1,0:T(4,128)}) fusion(bf16[256,64,2,2,128]{4,1,3,0,2:T(8,128)(2,1)} %concatenate.3, bf16[256,4,1,2,128]{4,3,2,1,0:T(2,128)(2,1)S(1)} %copy-done.15, pred[4,64]{1,0:T(4,128)(4,1)S(1)} %fusion.26), kind=kOutput, calls=%fused_computation.67 | convolution fusion | flops 34078784 | bytes 9445632 | tf_op jit(solution)/shard_map/sub | solution.py:27
  662.8 6.0 fusion.9
  672.5 206.0 %reduce-scatter.5.cloned.1.call-done = bf16[32,4,2048]{2,0,1:T(8,128)(2,1)} async-done(((bf16[256,4,2048]{2,0,1:T(8,128)(2,1)}), bf16[32,4,2048]{2,0,1:T(8,128)(2,1)}) %reduce-scatter.5.cloned.1.call-update) | async-done | bytes 524304 | tf_op jit(solution)/shard_map/reduce_scatter | solution.py:139
  (83 shorter events, 39.5 us)
Async XLA Ops:
  6.5 95.8 %copy-start = (bf16[256,2048]{1,0:T(8,128)(2,1)S(1)}, bf16[256,2048]{1,0:T(8,128)(2,1)}, u32[]{:S(2)}) copy-start(bf16[256,2048]{1,0:T(8,128)(2,1)} %param.11) | copy-start | bytes 3145732
  6.5 62.5 %all-gather.3.cloned.1.call-start = ((), (), s32[]{:S(2)}) async-start(), calls=%async_computation.2 | async-start | bytes 4718592 | tf_op jit(solution)/shard_map/all_gather | solution.py:111
  10.3 149.4 %reduce-scatter.3.cloned.1.call-start = ((), (), s32[]{:S(2)}) async-start(), calls=%async_computation.3 | async-start | bytes 4718592 | tf_op jit(solution)/shard_map/reduce_scatter | solution.py:114
  105.6 111.4 %all-gather.5.cloned.1.call-start = ((), (), s32[]{:S(2)}) async-start(), calls=%async_computation.4 | async-start | bytes 4718592 | tf_op jit(solution)/shard_map/all_gather | solution.py:128
  163.4 715.0 %reduce-scatter.5.cloned.1.call-start = ((), (), s32[]{:S(2)}) async-start(), calls=%async_computation.5 | async-start | bytes 4718592 | tf_op jit(solution)/shard_map/reduce_scatter | solution.py:139
  239.1 323.0 %copy-start.17 = (s32[2]{0:T(128)S(1)}, s32[2]{0:T(128)}, u32[]{:S(2)}) copy-start(s32[2]{0:T(128)} %param.15) | copy-start | bytes 28
  243.7 24.1 %collective-permute-start.14 = (bf16[256,4,2,2,128]{4,1,3,0,2:T(4,128)(2,1)S(1)}, bf16[256,4,2,2,128]{4,1,3,0,2:T(4,128)(2,1)S(1)}, u32[]{:S(2)}, u32[]{:S(2)}) collective-permute-start(bf16[256,4,2,2,128]{4,1,3,0,2:T(4,128)(2,1)S(1)} %copy.54), channel_id=1, source_target_pairs={{0,8},{8,16},{16,24},{24,32},{32,40},{40,48},{48,56},{56,64},{64,7... | collective-permute-start | bytes 3145736 | tf_op jit(solution)/shard_map/ppermute | solution.py:15
  247.4 42.9 %collective-permute-start.13 = (bf16[256,4,2,2,128]{4,1,3,0,2:T(4,128)(2,1)S(1)}, bf16[256,4,2,2,128]{4,1,3,0,2:T(4,128)(2,1)S(1)}, u32[]{:S(2)}, u32[]{:S(2)}) collective-permute-start(bf16[256,4,2,2,128]{4,1,3,0,2:T(4,128)(2,1)S(1)} %copy.54), channel_id=1, source_target_pairs={{0,16},{8,24},{16,32},{24,40},{32,48},{40,56},{48,64},{56,72},{64,... | collective-permute-start | bytes 3145736 | tf_op jit(solution)/shard_map/ppermute | solution.py:15
  250.6 62.1 %collective-permute-start.12 = (bf16[256,4,2,2,128]{4,1,3,0,2:T(4,128)(2,1)S(1)}, bf16[256,4,2,2,128]{4,1,3,0,2:T(4,128)(2,1)S(1)}, u32[]{:S(2)}, u32[]{:S(2)}) collective-permute-start(bf16[256,4,2,2,128]{4,1,3,0,2:T(4,128)(2,1)S(1)} %copy.54), channel_id=1, source_target_pairs={{0,24},{8,32},{16,40},{24,48},{32,56},{40,64},{48,72},{56,80},{64,... | collective-permute-start | bytes 3145736 | tf_op jit(solution)/shard_map/ppermute | solution.py:15
  254.0 91.3 %collective-permute-start.11 = (bf16[256,4,2,2,128]{4,1,3,0,2:T(4,128)(2,1)S(1)}, bf16[256,4,2,2,128]{4,1,3,0,2:T(4,128)(2,1)S(1)}, u32[]{:S(2)}, u32[]{:S(2)}) collective-permute-start(bf16[256,4,2,2,128]{4,1,3,0,2:T(4,128)(2,1)S(1)} %copy.54), channel_id=1, source_target_pairs={{0,32},{8,40},{16,48},{24,56},{32,64},{40,72},{48,80},{56,88},{64,... | collective-permute-start | bytes 3145736 | tf_op jit(solution)/shard_map/ppermute | solution.py:15
  257.4 130.2 %collective-permute-start.10 = (bf16[256,4,2,2,128]{4,1,3,0,2:T(4,128)(2,1)S(1)}, bf16[256,4,2,2,128]{4,1,3,0,2:T(4,128)(2,1)S(1)}, u32[]{:S(2)}, u32[]{:S(2)}) collective-permute-start(bf16[256,4,2,2,128]{4,1,3,0,2:T(4,128)(2,1)S(1)} %copy.54), channel_id=1, source_target_pairs={{0,40},{8,48},{16,56},{24,64},{32,72},{40,80},{48,88},{56,96},{64,... | collective-permute-start | bytes 3145736 | tf_op jit(solution)/shard_map/ppermute | solution.py:15
  267.8 245.7 %copy-start.4 = (bf16[256,4,2,2,128]{4,1,3,0,2:T(4,128)(2,1)}, bf16[256,4,2,2,128]{4,1,3,0,2:T(4,128)(2,1)S(1)}, u32[]{:S(2)}) copy-start(bf16[256,4,2,2,128]{4,1,3,0,2:T(4,128)(2,1)S(1)} %collective-permute-done.14) | copy-start | bytes 3145732
  267.8 156.0 %collective-permute-start.9 = (bf16[256,4,2,2,128]{4,1,3,0,2:T(4,128)(2,1)S(1)}, bf16[256,4,2,2,128]{4,1,3,0,2:T(4,128)(2,1)S(1)}, u32[]{:S(2)}, u32[]{:S(2)}) collective-permute-start(bf16[256,4,2,2,128]{4,1,3,0,2:T(4,128)(2,1)S(1)} %copy.54), channel_id=1, source_target_pairs={{0,48},{8,56},{16,64},{24,72},{32,80},{40,88},{48,96},{56,104},{64... | collective-permute-start | bytes 3145736 | tf_op jit(solution)/shard_map/ppermute | solution.py:15
  290.3 271.7 %copy-start.5 = (bf16[256,4,2,2,128]{4,1,3,0,2:T(4,128)(2,1)}, bf16[256,4,2,2,128]{4,1,3,0,2:T(4,128)(2,1)S(1)}, u32[]{:S(2)}) copy-start(bf16[256,4,2,2,128]{4,1,3,0,2:T(4,128)(2,1)S(1)} %collective-permute-done.13) | copy-start | bytes 3145732
  290.3 156.9 %collective-permute-start.8 = (bf16[256,4,2,2,128]{4,1,3,0,2:T(4,128)(2,1)S(1)}, bf16[256,4,2,2,128]{4,1,3,0,2:T(4,128)(2,1)S(1)}, u32[]{:S(2)}, u32[]{:S(2)}) collective-permute-start(bf16[256,4,2,2,128]{4,1,3,0,2:T(4,128)(2,1)S(1)} %copy.54), channel_id=1, source_target_pairs={{0,56},{8,64},{16,72},{24,80},{32,88},{40,96},{48,104},{56,112},{6... | collective-permute-start | bytes 3145736 | tf_op jit(solution)/shard_map/ppermute | solution.py:15
  312.7 249.2 %copy-start.6 = (bf16[256,4,2,2,128]{4,1,3,0,2:T(4,128)(2,1)}, bf16[256,4,2,2,128]{4,1,3,0,2:T(4,128)(2,1)S(1)}, u32[]{:S(2)}) copy-start(bf16[256,4,2,2,128]{4,1,3,0,2:T(4,128)(2,1)S(1)} %collective-permute-done.12) | copy-start | bytes 3145732
  312.7 156.7 %collective-permute-start.7 = (bf16[256,4,2,2,128]{4,1,3,0,2:T(4,128)(2,1)S(1)}, bf16[256,4,2,2,128]{4,1,3,0,2:T(4,128)(2,1)S(1)}, u32[]{:S(2)}, u32[]{:S(2)}) collective-permute-start(bf16[256,4,2,2,128]{4,1,3,0,2:T(4,128)(2,1)S(1)} %copy.54), channel_id=1, source_target_pairs={{0,64},{8,72},{16,80},{24,88},{32,96},{40,104},{48,112},{56,120},{... | collective-permute-start | bytes 3145736 | tf_op jit(solution)/shard_map/ppermute | solution.py:15
  345.3 216.6 %copy-start.7 = (bf16[256,4,2,2,128]{4,1,3,0,2:T(4,128)(2,1)}, bf16[256,4,2,2,128]{4,1,3,0,2:T(4,128)(2,1)S(1)}, u32[]{:S(2)}) copy-start(bf16[256,4,2,2,128]{4,1,3,0,2:T(4,128)(2,1)S(1)} %collective-permute-done.11) | copy-start | bytes 3145732
  345.3 145.9 %collective-permute-start.6 = (bf16[256,4,2,2,128]{4,1,3,0,2:T(4,128)(2,1)S(1)}, bf16[256,4,2,2,128]{4,1,3,0,2:T(4,128)(2,1)S(1)}, u32[]{:S(2)}, u32[]{:S(2)}) collective-permute-start(bf16[256,4,2,2,128]{4,1,3,0,2:T(4,128)(2,1)S(1)} %copy.54), channel_id=1, source_target_pairs={{0,72},{8,80},{16,88},{24,96},{32,104},{40,112},{48,120},{56,128},... | collective-permute-start | bytes 3145736 | tf_op jit(solution)/shard_map/ppermute | solution.py:15
  387.6 174.3 %copy-start.8 = (bf16[256,4,2,2,128]{4,1,3,0,2:T(4,128)(2,1)}, bf16[256,4,2,2,128]{4,1,3,0,2:T(4,128)(2,1)S(1)}, u32[]{:S(2)}) copy-start(bf16[256,4,2,2,128]{4,1,3,0,2:T(4,128)(2,1)S(1)} %collective-permute-done.10) | copy-start | bytes 3145732
  387.6 125.9 %collective-permute-start.5 = (bf16[256,4,2,2,128]{4,1,3,0,2:T(4,128)(2,1)S(1)}, bf16[256,4,2,2,128]{4,1,3,0,2:T(4,128)(2,1)S(1)}, u32[]{:S(2)}, u32[]{:S(2)}) collective-permute-start(bf16[256,4,2,2,128]{4,1,3,0,2:T(4,128)(2,1)S(1)} %copy.54), channel_id=1, source_target_pairs={{0,80},{8,88},{16,96},{24,104},{32,112},{40,120},{48,128},{56,136}... | collective-permute-start | bytes 3145736 | tf_op jit(solution)/shard_map/ppermute | solution.py:15
  423.8 138.1 %copy-start.9 = (bf16[256,4,2,2,128]{4,1,3,0,2:T(4,128)(2,1)}, bf16[256,4,2,2,128]{4,1,3,0,2:T(4,128)(2,1)S(1)}, u32[]{:S(2)}) copy-start(bf16[256,4,2,2,128]{4,1,3,0,2:T(4,128)(2,1)S(1)} %collective-permute-done.9) | copy-start | bytes 3145732
  423.8 139.6 %collective-permute-start.4 = (bf16[256,4,2,2,128]{4,1,3,0,2:T(4,128)(2,1)S(1)}, bf16[256,4,2,2,128]{4,1,3,0,2:T(4,128)(2,1)}, u32[]{:S(2)}, u32[]{:S(2)}) collective-permute-start(bf16[256,4,2,2,128]{4,1,3,0,2:T(4,128)(2,1)S(1)} %copy.54), channel_id=1, source_target_pairs={{0,88},{8,96},{16,104},{24,112},{32,120},{40,128},{48,136},{56,144... | collective-permute-start | bytes 3145736 | tf_op jit(solution)/shard_map/ppermute | solution.py:15
  447.2 114.7 %copy-start.10 = (bf16[256,4,2,2,128]{4,1,3,0,2:T(4,128)(2,1)}, bf16[256,4,2,2,128]{4,1,3,0,2:T(4,128)(2,1)S(1)}, u32[]{:S(2)}) copy-start(bf16[256,4,2,2,128]{4,1,3,0,2:T(4,128)(2,1)S(1)} %collective-permute-done.8) | copy-start | bytes 3145732
  447.2 116.2 %collective-permute-start.3 = (bf16[256,4,2,2,128]{4,1,3,0,2:T(4,128)(2,1)S(1)}, bf16[256,4,2,2,128]{4,1,3,0,2:T(4,128)(2,1)}, u32[]{:S(2)}, u32[]{:S(2)}) collective-permute-start(bf16[256,4,2,2,128]{4,1,3,0,2:T(4,128)(2,1)S(1)} %copy.54), channel_id=1, source_target_pairs={{0,96},{8,104},{16,112},{24,120},{32,128},{40,136},{48,144},{56,15... | collective-permute-start | bytes 3145736 | tf_op jit(solution)/shard_map/ppermute | solution.py:15
  469.4 92.5 %copy-start.11 = (bf16[256,4,2,2,128]{4,1,3,0,2:T(4,128)(2,1)}, bf16[256,4,2,2,128]{4,1,3,0,2:T(4,128)(2,1)S(1)}, u32[]{:S(2)}) copy-start(bf16[256,4,2,2,128]{4,1,3,0,2:T(4,128)(2,1)S(1)} %collective-permute-done.7) | copy-start | bytes 3145732
  469.4 94.0 %collective-permute-start.2 = (bf16[256,4,2,2,128]{4,1,3,0,2:T(4,128)(2,1)S(1)}, bf16[256,4,2,2,128]{4,1,3,0,2:T(4,128)(2,1)}, u32[]{:S(2)}, u32[]{:S(2)}) collective-permute-start(bf16[256,4,2,2,128]{4,1,3,0,2:T(4,128)(2,1)S(1)} %copy.54), channel_id=1, source_target_pairs={{0,104},{8,112},{16,120},{24,128},{32,136},{40,144},{48,152},{56,1... | collective-permute-start | bytes 3145736 | tf_op jit(solution)/shard_map/ppermute | solution.py:15
  491.2 72.2 %collective-permute-start.1 = (bf16[256,4,2,2,128]{4,1,3,0,2:T(4,128)(2,1)S(1)}, bf16[256,4,2,2,128]{4,1,3,0,2:T(4,128)(2,1)}, u32[]{:S(2)}, u32[]{:S(2)}) collective-permute-start(bf16[256,4,2,2,128]{4,1,3,0,2:T(4,128)(2,1)S(1)} %copy.54), channel_id=1, source_target_pairs={{0,112},{8,120},{16,128},{24,136},{32,144},{40,152},{48,160},{56,1... | collective-permute-start | bytes 3145736 | tf_op jit(solution)/shard_map/ppermute | solution.py:15
  513.5 62.1 %collective-permute-start = (bf16[256,4,2,2,128]{4,1,3,0,2:T(4,128)(2,1)S(1)}, bf16[256,4,2,2,128]{4,1,3,0,2:T(4,128)(2,1)}, u32[]{:S(2)}, u32[]{:S(2)}) collective-permute-start(bf16[256,4,2,2,128]{4,1,3,0,2:T(4,128)(2,1)S(1)} %copy.54), channel_id=1, source_target_pairs={{0,120},{8,128},{16,136},{24,144},{32,152},{40,160},{48,168},{56,1... | collective-permute-start | bytes 3145736 | tf_op jit(solution)/shard_map/ppermute | solution.py:15
  563.4 90.4 %copy-start.15 = (bf16[256,4,1,2,128]{4,3,2,1,0:T(2,128)(2,1)S(1)}, bf16[256,4,1,2,128]{4,3,2,1,0:T(2,128)(2,1)}, u32[]{:S(2)}) copy-start(bf16[256,4,1,2,128]{4,3,2,1,0:T(2,128)(2,1)} %slice.33) | copy-start | bytes 1572868
  672.4 206.0 %copy-start.3 = (bf16[32,4,2048]{2,0,1:T(8,128)(2,1)S(1)}, bf16[32,4,2048]{2,0,1:T(8,128)(2,1)}, u32[]{:S(2)}) copy-start(bf16[32,4,2048]{2,0,1:T(8,128)(2,1)} %reduce-scatter.3.cloned.1.call-done) | copy-start | bytes 1572868
  672.4 208.6 %copy-start.1 = (bf16[256,2048]{1,0:T(8,128)(2,1)S(1)}, bf16[256,2048]{1,0:T(8,128)(2,1)}, u32[]{:S(2)}) copy-start(bf16[256,2048]{1,0:T(8,128)(2,1)} %param.11) | copy-start | bytes 3145732
  (5 other events, 235.4 us)
Sparse Core Ops, SparseCore 0:
  10.4 58.6 all-gather.2
  105.7 53.9 reduce-scatter.2
  163.5 53.4 all-gather.4
  672.6 205.8 reduce-scatter.4
where the time goes:
time: 894 us; the launch traced here: 888 us
  waiting for transfers between devices  392 us (44%)
  starting transfers between devices  301 us (34%)
  local copies, waits for them, and re-layouts  129 us (14%)
  matrix products  42.4 us (5%)
  between operations  13.5 us (2%)
  other arithmetic  9.07 us (1%)
    ppermute x15, starting transfers between devices, passed_along(): lax.ppermute(value, axis, [(source, source + steps) for source in range(f...  301 us
    reduce_scatter x1, waiting for transfers between devices, local(): lax.psum_scatter(out_terms(temporal_mix, temporal_out, local_patches * la...  206 us
    concatenate x1, local copies, waits for them, and re-layouts, local(): window = jnp.concatenate(collected + [own_pairs], axis=1)  78.2 us
    all_gather x1, waiting for transfers between devices, local(): lax.all_gather(spatial_normed, 'patch', axis=0, tiled=True)  54 us
    reduce_scatter x1, waiting for transfers between devices, local(): lax.psum_scatter(out_terms(spatial_mix, spatial_out, local_patches * lax....  53.9 us
    all_gather x1, waiting for transfers between devices, local(): lax.all_gather(temporal_normed, 'patch', axis=0, tiled=True)  48.8 us
    ppermute x15, waiting for transfers between devices, passed_along(): lax.ppermute(value, axis, [(source, source + steps) for source in range(f...  29.1 us
  transfers between devices with their start and end apart: 19, of which 8 were waited for; matrix products, arithmetic and copies ran while one was open for 1% of the time, Pallas kernels for 0%

commit v1 on v0

v1 whole, which is shorter than its diff:
```python
import functools
import math

import jax
import jax.numpy as jnp
from jax import lax
from jax.experimental import pallas as pl
from jax.experimental.pallas import tpu as pltpu
from jax.sharding import Mesh
from jax.sharding import PartitionSpec as P

E = 128
SEQ = 64
SCALE = 1.0 / math.sqrt(E)
BF = jnp.bfloat16
F32 = jnp.float32
NZ = 8
VMEM_LIMIT = 56 * 1024 * 1024
OFFSETS = (0, -1, 1, -2, 2, -3, 3, 4)


def params():
    return pltpu.CompilerParams(vmem_limit_bytes=VMEM_LIMIT)


def vmem():
    return pl.BlockSpec(memory_space=pltpu.VMEM)


def smem():
    return pl.BlockSpec(memory_space=pltpu.SMEM)


def normed(values, gain):
    scaled = values * lax.rsqrt(jnp.mean(values * values, axis=-1, keepdims=True) + 1e-05)
    return (scaled * gain).astype(BF)


def softmax(scores):
    shifted = jnp.exp(scores - jnp.max(scores, axis=-1, keepdims=True))
    return (shifted / jnp.sum(shifted, axis=-1, keepdims=True)).astype(BF)


def dot(a, b):
    return jnp.dot(a, b, preferred_element_type=F32)


def dot_t(a, b):
    return lax.dot_general(a, b, (((1,), (1,)), ((), ())), preferred_element_type=F32)


def norm_kernel(x_ref, gain_ref, a_ref, b_ref):
    gain = gain_ref[...]
    half = a_ref.shape[0]
    a_ref[...] = normed(x_ref[:half].astype(F32), gain)
    b_ref[...] = normed(x_ref[half:].astype(F32), gain)


def norm_rows(rows, gain):
    count, width = rows.shape
    half = jax.ShapeDtypeStruct((count // 2, width), BF)
    return pl.pallas_call(
        norm_kernel,
        out_shape=(half, half),
        in_specs=[vmem(), vmem()],
        out_specs=(vmem(), vmem()),
        compiler_params=params(),
        cost_estimate=pl.CostEstimate(
            flops=4 * count * width, bytes_accessed=4 * count * width, transcendentals=0
        ),
    )(rows, gain)


def spatial_kernel(place_ref, weight_ref, *refs):
    out_ref = refs[-1]
    pieces = refs[:-1]
    place = place_ref[0]
    for frame in range(4):
        part, inner = frame // 2, frame % 2
        rows = jnp.concatenate(
            [pieces[2 * k + part][32 * inner : 32 * inner + 32, :] for k in range(NZ)], axis=0
        )
        qkv = dot(rows, weight_ref[...]).astype(BF)
        for head in range(2):
            low = head * E
            query = qkv[:, low : low + E]
            key = qkv[:, 256 + low : 256 + low + E]
            value = qkv[:, 512 + low : 512 + low + E]
            weights = softmax(dot_t(query, key) * SCALE)
            mixed = dot(weights, value).astype(BF)
            for k in range(NZ):
                target = lax.rem(place + (OFFSETS[k] + NZ), NZ)
                out_ref[target, 32 * frame : 32 * frame + 32, low : low + E] = mixed[
                    32 * k : 32 * k + 32
                ]


def spatial_attend(place, weight, pieces):
    return pl.pallas_call(
        spatial_kernel,
        out_shape=jax.ShapeDtypeStruct((NZ, 128, 256), BF),
        in_specs=[smem(), vmem()] + [vmem()] * len(pieces),
        out_specs=vmem(),
        compiler_params=params(),
        cost_estimate=pl.CostEstimate(
            flops=2 * 1024 * 2048 * 768 * 2, bytes_accessed=8 << 20, transcendentals=8 * 65536
        ),
    )(place, weight, *pieces)


def middle_kernel(mix_ref, weight_ref, rows_ref, gain_ref, middle_ref, send_ref, total):
    step = pl.program_id(0)
    mix = jnp.concatenate([mix_ref[k] for k in range(NZ)], axis=1)
    blocks = weight_ref.shape[0]
    weight = jnp.concatenate([weight_ref[k] for k in range(blocks)], axis=1)
    width = blocks * E
    total[:, pl.ds(pl.multiple_of(step * width, width), width)] = dot(mix, weight)

    @pl.when(step == pl.num_programs(0) - 1)
    def _():
        middle = (total[...] + rows_ref[...].astype(F32)).astype(BF)
        middle_ref[...] = middle
        values = middle.astype(F32)
        scaled = values * lax.rsqrt(jnp.mean(values * values, axis=-1, keepdims=True) + 1e-05)
        scaled = scaled * gain_ref[...]
        for group in range(4):
            chunk = jnp.concatenate(
                [scaled[32 * f + 8 * group : 32 * f + 8 * group + 8] for f in range(4)], axis=0
            ).astype(BF)
            for y in range(4):
                send_ref[(group // 2) * 8 + y * 2 + group % 2] = chunk


def middle_rows(mix, weight, rows, gain):
    steps = 4
    width = rows.shape[1]
    return pl.pallas_call(
        middle_kernel,
        grid=(steps,),
        out_shape=(
            jax.ShapeDtypeStruct((128, width), BF),
            jax.ShapeDtypeStruct((16, 32, width), BF),
        ),
        in_specs=[
            pl.BlockSpec((NZ, 128, 256), lambda i: (0, 0, 0)),
            pl.BlockSpec((16 // steps, 2048, E), lambda i: (i, 0, 0)),
            pl.BlockSpec((128, width), lambda i: (0, 0)),
            pl.BlockSpec((1, width), lambda i: (0, 0)),
        ],
        out_specs=(
            pl.BlockSpec((128, width), lambda i: (0, 0)),
            pl.BlockSpec((16, 32, width), lambda i: (0, 0, 0)),
        ),
        scratch_shapes=[pltpu.VMEM((128, width), F32)],
        compiler_params=params(),
        cost_estimate=pl.CostEstimate(
            flops=2 * 128 * 2048 * 2048, bytes_accessed=12 << 20, transcendentals=0
        ),
    )(mix, weight, rows, gain)


def temporal_kernel(start_ref, rows_ref, weight_ref, out_ref, qkv, mix, total):
    step = pl.program_id(0)
    kind = lax.rem(step, 4)
    rows_count = rows_ref.shape[0]

    @pl.when(kind < 3)
    def _():
        weight = weight_ref[:, 0].reshape(2048, 256)
        part = dot(rows_ref[...], weight).astype(BF).astype(F32)
        qkv[2 * kind] = part[:, :E]
        qkv[2 * kind + 1] = part[:, E:]

    @pl.when(kind == 3)
    def _():
        start = start_ref[0]
        late = lax.broadcasted_iota(jnp.int32, (SEQ, SEQ), 0)
        early = lax.broadcasted_iota(jnp.int32, (SEQ, SEQ), 1)
        allowed = (early <= late) & ((early >= start) == (late >= start))
        for head in range(2):
            for patch in range(8):
                frames = pl.ds(patch, SEQ, stride=8)
                query = qkv[0 + head, frames, :].astype(BF)
                key = qkv[2 + head, frames, :].astype(BF)
                value = qkv[4 + head, frames, :].astype(BF)
                scores = jnp.where(allowed, dot_t(query, key) * SCALE, -1e30)
                mix[head, frames, :] = dot(softmax(scores), value)
        mixed = jnp.concatenate([mix[0], mix[1]], axis=1).astype(BF)
        for block in range(8):
            cols = slice(256 * block, 256 * block + 256)
            part = dot(mixed, weight_ref[block, 0])

            @pl.when(step == 3)
            def _():
                total[:, cols] = part

            @pl.when(step == 7)
            def _():
                out_ref[:, cols] = (total[:, cols] + part).astype(BF)


def temporal_attend(start, rows, weight):
    count, width = rows.shape
    return pl.pallas_call(
        temporal_kernel,
        grid=(8,),
        out_shape=jax.ShapeDtypeStruct((count, width), BF),
        in_specs=[
            smem(),
            pl.BlockSpec((count, width), lambda i: (0, 0)),
            pl.BlockSpec((8, 1, 256, 256), lambda i: (0, i, 0, 0)),
        ],
        out_specs=pl.BlockSpec((count, width), lambda i: (0, 0)),
        scratch_shapes=[
            pltpu.VMEM((6, count, E), F32),
            pltpu.VMEM((2, count, E), F32),
            pltpu.VMEM((count, width), F32),
        ],
        compiler_params=params(),
        cost_estimate=pl.CostEstimate(
            flops=2 * 512 * 2048 * 2048, bytes_accessed=14 << 20, transcendentals=131072
        ),
    )(start, rows, weight)


def shifted(value, axis, step):
    count = lax.axis_size(axis)
    return lax.ppermute(value, axis, [(i, (i + step) % count) for i in range(count)])


def gathered_rows(chunks):
    up, down = list(chunks), list(chunks)
    pieces = {0: list(chunks)}
    for step in (1, 2, 3):
        up = [shifted(value, "z", 1) for value in up]
        down = [shifted(value, "z", -1) for value in down]
        pieces[-step], pieces[step] = up, down
    pieces[4] = [shifted(up[0], "z", 1), shifted(down[1], "z", -1)]
    return [value for offset in OFFSETS for value in pieces[offset]]


def local(stream, spatial_gain, spatial_qkv, spatial_out, temporal_gain, temporal_qkv, temporal_out, starts):
    patches, frames, width = stream.shape
    w, xl, y, c, z = (lax.axis_index(name) for name in ("w", "xl", "y", "c", "z"))

    rows = jnp.transpose(stream, (1, 0, 2)).reshape(frames * patches, width)
    chunks = norm_rows(rows, spatial_gain.reshape(1, width))
    pieces = gathered_rows(chunks)

    column = (w * 2 + xl) * 4 + y
    share = lax.dynamic_slice(spatial_out, (0, column * E), (256, E))
    parts = []
    for k in range(4):
        pairs = [
            (a * 8 + b, (b // 4) * 8 + (b + 4 * a + k) % 8) for a in range(2) for b in range(8)
        ]
        parts.append(lax.ppermute(share, ("c", "z"), pairs))
    ring = jnp.stack([parts[0], parts[3], parts[2], parts[1]] * 2)
    share = lax.dynamic_slice(ring, (lax.rem(8 - z, 4), 0, 0), (4, 256, E)).reshape(1024, E)
    whole_out = lax.all_gather(share, ("w", "xl", "y", "c"), axis=0, tiled=True)
    whole_out = whole_out.reshape(16, 2048, E)

    eighth = (w * 2 + xl) * 2 + c
    qkv_rows = lax.dynamic_slice(temporal_qkv, (eighth * 256, 0, 0), (256, 3, 256))
    out_cols = lax.dynamic_slice(temporal_out, (0, eighth * 256), (256, 256))
    share = jnp.concatenate([jnp.transpose(qkv_rows, (1, 0, 2)), out_cols[None]], axis=0)
    got = []
    for k in range(8):
        pairs = []
        for a in range(4):
            for b in range(8):
                order = a * 2 + b % 2
                pairs.append((a * 8 + b, (b // 2) * 8 + (order + k) % 8))
        low = 64 * (k // 2)
        got.append(lax.ppermute(share[:, low : low + 64], ("y", "z"), pairs))
    even = jnp.concatenate(got[0::2], axis=1)
    odd = jnp.concatenate(got[1::2], axis=1)
    swap = lax.rem(z, 2) == 1
    share = jnp.concatenate([jnp.where(swap, odd, even), jnp.where(swap, even, odd)], axis=0)
    quarter = lax.all_gather(share[None], ("w", "xl", "c"), axis=0, tiled=True)

    mix = spatial_attend(z.reshape(1), spatial_qkv.reshape(width, -1), pieces)
    mix = lax.all_to_all(mix, "z", 0, 0, tiled=True)
    middle, send = middle_rows(mix, whole_out, rows, temporal_gain.reshape(1, width))

    window = lax.all_to_all(send, ("xl", "y", "c"), 0, 0, tiled=True)
    start = lax.dynamic_slice(starts, (w,), (1,))
    partial = temporal_attend(start, window.reshape(512, width), quarter)
    back = lax.all_to_all(partial.reshape(16, 32, width), ("xl", "y", "c"), 0, 0, tiled=True)
    summed = jnp.sum(back.reshape(2, 4, 2, 4, 8, width).astype(F32), axis=1)
    out = middle.reshape(4, 2, 2, 8, width).astype(F32) + jnp.transpose(summed, (2, 0, 1, 3, 4))
    out = out.astype(BF).reshape(frames, patches, width)
    return jnp.transpose(out, (1, 0, 2))


def solution(mesh):
    names = ("w", "xl", "y", "c", "z")
    fine = Mesh(mesh.devices.reshape(2, 2, 4, 2, NZ), names)
    tm = ("w", "xl", "y", "c")
    placed = (
        P("z", tm, None),
        P(),
        P(None, None, "z"),
        P("z", None),
        P(),
        P(None, None, "z"),
        P("z", None),
        P(),
    )
    return jax.shard_map(
        local, mesh=fine, in_specs=placed, out_specs=P("z", tm, None), check_vma=False
    )
```

time: 894 us -> 262 us (0.29)
  waiting for transfers between devices: 392 us -> 63.3 us
  starting transfers between devices: 301 us -> 67.2 us
  local copies, waits for them, and re-layouts: 129 us -> 18.3 us
  blocking collectives: 0 us -> 51.4 us
  Pallas kernels: 0 us -> 44.9 us
  matrix products: 42.4 us -> 0 us
    reduce_scatter x2 -> x0, waiting for transfers between devices: 260 us -> none  [the longest x1 206 us: local(): lax.psum_scatter(out_terms(temporal_mix, temporal_out, local_patches * la...]
    ppermute x15 -> x26, starting transfers between devices: 301 us -> 54.2 us  [the longest x8 19.8 us: local(): got.append(lax.ppermute(share[:, low:low + 64], ('y', 'z'), pairs))]
    all_gather x2, waiting for transfers between devices: 103 us -> 0.01 us  [the longest x1 0.01 us: local(): quarter = lax.all_gather(share[None], ('w', 'xl', 'c'), axis=0, tiled=True)]
    concatenate x1 -> x2, local copies, waits for them, and re-layouts: 78.2 us -> 0.02 us  [the longest x1 0.01 us: local(): odd = jnp.concatenate(got[1::2], axis=1)]
    all_to_all x0 -> x2, blocking collectives: none -> 51.4 us  [the longest x1 33.1 us: local(): lax.all_to_all(partial.reshape(16, 32, width), ('xl', 'y', 'c'), 0, 0, ti...]
    pallas_call x0 -> x4, Pallas kernels: none -> 44.9 us  [the longest x1 24.9 us: temporal_attend(): pl.pallas_call(temporal_kernel, grid=(8,), out_shape=jax.ShapeDtypeStruct...]
    dot_general x6 -> x0, matrix products: 30 us -> none  [the longest x2 15.6 us: projector(): jnp.dot(row_block, flat_weight, preferred_element_type=jnp.float32)]
    all_to_all x0 -> x1, waiting for transfers between devices: none -> 27.5 us  [local(): window = lax.all_to_all(send, ('xl', 'y', 'c'), 0, 0, tiled=True)]
  transfers between devices with their start and end apart: 19 -> 29, of which waited for: 8 -> 19; matrix products, arithmetic and copies ran while one was open for 1% -> 7% of each run, Pallas kernels for 0% -> 8%
where the time goes in v1:
time: 262 us; the launch traced here: 261 us
  starting transfers between devices  67.2 us (26%)
  waiting for transfers between devices  63.3 us (24%)
  blocking collectives  51.4 us (20%)
  Pallas kernels  44.9 us (17%)
  local copies, waits for them, and re-layouts  18.3 us (7%)
  between operations  13.6 us (5%)
    all_to_all x1, blocking collectives, local(): lax.all_to_all(partial.reshape(16, 32, width), ('xl', 'y', 'c'), 0, 0, ti...  33.1 us
    all_to_all x1, waiting for transfers between devices, local(): window = lax.all_to_all(send, ('xl', 'y', 'c'), 0, 0, tiled=True)  27.5 us
    pallas_call x1, Pallas kernels, temporal_attend(): pl.pallas_call(temporal_kernel, grid=(8,), out_shape=jax.ShapeDtypeStruct...  24.9 us
    ppermute x8, starting transfers between devices, local(): got.append(lax.ppermute(share[:, low:low + 64], ('y', 'z'), pairs))  19.8 us
    ppermute x14, waiting for transfers between devices, shifted(): lax.ppermute(value, axis, [(i, (i + step) % count) for i in range(count)])  19.5 us
    ppermute x14, starting transfers between devices, shifted(): lax.ppermute(value, axis, [(i, (i + step) % count) for i in range(count)])  19.4 us
    all_to_all x1, blocking collectives, local(): mix = lax.all_to_all(mix, 'z', 0, 0, tiled=True)  18.3 us
    ppermute x4, starting transfers between devices, local(): parts.append(lax.ppermute(share, ('c', 'z'), pairs))  15 us
  transfers between devices with their start and end apart: 29, of which 19 were waited for; matrix products, arithmetic and copies ran while one was open for 7% of the time, Pallas kernels for 8%

profile of v1, /device:TPU:1, one launch (start us, length us, event | category | flops | bytes accessed | tf_op | source)
XLA Modules:
  0.0 261.0 jit_solution(14790344861858783629)
XLA Ops:
  7.5 10.2 %collective-permute-start.14 = (bf16[256,128]{1,0:T(8,128)(2,1)S(1)}, bf16[256,128]{1,0:T(8,128)(2,1)S(1)}, u32[]{:S(2)}, u32[]{:S(2)}) collective-permute-start(bf16[256,128]{1,0:T(8,128)(2,1)S(1)} %constant_dynamic-slice_fusion.1), channel_id=1, source_target_pairs={{0,0},{1,1},{2,2},{3,3},{4,12},{5,13},{6,14},{7,15},{8,4},{9,5},{1... | collective-permute-start | bytes 196616 | tf_op jit(solution)/shard_map/ppermute | solution.py:257
  17.8 4.3 %collective-permute-start.16 = (bf16[256,128]{1,0:T(8,128)(2,1)S(1)}, bf16[256,128]{1,0:T(8,128)(2,1)S(1)}, u32[]{:S(2)}, u32[]{:S(2)}) collective-permute-start(bf16[256,128]{1,0:T(8,128)(2,1)S(1)} %constant_dynamic-slice_fusion.1), channel_id=1, source_target_pairs={{0,2},{1,3},{2,4},{3,5},{4,14},{5,15},{6,8},{7,9},{8,6},{9,7},{10,... | collective-permute-start | bytes 196616 | tf_op jit(solution)/shard_map/ppermute | solution.py:257
  22.6 2.3 collective-permute-done.15
  24.9 1.3 collective-permute-done.16
  29.8 1.9 collective-permute-start.18
  31.7 2.2 collective-permute-start.22
  33.8 2.9 %collective-permute-start.19 = (bf16[4,64,256]{2,1,0:T(8,128)(2,1)}, bf16[4,64,256]{2,1,0:T(8,128)(2,1)S(1)}, u32[]{:S(2)}, u32[]{:S(2)}) collective-permute-start(bf16[4,64,256]{2,1,0:T(8,128)(2,1)} %get-tuple-element.17), channel_id=1, source_target_pairs={{0,3},{1,4},{2,19},{3,20},{4,35},{5,36},{6,51},{7,52},{16,5},{17,6... | collective-permute-start | bytes 393224 | tf_op jit(solution)/shard_map/ppermute | solution.py:275
  36.8 7.2 %collective-permute-start.20 = (bf16[4,64,256]{2,1,0:T(8,128)(2,1)}, bf16[4,64,256]{2,1,0:T(8,128)(2,1)S(1)}, u32[]{:S(2)}, u32[]{:S(2)}) collective-permute-start(bf16[4,64,256]{2,1,0:T(8,128)(2,1)} %get-tuple-element.18), channel_id=1, source_target_pairs={{0,5},{1,6},{2,21},{3,22},{4,37},{5,38},{6,53},{7,54},{16,7},{17,0... | collective-permute-start | bytes 393224 | tf_op jit(solution)/shard_map/ppermute | solution.py:275
  44.4 4.2 %collective-permute-start.24 = (bf16[4,64,256]{2,1,0:T(8,128)(2,1)}, bf16[4,64,256]{2,1,0:T(8,128)(2,1)S(1)}, u32[]{:S(2)}, u32[]{:S(2)}) collective-permute-start(bf16[4,64,256]{2,1,0:T(8,128)(2,1)} %get-tuple-element.18), channel_id=1, source_target_pairs={{0,4},{1,5},{2,20},{3,21},{4,36},{5,37},{6,52},{7,53},{16,6},{17,7... | collective-permute-start | bytes 393224 | tf_op jit(solution)/shard_map/ppermute | solution.py:275
  49.5 1.5 collective-permute-start.21
  51.9 3.9 %collective-permute-done.19 = bf16[4,64,256]{2,1,0:T(8,128)(2,1)S(1)} collective-permute-done((bf16[4,64,256]{2,1,0:T(8,128)(2,1)}, bf16[4,64,256]{2,1,0:T(8,128)(2,1)S(1)}, u32[]{:S(2)}, u32[]{:S(2)}) %collective-permute-start.19) | collective-permute-done | bytes 131104 | tf_op jit(solution)/shard_map/ppermute | solution.py:275
  55.8 4.8 %collective-permute-done.20 = bf16[4,64,256]{2,1,0:T(8,128)(2,1)S(1)} collective-permute-done((bf16[4,64,256]{2,1,0:T(8,128)(2,1)}, bf16[4,64,256]{2,1,0:T(8,128)(2,1)S(1)}, u32[]{:S(2)}, u32[]{:S(2)}) %collective-permute-start.20) | collective-permute-done | bytes 131104 | tf_op jit(solution)/shard_map/ppermute | solution.py:275
  60.8 2.5 collective-permute-done.25
  64.4 2.1 copy.21
  66.6 2.1 shard_map.82
  68.6 4.1 %collective-permute-start = (bf16[64,2048]{1,0:T(8,128)(2,1)}, bf16[64,2048]{1,0:T(8,128)(2,1)S(1)}, u32[]{:S(2)}, u32[]{:S(2)}) collective-permute-start(bf16[64,2048]{1,0:T(8,128)(2,1)} %get-tuple-element.9.refs_0_), channel_id=1, source_target_pairs={{0,1},{1,2},{2,3},{3,4},{4,5},{5,6},{6,7},{7,0},{8,9},{9,10},{10,1... | collective-permute-start | bytes 786440 | tf_op jit(solution)/shard_map/ppermute | solution.py:228
  72.7 3.0 %collective-permute-start.3 = (bf16[64,2048]{1,0:T(8,128)(2,1)}, bf16[64,2048]{1,0:T(8,128)(2,1)S(1)}, u32[]{:S(2)}, u32[]{:S(2)}) collective-permute-start(bf16[64,2048]{1,0:T(8,128)(2,1)} %get-tuple-element.10.refs_1_), channel_id=1, source_target_pairs={{0,7},{1,0},{2,1},{3,2},{4,3},{5,4},{6,5},{7,6},{8,15},{9,8},{10,9... | collective-permute-start | bytes 786440 | tf_op jit(solution)/shard_map/ppermute | solution.py:228
  75.7 2.3 collective-permute-start.1
  78.4 3.4 %collective-permute-done.refs_2_ = bf16[64,2048]{1,0:T(8,128)(2,1)S(1)} collective-permute-done((bf16[64,2048]{1,0:T(8,128)(2,1)}, bf16[64,2048]{1,0:T(8,128)(2,1)S(1)}, u32[]{:S(2)}, u32[]{:S(2)}) %collective-permute-start) | collective-permute-done | bytes 262176 | tf_op jit(solution)/shard_map/ppermute | solution.py:228
  84.5 2.9 %collective-permute-done.1.refs_3_ = bf16[64,2048]{1,0:T(8,128)(2,1)S(1)} collective-permute-done((bf16[64,2048]{1,0:T(8,128)(2,1)}, bf16[64,2048]{1,0:T(8,128)(2,1)S(1)}, u32[]{:S(2)}, u32[]{:S(2)}) %collective-permute-start.1) | collective-permute-done | bytes 262176 | tf_op jit(solution)/shard_map/ppermute | solution.py:228
  90.1 2.8 %collective-permute-done.4.refs_6_ = bf16[64,2048]{1,0:T(8,128)(2,1)S(1)} collective-permute-done((bf16[64,2048]{1,0:T(8,128)(2,1)S(1)}, bf16[64,2048]{1,0:T(8,128)(2,1)S(1)}, u32[]{:S(2)}, u32[]{:S(2)}) %collective-permute-start.4) | collective-permute-done | bytes 262176 | tf_op jit(solution)/shard_map/ppermute | solution.py:228
  95.7 3.0 %collective-permute-done.5.refs_7_ = bf16[64,2048]{1,0:T(8,128)(2,1)} collective-permute-done((bf16[64,2048]{1,0:T(8,128)(2,1)S(1)}, bf16[64,2048]{1,0:T(8,128)(2,1)}, u32[]{:S(2)}, u32[]{:S(2)}) %collective-permute-start.5) | collective-permute-done | bytes 262176 | tf_op jit(solution)/shard_map/ppermute | solution.py:228
  101.3 2.9 %collective-permute-done.8.refs_10_ = bf16[64,2048]{1,0:T(8,128)(2,1)} collective-permute-done((bf16[64,2048]{1,0:T(8,128)(2,1)S(1)}, bf16[64,2048]{1,0:T(8,128)(2,1)}, u32[]{:S(2)}, u32[]{:S(2)}) %collective-permute-start.8) | collective-permute-done | bytes 262176 | tf_op jit(solution)/shard_map/ppermute | solution.py:228
  107.0 4.9 %copy.20 = bf16[2048,3,256]{0,2,1:T(8,128)(2,1)} copy(bf16[2048,3,256]{2,0,1:T(8,128)(2,1)} %param.10) | data formatting | bytes 6291456 | tf_op args[2]
  111.9 4.7 %copy.22.weight_ref = bf16[2048,768]{1,0:T(8,128)(2,1)} copy(bf16[2048,768]{0,1:T(8,128)(2,1)} %bitcast.38) | data formatting | bytes 6291456 | tf_op jit(solution)/shard_map/reshape | solution.py:282
  117.2 10.8 %shard_map.83 = bf16[8,128,256]{2,1,0:T(8,128)(2,1)} custom-call(s32[1]{0:T(128)} %bitcast.place_ref, bf16[2048,768]{1,0:T(8,128)(2,1)} %copy.22.weight_ref, bf16[64,2048]{1,0:T(8,128)(2,1)} %get-tuple-element.9.refs_0_, bf16[64,2048]{1,0:T(8,128)(2,1)} %get-tuple-element.10.refs_1_, bf16[64,2048]{1,0:T(8,128)(2,1)} %copy-done.2, ...), custom_call_target="tpu_custom_call" | custom-call | flops 6442450944 | bytes 8388608 | tf_op jit(solution)/shard_map/pallas_call | solution.py:99
  128.0 18.3 %all_to_all.15.mix_ref = bf16[8,128,256]{2,1,0:T(8,128)(2,1)} all-to-all(bf16[8,128,256]{2,1,0:T(8,128)(2,1)} %shard_map.83), channel_id=1, replica_groups=mesh['w'=2,'xl'=2,'y'=4,'c'=2,'z'=8] {'z'}, dimensions={0} | all-to-all | bytes 1048576 | tf_op jit(solution)/shard_map/all_to_all | solution.py:283
  146.3 7.1 %shard_map.84 = (bf16[128,2048]{1,0:T(8,128)(2,1)}, bf16[16,32,2048]{2,1,0:T(8,128)(2,1)}) custom-call(bf16[8,128,256]{2,1,0:T(8,128)(2,1)} %all_to_all.15.mix_ref, bf16[16,2048,128]{2,1,0:T(8,128)(2,1)} %bitcast.39, bf16[128,2048]{1,0:T(8,128)(2,1)} %bitcast.42, f32[1,2048]{1,0:T(1,128)} %bitcast.49), custom_call_target="tpu_custom_call" | custom-call | flops 1073741824 | bytes 12582912 | tf_op jit(solution)/shard_map/pallas_call | solution.py:137
  153.4 13.0 %all-to-all-start.1 = ((bf16[16,32,2048]{2,1,0:T(8,128)(2,1)}), bf16[16,32,2048]{2,1,0:T(8,128)(2,1)}, u32[]{:S(2)}, u32[]{:S(2)}) async-start(bf16[16,32,2048]{2,1,0:T(8,128)(2,1)} %get-tuple-element.12), calls=%async_computation.1 | async-start | bytes 4194304 | tf_op jit(solution)/shard_map/all_to_all | solution.py:286
  166.9 27.5 %all-to-all-done.1 = bf16[16,32,2048]{2,1,0:T(8,128)(2,1)} async-done(((bf16[16,32,2048]{2,1,0:T(8,128)(2,1)}), bf16[16,32,2048]{2,1,0:T(8,128)(2,1)}, u32[]{:S(2)}, u32[]{:S(2)}) %all-to-all-start.1) | async-done | bytes 2097184 | tf_op jit(solution)/shard_map/all_to_all | solution.py:286
  194.4 24.9 %shard_map.85 = bf16[512,2048]{1,0:T(8,128)(2,1)} custom-call(s32[1]{0:T(128)} %dynamic_slice.17.start_ref, bf16[512,2048]{1,0:T(8,128)(2,1)} %bitcast.13.rows_ref, bf16[8,8,256,256]{3,2,1,0:T(8,128)(2,1)} %bitcast.50), custom_call_target="tpu_custom_call" | custom-call | flops 4294967296 | bytes 14680064 | tf_op jit(solution)/shard_map/pallas_call | solution.py:204
  219.4 33.1 %all_to_all.16 = bf16[16,32,2048]{2,1,0:T(8,128)(2,1)S(1)} all-to-all(bf16[16,32,2048]{2,1,0:T(8,128)(2,1)} %bitcast.43), channel_id=1, replica_groups=mesh['w'=2,'xl'=2,'y'=4,'c'=2,'z'=8] {'xl','y','c'}, dimensions={0} | all-to-all | bytes 4194304 | tf_op jit(solution)/shard_map/all_to_all | solution.py:289
  (83 shorter events, 25.5 us)
Async XLA Ops:
  6.5 22.5 %copy-start = (bf16[2048,3,256]{2,0,1:T(8,128)(2,1)S(1)}, bf16[2048,3,256]{2,0,1:T(8,128)(2,1)}, u32[]{:S(2)}) copy-start(bf16[2048,3,256]{2,0,1:T(8,128)(2,1)} %param.13) | copy-start | bytes 9437188
  6.5 139.8 %all-gather.4.cloned.1.call-start = ((), (), s32[]{:S(2)}) async-start(), calls=%async_computation.3 | async-start | bytes 8650752 | tf_op jit(solution)/shard_map/all_gather | solution.py:260
  7.5 15.1 %collective-permute-start.14 = (bf16[256,128]{1,0:T(8,128)(2,1)S(1)}, bf16[256,128]{1,0:T(8,128)(2,1)S(1)}, u32[]{:S(2)}, u32[]{:S(2)}) collective-permute-start(bf16[256,128]{1,0:T(8,128)(2,1)S(1)} %constant_dynamic-slice_fusion.1), channel_id=1, source_target_pairs={{0,0},{1,1},{2,2},{3,3},{4,12},{5,13},{6,14},{7,15},{8,4},{9,5},{1... | collective-permute-start | bytes 196616 | tf_op jit(solution)/shard_map/ppermute | solution.py:257
  17.7 7.1 %collective-permute-start.15 = (bf16[256,128]{1,0:T(8,128)(2,1)S(1)}, bf16[256,128]{1,0:T(8,128)(2,1)S(1)}, u32[]{:S(2)}, u32[]{:S(2)}) collective-permute-start(bf16[256,128]{1,0:T(8,128)(2,1)S(1)} %constant_dynamic-slice_fusion.1), channel_id=1, source_target_pairs={{0,3},{1,4},{2,5},{3,6},{4,15},{5,8},{6,9},{7,10},{8,7},{9,0},{10,... | collective-permute-start | bytes 196616 | tf_op jit(solution)/shard_map/ppermute | solution.py:257
  17.8 8.4 %collective-permute-start.16 = (bf16[256,128]{1,0:T(8,128)(2,1)S(1)}, bf16[256,128]{1,0:T(8,128)(2,1)S(1)}, u32[]{:S(2)}, u32[]{:S(2)}) collective-permute-start(bf16[256,128]{1,0:T(8,128)(2,1)S(1)} %constant_dynamic-slice_fusion.1), channel_id=1, source_target_pairs={{0,2},{1,3},{2,4},{3,5},{4,14},{5,15},{6,8},{7,9},{8,6},{9,7},{10,... | collective-permute-start | bytes 196616 | tf_op jit(solution)/shard_map/ppermute | solution.py:257
  22.1 5.0 %collective-permute-start.17 = (bf16[256,128]{1,0:T(8,128)(2,1)S(1)}, bf16[256,128]{1,0:T(8,128)(2,1)S(1)}, u32[]{:S(2)}, u32[]{:S(2)}) collective-permute-start(bf16[256,128]{1,0:T(8,128)(2,1)S(1)} %constant_dynamic-slice_fusion.1), channel_id=1, source_target_pairs={{0,1},{1,2},{2,3},{3,4},{4,13},{5,14},{6,15},{7,8},{8,5},{9,6},{10... | collective-permute-start | bytes 196616 | tf_op jit(solution)/shard_map/ppermute | solution.py:257
  28.0 138.9 %all-gather.6.cloned.1.call-start = ((), (), s32[]{:S(2)}) async-start(), calls=%async_computation.4 | async-start | bytes 9437184 | tf_op jit(solution)/shard_map/all_gather | solution.py:280
  29.8 14.6 %collective-permute-start.18 = (bf16[4,64,256]{2,1,0:T(8,128)(2,1)}, bf16[4,64,256]{2,1,0:T(8,128)(2,1)}, u32[]{:S(2)}, u32[]{:S(2)}) collective-permute-start(bf16[4,64,256]{2,1,0:T(8,128)(2,1)} %get-tuple-element.16), channel_id=1, source_target_pairs={{0,1},{1,2},{2,17},{3,18},{4,33},{5,34},{6,49},{7,50},{16,3},{17,4... | collective-permute-start | bytes 393224 | tf_op jit(solution)/shard_map/ppermute | solution.py:275
  31.7 17.8 %collective-permute-start.22 = (bf16[4,64,256]{2,1,0:T(8,128)(2,1)}, bf16[4,64,256]{2,1,0:T(8,128)(2,1)}, u32[]{:S(2)}, u32[]{:S(2)}) collective-permute-start(bf16[4,64,256]{2,1,0:T(8,128)(2,1)} %get-tuple-element.16), channel_id=1, source_target_pairs={{0,0},{1,1},{2,16},{3,17},{4,32},{5,33},{6,48},{7,49},{16,2},{17,3... | collective-permute-start | bytes 393224 | tf_op jit(solution)/shard_map/ppermute | solution.py:275
  33.8 22.0 %collective-permute-start.19 = (bf16[4,64,256]{2,1,0:T(8,128)(2,1)}, bf16[4,64,256]{2,1,0:T(8,128)(2,1)S(1)}, u32[]{:S(2)}, u32[]{:S(2)}) collective-permute-start(bf16[4,64,256]{2,1,0:T(8,128)(2,1)} %get-tuple-element.17), channel_id=1, source_target_pairs={{0,3},{1,4},{2,19},{3,20},{4,35},{5,36},{6,51},{7,52},{16,5},{17,6... | collective-permute-start | bytes 393224 | tf_op jit(solution)/shard_map/ppermute | solution.py:275
  36.8 23.9 %collective-permute-start.23 = (bf16[4,64,256]{2,1,0:T(8,128)(2,1)}, bf16[4,64,256]{2,1,0:T(8,128)(2,1)S(1)}, u32[]{:S(2)}, u32[]{:S(2)}) collective-permute-start(bf16[4,64,256]{2,1,0:T(8,128)(2,1)} %get-tuple-element.17), channel_id=1, source_target_pairs={{0,2},{1,3},{2,18},{3,19},{4,34},{5,35},{6,50},{7,51},{16,4},{17,5... | collective-permute-start | bytes 393224 | tf_op jit(solution)/shard_map/ppermute | solution.py:275
  36.8 23.9 %collective-permute-start.20 = (bf16[4,64,256]{2,1,0:T(8,128)(2,1)}, bf16[4,64,256]{2,1,0:T(8,128)(2,1)S(1)}, u32[]{:S(2)}, u32[]{:S(2)}) collective-permute-start(bf16[4,64,256]{2,1,0:T(8,128)(2,1)} %get-tuple-element.18), channel_id=1, source_target_pairs={{0,5},{1,6},{2,21},{3,22},{4,37},{5,38},{6,53},{7,54},{16,7},{17,0... | collective-permute-start | bytes 393224 | tf_op jit(solution)/shard_map/ppermute | solution.py:275
  44.4 16.3 %collective-permute-start.24 = (bf16[4,64,256]{2,1,0:T(8,128)(2,1)}, bf16[4,64,256]{2,1,0:T(8,128)(2,1)S(1)}, u32[]{:S(2)}, u32[]{:S(2)}) collective-permute-start(bf16[4,64,256]{2,1,0:T(8,128)(2,1)} %get-tuple-element.18), channel_id=1, source_target_pairs={{0,4},{1,5},{2,20},{3,21},{4,36},{5,37},{6,52},{7,53},{16,6},{17,7... | collective-permute-start | bytes 393224 | tf_op jit(solution)/shard_map/ppermute | solution.py:275
  49.5 11.2 %collective-permute-start.21 = (bf16[4,64,256]{2,1,0:T(8,128)(2,1)}, bf16[4,64,256]{2,1,0:T(8,128)(2,1)S(1)}, u32[]{:S(2)}, u32[]{:S(2)}) collective-permute-start(bf16[4,64,256]{2,1,0:T(8,128)(2,1)} %get-tuple-element.15), channel_id=1, source_target_pairs={{0,7},{1,0},{2,23},{3,16},{4,39},{5,32},{6,55},{7,48},{16,1},{17,2... | collective-permute-start | bytes 393224 | tf_op jit(solution)/shard_map/ppermute | solution.py:275
  55.8 7.4 %collective-permute-start.25 = (bf16[4,64,256]{2,1,0:T(8,128)(2,1)}, bf16[4,64,256]{2,1,0:T(8,128)(2,1)S(1)}, u32[]{:S(2)}, u32[]{:S(2)}) collective-permute-start(bf16[4,64,256]{2,1,0:T(8,128)(2,1)} %get-tuple-element.15), channel_id=1, source_target_pairs={{0,6},{1,7},{2,22},{3,23},{4,38},{5,39},{6,54},{7,55},{16,0},{17,1... | collective-permute-start | bytes 393224 | tf_op jit(solution)/shard_map/ppermute | solution.py:275
  68.6 13.2 %collective-permute-start = (bf16[64,2048]{1,0:T(8,128)(2,1)}, bf16[64,2048]{1,0:T(8,128)(2,1)S(1)}, u32[]{:S(2)}, u32[]{:S(2)}) collective-permute-start(bf16[64,2048]{1,0:T(8,128)(2,1)} %get-tuple-element.9.refs_0_), channel_id=1, source_target_pairs={{0,1},{1,2},{2,3},{3,4},{4,5},{5,6},{6,7},{7,0},{8,9},{9,10},{10,1... | collective-permute-start | bytes 786440 | tf_op jit(solution)/shard_map/ppermute | solution.py:228
  72.7 10.8 %collective-permute-start.3 = (bf16[64,2048]{1,0:T(8,128)(2,1)}, bf16[64,2048]{1,0:T(8,128)(2,1)S(1)}, u32[]{:S(2)}, u32[]{:S(2)}) collective-permute-start(bf16[64,2048]{1,0:T(8,128)(2,1)} %get-tuple-element.10.refs_1_), channel_id=1, source_target_pairs={{0,7},{1,0},{2,1},{3,2},{4,3},{5,4},{6,5},{7,6},{8,15},{9,8},{10,9... | collective-permute-start | bytes 786440 | tf_op jit(solution)/shard_map/ppermute | solution.py:228
  75.7 11.7 %collective-permute-start.1 = (bf16[64,2048]{1,0:T(8,128)(2,1)}, bf16[64,2048]{1,0:T(8,128)(2,1)S(1)}, u32[]{:S(2)}, u32[]{:S(2)}) collective-permute-start(bf16[64,2048]{1,0:T(8,128)(2,1)} %get-tuple-element.10.refs_1_), channel_id=1, source_target_pairs={{0,1},{1,2},{2,3},{3,4},{4,5},{5,6},{6,7},{7,0},{8,9},{9,10},{10,1... | collective-permute-start | bytes 786440 | tf_op jit(solution)/shard_map/ppermute | solution.py:228
  78.0 11.1 %collective-permute-start.2 = (bf16[64,2048]{1,0:T(8,128)(2,1)}, bf16[64,2048]{1,0:T(8,128)(2,1)S(1)}, u32[]{:S(2)}, u32[]{:S(2)}) collective-permute-start(bf16[64,2048]{1,0:T(8,128)(2,1)} %get-tuple-element.9.refs_0_), channel_id=1, source_target_pairs={{0,7},{1,0},{2,1},{3,2},{4,3},{5,4},{6,5},{7,6},{8,15},{9,8},{10,9... | collective-permute-start | bytes 786440 | tf_op jit(solution)/shard_map/ppermute | solution.py:228
  81.8 30.1 %copy-start.2 = (bf16[64,2048]{1,0:T(8,128)(2,1)}, bf16[64,2048]{1,0:T(8,128)(2,1)S(1)}, u32[]{:S(2)}) copy-start(bf16[64,2048]{1,0:T(8,128)(2,1)S(1)} %collective-permute-done.refs_2_) | copy-start | bytes 786436
  81.8 11.1 %collective-permute-start.4 = (bf16[64,2048]{1,0:T(8,128)(2,1)S(1)}, bf16[64,2048]{1,0:T(8,128)(2,1)S(1)}, u32[]{:S(2)}, u32[]{:S(2)}) collective-permute-start(bf16[64,2048]{1,0:T(8,128)(2,1)S(1)} %collective-permute-done.refs_2_), channel_id=1, source_target_pairs={{0,1},{1,2},{2,3},{3,4},{4,5},{5,6},{6,7},{7,0},{8,9},{9,10},{10,1... | collective-permute-start | bytes 786440 | tf_op jit(solution)/shard_map/ppermute | solution.py:228
  83.5 11.1 %collective-permute-start.7 = (bf16[64,2048]{1,0:T(8,128)(2,1)S(1)}, bf16[64,2048]{1,0:T(8,128)(2,1)S(1)}, u32[]{:S(2)}, u32[]{:S(2)}) collective-permute-start(bf16[64,2048]{1,0:T(8,128)(2,1)S(1)} %collective-permute-done.3.refs_5_), channel_id=1, source_target_pairs={{0,7},{1,0},{2,1},{3,2},{4,3},{5,4},{6,5},{7,6},{8,15},{9,8},{10,9... | collective-permute-start | bytes 786440 | tf_op jit(solution)/shard_map/ppermute | solution.py:228
  87.4 11.2 %collective-permute-start.5 = (bf16[64,2048]{1,0:T(8,128)(2,1)S(1)}, bf16[64,2048]{1,0:T(8,128)(2,1)}, u32[]{:S(2)}, u32[]{:S(2)}) collective-permute-start(bf16[64,2048]{1,0:T(8,128)(2,1)S(1)} %collective-permute-done.1.refs_3_), channel_id=1, source_target_pairs={{0,1},{1,2},{2,3},{3,4},{4,5},{5,6},{6,7},{7,0},{8,9},{9,10},{10,1... | collective-permute-start | bytes 786440 | tf_op jit(solution)/shard_map/ppermute | solution.py:228
  89.1 11.2 %collective-permute-start.6 = (bf16[64,2048]{1,0:T(8,128)(2,1)S(1)}, bf16[64,2048]{1,0:T(8,128)(2,1)}, u32[]{:S(2)}, u32[]{:S(2)}) collective-permute-start(bf16[64,2048]{1,0:T(8,128)(2,1)S(1)} %collective-permute-done.2.refs_4_), channel_id=1, source_target_pairs={{0,7},{1,0},{2,1},{3,2},{4,3},{5,4},{6,5},{7,6},{8,15},{9,8},{10,9... | collective-permute-start | bytes 786440 | tf_op jit(solution)/shard_map/ppermute | solution.py:228
  92.9 11.3 %collective-permute-start.8 = (bf16[64,2048]{1,0:T(8,128)(2,1)S(1)}, bf16[64,2048]{1,0:T(8,128)(2,1)}, u32[]{:S(2)}, u32[]{:S(2)}) collective-permute-start(bf16[64,2048]{1,0:T(8,128)(2,1)S(1)} %collective-permute-done.4.refs_6_), channel_id=1, source_target_pairs={{0,1},{1,2},{2,3},{3,4},{4,5},{5,6},{6,7},{7,0},{8,9},{9,10},{10,1... | collective-permute-start | bytes 786440 | tf_op jit(solution)/shard_map/ppermute | solution.py:228
  94.6 11.3 %collective-permute-start.11 = (bf16[64,2048]{1,0:T(8,128)(2,1)S(1)}, bf16[64,2048]{1,0:T(8,128)(2,1)}, u32[]{:S(2)}, u32[]{:S(2)}) collective-permute-start(bf16[64,2048]{1,0:T(8,128)(2,1)S(1)} %collective-permute-done.7.refs_9_), channel_id=1, source_target_pairs={{0,7},{1,0},{2,1},{3,2},{4,3},{5,4},{6,5},{7,6},{8,15},{9,8},{10,9... | collective-permute-start | bytes 786440 | tf_op jit(solution)/shard_map/ppermute | solution.py:228
  98.7 17.9 %collective-permute-start.9 = (bf16[64,2048]{1,0:T(8,128)(2,1)}, bf16[64,2048]{1,0:T(8,128)(2,1)}, u32[]{:S(2)}, u32[]{:S(2)}) collective-permute-start(bf16[64,2048]{1,0:T(8,128)(2,1)} %collective-permute-done.5.refs_7_), channel_id=1, source_target_pairs={{0,1},{1,2},{2,3},{3,4},{4,5},{5,6},{6,7},{7,0},{8,9},{9,10},{10,1... | collective-permute-start | bytes 786440 | tf_op jit(solution)/shard_map/ppermute | solution.py:228
  100.3 16.2 %collective-permute-start.10 = (bf16[64,2048]{1,0:T(8,128)(2,1)}, bf16[64,2048]{1,0:T(8,128)(2,1)}, u32[]{:S(2)}, u32[]{:S(2)}) collective-permute-start(bf16[64,2048]{1,0:T(8,128)(2,1)} %collective-permute-done.6.refs_8_), channel_id=1, source_target_pairs={{0,7},{1,0},{2,1},{3,2},{4,3},{5,4},{6,5},{7,6},{8,15},{9,8},{10,9... | collective-permute-start | bytes 786440 | tf_op jit(solution)/shard_map/ppermute | solution.py:228
  104.3 12.3 %collective-permute-start.12 = (bf16[64,2048]{1,0:T(8,128)(2,1)}, bf16[64,2048]{1,0:T(8,128)(2,1)}, u32[]{:S(2)}, u32[]{:S(2)}) collective-permute-start(bf16[64,2048]{1,0:T(8,128)(2,1)} %collective-permute-done.8.refs_10_), channel_id=1, source_target_pairs={{0,1},{1,2},{2,3},{3,4},{4,5},{5,6},{6,7},{7,0},{8,9},{9,10},{10,1... | collective-permute-start | bytes 786440 | tf_op jit(solution)/shard_map/ppermute | solution.py:228
  106.0 11.2 %collective-permute-start.13 = (bf16[64,2048]{1,0:T(8,128)(2,1)}, bf16[64,2048]{1,0:T(8,128)(2,1)}, u32[]{:S(2)}, u32[]{:S(2)}) collective-permute-start(bf16[64,2048]{1,0:T(8,128)(2,1)} %collective-permute-done.11.refs_13_), channel_id=1, source_target_pairs={{0,7},{1,0},{2,1},{3,2},{4,3},{5,4},{6,5},{7,6},{8,15},{9,8},{10,9... | collective-permute-start | bytes 786440 | tf_op jit(solution)/shard_map/ppermute | solution.py:228
  153.4 41.1 %all-to-all-start.1 = ((bf16[16,32,2048]{2,1,0:T(8,128)(2,1)}), bf16[16,32,2048]{2,1,0:T(8,128)(2,1)}, u32[]{:S(2)}, u32[]{:S(2)}) async-start(bf16[16,32,2048]{2,1,0:T(8,128)(2,1)} %get-tuple-element.12), calls=%async_computation.1 | async-start | bytes 4194304 | tf_op jit(solution)/shard_map/all_to_all | solution.py:286
  219.4 33.5 %copy-start.1 = (bf16[128,2048]{1,0:T(8,128)(2,1)S(1)}, bf16[128,2048]{1,0:T(8,128)(2,1)}, u32[]{:S(2)}) copy-start(bf16[128,2048]{1,0:T(8,128)(2,1)} %get-tuple-element.11) | copy-start | bytes 1572868
  (6 other events, 56.2 us)
Sparse Core Ops, SparseCore 0:
  28.1 63.9 all-gather.3
  94.0 51.8 all-gather.5

commit v2 on v1

--- a/solution.py
+++ b/solution.py
@@ -110,7 +110,9 @@
 
 def middle_kernel(mix_ref, weight_ref, rows_ref, gain_ref, middle_ref, send_ref, total):
     step = pl.program_id(0)
-    mix = jnp.concatenate([mix_ref[k] for k in range(NZ)], axis=1)
+    mix = jnp.concatenate(
+        [mix_ref[k, :, head * E : head * E + E] for head in range(2) for k in range(NZ)], axis=1
+    )
     blocks = weight_ref.shape[0]
     weight = jnp.concatenate([weight_ref[k] for k in range(blocks)], axis=1)
     width = blocks * E
@@ -159,44 +161,52 @@
     )(mix, weight, rows, gain)
 
 
-def temporal_kernel(start_ref, rows_ref, weight_ref, out_ref, qkv, mix, total):
+def temporal_kernel(start_ref, rows_ref, weight_ref, last_ref, out_ref, qkv, mix, bias):
     step = pl.program_id(0)
-    kind = lax.rem(step, 4)
+    kind = lax.rem(step, 3)
     rows_count = rows_ref.shape[0]
 
-    @pl.when(kind < 3)
+    @pl.when(step < 6)
     def _():
         weight = weight_ref[:, 0].reshape(2048, 256)
-        part = dot(rows_ref[...], weight).astype(BF).astype(F32)
-        qkv[2 * kind] = part[:, :E]
-        qkv[2 * kind + 1] = part[:, E:]
-
-    @pl.when(kind == 3)
+        qkv[kind] = dot(rows_ref[...], weight).astype(BF)
+
+    @pl.when(step == 0)
     def _():
         start = start_ref[0]
-        late = lax.broadcasted_iota(jnp.int32, (SEQ, SEQ), 0)
-        early = lax.broadcasted_iota(jnp.int32, (SEQ, SEQ), 1)
-        allowed = (early <= late) & ((early >= start) == (late >= start))
-        for head in range(2):
-            for patch in range(8):
-                frames = pl.ds(patch, SEQ, stride=8)
-                query = qkv[0 + head, frames, :].astype(BF)
-                key = qkv[2 + head, frames, :].astype(BF)
-                value = qkv[4 + head, frames, :].astype(BF)
-                scores = jnp.where(allowed, dot_t(query, key) * SCALE, -1e30)
-                mix[head, frames, :] = dot(softmax(scores), value)
-        mixed = jnp.concatenate([mix[0], mix[1]], axis=1).astype(BF)
-        for block in range(8):
-            cols = slice(256 * block, 256 * block + 256)
-            part = dot(mixed, weight_ref[block, 0])
-
-            @pl.when(step == 3)
-            def _():
-                total[:, cols] = part
-
-            @pl.when(step == 7)
-            def _():
-                out_ref[:, cols] = (total[:, cols] + part).astype(BF)
+        late = lax.broadcasted_iota(jnp.int32, (rows_count, rows_count), 0)
+        early = lax.broadcasted_iota(jnp.int32, (rows_count, rows_count), 1)
+        same = (late & 7) == (early & 7)
+        allowed = same & (early <= late) & ((early >= 8 * start) == (late >= 8 * start))
+        bias[...] = jnp.where(allowed, 0.0, -1e30)
+
+    def attend(pair):
+        block = 128
+        for low in range(0, rows_count, block):
+            for head in range(2):
+                cols = slice(head * E, head * E + E)
+                query = qkv[0, low : low + block, cols]
+                key = qkv[1, : low + block, cols]
+                value = qkv[2, : low + block, cols]
+                scores = dot_t(query, key) * SCALE
+                hidden = bias[low : low + block, : low + block]
+                scores = jnp.where(hidden < 0.0, hidden, scores)
+                at = 256 * pair + head * E
+                mix[low : low + block, at : at + E] = dot(softmax(scores), value).astype(BF)
+
+    @pl.when(step == 2)
+    def _():
+        attend(0)
+
+    @pl.when(step == 5)
+    def _():
+        attend(1)
+
+    @pl.when(step >= 6)
+    def _():
+        for block in range(4):
+            weight = last_ref[block].reshape(512, 256)
+            out_ref[:, 256 * block : 256 * block + 256] = dot(mix[...], weight).astype(BF)
 
 
 def temporal_attend(start, rows, weight):
@@ -208,19 +218,20 @@
         in_specs=[
             smem(),
             pl.BlockSpec((count, width), lambda i: (0, 0)),
-            pl.BlockSpec((8, 1, 256, 256), lambda i: (0, i, 0, 0)),
+            pl.BlockSpec((8, 1, 256, 256), lambda i: (0, jnp.minimum(i, 5), 0, 0)),
+            pl.BlockSpec((4, 2, 256, 256), lambda i: (jnp.maximum(i - 6, 0), 3, 0, 0)),
         ],
-        out_specs=pl.BlockSpec((count, width), lambda i: (0, 0)),
+        out_specs=pl.BlockSpec((count, width // 2), lambda i: (0, jnp.maximum(i - 6, 0))),
         scratch_shapes=[
-            pltpu.VMEM((6, count, E), F32),
-            pltpu.VMEM((2, count, E), F32),
-            pltpu.VMEM((count, width), F32),
+            pltpu.VMEM((3, count, 256), BF),
+            pltpu.VMEM((count, 512), BF),
+            pltpu.VMEM((count, count), F32),
         ],
         compiler_params=params(),
         cost_estimate=pl.CostEstimate(
             flops=2 * 512 * 2048 * 2048, bytes_accessed=14 << 20, transcendentals=131072
         ),
-    )(start, rows, weight)
+    )(start, rows, weight, weight)
 
 
 def shifted(value, axis, step):
@@ -248,36 +259,29 @@
     pieces = gathered_rows(chunks)
 
     column = (w * 2 + xl) * 4 + y
-    share = lax.dynamic_slice(spatial_out, (0, column * E), (256, E))
-    parts = []
+    eighth = (w * 2 + xl) * 2 + c
+    out_share = lax.dynamic_slice(spatial_out, (c * E, column * E), (E, E))
+    qkv_share = lax.dynamic_slice(temporal_qkv, (eighth * 256 + y * 64, 0, 0), (64, 3, 256))
+    qkv_share = jnp.transpose(qkv_share.reshape(64, 6, E), (1, 0, 2)).reshape(384, E)
+    last_share = lax.dynamic_slice(temporal_out, (y * 64, eighth * 256), (64, 256))
+    last_share = jnp.transpose(last_share.reshape(64, 2, E), (1, 0, 2)).reshape(E, E)
+    share = jnp.concatenate([out_share, qkv_share, last_share], axis=0)
+    shares = lax.all_gather(share, "z", axis=0, tiled=False)
+
+    whole_out = lax.all_gather(
+        shares[:, :E].reshape(1024, E), ("w", "xl", "y", "c"), axis=0, tiled=True
+    ).reshape(16, 2048, E)
+
+    mine = shares[:, E:].reshape(4, 2, 8, 64, E)
+    got = []
     for k in range(4):
-        pairs = [
-            (a * 8 + b, (b // 4) * 8 + (b + 4 * a + k) % 8) for a in range(2) for b in range(8)
-        ]
-        parts.append(lax.ppermute(share, ("c", "z"), pairs))
-    ring = jnp.stack([parts[0], parts[3], parts[2], parts[1]] * 2)
-    share = lax.dynamic_slice(ring, (lax.rem(8 - z, 4), 0, 0), (4, 256, E)).reshape(1024, E)
-    whole_out = lax.all_gather(share, ("w", "xl", "y", "c"), axis=0, tiled=True)
-    whole_out = whole_out.reshape(16, 2048, E)
-
-    eighth = (w * 2 + xl) * 2 + c
-    qkv_rows = lax.dynamic_slice(temporal_qkv, (eighth * 256, 0, 0), (256, 3, 256))
-    out_cols = lax.dynamic_slice(temporal_out, (0, eighth * 256), (256, 256))
-    share = jnp.concatenate([jnp.transpose(qkv_rows, (1, 0, 2)), out_cols[None]], axis=0)
-    got = []
-    for k in range(8):
-        pairs = []
-        for a in range(4):
-            for b in range(8):
-                order = a * 2 + b % 2
-                pairs.append((a * 8 + b, (b // 2) * 8 + (order + k) % 8))
-        low = 64 * (k // 2)
-        got.append(lax.ppermute(share[:, low : low + 64], ("y", "z"), pairs))
-    even = jnp.concatenate(got[0::2], axis=1)
-    odd = jnp.concatenate(got[1::2], axis=1)
-    swap = lax.rem(z, 2) == 1
-    share = jnp.concatenate([jnp.where(swap, odd, even), jnp.where(swap, even, odd)], axis=0)
-    quarter = lax.all_gather(share[None], ("w", "xl", "c"), axis=0, tiled=True)
+        part = lax.dynamic_index_in_dim(mine, lax.rem(y + k, 4), 0, keepdims=False)
+        got.append(shifted(part, "y", k) if k else part)
+    ring = jnp.stack([got[0], got[3], got[2], got[1]] * 2)
+    got = lax.dynamic_slice(ring, (lax.rem(4 - y, 4), 0, 0, 0, 0), (4, 2, 8, 64, E))
+    got = jnp.transpose(got.reshape(4, 2, 4, 2, 64, E), (1, 2, 0, 4, 3, 5)).reshape(2, 4, 256, 256)
+    quarter = jnp.concatenate([got[:, :3].reshape(6, 256, 256), got[:, 3]], axis=0)
+    quarter = lax.all_gather(quarter[None], ("w", "xl", "c"), axis=0, tiled=True)
 
     mix = spatial_attend(z.reshape(1), spatial_qkv.reshape(width, -1), pieces)
     mix = lax.all_to_all(mix, "z", 0, 0, tiled=True)

time: 262 us -> 265 us (1.011)
  starting transfers between devices: 67.2 us -> 40.6 us
  waiting for transfers between devices: 63.3 us -> 82.7 us
  local copies, waits for them, and re-layouts: 18.3 us -> 36.8 us
  Pallas kernels: 44.9 us -> 37.2 us
    all_gather x2 -> x3, waiting for transfers between devices: 0.01 us -> 39.1 us  [the longest x1 39.1 us: local(): shares = lax.all_gather(share, 'z', axis=0, tiled=False)]
    ppermute x12 -> x0, starting transfers between devices: 34.8 us -> none  [the longest x8 19.8 us: local(): got.append(lax.ppermute(share[:, low:low + 64], ('y', 'z'), pairs))]
    ppermute x12 -> x0, waiting for transfers between devices: 16.2 us -> none  [the longest x8 11.7 us: local(): got.append(lax.ppermute(share[:, low:low + 64], ('y', 'z'), pairs))]
    pallas_call x1, Pallas kernels: 24.9 us -> 17.2 us  [temporal_attend(): pl.pallas_call(temporal_kernel, grid=(8,), out_shape=jax.ShapeDtypeStruct...]
    unnamed x32 -> x27, local copies, waits for them, and re-layouts: 6.92 us -> 14.5 us
    all_to_all x1, starting transfers between devices: 13 us -> 17.9 us  [local(): window = lax.all_to_all(send, ('xl', 'y', 'c'), 0, 0, tiled=True)]
    ppermute x14 -> x17, waiting for transfers between devices: 19.5 us -> 16 us  [shifted(): lax.ppermute(value, axis, [(i, (i + step) % count) for i in range(count)])]
    ppermute x14 -> x17, starting transfers between devices: 19.4 us -> 22.6 us  [shifted(): lax.ppermute(value, axis, [(i, (i + step) % count) for i in range(count)])]
  transfers between devices with their start and end apart: 29 -> 21, of which waited for: 19 -> 9; matrix products, arithmetic and copies ran while one was open for 7% -> 11% of each run, Pallas kernels for 8% -> 8%
where the time goes in v2:
time: 265 us; the launch traced here: 264 us
  waiting for transfers between devices  82.7 us (31%)
  blocking collectives  51.3 us (19%)
  starting transfers between devices  40.6 us (15%)
  Pallas kernels  37.2 us (14%)
  local copies, waits for them, and re-layouts  36.8 us (14%)
  between operations  13.3 us (5%)
    all_gather x1, waiting for transfers between devices, local(): shares = lax.all_gather(share, 'z', axis=0, tiled=False)  39.1 us
    all_to_all x1, blocking collectives, local(): lax.all_to_all(partial.reshape(16, 32, width), ('xl', 'y', 'c'), 0, 0, ti...  32.8 us
    all_to_all x1, waiting for transfers between devices, local(): window = lax.all_to_all(send, ('xl', 'y', 'c'), 0, 0, tiled=True)  27.5 us
    ppermute x17, starting transfers between devices, shifted(): lax.ppermute(value, axis, [(i, (i + step) % count) for i in range(count)])  22.6 us
    all_to_all x1, blocking collectives, local(): mix = lax.all_to_all(mix, 'z', 0, 0, tiled=True)  18.5 us
    all_to_all x1, starting transfers between devices, local(): window = lax.all_to_all(send, ('xl', 'y', 'c'), 0, 0, tiled=True)  17.9 us
    pallas_call x1, Pallas kernels, temporal_attend(): pl.pallas_call(temporal_kernel, grid=(8,), out_shape=jax.ShapeDtypeStruct...  17.2 us
    ppermute x17, waiting for transfers between devices, shifted(): lax.ppermute(value, axis, [(i, (i + step) % count) for i in range(count)])  16 us
  transfers between devices with their start and end apart: 21, of which 9 were waited for; matrix products, arithmetic and copies ran while one was open for 11% of the time, Pallas kernels for 8%

profile of v2, /device:TPU:1, one launch (start us, length us, event | category | flops | bytes accessed | tf_op | source)
XLA Modules:
  0.0 264.2 jit_solution(1831091016593877411)
XLA Ops:
  10.2 39.1 %all-gather.8.cloned.1.call-done = bf16[5120,128]{1,0:T(8,128)(2,1)} async-done(((bf16[640,128]{1,0:T(8,128)(2,1)}), bf16[5120,128]{1,0:T(8,128)(2,1)}) %all-gather.8.cloned.1.call-update) | async-done | bytes 1310736 | tf_op jit(solution)/shard_map/all_gather | solution.py:269
  49.3 1.7 slice.16
  51.1 1.3 slice.17
  54.3 2.5 collective-permute-start.14
  57.9 5.4 %collective-permute-done.14 = bf16[2,8,64,128]{3,2,1,0:T(8,128)(2,1)S(1)} collective-permute-done((bf16[2,8,64,128]{3,2,1,0:T(8,128)(2,1)}, bf16[2,8,64,128]{3,2,1,0:T(8,128)(2,1)S(1)}, u32[]{:S(2)}, u32[]{:S(2)}) %collective-permute-start.14) | collective-permute-done | bytes 262176 | tf_op jit(solution)/shard_map/ppermute | solution.py:239
  64.1 1.7 bitcast_dynamic-update-slice_fusion.2
  67.3 1.7 dynamic-slice_dynamic-update-slice_fusion.1
  69.7 1.7 bitcast_dynamic-update-slice_fusion.3
  72.1 1.3 constant_dynamic-slice_fusion
  73.4 2.1 copy.40
  75.4 2.5 reshape.74
  80.3 2.1 copy.35
  82.4 2.0 shard_map.82
  85.2 2.2 collective-permute-start.3
  87.4 2.7 %collective-permute-start.2 = (bf16[64,2048]{1,0:T(8,128)(2,1)}, bf16[64,2048]{1,0:T(8,128)(2,1)S(1)}, u32[]{:S(2)}, u32[]{:S(2)}) collective-permute-start(bf16[64,2048]{1,0:T(8,128)(2,1)} %get-tuple-element.9.refs_0_), channel_id=1, source_target_pairs={{0,7},{1,0},{2,1},{3,2},{4,3},{5,4},{6,5},{7,6},{8,15},{9,8},{10,9... | collective-permute-start | bytes 786440 | tf_op jit(solution)/shard_map/ppermute | solution.py:239
  91.4 2.7 %collective-permute-start.7 = (bf16[64,2048]{1,0:T(8,128)(2,1)S(1)}, bf16[64,2048]{1,0:T(8,128)(2,1)S(1)}, u32[]{:S(2)}, u32[]{:S(2)}) collective-permute-start(bf16[64,2048]{1,0:T(8,128)(2,1)S(1)} %collective-permute-done.3.refs_5_), channel_id=1, source_target_pairs={{0,7},{1,0},{2,1},{3,2},{4,3},{5,4},{6,5},{7,6},{8,15},{9,8},{10,9... | collective-permute-start | bytes 786440 | tf_op jit(solution)/shard_map/ppermute | solution.py:239
  94.6 2.7 %collective-permute-start.6 = (bf16[64,2048]{1,0:T(8,128)(2,1)S(1)}, bf16[64,2048]{1,0:T(8,128)(2,1)}, u32[]{:S(2)}, u32[]{:S(2)}) collective-permute-start(bf16[64,2048]{1,0:T(8,128)(2,1)S(1)} %collective-permute-done.2.refs_4_), channel_id=1, source_target_pairs={{0,7},{1,0},{2,1},{3,2},{4,3},{5,4},{6,5},{7,6},{8,15},{9,8},{10,9... | collective-permute-start | bytes 786440 | tf_op jit(solution)/shard_map/ppermute | solution.py:239
  97.3 2.2 collective-permute-done.4.refs_6_
  99.5 2.7 %collective-permute-start.11 = (bf16[64,2048]{1,0:T(8,128)(2,1)S(1)}, bf16[64,2048]{1,0:T(8,128)(2,1)}, u32[]{:S(2)}, u32[]{:S(2)}) collective-permute-start(bf16[64,2048]{1,0:T(8,128)(2,1)S(1)} %collective-permute-done.7.refs_9_), channel_id=1, source_target_pairs={{0,7},{1,0},{2,1},{3,2},{4,3},{5,4},{6,5},{7,6},{8,15},{9,8},{10,9... | collective-permute-start | bytes 786440 | tf_op jit(solution)/shard_map/ppermute | solution.py:239
  102.2 2.9 %collective-permute-done.5.refs_7_ = bf16[64,2048]{1,0:T(8,128)(2,1)} collective-permute-done((bf16[64,2048]{1,0:T(8,128)(2,1)S(1)}, bf16[64,2048]{1,0:T(8,128)(2,1)}, u32[]{:S(2)}, u32[]{:S(2)}) %collective-permute-start.5) | collective-permute-done | bytes 262176 | tf_op jit(solution)/shard_map/ppermute | solution.py:239
  105.1 2.7 %collective-permute-start.10 = (bf16[64,2048]{1,0:T(8,128)(2,1)}, bf16[64,2048]{1,0:T(8,128)(2,1)}, u32[]{:S(2)}, u32[]{:S(2)}) collective-permute-start(bf16[64,2048]{1,0:T(8,128)(2,1)} %collective-permute-done.6.refs_8_), channel_id=1, source_target_pairs={{0,7},{1,0},{2,1},{3,2},{4,3},{5,4},{6,5},{7,6},{8,15},{9,8},{10,9... | collective-permute-start | bytes 786440 | tf_op jit(solution)/shard_map/ppermute | solution.py:239
  107.8 2.9 %collective-permute-done.8.refs_10_ = bf16[64,2048]{1,0:T(8,128)(2,1)} collective-permute-done((bf16[64,2048]{1,0:T(8,128)(2,1)S(1)}, bf16[64,2048]{1,0:T(8,128)(2,1)}, u32[]{:S(2)}, u32[]{:S(2)}) %collective-permute-start.8) | collective-permute-done | bytes 262176 | tf_op jit(solution)/shard_map/ppermute | solution.py:239
  110.7 2.7 %collective-permute-start.13 = (bf16[64,2048]{1,0:T(8,128)(2,1)}, bf16[64,2048]{1,0:T(8,128)(2,1)}, u32[]{:S(2)}, u32[]{:S(2)}) collective-permute-start(bf16[64,2048]{1,0:T(8,128)(2,1)} %collective-permute-done.11.refs_13_), channel_id=1, source_target_pairs={{0,7},{1,0},{2,1},{3,2},{4,3},{5,4},{6,5},{7,6},{8,15},{9,8},{10,9... | collective-permute-start | bytes 786440 | tf_op jit(solution)/shard_map/ppermute | solution.py:239
  113.4 4.7 %copy.34 = bf16[2048,3,256]{0,2,1:T(8,128)(2,1)} copy(bf16[2048,3,256]{2,0,1:T(8,128)(2,1)} %param.10) | data formatting | bytes 6291456 | tf_op args[2]
  118.1 4.7 %copy.36.weight_ref = bf16[2048,768]{1,0:T(8,128)(2,1)} copy(bf16[2048,768]{0,1:T(8,128)(2,1)} %bitcast.51) | data formatting | bytes 6291456 | tf_op jit(solution)/shard_map/reshape | solution.py:286
  122.7 10.8 %shard_map.83 = bf16[8,128,256]{2,1,0:T(8,128)(2,1)} custom-call(s32[1]{0:T(128)} %bitcast.place_ref, bf16[2048,768]{1,0:T(8,128)(2,1)} %copy.36.weight_ref, bf16[64,2048]{1,0:T(8,128)(2,1)} %get-tuple-element.9.refs_0_, bf16[64,2048]{1,0:T(8,128)(2,1)} %get-tuple-element.10.refs_1_, bf16[64,2048]{1,0:T(8,128)(2,1)} %copy-done.3, ...), custom_call_target="tpu_custom_call" | custom-call | flops 6442450944 | bytes 8388608 | tf_op jit(solution)/shard_map/pallas_call | solution.py:99
  133.6 18.5 %all_to_all.15.mix_ref = bf16[8,128,256]{2,1,0:T(8,128)(2,1)} all-to-all(bf16[8,128,256]{2,1,0:T(8,128)(2,1)} %shard_map.83), channel_id=1, replica_groups=mesh['w'=2,'xl'=2,'y'=4,'c'=2,'z'=8] {'z'}, dimensions={0} | all-to-all | bytes 1048576 | tf_op jit(solution)/shard_map/all_to_all | solution.py:287
  152.1 7.1 %shard_map.84 = (bf16[128,2048]{1,0:T(8,128)(2,1)}, bf16[16,32,2048]{2,1,0:T(8,128)(2,1)}) custom-call(bf16[8,128,256]{2,1,0:T(8,128)(2,1)} %all_to_all.15.mix_ref, bf16[16,2048,128]{2,1,0:T(8,128)(2,1)} %bitcast.53, bf16[128,2048]{1,0:T(8,128)(2,1)} %bitcast.58, f32[1,2048]{1,0:T(1,128)} %bitcast.72), custom_call_target="tpu_custom_call" | custom-call | flops 1073741824 | bytes 12582912 | tf_op jit(solution)/shard_map/pallas_call | solution.py:139
  159.3 17.9 %all-to-all-start.1 = ((bf16[16,32,2048]{2,1,0:T(8,128)(2,1)}), bf16[16,32,2048]{2,1,0:T(8,128)(2,1)}, u32[]{:S(2)}, u32[]{:S(2)}) async-start(bf16[16,32,2048]{2,1,0:T(8,128)(2,1)} %get-tuple-element.12), calls=%async_computation.1 | async-start | bytes 4194304 | tf_op jit(solution)/shard_map/all_to_all | solution.py:290
  177.7 27.5 %all-to-all-done.1 = bf16[16,32,2048]{2,1,0:T(8,128)(2,1)} async-done(((bf16[16,32,2048]{2,1,0:T(8,128)(2,1)}), bf16[16,32,2048]{2,1,0:T(8,128)(2,1)}, u32[]{:S(2)}, u32[]{:S(2)}) %all-to-all-start.1) | async-done | bytes 2097184 | tf_op jit(solution)/shard_map/all_to_all | solution.py:290
  205.2 17.2 %shard_map.85 = bf16[512,2048]{1,0:T(8,128)(2,1)} custom-call(s32[1]{0:T(128)} %dynamic_slice.31.start_ref, bf16[512,2048]{1,0:T(8,128)(2,1)} %bitcast.14.rows_ref, bf16[8,8,256,256]{3,2,1,0:T(8,128)(2,1)} %bitcast.49, bf16[8,8,256,256]{3,2,1,0:T(8,128)(2,1)} %bitcast.50), custom_call_target="tpu_custom_call" | custom-call | flops 4294967296 | bytes 14680064 | tf_op jit(solution)/shard_map/pallas_call | solution.py:214
  222.4 32.8 %all_to_all.16 = bf16[16,32,2048]{2,1,0:T(8,128)(2,1)S(1)} all-to-all(bf16[16,32,2048]{2,1,0:T(8,128)(2,1)} %bitcast.52), channel_id=1, replica_groups=mesh['w'=2,'xl'=2,'y'=4,'c'=2,'z'=8] {'xl','y','c'}, dimensions={0} | all-to-all | bytes 4194304 | tf_op jit(solution)/shard_map/all_to_all | solution.py:293
  (73 shorter events, 18.3 us)
Async XLA Ops:
  6.5 1.9 copy-start
  6.5 42.7 %all-gather.8.cloned.1.call-start = ((), (), s32[]{:S(2)}) async-start(), calls=%async_computation.4 | async-start | bytes 1474560 | tf_op jit(solution)/shard_map/all_gather | solution.py:269
  10.1 142.0 %all-gather.6.cloned.1.call-start = ((), (), s32[]{:S(2)}) async-start(), calls=%async_computation.3 | async-start | bytes 8650752 | tf_op jit(solution)/shard_map/all_gather | solution.py:271
  51.0 126.8 %all-gather.10.cloned.1.call-start = ((), (), s32[]{:S(2)}) async-start(), calls=%async_computation.5 | async-start | bytes 9437184 | tf_op jit(solution)/shard_map/all_gather | solution.py:284
  52.4 1.0 copy-start.1
  54.3 9.0 %collective-permute-start.14 = (bf16[2,8,64,128]{3,2,1,0:T(8,128)(2,1)}, bf16[2,8,64,128]{3,2,1,0:T(8,128)(2,1)S(1)}, u32[]{:S(2)}, u32[]{:S(2)}) collective-permute-start(bf16[2,8,64,128]{3,2,1,0:T(8,128)(2,1)} %get-tuple-element.16), channel_id=1, source_target_pairs={{0,48},{16,0},{32,16},{48,32},{1,49},{17,1},{33,17},{49,33},{2,50}... | collective-permute-start | bytes 786440 | tf_op jit(solution)/shard_map/ppermute | solution.py:239
  56.8 7.3 %collective-permute-start.15 = (bf16[2,8,64,128]{3,2,1,0:T(8,128)(2,1)}, bf16[2,8,64,128]{3,2,1,0:T(8,128)(2,1)}, u32[]{:S(2)}, u32[]{:S(2)}) collective-permute-start(bf16[2,8,64,128]{3,2,1,0:T(8,128)(2,1)} %get-tuple-element.15), channel_id=1, source_target_pairs={{0,32},{16,48},{32,0},{48,16},{1,33},{17,49},{33,1},{49,17},{2,34}... | collective-permute-start | bytes 786440 | tf_op jit(solution)/shard_map/ppermute | solution.py:239
  57.3 9.2 %collective-permute-start.16 = (bf16[2,8,64,128]{3,2,1,0:T(8,128)(2,1)}, bf16[2,8,64,128]{3,2,1,0:T(8,128)(2,1)S(1)}, u32[]{:S(2)}, u32[]{:S(2)}) collective-permute-start(bf16[2,8,64,128]{3,2,1,0:T(8,128)(2,1)} %get-tuple-element.13), channel_id=1, source_target_pairs={{0,16},{16,32},{32,48},{48,0},{1,17},{17,33},{33,49},{49,1},{2,18}... | collective-permute-start | bytes 786440 | tf_op jit(solution)/shard_map/ppermute | solution.py:239
  78.0 1.2 slice-start
  84.5 6.9 %collective-permute-start = (bf16[64,2048]{1,0:T(8,128)(2,1)}, bf16[64,2048]{1,0:T(8,128)(2,1)S(1)}, u32[]{:S(2)}, u32[]{:S(2)}) collective-permute-start(bf16[64,2048]{1,0:T(8,128)(2,1)} %get-tuple-element.9.refs_0_), channel_id=1, source_target_pairs={{0,1},{1,2},{2,3},{3,4},{4,5},{5,6},{6,7},{7,0},{8,9},{9,10},{10,1... | collective-permute-start | bytes 786440 | tf_op jit(solution)/shard_map/ppermute | solution.py:239
  85.2 6.2 %collective-permute-start.3 = (bf16[64,2048]{1,0:T(8,128)(2,1)}, bf16[64,2048]{1,0:T(8,128)(2,1)S(1)}, u32[]{:S(2)}, u32[]{:S(2)}) collective-permute-start(bf16[64,2048]{1,0:T(8,128)(2,1)} %get-tuple-element.10.refs_1_), channel_id=1, source_target_pairs={{0,7},{1,0},{2,1},{3,2},{4,3},{5,4},{6,5},{7,6},{8,15},{9,8},{10,9... | collective-permute-start | bytes 786440 | tf_op jit(solution)/shard_map/ppermute | solution.py:239
  87.4 7.2 %collective-permute-start.1 = (bf16[64,2048]{1,0:T(8,128)(2,1)}, bf16[64,2048]{1,0:T(8,128)(2,1)S(1)}, u32[]{:S(2)}, u32[]{:S(2)}) collective-permute-start(bf16[64,2048]{1,0:T(8,128)(2,1)} %get-tuple-element.10.refs_1_), channel_id=1, source_target_pairs={{0,1},{1,2},{2,3},{3,4},{4,5},{5,6},{6,7},{7,0},{8,9},{9,10},{10,1... | collective-permute-start | bytes 786440 | tf_op jit(solution)/shard_map/ppermute | solution.py:239
  87.4 7.2 %collective-permute-start.2 = (bf16[64,2048]{1,0:T(8,128)(2,1)}, bf16[64,2048]{1,0:T(8,128)(2,1)S(1)}, u32[]{:S(2)}, u32[]{:S(2)}) collective-permute-start(bf16[64,2048]{1,0:T(8,128)(2,1)} %get-tuple-element.9.refs_0_), channel_id=1, source_target_pairs={{0,7},{1,0},{2,1},{3,2},{4,3},{5,4},{6,5},{7,6},{8,15},{9,8},{10,9... | collective-permute-start | bytes 786440 | tf_op jit(solution)/shard_map/ppermute | solution.py:239
  91.4 26.7 %copy-start.3 = (bf16[64,2048]{1,0:T(8,128)(2,1)}, bf16[64,2048]{1,0:T(8,128)(2,1)S(1)}, u32[]{:S(2)}) copy-start(bf16[64,2048]{1,0:T(8,128)(2,1)S(1)} %collective-permute-done.refs_2_) | copy-start | bytes 786436
  91.4 8.1 %collective-permute-start.4 = (bf16[64,2048]{1,0:T(8,128)(2,1)S(1)}, bf16[64,2048]{1,0:T(8,128)(2,1)S(1)}, u32[]{:S(2)}, u32[]{:S(2)}) collective-permute-start(bf16[64,2048]{1,0:T(8,128)(2,1)S(1)} %collective-permute-done.refs_2_), channel_id=1, source_target_pairs={{0,1},{1,2},{2,3},{3,4},{4,5},{5,6},{6,7},{7,0},{8,9},{9,10},{10,1... | collective-permute-start | bytes 786440 | tf_op jit(solution)/shard_map/ppermute | solution.py:239
  91.4 8.1 %copy-start.4 = (bf16[64,2048]{1,0:T(8,128)(2,1)}, bf16[64,2048]{1,0:T(8,128)(2,1)S(1)}, u32[]{:S(2)}) copy-start(bf16[64,2048]{1,0:T(8,128)(2,1)S(1)} %collective-permute-done.3.refs_5_) | copy-start | bytes 786436
  91.4 8.1 %collective-permute-start.7 = (bf16[64,2048]{1,0:T(8,128)(2,1)S(1)}, bf16[64,2048]{1,0:T(8,128)(2,1)S(1)}, u32[]{:S(2)}, u32[]{:S(2)}) collective-permute-start(bf16[64,2048]{1,0:T(8,128)(2,1)S(1)} %collective-permute-done.3.refs_5_), channel_id=1, source_target_pairs={{0,7},{1,0},{2,1},{3,2},{4,3},{5,4},{6,5},{7,6},{8,15},{9,8},{10,9... | collective-permute-start | bytes 786440 | tf_op jit(solution)/shard_map/ppermute | solution.py:239
  94.6 4.9 %copy-start.5 = (bf16[64,2048]{1,0:T(8,128)(2,1)}, bf16[64,2048]{1,0:T(8,128)(2,1)S(1)}, u32[]{:S(2)}) copy-start(bf16[64,2048]{1,0:T(8,128)(2,1)S(1)} %collective-permute-done.1.refs_3_) | copy-start | bytes 786436
  94.6 10.5 %collective-permute-start.5 = (bf16[64,2048]{1,0:T(8,128)(2,1)S(1)}, bf16[64,2048]{1,0:T(8,128)(2,1)}, u32[]{:S(2)}, u32[]{:S(2)}) collective-permute-start(bf16[64,2048]{1,0:T(8,128)(2,1)S(1)} %collective-permute-done.1.refs_3_), channel_id=1, source_target_pairs={{0,1},{1,2},{2,3},{3,4},{4,5},{5,6},{6,7},{7,0},{8,9},{9,10},{10,1... | collective-permute-start | bytes 786440 | tf_op jit(solution)/shard_map/ppermute | solution.py:239
  94.6 10.5 %copy-start.6 = (bf16[64,2048]{1,0:T(8,128)(2,1)}, bf16[64,2048]{1,0:T(8,128)(2,1)S(1)}, u32[]{:S(2)}) copy-start(bf16[64,2048]{1,0:T(8,128)(2,1)S(1)} %collective-permute-done.2.refs_4_) | copy-start | bytes 786436
  94.6 10.5 %collective-permute-start.6 = (bf16[64,2048]{1,0:T(8,128)(2,1)S(1)}, bf16[64,2048]{1,0:T(8,128)(2,1)}, u32[]{:S(2)}, u32[]{:S(2)}) collective-permute-start(bf16[64,2048]{1,0:T(8,128)(2,1)S(1)} %collective-permute-done.2.refs_4_), channel_id=1, source_target_pairs={{0,7},{1,0},{2,1},{3,2},{4,3},{5,4},{6,5},{7,6},{8,15},{9,8},{10,9... | collective-permute-start | bytes 786440 | tf_op jit(solution)/shard_map/ppermute | solution.py:239
  99.5 5.6 %copy-start.7 = (bf16[64,2048]{1,0:T(8,128)(2,1)}, bf16[64,2048]{1,0:T(8,128)(2,1)S(1)}, u32[]{:S(2)}) copy-start(bf16[64,2048]{1,0:T(8,128)(2,1)S(1)} %collective-permute-done.4.refs_6_) | copy-start | bytes 786436
  99.5 11.2 %collective-permute-start.8 = (bf16[64,2048]{1,0:T(8,128)(2,1)S(1)}, bf16[64,2048]{1,0:T(8,128)(2,1)}, u32[]{:S(2)}, u32[]{:S(2)}) collective-permute-start(bf16[64,2048]{1,0:T(8,128)(2,1)S(1)} %collective-permute-done.4.refs_6_), channel_id=1, source_target_pairs={{0,1},{1,2},{2,3},{3,4},{4,5},{5,6},{6,7},{7,0},{8,9},{9,10},{10,1... | collective-permute-start | bytes 786440 | tf_op jit(solution)/shard_map/ppermute | solution.py:239
  99.5 11.2 %copy-start.8 = (bf16[64,2048]{1,0:T(8,128)(2,1)}, bf16[64,2048]{1,0:T(8,128)(2,1)S(1)}, u32[]{:S(2)}) copy-start(bf16[64,2048]{1,0:T(8,128)(2,1)S(1)} %collective-permute-done.7.refs_9_) | copy-start | bytes 786436
  99.5 11.2 %collective-permute-start.11 = (bf16[64,2048]{1,0:T(8,128)(2,1)S(1)}, bf16[64,2048]{1,0:T(8,128)(2,1)}, u32[]{:S(2)}, u32[]{:S(2)}) collective-permute-start(bf16[64,2048]{1,0:T(8,128)(2,1)S(1)} %collective-permute-done.7.refs_9_), channel_id=1, source_target_pairs={{0,7},{1,0},{2,1},{3,2},{4,3},{5,4},{6,5},{7,6},{8,15},{9,8},{10,9... | collective-permute-start | bytes 786440 | tf_op jit(solution)/shard_map/ppermute | solution.py:239
  105.1 17.6 %collective-permute-start.9 = (bf16[64,2048]{1,0:T(8,128)(2,1)}, bf16[64,2048]{1,0:T(8,128)(2,1)}, u32[]{:S(2)}, u32[]{:S(2)}) collective-permute-start(bf16[64,2048]{1,0:T(8,128)(2,1)} %collective-permute-done.5.refs_7_), channel_id=1, source_target_pairs={{0,1},{1,2},{2,3},{3,4},{4,5},{5,6},{6,7},{7,0},{8,9},{9,10},{10,1... | collective-permute-start | bytes 786440 | tf_op jit(solution)/shard_map/ppermute | solution.py:239
  105.1 17.6 %collective-permute-start.10 = (bf16[64,2048]{1,0:T(8,128)(2,1)}, bf16[64,2048]{1,0:T(8,128)(2,1)}, u32[]{:S(2)}, u32[]{:S(2)}) collective-permute-start(bf16[64,2048]{1,0:T(8,128)(2,1)} %collective-permute-done.6.refs_8_), channel_id=1, source_target_pairs={{0,7},{1,0},{2,1},{3,2},{4,3},{5,4},{6,5},{7,6},{8,15},{9,8},{10,9... | collective-permute-start | bytes 786440 | tf_op jit(solution)/shard_map/ppermute | solution.py:239
  110.7 12.0 %collective-permute-start.12 = (bf16[64,2048]{1,0:T(8,128)(2,1)}, bf16[64,2048]{1,0:T(8,128)(2,1)}, u32[]{:S(2)}, u32[]{:S(2)}) collective-permute-start(bf16[64,2048]{1,0:T(8,128)(2,1)} %collective-permute-done.8.refs_10_), channel_id=1, source_target_pairs={{0,1},{1,2},{2,3},{3,4},{4,5},{5,6},{6,7},{7,0},{8,9},{9,10},{10,1... | collective-permute-start | bytes 786440 | tf_op jit(solution)/shard_map/ppermute | solution.py:239
  110.7 12.0 %collective-permute-start.13 = (bf16[64,2048]{1,0:T(8,128)(2,1)}, bf16[64,2048]{1,0:T(8,128)(2,1)}, u32[]{:S(2)}, u32[]{:S(2)}) collective-permute-start(bf16[64,2048]{1,0:T(8,128)(2,1)} %collective-permute-done.11.refs_13_), channel_id=1, source_target_pairs={{0,7},{1,0},{2,1},{3,2},{4,3},{5,4},{6,5},{7,6},{8,15},{9,8},{10,9... | collective-permute-start | bytes 786440 | tf_op jit(solution)/shard_map/ppermute | solution.py:239
  159.3 17.9 %copy-start.9 = (s32[2]{0:T(128)S(1)}, s32[2]{0:T(128)}, u32[]{:S(2)}) copy-start(s32[2]{0:T(128)} %param.15) | copy-start | bytes 28
  159.3 46.0 %all-to-all-start.1 = ((bf16[16,32,2048]{2,1,0:T(8,128)(2,1)}), bf16[16,32,2048]{2,1,0:T(8,128)(2,1)}, u32[]{:S(2)}, u32[]{:S(2)}) async-start(bf16[16,32,2048]{2,1,0:T(8,128)(2,1)} %get-tuple-element.12), calls=%async_computation.1 | async-start | bytes 4194304 | tf_op jit(solution)/shard_map/all_to_all | solution.py:290
  255.2 1.0 copy-start.2
Sparse Core Ops, SparseCore 0:
  10.2 38.9 all-gather.7
  51.8 61.0 all-gather.5
  114.8 51.8 all-gather.9

commit v3 on v2

--- a/solution.py
+++ b/solution.py
@@ -49,26 +49,97 @@
     return lax.dot_general(a, b, (((1,), (1,)), ((), ())), preferred_element_type=F32)
 
 
-def norm_kernel(x_ref, gain_ref, a_ref, b_ref):
+def norm_kernel(x_ref, gain_ref, a_ref, b_ref, rows_ref):
     gain = gain_ref[...]
+    values = jnp.transpose(x_ref[...].astype(F32), (1, 0, 2)).reshape(rows_ref.shape)
     half = a_ref.shape[0]
-    a_ref[...] = normed(x_ref[:half].astype(F32), gain)
-    b_ref[...] = normed(x_ref[half:].astype(F32), gain)
-
-
-def norm_rows(rows, gain):
-    count, width = rows.shape
+    rows_ref[...] = values.astype(BF)
+    a_ref[...] = normed(values[:half], gain)
+    b_ref[...] = normed(values[half:], gain)
+
+
+def norm_rows(stream, gain):
+    patches, frames, width = stream.shape
+    count = patches * frames
     half = jax.ShapeDtypeStruct((count // 2, width), BF)
     return pl.pallas_call(
         norm_kernel,
-        out_shape=(half, half),
+        out_shape=(half, half, jax.ShapeDtypeStruct((count, width), BF)),
         in_specs=[vmem(), vmem()],
-        out_specs=(vmem(), vmem()),
+        out_specs=(vmem(), vmem(), vmem()),
         compiler_params=params(),
         cost_estimate=pl.CostEstimate(
-            flops=4 * count * width, bytes_accessed=4 * count * width, transcendentals=0
-        ),
-    )(rows, gain)
+            flops=4 * count * width, bytes_accessed=6 * count * width, transcendentals=0
+        ),
+    )(stream, gain)
+
+
+def cut_kernel(place_ref, out_ref, qkv_ref, last_ref, share_ref):
+    share_ref[0] = out_ref[...]
+    for kind in range(3):
+        share_ref[1 + kind] = qkv_ref[kind]
+    share_ref[4] = last_ref[...]
+
+
+def cut_share(place, spatial_out, temporal_qkv, temporal_out):
+    return pl.pallas_call(
+        cut_kernel,
+        grid_spec=pltpu.PrefetchScalarGridSpec(
+            num_scalar_prefetch=1,
+            grid=(1,),
+            in_specs=[
+                pl.BlockSpec((64, 256), lambda i, at: (at[0], at[1])),
+                pl.BlockSpec((3, 64, 256), lambda i, at: (0, at[2], 0)),
+                pl.BlockSpec((64, 256), lambda i, at: (at[3], at[4])),
+            ],
+            out_specs=pl.BlockSpec((5, 64, 256), lambda i, at: (0, 0, 0)),
+        ),
+        out_shape=jax.ShapeDtypeStruct((5, 64, 256), BF),
+        compiler_params=params(),
+        cost_estimate=pl.CostEstimate(flops=0, bytes_accessed=320 << 10, transcendentals=0),
+    )(place, spatial_out, temporal_qkv, temporal_out)
+
+
+def split_kernel(y_ref, shares_ref, out_ref, *sends):
+    for k in range(NZ):
+        out_ref[k] = shares_ref[k, 0]
+    for step in range(4):
+        pair = lax.rem(y_ref[0] + step, 4)
+        for k in range(2):
+            sends[step][k] = shares_ref[2 * pair + k, 1:]
+
+
+def split_shares(y, shares):
+    send = jax.ShapeDtypeStruct((2, 4, 64, 256), BF)
+    return pl.pallas_call(
+        split_kernel,
+        out_shape=(jax.ShapeDtypeStruct((NZ, 64, 256), BF),) + (send,) * 4,
+        in_specs=[smem(), vmem()],
+        out_specs=(vmem(),) * 5,
+        compiler_params=params(),
+        cost_estimate=pl.CostEstimate(flops=0, bytes_accessed=3 << 20, transcendentals=0),
+    )(y, shares)
+
+
+def join_kernel(y_ref, *refs):
+    out_ref = refs[-1]
+    for step in range(4):
+        low = pl.multiple_of(64 * lax.rem(y_ref[0] + (4 - step), 4), 64)
+        for pair in range(2):
+            for kind in range(4):
+                block = 3 * pair + kind if kind < 3 else 6 + pair
+                out_ref[block, pl.ds(low, 64), :] = refs[step][pair, kind]
+
+
+def join_shares(y, got):
+    return pl.pallas_call(
+        join_kernel,
+        out_shape=jax.ShapeDtypeStruct((8, 256, 256), BF),
+        in_specs=[smem()] + [vmem()] * 4,
+        out_specs=vmem(),
+        compiler_params=params(),
+        cost_estimate=pl.CostEstimate(flops=0, bytes_accessed=2 << 20, transcendentals=0),
+    )(y, *got)
 
 
 def spatial_kernel(place_ref, weight_ref, *refs):
@@ -80,12 +151,12 @@
         rows = jnp.concatenate(
             [pieces[2 * k + part][32 * inner : 32 * inner + 32, :] for k in range(NZ)], axis=0
         )
-        qkv = dot(rows, weight_ref[...]).astype(BF)
+        qkv = [dot(rows, weight_ref[kind]).astype(BF) for kind in range(3)]
         for head in range(2):
             low = head * E
-            query = qkv[:, low : low + E]
-            key = qkv[:, 256 + low : 256 + low + E]
-            value = qkv[:, 512 + low : 512 + low + E]
+            query = qkv[0][:, low : low + E]
+            key = qkv[1][:, low : low + E]
+            value = qkv[2][:, low : low + E]
             weights = softmax(dot_t(query, key) * SCALE)
             mixed = dot(weights, value).astype(BF)
             for k in range(NZ):
@@ -110,13 +181,13 @@
 
 def middle_kernel(mix_ref, weight_ref, rows_ref, gain_ref, middle_ref, send_ref, total):
     step = pl.program_id(0)
-    mix = jnp.concatenate(
-        [mix_ref[k, :, head * E : head * E + E] for head in range(2) for k in range(NZ)], axis=1
-    )
-    blocks = weight_ref.shape[0]
-    weight = jnp.concatenate([weight_ref[k] for k in range(blocks)], axis=1)
-    width = blocks * E
-    total[:, pl.ds(pl.multiple_of(step * width, width), width)] = dot(mix, weight)
+    mix = jnp.concatenate([mix_ref[k] for k in range(NZ)], axis=1)
+    for block in range(weight_ref.shape[0]):
+        weight = jnp.concatenate(
+            [weight_ref[block, quarter, k] for k in range(NZ) for quarter in range(4)], axis=0
+        )
+        low = pl.multiple_of((step * weight_ref.shape[0] + block) * 256, 256)
+        total[:, pl.ds(low, 256)] = dot(mix, weight)
 
     @pl.when(step == pl.num_programs(0) - 1)
     def _():
@@ -145,7 +216,7 @@
         ),
         in_specs=[
             pl.BlockSpec((NZ, 128, 256), lambda i: (0, 0, 0)),
-            pl.BlockSpec((16 // steps, 2048, E), lambda i: (i, 0, 0)),
+            pl.BlockSpec((8 // steps, 4, NZ, 64, 256), lambda i: (i, 0, 0, 0, 0)),
             pl.BlockSpec((128, width), lambda i: (0, 0)),
             pl.BlockSpec((1, width), lambda i: (0, 0)),
         ],
@@ -254,37 +325,35 @@
     patches, frames, width = stream.shape
     w, xl, y, c, z = (lax.axis_index(name) for name in ("w", "xl", "y", "c", "z"))
 
-    rows = jnp.transpose(stream, (1, 0, 2)).reshape(frames * patches, width)
-    chunks = norm_rows(rows, spatial_gain.reshape(1, width))
-    pieces = gathered_rows(chunks)
-
-    column = (w * 2 + xl) * 4 + y
-    eighth = (w * 2 + xl) * 2 + c
-    out_share = lax.dynamic_slice(spatial_out, (c * E, column * E), (E, E))
-    qkv_share = lax.dynamic_slice(temporal_qkv, (eighth * 256 + y * 64, 0, 0), (64, 3, 256))
-    qkv_share = jnp.transpose(qkv_share.reshape(64, 6, E), (1, 0, 2)).reshape(384, E)
-    last_share = lax.dynamic_slice(temporal_out, (y * 64, eighth * 256), (64, 256))
-    last_share = jnp.transpose(last_share.reshape(64, 2, E), (1, 0, 2)).reshape(E, E)
-    share = jnp.concatenate([out_share, qkv_share, last_share], axis=0)
+    place = jnp.stack(
+        [
+            lax.rem(y, 2) * 2 + c,
+            (w * 2 + xl) * 2 + y // 2,
+            ((w * 2 + xl) * 2 + c) * 4 + y,
+            y,
+            (w * 2 + xl) * 2 + c,
+        ]
+    ).astype(jnp.int32)
+    share = cut_share(place, spatial_out, jnp.transpose(temporal_qkv, (1, 0, 2)), temporal_out)
     shares = lax.all_gather(share, "z", axis=0, tiled=False)
 
-    whole_out = lax.all_gather(
-        shares[:, :E].reshape(1024, E), ("w", "xl", "y", "c"), axis=0, tiled=True
-    ).reshape(16, 2048, E)
-
-    mine = shares[:, E:].reshape(4, 2, 8, 64, E)
-    got = []
-    for k in range(4):
-        part = lax.dynamic_index_in_dim(mine, lax.rem(y + k, 4), 0, keepdims=False)
-        got.append(shifted(part, "y", k) if k else part)
-    ring = jnp.stack([got[0], got[3], got[2], got[1]] * 2)
-    got = lax.dynamic_slice(ring, (lax.rem(4 - y, 4), 0, 0, 0, 0), (4, 2, 8, 64, E))
-    got = jnp.transpose(got.reshape(4, 2, 4, 2, 64, E), (1, 2, 0, 4, 3, 5)).reshape(2, 4, 256, 256)
-    quarter = jnp.concatenate([got[:, :3].reshape(6, 256, 256), got[:, 3]], axis=0)
+    first, second, rows = norm_rows(stream, spatial_gain.reshape(1, width))
+    pieces = gathered_rows((first, second))
+    *pieces, shares = lax.optimization_barrier((*pieces, shares))
+
+    out_share, *sends = split_shares(y.reshape(1), shares)
+    whole_out = lax.all_gather(out_share, ("w", "xl", "y", "c"), axis=0, tiled=False)
+    whole_out = whole_out.reshape(8, 4, NZ, 64, 256)
+
+    got = [sends[0]] + [shifted(sends[k], "y", k) for k in range(1, 4)]
+
+    weight = jnp.transpose(spatial_qkv, (1, 0, 2))
+    mix = spatial_attend(z.reshape(1), weight, pieces)
+    mix, *got = lax.optimization_barrier((mix, *got))
+    mix = lax.all_to_all(mix, "z", 0, 0, tiled=True)
+    quarter = join_shares(y.reshape(1), got)
     quarter = lax.all_gather(quarter[None], ("w", "xl", "c"), axis=0, tiled=True)
 
-    mix = spatial_attend(z.reshape(1), spatial_qkv.reshape(width, -1), pieces)
-    mix = lax.all_to_all(mix, "z", 0, 0, tiled=True)
     middle, send = middle_rows(mix, whole_out, rows, temporal_gain.reshape(1, width))
 
     window = lax.all_to_all(send, ("xl", "y", "c"), 0, 0, tiled=True)

time: 265 us -> 264 us (level)
  waiting for transfers between devices: 82.7 us -> 117 us
  local copies, waits for them, and re-layouts: 36.8 us -> 5.29 us
  starting transfers between devices: 40.6 us -> 32.6 us
  Pallas kernels: 37.2 us -> 44.4 us
    all_gather x1, waiting for transfers between devices: 0.01 us -> 60.2 us  [local(): lax.all_gather(quarter[None], ('w', 'xl', 'c'), axis=0, tiled=True)]
    all_gather x1, waiting for transfers between devices: 39.1 us -> 0.01 us  [local(): shares = lax.all_gather(share, 'z', axis=0, tiled=False)]
    all_to_all x1, waiting for transfers between devices: 27.5 us -> 0.01 us  [local(): window = lax.all_to_all(send, ('xl', 'y', 'c'), 0, 0, tiled=True)]
    all_gather x1, waiting for transfers between devices: 0.01 us -> 21.5 us  [local(): lax.all_gather(out_share, ('w', 'xl', 'y', 'c'), axis=0, tiled=False)]
    ppermute x17, waiting for transfers between devices: 16 us -> 34.7 us  [shifted(): lax.ppermute(value, axis, [(i, (i + step) % count) for i in range(count)])]
    all_to_all x1, starting transfers between devices: 17.9 us -> 4.47 us  [local(): window = lax.all_to_all(send, ('xl', 'y', 'c'), 0, 0, tiled=True)]
    unnamed x27 -> x40, local copies, waits for them, and re-layouts: 14.5 us -> 2.89 us
    pallas_call x1 -> x4, Pallas kernels: 2.05 us -> 9.48 us  [the longest x1 2.51 us: norm_rows(): pl.pallas_call(norm_kernel, out_shape=(half, half, jax.ShapeDtypeStruct((...]
  transfers between devices with their start and end apart: 21 -> 21, of which waited for: 9 -> 10; matrix products, arithmetic and copies ran while one was open for 11% -> 0% of each run, Pallas kernels for 8% -> 9%
where the time goes in v3:
time: 264 us
  waiting for transfers between devices  117 us (44%)
  blocking collectives  51.2 us (19%)
  Pallas kernels  44.4 us (17%)
  starting transfers between devices  32.6 us (12%)
  between operations  13.3 us (5%)
  local copies, waits for them, and re-layouts  5.29 us (2%)
    all_gather x1, waiting for transfers between devices, local(): lax.all_gather(quarter[None], ('w', 'xl', 'c'), axis=0, tiled=True)  60.2 us
    ppermute x17, waiting for transfers between devices, shifted(): lax.ppermute(value, axis, [(i, (i + step) % count) for i in range(count)])  34.7 us
    all_to_all x1, blocking collectives, local(): lax.all_to_all(partial.reshape(16, 32, width), ('xl', 'y', 'c'), 0, 0, ti...  31.4 us
    ppermute x17, starting transfers between devices, shifted(): lax.ppermute(value, axis, [(i, (i + step) % count) for i in range(count)])  28 us
    all_gather x1, waiting for transfers between devices, local(): lax.all_gather(out_share, ('w', 'xl', 'y', 'c'), axis=0, tiled=False)  21.5 us
    all_to_all x1, blocking collectives, local(): mix = lax.all_to_all(mix, 'z', 0, 0, tiled=True)  19.7 us
    pallas_call x1, Pallas kernels, temporal_attend(): pl.pallas_call(temporal_kernel, grid=(8,), out_shape=jax.ShapeDtypeStruct...  17.2 us
    pallas_call x1, Pallas kernels, spatial_attend(): pl.pallas_call(spatial_kernel, out_shape=jax.ShapeDtypeStruct((NZ, 128, 2...  10.7 us
  transfers between devices with their start and end apart: 21, of which 10 were waited for; matrix products, arithmetic and copies ran while one was open for 0% of the time, Pallas kernels for 9%

profile of v3, /device:TPU:1, one launch (start us, length us, event | category | flops | bytes accessed | tf_op | source)
XLA Modules:
  0.0 263.8 jit_solution(5781548592165484743)
XLA Ops:
  7.1 2.3 shard_map.83
  9.5 2.5 shard_map.82
  12.0 2.5 collective-permute-start
  14.4 3.9 %collective-permute-start.3 = (bf16[64,2048]{1,0:T(8,128)(2,1)}, bf16[64,2048]{1,0:T(8,128)(2,1)S(1)}, u32[]{:S(2)}, u32[]{:S(2)}) collective-permute-start(bf16[64,2048]{1,0:T(8,128)(2,1)} %get-tuple-element.40.refs_1_), channel_id=1, source_target_pairs={{0,7},{1,0},{2,1},{3,2},{4,3},{5,4},{6,5},{7,6},{8,15},{9,8},{10,9... | collective-permute-start | bytes 786440 | tf_op jit(solution)/shard_map/ppermute | solution.py:310
  18.4 1.5 collective-permute-start.2
  19.8 4.8 %collective-permute-done.refs_2_ = bf16[64,2048]{1,0:T(8,128)(2,1)S(1)} collective-permute-done((bf16[64,2048]{1,0:T(8,128)(2,1)}, bf16[64,2048]{1,0:T(8,128)(2,1)S(1)}, u32[]{:S(2)}, u32[]{:S(2)}) %collective-permute-start) | collective-permute-done | bytes 262176 | tf_op jit(solution)/shard_map/ppermute | solution.py:310
  24.6 2.7 %collective-permute-start.7 = (bf16[64,2048]{1,0:T(8,128)(2,1)S(1)}, bf16[64,2048]{1,0:T(8,128)(2,1)S(1)}, u32[]{:S(2)}, u32[]{:S(2)}) collective-permute-start(bf16[64,2048]{1,0:T(8,128)(2,1)S(1)} %collective-permute-done.3.refs_5_), channel_id=1, source_target_pairs={{0,7},{1,0},{2,1},{3,2},{4,3},{5,4},{6,5},{7,6},{8,15},{9,8},{10,9... | collective-permute-start | bytes 786440 | tf_op jit(solution)/shard_map/ppermute | solution.py:310
  27.3 4.1 %collective-permute-done.2.refs_4_ = bf16[64,2048]{1,0:T(8,128)(2,1)S(1)} collective-permute-done((bf16[64,2048]{1,0:T(8,128)(2,1)}, bf16[64,2048]{1,0:T(8,128)(2,1)S(1)}, u32[]{:S(2)}, u32[]{:S(2)}) %collective-permute-start.2) | collective-permute-done | bytes 262176 | tf_op jit(solution)/shard_map/ppermute | solution.py:310
  31.4 3.4 %collective-permute-start.6 = (bf16[64,2048]{1,0:T(8,128)(2,1)S(1)}, bf16[64,2048]{1,0:T(8,128)(2,1)S(1)}, u32[]{:S(2)}, u32[]{:S(2)}) collective-permute-start(bf16[64,2048]{1,0:T(8,128)(2,1)S(1)} %collective-permute-done.2.refs_4_), channel_id=1, source_target_pairs={{0,7},{1,0},{2,1},{3,2},{4,3},{5,4},{6,5},{7,6},{8,15},{9,8},{10,9... | collective-permute-start | bytes 786440 | tf_op jit(solution)/shard_map/ppermute | solution.py:310
  34.9 7.6 %collective-permute-done.4.refs_6_ = bf16[64,2048]{1,0:T(8,128)(2,1)S(1)} collective-permute-done((bf16[64,2048]{1,0:T(8,128)(2,1)S(1)}, bf16[64,2048]{1,0:T(8,128)(2,1)S(1)}, u32[]{:S(2)}, u32[]{:S(2)}) %collective-permute-start.4) | collective-permute-done | bytes 262176 | tf_op jit(solution)/shard_map/ppermute | solution.py:310
  42.4 2.7 %collective-permute-start.11 = (bf16[64,2048]{1,0:T(8,128)(2,1)S(1)}, bf16[64,2048]{1,0:T(8,128)(2,1)S(1)}, u32[]{:S(2)}, u32[]{:S(2)}) collective-permute-start(bf16[64,2048]{1,0:T(8,128)(2,1)S(1)} %collective-permute-done.7.refs_9_), channel_id=1, source_target_pairs={{0,7},{1,0},{2,1},{3,2},{4,3},{5,4},{6,5},{7,6},{8,15},{9,8},{10,9... | collective-permute-start | bytes 786440 | tf_op jit(solution)/shard_map/ppermute | solution.py:310
  45.1 7.1 %collective-permute-done.6.refs_8_ = bf16[64,2048]{1,0:T(8,128)(2,1)S(1)} collective-permute-done((bf16[64,2048]{1,0:T(8,128)(2,1)S(1)}, bf16[64,2048]{1,0:T(8,128)(2,1)S(1)}, u32[]{:S(2)}, u32[]{:S(2)}) %collective-permute-start.6) | collective-permute-done | bytes 262176 | tf_op jit(solution)/shard_map/ppermute | solution.py:310
  52.2 3.5 %collective-permute-start.10 = (bf16[64,2048]{1,0:T(8,128)(2,1)S(1)}, bf16[64,2048]{1,0:T(8,128)(2,1)S(1)}, u32[]{:S(2)}, u32[]{:S(2)}) collective-permute-start(bf16[64,2048]{1,0:T(8,128)(2,1)S(1)} %collective-permute-done.6.refs_8_), channel_id=1, source_target_pairs={{0,7},{1,0},{2,1},{3,2},{4,3},{5,4},{6,5},{7,6},{8,15},{9,8},{10,9... | collective-permute-start | bytes 786440 | tf_op jit(solution)/shard_map/ppermute | solution.py:310
  55.7 3.6 %collective-permute-done.8.refs_10_ = bf16[64,2048]{1,0:T(8,128)(2,1)S(1)} collective-permute-done((bf16[64,2048]{1,0:T(8,128)(2,1)S(1)}, bf16[64,2048]{1,0:T(8,128)(2,1)S(1)}, u32[]{:S(2)}, u32[]{:S(2)}) %collective-permute-start.8) | collective-permute-done | bytes 262176 | tf_op jit(solution)/shard_map/ppermute | solution.py:310
  59.4 2.7 %collective-permute-start.13 = (bf16[64,2048]{1,0:T(8,128)(2,1)S(1)}, bf16[64,2048]{1,0:T(8,128)(2,1)}, u32[]{:S(2)}, u32[]{:S(2)}) collective-permute-start(bf16[64,2048]{1,0:T(8,128)(2,1)S(1)} %collective-permute-done.11.refs_13_), channel_id=1, source_target_pairs={{0,7},{1,0},{2,1},{3,2},{4,3},{5,4},{6,5},{7,6},{8,15},{9,8},{10,9... | collective-permute-start | bytes 786440 | tf_op jit(solution)/shard_map/ppermute | solution.py:310
  62.1 1.9 collective-permute-done.10.refs_12_
  63.9 4.8 %collective-permute-done.12.refs_14_ = bf16[64,2048]{1,0:T(8,128)(2,1)S(1)} collective-permute-done((bf16[64,2048]{1,0:T(8,128)(2,1)S(1)}, bf16[64,2048]{1,0:T(8,128)(2,1)S(1)}, u32[]{:S(2)}, u32[]{:S(2)}) %collective-permute-start.12) | collective-permute-done | bytes 262176 | tf_op jit(solution)/shard_map/ppermute | solution.py:310
  69.6 2.5 shard_map.85
  72.1 1.6 collective-permute-start.14
  73.7 2.6 collective-permute-start.15
  76.3 1.1 collective-permute-start.16
  77.5 10.7 %shard_map.84 = bf16[8,128,256]{2,1,0:T(8,128)(2,1)} custom-call(s32[1]{0:T(128)} %bitcast.place_ref, bf16[3,2048,256]{2,1,0:T(8,128)(2,1)} %bitcast.38, bf16[64,2048]{1,0:T(8,128)(2,1)} %get-tuple-element.39.refs_0_, bf16[64,2048]{1,0:T(8,128)(2,1)} %get-tuple-element.40.refs_1_, bf16[64,2048]{1,0:T(8,128)(2,1)} %copy-done.6, bf16[64,2048]{1,0:T(8,128)(2,1)} %copy-done.9, ...), custom_call_target="tpu_custom_call" | custom-call | flops 6442450944 | bytes 8388608 | tf_op jit(solution)/shard_map/pallas_call | solution.py:170
  89.0 2.2 shard_map.87
  91.3 19.7 %all_to_all.15.mix_ref = bf16[8,128,256]{2,1,0:T(8,128)(2,1)} all-to-all(bf16[8,128,256]{2,1,0:T(8,128)(2,1)S(1)} %copy-done.1), channel_id=1, replica_groups=mesh['w'=2,'xl'=2,'y'=4,'c'=2,'z'=8] {'z'}, dimensions={0} | all-to-all | bytes 1048576 | tf_op jit(solution)/shard_map/all_to_all | solution.py:353
  111.1 21.5 %all-gather.9.cloned.1.call-done = bf16[256,64,256]{2,1,0:T(8,128)(2,1)} async-done(((bf16[8,64,256]{2,1,0:T(8,128)(2,1)}), bf16[256,64,256]{2,1,0:T(8,128)(2,1)}) %all-gather.9.cloned.1.call-update) | async-done | bytes 8388624 | tf_op jit(solution)/shard_map/all_gather | solution.py:345
  132.6 7.1 %shard_map.86 = (bf16[128,2048]{1,0:T(8,128)(2,1)}, bf16[16,32,2048]{2,1,0:T(8,128)(2,1)}) custom-call(bf16[8,128,256]{2,1,0:T(8,128)(2,1)} %all_to_all.15.mix_ref, bf16[8,4,8,64,256]{4,3,2,1,0:T(8,128)(2,1)} %bitcast.30, bf16[128,2048]{1,0:T(8,128)(2,1)} %get-tuple-element.62.rows_ref, f32[1,2048]{1,0:T(1,128)} %bitcast.37), custom_call_target="tpu_custom_call" | custom-call | flops 1073741824 | bytes 12582912 | tf_op jit(solution)/shard_map/pallas_call | solution.py:210
  139.7 4.5 %all-to-all-start.1 = ((bf16[16,32,2048]{2,1,0:T(8,128)(2,1)}), bf16[16,32,2048]{2,1,0:T(8,128)(2,1)S(1)}, u32[]{:S(2)}, u32[]{:S(2)}) async-start(bf16[16,32,2048]{2,1,0:T(8,128)(2,1)} %get-tuple-element.64), calls=%async_computation.1 | async-start | bytes 4194304 | tf_op jit(solution)/shard_map/all_to_all | solution.py:359
  144.7 60.2 %all-gather.11.cloned.1.call-done = bf16[64,256,256]{2,1,0:T(8,128)(2,1)} async-done(((bf16[8,256,256]{2,1,0:T(8,128)(2,1)}), bf16[64,256,256]{2,1,0:T(8,128)(2,1)}) %all-gather.11.cloned.1.call-update) | async-done | bytes 8388624 | tf_op jit(solution)/shard_map/all_gather | solution.py:355
  204.9 1.3 copy-done
  206.3 17.2 %shard_map.88 = bf16[512,2048]{1,0:T(8,128)(2,1)} custom-call(s32[1]{0:T(128)} %dynamic_slice.3.start_ref, bf16[512,2048]{1,0:T(8,128)(2,1)} %bitcast.28, bf16[8,8,256,256]{3,2,1,0:T(8,128)(2,1)} %bitcast.26, bf16[8,8,256,256]{3,2,1,0:T(8,128)(2,1)} %bitcast.27), custom_call_target="tpu_custom_call" | custom-call | flops 4294967296 | bytes 14680064 | tf_op jit(solution)/shard_map/pallas_call | solution.py:285
  223.5 31.4 %all_to_all.16 = bf16[16,32,2048]{2,1,0:T(8,128)(2,1)S(1)} all-to-all(bf16[16,32,2048]{2,1,0:T(8,128)(2,1)} %bitcast.29), channel_id=1, replica_groups=mesh['w'=2,'xl'=2,'y'=4,'c'=2,'z'=8] {'xl','y','c'}, dimensions={0} | all-to-all | bytes 4194304 | tf_op jit(solution)/shard_map/all_to_all | solution.py:362
  256.1 1.2 copy.13
  (68 shorter events, 4.2 us)
Async XLA Ops:
  6.5 63.0 %all-gather.7.cloned.1.call-start = ((), (), s32[]{:S(2)}) async-start(), calls=%async_computation.3 | async-start | bytes 1474560 | tf_op jit(solution)/shard_map/all_gather | solution.py:338
  9.4 123.2 %all-gather.9.cloned.1.call-start = ((), (), s32[]{:S(2)}) async-start(), calls=%async_computation.4 | async-start | bytes 8650752 | tf_op jit(solution)/shard_map/all_gather | solution.py:345
  12.0 12.6 %collective-permute-start = (bf16[64,2048]{1,0:T(8,128)(2,1)}, bf16[64,2048]{1,0:T(8,128)(2,1)S(1)}, u32[]{:S(2)}, u32[]{:S(2)}) collective-permute-start(bf16[64,2048]{1,0:T(8,128)(2,1)} %get-tuple-element.39.refs_0_), channel_id=1, source_target_pairs={{0,1},{1,2},{2,3},{3,4},{4,5},{5,6},{6,7},{7,0},{8,9},{9,10},{10,1... | collective-permute-start | bytes 786440 | tf_op jit(solution)/shard_map/ppermute | solution.py:310
  14.4 10.2 %collective-permute-start.3 = (bf16[64,2048]{1,0:T(8,128)(2,1)}, bf16[64,2048]{1,0:T(8,128)(2,1)S(1)}, u32[]{:S(2)}, u32[]{:S(2)}) collective-permute-start(bf16[64,2048]{1,0:T(8,128)(2,1)} %get-tuple-element.40.refs_1_), channel_id=1, source_target_pairs={{0,7},{1,0},{2,1},{3,2},{4,3},{5,4},{6,5},{7,6},{8,15},{9,8},{10,9... | collective-permute-start | bytes 786440 | tf_op jit(solution)/shard_map/ppermute | solution.py:310
  18.4 13.1 %collective-permute-start.2 = (bf16[64,2048]{1,0:T(8,128)(2,1)}, bf16[64,2048]{1,0:T(8,128)(2,1)S(1)}, u32[]{:S(2)}, u32[]{:S(2)}) collective-permute-start(bf16[64,2048]{1,0:T(8,128)(2,1)} %get-tuple-element.39.refs_0_), channel_id=1, source_target_pairs={{0,7},{1,0},{2,1},{3,2},{4,3},{5,4},{6,5},{7,6},{8,15},{9,8},{10,9... | collective-permute-start | bytes 786440 | tf_op jit(solution)/shard_map/ppermute | solution.py:310
  19.8 15.0 %collective-permute-start.1 = (bf16[64,2048]{1,0:T(8,128)(2,1)}, bf16[64,2048]{1,0:T(8,128)(2,1)S(1)}, u32[]{:S(2)}, u32[]{:S(2)}) collective-permute-start(bf16[64,2048]{1,0:T(8,128)(2,1)} %get-tuple-element.40.refs_1_), channel_id=1, source_target_pairs={{0,1},{1,2},{2,3},{3,4},{4,5},{5,6},{6,7},{7,0},{8,9},{9,10},{10,1... | collective-permute-start | bytes 786440 | tf_op jit(solution)/shard_map/ppermute | solution.py:310
  24.6 52.7 %copy-start.6 = (bf16[64,2048]{1,0:T(8,128)(2,1)}, bf16[64,2048]{1,0:T(8,128)(2,1)S(1)}, u32[]{:S(2)}) copy-start(bf16[64,2048]{1,0:T(8,128)(2,1)S(1)} %collective-permute-done.refs_2_) | copy-start | bytes 786436
  24.6 17.8 %collective-permute-start.4 = (bf16[64,2048]{1,0:T(8,128)(2,1)S(1)}, bf16[64,2048]{1,0:T(8,128)(2,1)S(1)}, u32[]{:S(2)}, u32[]{:S(2)}) collective-permute-start(bf16[64,2048]{1,0:T(8,128)(2,1)S(1)} %collective-permute-done.refs_2_), channel_id=1, source_target_pairs={{0,1},{1,2},{2,3},{3,4},{4,5},{5,6},{6,7},{7,0},{8,9},{9,10},{10,1... | collective-permute-start | bytes 786440 | tf_op jit(solution)/shard_map/ppermute | solution.py:310
  24.6 52.7 %copy-start.7 = (bf16[64,2048]{1,0:T(8,128)(2,1)}, bf16[64,2048]{1,0:T(8,128)(2,1)S(1)}, u32[]{:S(2)}) copy-start(bf16[64,2048]{1,0:T(8,128)(2,1)S(1)} %collective-permute-done.3.refs_5_) | copy-start | bytes 786436
  24.6 17.8 %collective-permute-start.7 = (bf16[64,2048]{1,0:T(8,128)(2,1)S(1)}, bf16[64,2048]{1,0:T(8,128)(2,1)S(1)}, u32[]{:S(2)}, u32[]{:S(2)}) collective-permute-start(bf16[64,2048]{1,0:T(8,128)(2,1)S(1)} %collective-permute-done.3.refs_5_), channel_id=1, source_target_pairs={{0,7},{1,0},{2,1},{3,2},{4,3},{5,4},{6,5},{7,6},{8,15},{9,8},{10,9... | collective-permute-start | bytes 786440 | tf_op jit(solution)/shard_map/ppermute | solution.py:310
  31.4 45.9 %copy-start.8 = (bf16[64,2048]{1,0:T(8,128)(2,1)}, bf16[64,2048]{1,0:T(8,128)(2,1)S(1)}, u32[]{:S(2)}) copy-start(bf16[64,2048]{1,0:T(8,128)(2,1)S(1)} %collective-permute-done.2.refs_4_) | copy-start | bytes 786436
  31.4 20.8 %collective-permute-start.6 = (bf16[64,2048]{1,0:T(8,128)(2,1)S(1)}, bf16[64,2048]{1,0:T(8,128)(2,1)S(1)}, u32[]{:S(2)}, u32[]{:S(2)}) collective-permute-start(bf16[64,2048]{1,0:T(8,128)(2,1)S(1)} %collective-permute-done.2.refs_4_), channel_id=1, source_target_pairs={{0,7},{1,0},{2,1},{3,2},{4,3},{5,4},{6,5},{7,6},{8,15},{9,8},{10,9... | collective-permute-start | bytes 786440 | tf_op jit(solution)/shard_map/ppermute | solution.py:310
  34.9 42.5 %copy-start.9 = (bf16[64,2048]{1,0:T(8,128)(2,1)}, bf16[64,2048]{1,0:T(8,128)(2,1)S(1)}, u32[]{:S(2)}) copy-start(bf16[64,2048]{1,0:T(8,128)(2,1)S(1)} %collective-permute-done.1.refs_3_) | copy-start | bytes 786436
  34.9 20.9 %collective-permute-start.5 = (bf16[64,2048]{1,0:T(8,128)(2,1)S(1)}, bf16[64,2048]{1,0:T(8,128)(2,1)S(1)}, u32[]{:S(2)}, u32[]{:S(2)}) collective-permute-start(bf16[64,2048]{1,0:T(8,128)(2,1)S(1)} %collective-permute-done.1.refs_3_), channel_id=1, source_target_pairs={{0,1},{1,2},{2,3},{3,4},{4,5},{5,6},{6,7},{7,0},{8,9},{9,10},{10,1... | collective-permute-start | bytes 786440 | tf_op jit(solution)/shard_map/ppermute | solution.py:310
  42.4 34.9 %copy-start.10 = (bf16[64,2048]{1,0:T(8,128)(2,1)}, bf16[64,2048]{1,0:T(8,128)(2,1)S(1)}, u32[]{:S(2)}) copy-start(bf16[64,2048]{1,0:T(8,128)(2,1)S(1)} %collective-permute-done.4.refs_6_) | copy-start | bytes 786436
  42.4 16.9 %collective-permute-start.8 = (bf16[64,2048]{1,0:T(8,128)(2,1)S(1)}, bf16[64,2048]{1,0:T(8,128)(2,1)S(1)}, u32[]{:S(2)}, u32[]{:S(2)}) collective-permute-start(bf16[64,2048]{1,0:T(8,128)(2,1)S(1)} %collective-permute-done.4.refs_6_), channel_id=1, source_target_pairs={{0,1},{1,2},{2,3},{3,4},{4,5},{5,6},{6,7},{7,0},{8,9},{9,10},{10,1... | collective-permute-start | bytes 786440 | tf_op jit(solution)/shard_map/ppermute | solution.py:310
  42.4 34.9 %copy-start.11 = (bf16[64,2048]{1,0:T(8,128)(2,1)}, bf16[64,2048]{1,0:T(8,128)(2,1)S(1)}, u32[]{:S(2)}) copy-start(bf16[64,2048]{1,0:T(8,128)(2,1)S(1)} %collective-permute-done.7.refs_9_) | copy-start | bytes 786436
  42.4 16.9 %collective-permute-start.11 = (bf16[64,2048]{1,0:T(8,128)(2,1)S(1)}, bf16[64,2048]{1,0:T(8,128)(2,1)S(1)}, u32[]{:S(2)}, u32[]{:S(2)}) collective-permute-start(bf16[64,2048]{1,0:T(8,128)(2,1)S(1)} %collective-permute-done.7.refs_9_), channel_id=1, source_target_pairs={{0,7},{1,0},{2,1},{3,2},{4,3},{5,4},{6,5},{7,6},{8,15},{9,8},{10,9... | collective-permute-start | bytes 786440 | tf_op jit(solution)/shard_map/ppermute | solution.py:310
  52.2 25.2 %copy-start.12 = (bf16[64,2048]{1,0:T(8,128)(2,1)}, bf16[64,2048]{1,0:T(8,128)(2,1)S(1)}, u32[]{:S(2)}) copy-start(bf16[64,2048]{1,0:T(8,128)(2,1)S(1)} %collective-permute-done.6.refs_8_) | copy-start | bytes 786436
  52.2 11.7 %collective-permute-start.10 = (bf16[64,2048]{1,0:T(8,128)(2,1)S(1)}, bf16[64,2048]{1,0:T(8,128)(2,1)S(1)}, u32[]{:S(2)}, u32[]{:S(2)}) collective-permute-start(bf16[64,2048]{1,0:T(8,128)(2,1)S(1)} %collective-permute-done.6.refs_8_), channel_id=1, source_target_pairs={{0,7},{1,0},{2,1},{3,2},{4,3},{5,4},{6,5},{7,6},{8,15},{9,8},{10,9... | collective-permute-start | bytes 786440 | tf_op jit(solution)/shard_map/ppermute | solution.py:310
  55.7 21.7 %copy-start.13 = (bf16[64,2048]{1,0:T(8,128)(2,1)}, bf16[64,2048]{1,0:T(8,128)(2,1)S(1)}, u32[]{:S(2)}) copy-start(bf16[64,2048]{1,0:T(8,128)(2,1)S(1)} %collective-permute-done.5.refs_7_) | copy-start | bytes 786436
  55.7 8.2 %collective-permute-start.9 = (bf16[64,2048]{1,0:T(8,128)(2,1)S(1)}, bf16[64,2048]{1,0:T(8,128)(2,1)S(1)}, u32[]{:S(2)}, u32[]{:S(2)}) collective-permute-start(bf16[64,2048]{1,0:T(8,128)(2,1)S(1)} %collective-permute-done.5.refs_7_), channel_id=1, source_target_pairs={{0,1},{1,2},{2,3},{3,4},{4,5},{5,6},{6,7},{7,0},{8,9},{9,10},{10,1... | collective-permute-start | bytes 786440 | tf_op jit(solution)/shard_map/ppermute | solution.py:310
  59.4 18.0 %copy-start.14 = (bf16[64,2048]{1,0:T(8,128)(2,1)}, bf16[64,2048]{1,0:T(8,128)(2,1)S(1)}, u32[]{:S(2)}) copy-start(bf16[64,2048]{1,0:T(8,128)(2,1)S(1)} %collective-permute-done.8.refs_10_) | copy-start | bytes 786436
  59.4 9.4 %collective-permute-start.12 = (bf16[64,2048]{1,0:T(8,128)(2,1)S(1)}, bf16[64,2048]{1,0:T(8,128)(2,1)S(1)}, u32[]{:S(2)}, u32[]{:S(2)}) collective-permute-start(bf16[64,2048]{1,0:T(8,128)(2,1)S(1)} %collective-permute-done.8.refs_10_), channel_id=1, source_target_pairs={{0,1},{1,2},{2,3},{3,4},{4,5},{5,6},{6,7},{7,0},{8,9},{9,10},{10,1... | collective-permute-start | bytes 786440 | tf_op jit(solution)/shard_map/ppermute | solution.py:310
  59.4 18.0 %copy-start.15 = (bf16[64,2048]{1,0:T(8,128)(2,1)}, bf16[64,2048]{1,0:T(8,128)(2,1)S(1)}, u32[]{:S(2)}) copy-start(bf16[64,2048]{1,0:T(8,128)(2,1)S(1)} %collective-permute-done.11.refs_13_) | copy-start | bytes 786436
  59.4 10.2 %collective-permute-start.13 = (bf16[64,2048]{1,0:T(8,128)(2,1)S(1)}, bf16[64,2048]{1,0:T(8,128)(2,1)}, u32[]{:S(2)}, u32[]{:S(2)}) collective-permute-start(bf16[64,2048]{1,0:T(8,128)(2,1)S(1)} %collective-permute-done.11.refs_13_), channel_id=1, source_target_pairs={{0,7},{1,0},{2,1},{3,2},{4,3},{5,4},{6,5},{7,6},{8,15},{9,8},{10,9... | collective-permute-start | bytes 786440 | tf_op jit(solution)/shard_map/ppermute | solution.py:310
  63.9 13.5 %copy-start.17 = (bf16[64,2048]{1,0:T(8,128)(2,1)}, bf16[64,2048]{1,0:T(8,128)(2,1)S(1)}, u32[]{:S(2)}) copy-start(bf16[64,2048]{1,0:T(8,128)(2,1)S(1)} %collective-permute-done.9.refs_11_) | copy-start | bytes 786436
  72.0 132.9 %all-gather.11.cloned.1.call-start = ((), (), s32[]{:S(2)}) async-start(), calls=%async_computation.5 | async-start | bytes 9437184 | tf_op jit(solution)/shard_map/all_gather | solution.py:355
  72.1 16.0 %collective-permute-start.14 = (bf16[2,4,64,256]{3,2,1,0:T(8,128)(2,1)}, bf16[2,4,64,256]{3,2,1,0:T(8,128)(2,1)S(1)}, u32[]{:S(2)}, u32[]{:S(2)}) collective-permute-start(bf16[2,4,64,256]{3,2,1,0:T(8,128)(2,1)} %get-tuple-element.57), channel_id=1, source_target_pairs={{0,16},{16,32},{32,48},{48,0},{1,17},{17,33},{33,49},{49,1},{2,18}... | collective-permute-start | bytes 786440 | tf_op jit(solution)/shard_map/ppermute | solution.py:310
  73.7 14.5 %collective-permute-start.15 = (bf16[2,4,64,256]{3,2,1,0:T(8,128)(2,1)}, bf16[2,4,64,256]{3,2,1,0:T(8,128)(2,1)S(1)}, u32[]{:S(2)}, u32[]{:S(2)}) collective-permute-start(bf16[2,4,64,256]{3,2,1,0:T(8,128)(2,1)} %get-tuple-element.58), channel_id=1, source_target_pairs={{0,32},{16,48},{32,0},{48,16},{1,33},{17,49},{33,1},{49,17},{2,34}... | collective-permute-start | bytes 786440 | tf_op jit(solution)/shard_map/ppermute | solution.py:310
  76.3 11.9 %collective-permute-start.16 = (bf16[2,4,64,256]{3,2,1,0:T(8,128)(2,1)}, bf16[2,4,64,256]{3,2,1,0:T(8,128)(2,1)S(1)}, u32[]{:S(2)}, u32[]{:S(2)}) collective-permute-start(bf16[2,4,64,256]{3,2,1,0:T(8,128)(2,1)} %get-tuple-element.59), channel_id=1, source_target_pairs={{0,48},{16,0},{32,16},{48,32},{1,49},{17,1},{33,17},{49,33},{2,50}... | collective-permute-start | bytes 786440 | tf_op jit(solution)/shard_map/ppermute | solution.py:310
  139.7 65.3 %all-to-all-start.1 = ((bf16[16,32,2048]{2,1,0:T(8,128)(2,1)}), bf16[16,32,2048]{2,1,0:T(8,128)(2,1)S(1)}, u32[]{:S(2)}, u32[]{:S(2)}) async-start(bf16[16,32,2048]{2,1,0:T(8,128)(2,1)} %get-tuple-element.64), calls=%async_computation.1 | async-start | bytes 4194304 | tf_op jit(solution)/shard_map/all_to_all | solution.py:359
  (9 other events, 34.6 us)
Sparse Core Ops, SparseCore 0:
  9.5 44.5 all-gather.6
  72.2 60.3 all-gather.8
  134.5 70.4 all-gather.10

commit v4 on v3

--- a/solution.py
+++ b/solution.py
@@ -49,76 +49,87 @@
     return lax.dot_general(a, b, (((1,), (1,)), ((), ())), preferred_element_type=F32)
 
 
-def norm_kernel(x_ref, gain_ref, a_ref, b_ref, rows_ref):
+def norm_kernel(place_ref, x_ref, gain_ref, qkv_ref, last_ref, a_ref, b_ref, rows_ref):
     gain = gain_ref[...]
     values = jnp.transpose(x_ref[...].astype(F32), (1, 0, 2)).reshape(rows_ref.shape)
-    half = a_ref.shape[0]
+    half = rows_ref.shape[0] // 2
     rows_ref[...] = values.astype(BF)
-    a_ref[...] = normed(values[:half], gain)
-    b_ref[...] = normed(values[half:], gain)
-
-
-def norm_rows(stream, gain):
+    a_ref[:half] = normed(values[:half], gain)
+    b_ref[:half] = normed(values[half:], gain)
+    shares = (qkv_ref[0], qkv_ref[1], qkv_ref[2], last_ref[...])
+    for chunk, ref in enumerate((a_ref, b_ref)):
+        for group in range(8):
+            share = shares[2 * chunk + group // 4]
+            low = 16 * (group % 4)
+            ref[half:, 256 * group : 256 * group + 256] = share[low : low + 16]
+
+
+def norm_rows(place, stream, gain, temporal_qkv, temporal_out):
     patches, frames, width = stream.shape
     count = patches * frames
-    half = jax.ShapeDtypeStruct((count // 2, width), BF)
+    half = jax.ShapeDtypeStruct((count // 2 + 16, width), BF)
+    whole = lambda *shape: pl.BlockSpec(shape, lambda i, at: (0,) * len(shape))
     return pl.pallas_call(
         norm_kernel,
-        out_shape=(half, half, jax.ShapeDtypeStruct((count, width), BF)),
-        in_specs=[vmem(), vmem()],
-        out_specs=(vmem(), vmem(), vmem()),
-        compiler_params=params(),
-        cost_estimate=pl.CostEstimate(
-            flops=4 * count * width, bytes_accessed=6 * count * width, transcendentals=0
-        ),
-    )(stream, gain)
-
-
-def cut_kernel(place_ref, out_ref, qkv_ref, last_ref, share_ref):
-    share_ref[0] = out_ref[...]
-    for kind in range(3):
-        share_ref[1 + kind] = qkv_ref[kind]
-    share_ref[4] = last_ref[...]
-
-
-def cut_share(place, spatial_out, temporal_qkv, temporal_out):
-    return pl.pallas_call(
-        cut_kernel,
         grid_spec=pltpu.PrefetchScalarGridSpec(
             num_scalar_prefetch=1,
             grid=(1,),
             in_specs=[
+                whole(patches, frames, width),
+                whole(1, width),
+                pl.BlockSpec((3, 64, 256), lambda i, at: (0, at[2], 0)),
                 pl.BlockSpec((64, 256), lambda i, at: (at[0], at[1])),
-                pl.BlockSpec((3, 64, 256), lambda i, at: (0, at[2], 0)),
-                pl.BlockSpec((64, 256), lambda i, at: (at[3], at[4])),
             ],
-            out_specs=pl.BlockSpec((5, 64, 256), lambda i, at: (0, 0, 0)),
-        ),
-        out_shape=jax.ShapeDtypeStruct((5, 64, 256), BF),
-        compiler_params=params(),
-        cost_estimate=pl.CostEstimate(flops=0, bytes_accessed=320 << 10, transcendentals=0),
-    )(place, spatial_out, temporal_qkv, temporal_out)
-
-
-def split_kernel(y_ref, shares_ref, out_ref, *sends):
+            out_specs=(
+                whole(count // 2 + 16, width),
+                whole(count // 2 + 16, width),
+                whole(count, width),
+            ),
+        ),
+        out_shape=(half, half, jax.ShapeDtypeStruct((count, width), BF)),
+        compiler_params=params(),
+        cost_estimate=pl.CostEstimate(
+            flops=4 * count * width, bytes_accessed=6 * count * width, transcendentals=0
+        ),
+    )(place, stream, gain, temporal_qkv, temporal_out)
+
+
+def split_kernel(place_ref, *refs):
+    pieces = refs[: 2 * NZ]
+    out_ref, sends = refs[2 * NZ], refs[2 * NZ + 1 :]
+    z, y = place_ref[0], place_ref[1]
     for k in range(NZ):
-        out_ref[k] = shares_ref[k, 0]
-    for step in range(4):
-        pair = lax.rem(y_ref[0] + step, 4)
-        for k in range(2):
-            sends[step][k] = shares_ref[2 * pair + k, 1:]
-
-
-def split_shares(y, shares):
-    send = jax.ShapeDtypeStruct((2, 4, 64, 256), BF)
+        source = lax.rem(z + (OFFSETS[k] + NZ), NZ)
+        step = lax.rem(source // 2 + 4 - y, 4)
+        pair = lax.rem(source, 2)
+        for block in range(4):
+            ref = pieces[2 * k + block // 2]
+            for group in range(4):
+                low = 256 * (4 * (block % 2) + group)
+                value = ref[:, low : low + 256]
+                rows = slice(16 * group, 16 * group + 16)
+                if block == 3:
+                    out_ref[source, rows] = value
+                else:
+                    sends[0][step, pair, block, rows] = value
+
+
+def split_shares(place, pieces):
     return pl.pallas_call(
         split_kernel,
-        out_shape=(jax.ShapeDtypeStruct((NZ, 64, 256), BF),) + (send,) * 4,
-        in_specs=[smem(), vmem()],
-        out_specs=(vmem(),) * 5,
-        compiler_params=params(),
-        cost_estimate=pl.CostEstimate(flops=0, bytes_accessed=3 << 20, transcendentals=0),
-    )(y, shares)
+        grid=(1,),
+        out_shape=(
+            jax.ShapeDtypeStruct((NZ, 64, 256), BF),
+            jax.ShapeDtypeStruct((4, 2, 3, 64, 256), BF),
+        ),
+        in_specs=[smem()] + [pl.BlockSpec((16, 2048), lambda i: (4, 0))] * len(pieces),
+        out_specs=(
+            pl.BlockSpec((NZ, 64, 256), lambda i: (0, 0, 0)),
+            pl.BlockSpec((4, 2, 3, 64, 256), lambda i: (0, 0, 0, 0, 0)),
+        ),
+        compiler_params=params(),
+        cost_estimate=pl.CostEstimate(flops=0, bytes_accessed=2 << 20, transcendentals=0),
+    )(place, *pieces)
 
 
 def join_kernel(y_ref, *refs):
@@ -126,15 +137,14 @@
     for step in range(4):
         low = pl.multiple_of(64 * lax.rem(y_ref[0] + (4 - step), 4), 64)
         for pair in range(2):
-            for kind in range(4):
-                block = 3 * pair + kind if kind < 3 else 6 + pair
-                out_ref[block, pl.ds(low, 64), :] = refs[step][pair, kind]
+            for kind in range(3):
+                out_ref[3 * pair + kind, pl.ds(low, 64), :] = refs[step][pair, kind]
 
 
 def join_shares(y, got):
     return pl.pallas_call(
         join_kernel,
-        out_shape=jax.ShapeDtypeStruct((8, 256, 256), BF),
+        out_shape=jax.ShapeDtypeStruct((6, 256, 256), BF),
         in_specs=[smem()] + [vmem()] * 4,
         out_specs=vmem(),
         compiler_params=params(),
@@ -179,12 +189,35 @@
     )(place, weight, *pieces)
 
 
+def column_block(weight_ref, block):
+    return jnp.concatenate(
+        [weight_ref[block, quarter, k] for k in range(NZ) for quarter in range(4)], axis=0
+    )
+
+
+def join_blocks_kernel(z_ref, *refs):
+    out_ref = refs[-1]
+    for step in range(4):
+        out_ref[lax.rem(z_ref[0] + (4 - step), 4)] = refs[step][...]
+
+
+def join_blocks(z, parts):
+    return pl.pallas_call(
+        join_blocks_kernel,
+        out_shape=jax.ShapeDtypeStruct((4, 128, 256), BF),
+        in_specs=[smem()] + [vmem()] * 4,
+        out_specs=vmem(),
+        compiler_params=params(),
+        cost_estimate=pl.CostEstimate(flops=0, bytes_accessed=512 << 10, transcendentals=0),
+    )(z, *parts)
+
+
 def middle_kernel(mix_ref, weight_ref, rows_ref, gain_ref, middle_ref, send_ref, total):
     step = pl.program_id(0)
     mix = jnp.concatenate([mix_ref[k] for k in range(NZ)], axis=1)
     for block in range(weight_ref.shape[0]):
         weight = jnp.concatenate(
-            [weight_ref[block, quarter, k] for k in range(NZ) for quarter in range(4)], axis=0
+            [weight_ref[block, head, k // 4, k % 4] for k in range(NZ) for head in range(2)], axis=0
         )
         low = pl.multiple_of((step * weight_ref.shape[0] + block) * 256, 256)
         total[:, pl.ds(low, 256)] = dot(mix, weight)
@@ -216,7 +249,7 @@
         ),
         in_specs=[
             pl.BlockSpec((NZ, 128, 256), lambda i: (0, 0, 0)),
-            pl.BlockSpec((8 // steps, 4, NZ, 64, 256), lambda i: (i, 0, 0, 0, 0)),
+            pl.BlockSpec((8 // steps, 2, 2, 4, 128, 256), lambda i: (i, 0, 0, 0, 0, 0)),
             pl.BlockSpec((128, width), lambda i: (0, 0)),
             pl.BlockSpec((1, width), lambda i: (0, 0)),
         ],
@@ -232,15 +265,12 @@
     )(mix, weight, rows, gain)
 
 
-def temporal_kernel(start_ref, rows_ref, weight_ref, last_ref, out_ref, qkv, mix, bias):
+def temporal_kernel(start_ref, rows_ref, weight_ref, out_ref, qkv, bias):
     step = pl.program_id(0)
     kind = lax.rem(step, 3)
     rows_count = rows_ref.shape[0]
-
-    @pl.when(step < 6)
-    def _():
-        weight = weight_ref[:, 0].reshape(2048, 256)
-        qkv[kind] = dot(rows_ref[...], weight).astype(BF)
+    weight = weight_ref[:, 0].reshape(2048, 256)
+    qkv[kind] = dot(rows_ref[...], weight).astype(BF)
 
     @pl.when(step == 0)
     def _():
@@ -263,7 +293,8 @@
                 hidden = bias[low : low + block, : low + block]
                 scores = jnp.where(hidden < 0.0, hidden, scores)
                 at = 256 * pair + head * E
-                mix[low : low + block, at : at + E] = dot(softmax(scores), value).astype(BF)
+                mixed = dot(softmax(scores), value).astype(BF)
+                out_ref[low // 32 : low // 32 + 4, :, at : at + E] = mixed.reshape(4, 32, E)
 
     @pl.when(step == 2)
     def _():
@@ -273,36 +304,77 @@
     def _():
         attend(1)
 
-    @pl.when(step >= 6)
-    def _():
-        for block in range(4):
-            weight = last_ref[block].reshape(512, 256)
-            out_ref[:, 256 * block : 256 * block + 256] = dot(mix[...], weight).astype(BF)
-
 
 def temporal_attend(start, rows, weight):
     count, width = rows.shape
     return pl.pallas_call(
         temporal_kernel,
-        grid=(8,),
-        out_shape=jax.ShapeDtypeStruct((count, width), BF),
+        grid=(6,),
+        out_shape=jax.ShapeDtypeStruct((16, 32, 512), BF),
         in_specs=[
             smem(),
             pl.BlockSpec((count, width), lambda i: (0, 0)),
-            pl.BlockSpec((8, 1, 256, 256), lambda i: (0, jnp.minimum(i, 5), 0, 0)),
-            pl.BlockSpec((4, 2, 256, 256), lambda i: (jnp.maximum(i - 6, 0), 3, 0, 0)),
+            pl.BlockSpec((8, 1, 256, 256), lambda i: (0, i, 0, 0)),
         ],
-        out_specs=pl.BlockSpec((count, width // 2), lambda i: (0, jnp.maximum(i - 6, 0))),
+        out_specs=pl.BlockSpec((16, 32, 512), lambda i: (0, 0, 0)),
         scratch_shapes=[
             pltpu.VMEM((3, count, 256), BF),
-            pltpu.VMEM((count, 512), BF),
             pltpu.VMEM((count, count), F32),
         ],
         compiler_params=params(),
         cost_estimate=pl.CostEstimate(
-            flops=2 * 512 * 2048 * 2048, bytes_accessed=14 << 20, transcendentals=131072
-        ),
-    )(start, rows, weight, weight)
+            flops=2 * 512 * 2048 * 1536, bytes_accessed=9 << 20, transcendentals=131072
+        ),
+    )(start, rows, weight)
+
+
+def last_kernel(mix_ref, weight_ref, middle_ref, out_ref, total):
+    step = pl.program_id(0)
+    mix = jnp.concatenate(
+        [
+            jnp.concatenate([mix_ref[xl * 8 + y * 2 + c] for xl in range(2) for c in range(2)], axis=0)
+            for y in range(4)
+        ],
+        axis=1,
+    )
+    for block in range(weight_ref.shape[0]):
+        low = pl.multiple_of((step * weight_ref.shape[0] + block) * 256, 256)
+        total[:, pl.ds(low, 256)] = dot(mix, column_block(weight_ref, block))
+
+    @pl.when(step == pl.num_programs(0) - 1)
+    def _():
+        for group in range(4):
+            rows = total[32 * group : 32 * group + 32].reshape(4, 8, -1)
+            middle = jnp.stack(
+                [
+                    middle_ref[32 * f : 32 * f + 32].astype(F32)[8 * group : 8 * group + 8]
+                    for f in range(4)
+                ],
+                axis=0,
+            )
+            out = jnp.transpose(rows + middle, (1, 0, 2)).astype(BF)
+            out_ref[8 * group : 8 * group + 8] = out
+
+
+def last_rows(mix, weight, middle):
+    steps = 4
+    width = middle.shape[1]
+    return pl.pallas_call(
+        last_kernel,
+        grid=(steps,),
+        out_shape=jax.ShapeDtypeStruct((32, 4, width), BF),
+        in_specs=[
+            pl.BlockSpec((16, 32, 512), lambda i: (0, 0, 0)),
+            pl.BlockSpec((8 // steps, 4, NZ, 64, 256), lambda i: (i, 0, 0, 0, 0)),
+            pl.BlockSpec((128, width), lambda i: (0, 0)),
+        ],
+        out_specs=pl.BlockSpec((32, 4, width), lambda i: (0, 0, 0)),
+        scratch_shapes=[pltpu.VMEM((128, width), F32)],
+        compiler_params=params(),
+        cost_estimate=pl.CostEstimate(
+            flops=2 * 128 * 2048 * 2048, bytes_accessed=12 << 20, transcendentals=0
+        ),
+    )(mix, weight, middle)
 
 
 def shifted(value, axis, step):
@@ -330,40 +402,49 @@
             lax.rem(y, 2) * 2 + c,
             (w * 2 + xl) * 2 + y // 2,
             ((w * 2 + xl) * 2 + c) * 4 + y,
-            y,
-            (w * 2 + xl) * 2 + c,
         ]
     ).astype(jnp.int32)
-    share = cut_share(place, spatial_out, jnp.transpose(temporal_qkv, (1, 0, 2)), temporal_out)
-    shares = lax.all_gather(share, "z", axis=0, tiled=False)
-
-    first, second, rows = norm_rows(stream, spatial_gain.reshape(1, width))
+
+    block = lax.dynamic_slice(
+        spatial_out, (lax.rem(y, 2) * 128, place[1] * 256), (128, 256)
+    )
+    parts = []
+    for k in range(4):
+        pairs = [
+            (a * 8 + b, (b // 4) * 8 + (b + 4 * a + k) % 8) for a in range(2) for b in range(8)
+        ]
+        parts.append(lax.ppermute(block, ("c", "z"), pairs))
+    gathered = join_blocks(z.reshape(1), parts)
+    whole_out = lax.all_gather(gathered, ("w", "xl", "y", "c"), axis=0, tiled=False)
+    whole_out = whole_out.reshape(8, 2, 2, 4, 128, 256)
+
+    stream, parts = lax.optimization_barrier((stream, parts))
+    first, second, rows = norm_rows(
+        place, stream, spatial_gain.reshape(1, width), jnp.transpose(temporal_qkv, (1, 0, 2)), temporal_out
+    )
     pieces = gathered_rows((first, second))
-    *pieces, shares = lax.optimization_barrier((*pieces, shares))
-
-    out_share, *sends = split_shares(y.reshape(1), shares)
-    whole_out = lax.all_gather(out_share, ("w", "xl", "y", "c"), axis=0, tiled=False)
-    whole_out = whole_out.reshape(8, 4, NZ, 64, 256)
-
+
+    last_share, sends = split_shares(jnp.stack([z, y]).astype(jnp.int32), pieces)
     got = [sends[0]] + [shifted(sends[k], "y", k) for k in range(1, 4)]
 
     weight = jnp.transpose(spatial_qkv, (1, 0, 2))
     mix = spatial_attend(z.reshape(1), weight, pieces)
     mix, *got = lax.optimization_barrier((mix, *got))
+    quarter = join_shares(y.reshape(1), got)
+    mix, quarter = lax.optimization_barrier((mix, quarter))
+    quarter = lax.all_gather(quarter[None], ("w", "xl", "c"), axis=0, tiled=True)
     mix = lax.all_to_all(mix, "z", 0, 0, tiled=True)
-    quarter = join_shares(y.reshape(1), got)
-    quarter = lax.all_gather(quarter[None], ("w", "xl", "c"), axis=0, tiled=True)
 
     middle, send = middle_rows(mix, whole_out, rows, temporal_gain.reshape(1, width))
+    last_share, middle = lax.optimization_barrier((last_share, middle))
+    whole_last = lax.all_gather(last_share, ("w", "xl", "y", "c"), axis=0, tiled=False)
+    whole_last = whole_last.reshape(8, 4, NZ, 64, 256)
 
     window = lax.all_to_all(send, ("xl", "y", "c"), 0, 0, tiled=True)
     start = lax.dynamic_slice(starts, (w,), (1,))
-    partial = temporal_attend(start, window.reshape(512, width), quarter)
-    back = lax.all_to_all(partial.reshape(16, 32, width), ("xl", "y", "c"), 0, 0, tiled=True)
-    summed = jnp.sum(back.reshape(2, 4, 2, 4, 8, width).astype(F32), axis=1)
-    out = middle.reshape(4, 2, 2, 8, width).astype(F32) + jnp.transpose(summed, (2, 0, 1, 3, 4))
-    out = out.astype(BF).reshape(frames, patches, width)
-    return jnp.transpose(out, (1, 0, 2))
+    mix = temporal_attend(start, window.reshape(512, width), quarter)
+    mix = lax.all_to_all(mix, ("xl", "y", "c"), 0, 0, tiled=True)
+    return last_rows(mix, whole_last, middle)
 
 
 def solution(mesh):

time: 264 us -> 237 us (0.90)
  waiting for transfers between devices: 117 us -> 76.6 us
  starting transfers between devices: 32.6 us -> 47.5 us
  blocking collectives: 51.2 us -> 42.4 us
  Pallas kernels: 44.4 us -> 48.5 us
    all_gather x1, waiting for transfers between devices: 60.2 us -> 7.36 us  [local(): lax.all_gather(quarter[None], ('w', 'xl', 'c'), axis=0, tiled=True)]
    all_to_all x1, waiting for transfers between devices: 0.01 us -> 21.6 us  [local(): window = lax.all_to_all(send, ('xl', 'y', 'c'), 0, 0, tiled=True)]
    ppermute x0 -> x4, starting transfers between devices: none -> 13.8 us  [local(): parts.append(lax.ppermute(block, ('c', 'z'), pairs))]
    all_gather x2, waiting for transfers between devices: 21.5 us -> 12 us  [the longest x1 12 us: local(): lax.all_gather(last_share, ('w', 'xl', 'y', 'c'), axis=0, tiled=False)]
    all_to_all x1, blocking collectives: 31.4 us -> 22.6 us  [local(): mix = lax.all_to_all(mix, ('xl', 'y', 'c'), 0, 0, tiled=True)]
    ppermute x0 -> x4, waiting for transfers between devices: none -> 3.92 us  [local(): parts.append(lax.ppermute(block, ('c', 'z'), pairs))]
    pallas_call x5 -> x6, Pallas kernels: 26.7 us -> 30.3 us  [the longest x1 14.6 us: temporal_attend(): pl.pallas_call(temporal_kernel, grid=(6,), out_shape=jax.ShapeDtypeStruct...]
    ppermute x17, waiting for transfers between devices: 34.7 us -> 31.7 us  [shifted(): lax.ppermute(value, axis, [(i, (i + step) % count) for i in range(count)])]
  transfers between devices with their start and end apart: 21 -> 25, of which waited for: 10 -> 15; matrix products, arithmetic and copies ran while one was open for 0% -> 2% of each run, Pallas kernels for 9% -> 17%
where the time goes in v4:
time: 237 us
  waiting for transfers between devices  76.6 us (32%)
  Pallas kernels  48.5 us (20%)
  starting transfers between devices  47.5 us (20%)
  blocking collectives  42.4 us (18%)
  between operations  13.3 us (6%)
  local copies, waits for them, and re-layouts  7.02 us (3%)
    ppermute x17, waiting for transfers between devices, shifted(): lax.ppermute(value, axis, [(i, (i + step) % count) for i in range(count)])  31.7 us
    ppermute x17, starting transfers between devices, shifted(): lax.ppermute(value, axis, [(i, (i + step) % count) for i in range(count)])  27.3 us
    all_to_all x1, blocking collectives, local(): mix = lax.all_to_all(mix, ('xl', 'y', 'c'), 0, 0, tiled=True)  22.6 us
    all_to_all x1, waiting for transfers between devices, local(): window = lax.all_to_all(send, ('xl', 'y', 'c'), 0, 0, tiled=True)  21.6 us
    all_to_all x1, blocking collectives, local(): mix = lax.all_to_all(mix, 'z', 0, 0, tiled=True)  19.8 us
    pallas_call x1, Pallas kernels, temporal_attend(): pl.pallas_call(temporal_kernel, grid=(6,), out_shape=jax.ShapeDtypeStruct...  14.6 us
    ppermute x4, starting transfers between devices, local(): parts.append(lax.ppermute(block, ('c', 'z'), pairs))  13.8 us
    all_gather x1, waiting for transfers between devices, local(): lax.all_gather(last_share, ('w', 'xl', 'y', 'c'), axis=0, tiled=False)  12 us
  transfers between devices with their start and end apart: 25, of which 15 were waited for; matrix products, arithmetic and copies ran while one was open for 2% of the time, Pallas kernels for 17%

profile of v4, /device:TPU:1, one launch (start us, length us, event | category | flops | bytes accessed | tf_op | source)
XLA Modules:
  0.0 236.7 jit_solution(2255097177236596772)
XLA Ops:
  7.4 10.2 %collective-permute-start = (bf16[128,256]{1,0:T(8,128)(2,1)S(1)}, bf16[128,256]{1,0:T(8,128)(2,1)S(1)}, u32[]{:S(2)}, u32[]{:S(2)}) collective-permute-start(bf16[128,256]{1,0:T(8,128)(2,1)S(1)} %dynamic_slice.7), channel_id=1, source_target_pairs={{0,0},{1,1},{2,2},{3,3},{4,12},{5,13},{6,14},{7,15},{8,4},{9,5},{1... | collective-permute-start | bytes 196616 | tf_op jit(solution)/shard_map/ppermute | solution.py:416
  18.4 2.8 %collective-permute-start.3 = (bf16[128,256]{1,0:T(8,128)(2,1)S(1)}, bf16[128,256]{1,0:T(8,128)(2,1)S(1)}, u32[]{:S(2)}, u32[]{:S(2)}) collective-permute-start(bf16[128,256]{1,0:T(8,128)(2,1)S(1)} %dynamic_slice.7), channel_id=1, source_target_pairs={{0,3},{1,4},{2,5},{3,6},{4,15},{5,8},{6,9},{7,10},{8,7},{9,0},{10,... | collective-permute-start | bytes 196616 | tf_op jit(solution)/shard_map/ppermute | solution.py:416
  25.7 1.7 shard_map.86
  28.1 3.2 %shard_map.82 = (bf16[80,2048]{1,0:T(8,128)(2,1)}, bf16[80,2048]{1,0:T(8,128)(2,1)}, bf16[128,2048]{1,0:T(8,128)(2,1)}) custom-call(s32[3]{0:T(128)} %pad_add_fusion.place_ref, bf16[32,4,2048]{2,1,0:T(4,128)(2,1)} %x_ref, f32[1,2048]{1,0:T(1,128)} %bitcast.25, bf16[3,2048,256]{2,1,0:T(8,128)(2,1)} %bitcast.23, bf16[256,2048]{1,0:T(8,128)(2,1)} %last_ref.1), custom_call_target="tpu_custom_call" | custom-call | flops 1048576 | bytes 1572864 | tf_op jit(solution)/shard_map/pallas_call | solution.py:72
  31.4 3.9 %collective-permute-start.4 = (bf16[80,2048]{1,0:T(8,128)(2,1)}, bf16[80,2048]{1,0:T(8,128)(2,1)S(1)}, u32[]{:S(2)}, u32[]{:S(2)}) collective-permute-start(bf16[80,2048]{1,0:T(8,128)(2,1)} %get-tuple-element.23.refs_0_), channel_id=1, source_target_pairs={{0,1},{1,2},{2,3},{3,4},{4,5},{5,6},{6,7},{7,0},{8,9},{9,10},{10,1... | collective-permute-start | bytes 983048 | tf_op jit(solution)/shard_map/ppermute | solution.py:382
  38.0 5.3 %collective-permute-done.4.refs_2_ = bf16[80,2048]{1,0:T(8,128)(2,1)S(1)} collective-permute-done((bf16[80,2048]{1,0:T(8,128)(2,1)}, bf16[80,2048]{1,0:T(8,128)(2,1)S(1)}, u32[]{:S(2)}, u32[]{:S(2)}) %collective-permute-start.4) | collective-permute-done | bytes 327712 | tf_op jit(solution)/shard_map/ppermute | solution.py:382
  43.3 2.0 collective-permute-start.8
  46.4 3.9 %collective-permute-done.5.refs_3_ = bf16[80,2048]{1,0:T(8,128)(2,1)S(1)} collective-permute-done((bf16[80,2048]{1,0:T(8,128)(2,1)}, bf16[80,2048]{1,0:T(8,128)(2,1)S(1)}, u32[]{:S(2)}, u32[]{:S(2)}) %collective-permute-start.5) | collective-permute-done | bytes 327712 | tf_op jit(solution)/shard_map/ppermute | solution.py:382
  50.3 2.1 collective-permute-start.9
  53.4 3.9 %collective-permute-done.8.refs_6_ = bf16[80,2048]{1,0:T(8,128)(2,1)S(1)} collective-permute-done((bf16[80,2048]{1,0:T(8,128)(2,1)S(1)}, bf16[80,2048]{1,0:T(8,128)(2,1)S(1)}, u32[]{:S(2)}, u32[]{:S(2)}) %collective-permute-start.8) | collective-permute-done | bytes 327712 | tf_op jit(solution)/shard_map/ppermute | solution.py:382
  57.3 2.0 collective-permute-start.12
  60.5 3.9 %collective-permute-done.9.refs_7_ = bf16[80,2048]{1,0:T(8,128)(2,1)S(1)} collective-permute-done((bf16[80,2048]{1,0:T(8,128)(2,1)S(1)}, bf16[80,2048]{1,0:T(8,128)(2,1)S(1)}, u32[]{:S(2)}, u32[]{:S(2)}) %collective-permute-start.9) | collective-permute-done | bytes 327712 | tf_op jit(solution)/shard_map/ppermute | solution.py:382
  64.3 2.0 collective-permute-start.13
  67.5 4.0 %collective-permute-done.12.refs_10_ = bf16[80,2048]{1,0:T(8,128)(2,1)S(1)} collective-permute-done((bf16[80,2048]{1,0:T(8,128)(2,1)S(1)}, bf16[80,2048]{1,0:T(8,128)(2,1)S(1)}, u32[]{:S(2)}, u32[]{:S(2)}) %collective-permute-start.12) | collective-permute-done | bytes 327712 | tf_op jit(solution)/shard_map/ppermute | solution.py:382
  71.5 2.0 collective-permute-start.16
  75.3 3.2 %collective-permute-done.13.refs_11_ = bf16[80,2048]{1,0:T(8,128)(2,1)S(1)} collective-permute-done((bf16[80,2048]{1,0:T(8,128)(2,1)S(1)}, bf16[80,2048]{1,0:T(8,128)(2,1)S(1)}, u32[]{:S(2)}, u32[]{:S(2)}) %collective-permute-start.13) | collective-permute-done | bytes 327712 | tf_op jit(solution)/shard_map/ppermute | solution.py:382
  78.5 2.0 collective-permute-done.14.refs_12_
  80.5 5.0 %collective-permute-done.16.refs_14_ = bf16[80,2048]{1,0:T(8,128)(2,1)S(1)} collective-permute-done((bf16[80,2048]{1,0:T(8,128)(2,1)S(1)}, bf16[80,2048]{1,0:T(8,128)(2,1)S(1)}, u32[]{:S(2)}, u32[]{:S(2)}) %collective-permute-start.16) | collective-permute-done | bytes 327712 | tf_op jit(solution)/shard_map/ppermute | solution.py:382
  87.0 2.3 shard_map.84
  89.3 2.0 slice_bitcast_fusion
  92.6 2.6 %collective-permute-start.19 = (bf16[2,3,64,256]{3,2,1,0:T(8,128)(2,1)S(1)}, bf16[2,3,64,256]{3,2,1,0:T(8,128)(2,1)S(1)}, u32[]{:S(2)}, u32[]{:S(2)}) collective-permute-start(bf16[2,3,64,256]{3,2,1,0:T(8,128)(2,1)S(1)} %get-tuple-element.40), channel_id=1, source_target_pairs={{0,32},{16,48},{32,0},{48,16},{1,33},{17,49},{33,1},{49,17},{2,34}... | collective-permute-start | bytes 589832 | tf_op jit(solution)/shard_map/ppermute | solution.py:382
  96.3 11.1 %shard_map.83 = bf16[8,128,256]{2,1,0:T(8,128)(2,1)} custom-call(s32[1]{0:T(128)} %bitcast.place_ref.z_ref, bf16[3,2048,256]{2,1,0:T(8,128)(2,1)} %bitcast.28, bf16[80,2048]{1,0:T(8,128)(2,1)} %get-tuple-element.23.refs_0_, bf16[80,2048]{1,0:T(8,128)(2,1)} %get-tuple-element.24.refs_1_, bf16[80,2048]{1,0:T(8,128)(2,1)} %copy-done.1, ...), custom_call_target="tpu_custom_call" | custom-call | flops 6442450944 | bytes 8388608 | tf_op jit(solution)/shard_map/pallas_call | solution.py:180
  108.1 2.2 shard_map.85
  110.4 19.8 %all_to_all.15.mix_ref = bf16[8,128,256]{2,1,0:T(8,128)(2,1)} all-to-all(bf16[8,128,256]{2,1,0:T(8,128)(2,1)} %shard_map.83), channel_id=1, replica_groups=mesh['w'=2,'xl'=2,'y'=4,'c'=2,'z'=8] {'z'}, dimensions={0} | all-to-all | bytes 1048576 | tf_op jit(solution)/shard_map/all_to_all | solution.py:436
  130.2 7.2 %shard_map.87 = (bf16[128,2048]{1,0:T(8,128)(2,1)}, bf16[16,32,2048]{2,1,0:T(8,128)(2,1)}) custom-call(bf16[8,128,256]{2,1,0:T(8,128)(2,1)} %all_to_all.15.mix_ref, bf16[8,2,2,4,128,256]{5,4,3,2,1,0:T(8,128)(2,1)} %bitcast.22, bf16[128,2048]{1,0:T(8,128)(2,1)} %get-tuple-element.32.rows_ref, f32[1,2048]{1,0:T(1,128)} %bitcast.26), custom_call_target="tpu_custom_call" | custom-call | flops 1073741824 | bytes 12582912 | tf_op jit(solution)/shard_map/pallas_call | solution.py:243
  137.4 6.4 %all-to-all-start.1 = ((bf16[16,32,2048]{2,1,0:T(8,128)(2,1)}), bf16[16,32,2048]{2,1,0:T(8,128)(2,1)S(1)}, u32[]{:S(2)}, u32[]{:S(2)}) async-start(bf16[16,32,2048]{2,1,0:T(8,128)(2,1)} %get-tuple-element.33), calls=%async_computation.1 | async-start | bytes 4194304 | tf_op jit(solution)/shard_map/all_to_all | solution.py:443
  144.3 7.4 %all-gather.9.cloned.1.call-done = bf16[48,256,256]{2,1,0:T(8,128)(2,1)} async-done(((bf16[6,256,256]{2,1,0:T(8,128)(2,1)}), bf16[48,256,256]{2,1,0:T(8,128)(2,1)}) %all-gather.9.cloned.1.call-update) | async-done | bytes 6291472 | tf_op jit(solution)/shard_map/all_gather | solution.py:435
  151.7 21.6 %all-to-all-done.1 = bf16[16,32,2048]{2,1,0:T(8,128)(2,1)S(1)} async-done(((bf16[16,32,2048]{2,1,0:T(8,128)(2,1)}), bf16[16,32,2048]{2,1,0:T(8,128)(2,1)S(1)}, u32[]{:S(2)}, u32[]{:S(2)}) %all-to-all-start.1) | async-done | bytes 2097184 | tf_op jit(solution)/shard_map/all_to_all | solution.py:443
  174.6 14.6 %shard_map.88 = bf16[16,32,512]{2,1,0:T(8,128)(2,1)} custom-call(s32[1]{0:T(128)} %dynamic_slice.6.start_ref, bf16[512,2048]{1,0:T(8,128)(2,1)} %bitcast.24, bf16[8,6,256,256]{3,2,1,0:T(8,128)(2,1)} %bitcast.27), custom_call_target="tpu_custom_call" | custom-call | flops 3221225472 | bytes 9437184 | tf_op jit(solution)/shard_map/pallas_call | solution.py:310
  189.2 22.6 %all_to_all.16.mix_ref = bf16[16,32,512]{2,1,0:T(8,128)(2,1)} all-to-all(bf16[16,32,512]{2,1,0:T(8,128)(2,1)} %shard_map.88), channel_id=1, replica_groups=mesh['w'=2,'xl'=2,'y'=4,'c'=2,'z'=8] {'xl','y','c'}, dimensions={0} | all-to-all | bytes 1048576 | tf_op jit(solution)/shard_map/all_to_all | solution.py:446
  211.8 12.0 %all-gather.11.cloned.1.call-done = bf16[256,64,256]{2,1,0:T(8,128)(2,1)} async-done(((bf16[8,64,256]{2,1,0:T(8,128)(2,1)}), bf16[256,64,256]{2,1,0:T(8,128)(2,1)}) %all-gather.11.cloned.1.call-update) | async-done | bytes 8388624 | tf_op jit(solution)/shard_map/all_gather | solution.py:440
  223.8 6.4 %shard_map.89 = bf16[32,4,2048]{2,1,0:T(4,128)(2,1)} custom-call(bf16[16,32,512]{2,1,0:T(8,128)(2,1)} %all_to_all.16.mix_ref, bf16[8,4,8,64,256]{4,3,2,1,0:T(8,128)(2,1)} %bitcast.21, bf16[128,2048]{1,0:T(8,128)(2,1)} %get-tuple-element.38.middle_ref), custom_call_target="tpu_custom_call" | custom-call | flops 1073741824 | bytes 12582912 | tf_op jit(solution)/shard_map/pallas_call | solution.py:362
  (82 shorter events, 22.4 us)
Async XLA Ops:
  6.5 123.6 %all-gather.7.cloned.1.call-start = ((), (), s32[]{:S(2)}) async-start(), calls=%async_computation.3 | async-start | bytes 8650752 | tf_op jit(solution)/shard_map/all_gather | solution.py:418
  7.4 13.8 %collective-permute-start = (bf16[128,256]{1,0:T(8,128)(2,1)S(1)}, bf16[128,256]{1,0:T(8,128)(2,1)S(1)}, u32[]{:S(2)}, u32[]{:S(2)}) collective-permute-start(bf16[128,256]{1,0:T(8,128)(2,1)S(1)} %dynamic_slice.7), channel_id=1, source_target_pairs={{0,0},{1,1},{2,2},{3,3},{4,12},{5,13},{6,14},{7,15},{8,4},{9,5},{1... | collective-permute-start | bytes 196616 | tf_op jit(solution)/shard_map/ppermute | solution.py:416
  17.6 5.0 %collective-permute-start.1 = (bf16[128,256]{1,0:T(8,128)(2,1)S(1)}, bf16[128,256]{1,0:T(8,128)(2,1)S(1)}, u32[]{:S(2)}, u32[]{:S(2)}) collective-permute-start(bf16[128,256]{1,0:T(8,128)(2,1)S(1)} %dynamic_slice.7), channel_id=1, source_target_pairs={{0,1},{1,2},{2,3},{3,4},{4,13},{5,14},{6,15},{7,8},{8,5},{9,6},{10... | collective-permute-start | bytes 196616 | tf_op jit(solution)/shard_map/ppermute | solution.py:416
  17.7 6.0 %collective-permute-start.2 = (bf16[128,256]{1,0:T(8,128)(2,1)S(1)}, bf16[128,256]{1,0:T(8,128)(2,1)S(1)}, u32[]{:S(2)}, u32[]{:S(2)}) collective-permute-start(bf16[128,256]{1,0:T(8,128)(2,1)S(1)} %dynamic_slice.7), channel_id=1, source_target_pairs={{0,2},{1,3},{2,4},{3,5},{4,14},{5,15},{6,8},{7,9},{8,6},{9,7},{10,... | collective-permute-start | bytes 196616 | tf_op jit(solution)/shard_map/ppermute | solution.py:416
  18.4 6.7 %collective-permute-start.3 = (bf16[128,256]{1,0:T(8,128)(2,1)S(1)}, bf16[128,256]{1,0:T(8,128)(2,1)S(1)}, u32[]{:S(2)}, u32[]{:S(2)}) collective-permute-start(bf16[128,256]{1,0:T(8,128)(2,1)S(1)} %dynamic_slice.7), channel_id=1, source_target_pairs={{0,3},{1,4},{2,5},{3,6},{4,15},{5,8},{6,9},{7,10},{8,7},{9,0},{10,... | collective-permute-start | bytes 196616 | tf_op jit(solution)/shard_map/ppermute | solution.py:416
  27.4 124.3 %all-gather.9.cloned.1.call-start = ((), (), s32[]{:S(2)}) async-start(), calls=%async_computation.4 | async-start | bytes 7077888 | tf_op jit(solution)/shard_map/all_gather | solution.py:435
  31.4 11.9 %collective-permute-start.4 = (bf16[80,2048]{1,0:T(8,128)(2,1)}, bf16[80,2048]{1,0:T(8,128)(2,1)S(1)}, u32[]{:S(2)}, u32[]{:S(2)}) collective-permute-start(bf16[80,2048]{1,0:T(8,128)(2,1)} %get-tuple-element.23.refs_0_), channel_id=1, source_target_pairs={{0,1},{1,2},{2,3},{3,4},{4,5},{5,6},{6,7},{7,0},{8,9},{9,10},{10,1... | collective-permute-start | bytes 983048 | tf_op jit(solution)/shard_map/ppermute | solution.py:382
  35.3 10.0 %collective-permute-start.7 = (bf16[80,2048]{1,0:T(8,128)(2,1)}, bf16[80,2048]{1,0:T(8,128)(2,1)S(1)}, u32[]{:S(2)}, u32[]{:S(2)}) collective-permute-start(bf16[80,2048]{1,0:T(8,128)(2,1)} %get-tuple-element.24.refs_1_), channel_id=1, source_target_pairs={{0,7},{1,0},{2,1},{3,2},{4,3},{5,4},{6,5},{7,6},{8,15},{9,8},{10,9... | collective-permute-start | bytes 983048 | tf_op jit(solution)/shard_map/ppermute | solution.py:382
  35.3 15.0 %collective-permute-start.5 = (bf16[80,2048]{1,0:T(8,128)(2,1)}, bf16[80,2048]{1,0:T(8,128)(2,1)S(1)}, u32[]{:S(2)}, u32[]{:S(2)}) collective-permute-start(bf16[80,2048]{1,0:T(8,128)(2,1)} %get-tuple-element.24.refs_1_), channel_id=1, source_target_pairs={{0,1},{1,2},{2,3},{3,4},{4,5},{5,6},{6,7},{7,0},{8,9},{9,10},{10,1... | collective-permute-start | bytes 983048 | tf_op jit(solution)/shard_map/ppermute | solution.py:382
  36.7 15.7 %collective-permute-start.6 = (bf16[80,2048]{1,0:T(8,128)(2,1)}, bf16[80,2048]{1,0:T(8,128)(2,1)S(1)}, u32[]{:S(2)}, u32[]{:S(2)}) collective-permute-start(bf16[80,2048]{1,0:T(8,128)(2,1)} %get-tuple-element.23.refs_0_), channel_id=1, source_target_pairs={{0,7},{1,0},{2,1},{3,2},{4,3},{5,4},{6,5},{7,6},{8,15},{9,8},{10,9... | collective-permute-start | bytes 983048 | tf_op jit(solution)/shard_map/ppermute | solution.py:382
  43.3 42.8 %copy-start.1 = (bf16[80,2048]{1,0:T(8,128)(2,1)}, bf16[80,2048]{1,0:T(8,128)(2,1)S(1)}, u32[]{:S(2)}) copy-start(bf16[80,2048]{1,0:T(8,128)(2,1)S(1)} %collective-permute-done.4.refs_2_) | copy-start | bytes 983044
  43.3 14.0 %collective-permute-start.8 = (bf16[80,2048]{1,0:T(8,128)(2,1)S(1)}, bf16[80,2048]{1,0:T(8,128)(2,1)S(1)}, u32[]{:S(2)}, u32[]{:S(2)}) collective-permute-start(bf16[80,2048]{1,0:T(8,128)(2,1)S(1)} %collective-permute-done.4.refs_2_), channel_id=1, source_target_pairs={{0,1},{1,2},{2,3},{3,4},{4,5},{5,6},{6,7},{7,0},{8,9},{9,10},{10,1... | collective-permute-start | bytes 983048 | tf_op jit(solution)/shard_map/ppermute | solution.py:382
  45.3 40.8 %copy-start.2 = (bf16[80,2048]{1,0:T(8,128)(2,1)}, bf16[80,2048]{1,0:T(8,128)(2,1)S(1)}, u32[]{:S(2)}) copy-start(bf16[80,2048]{1,0:T(8,128)(2,1)S(1)} %collective-permute-done.7.refs_5_) | copy-start | bytes 983044
  45.3 14.0 %collective-permute-start.11 = (bf16[80,2048]{1,0:T(8,128)(2,1)S(1)}, bf16[80,2048]{1,0:T(8,128)(2,1)S(1)}, u32[]{:S(2)}, u32[]{:S(2)}) collective-permute-start(bf16[80,2048]{1,0:T(8,128)(2,1)S(1)} %collective-permute-done.7.refs_5_), channel_id=1, source_target_pairs={{0,7},{1,0},{2,1},{3,2},{4,3},{5,4},{6,5},{7,6},{8,15},{9,8},{10,9... | collective-permute-start | bytes 983048 | tf_op jit(solution)/shard_map/ppermute | solution.py:382
  50.3 35.7 %copy-start.3 = (bf16[80,2048]{1,0:T(8,128)(2,1)}, bf16[80,2048]{1,0:T(8,128)(2,1)S(1)}, u32[]{:S(2)}) copy-start(bf16[80,2048]{1,0:T(8,128)(2,1)S(1)} %collective-permute-done.5.refs_3_) | copy-start | bytes 983044
  50.3 14.0 %collective-permute-start.9 = (bf16[80,2048]{1,0:T(8,128)(2,1)S(1)}, bf16[80,2048]{1,0:T(8,128)(2,1)S(1)}, u32[]{:S(2)}, u32[]{:S(2)}) collective-permute-start(bf16[80,2048]{1,0:T(8,128)(2,1)S(1)} %collective-permute-done.5.refs_3_), channel_id=1, source_target_pairs={{0,1},{1,2},{2,3},{3,4},{4,5},{5,6},{6,7},{7,0},{8,9},{9,10},{10,1... | collective-permute-start | bytes 983048 | tf_op jit(solution)/shard_map/ppermute | solution.py:382
  52.4 33.6 %copy-start.4 = (bf16[80,2048]{1,0:T(8,128)(2,1)}, bf16[80,2048]{1,0:T(8,128)(2,1)S(1)}, u32[]{:S(2)}) copy-start(bf16[80,2048]{1,0:T(8,128)(2,1)S(1)} %collective-permute-done.6.refs_4_) | copy-start | bytes 983044
  52.4 13.9 %collective-permute-start.10 = (bf16[80,2048]{1,0:T(8,128)(2,1)S(1)}, bf16[80,2048]{1,0:T(8,128)(2,1)S(1)}, u32[]{:S(2)}, u32[]{:S(2)}) collective-permute-start(bf16[80,2048]{1,0:T(8,128)(2,1)S(1)} %collective-permute-done.6.refs_4_), channel_id=1, source_target_pairs={{0,7},{1,0},{2,1},{3,2},{4,3},{5,4},{6,5},{7,6},{8,15},{9,8},{10,9... | collective-permute-start | bytes 983048 | tf_op jit(solution)/shard_map/ppermute | solution.py:382
  57.3 28.7 %copy-start.5 = (bf16[80,2048]{1,0:T(8,128)(2,1)}, bf16[80,2048]{1,0:T(8,128)(2,1)S(1)}, u32[]{:S(2)}) copy-start(bf16[80,2048]{1,0:T(8,128)(2,1)S(1)} %collective-permute-done.8.refs_6_) | copy-start | bytes 983044
  57.3 14.1 %collective-permute-start.12 = (bf16[80,2048]{1,0:T(8,128)(2,1)S(1)}, bf16[80,2048]{1,0:T(8,128)(2,1)S(1)}, u32[]{:S(2)}, u32[]{:S(2)}) collective-permute-start(bf16[80,2048]{1,0:T(8,128)(2,1)S(1)} %collective-permute-done.8.refs_6_), channel_id=1, source_target_pairs={{0,1},{1,2},{2,3},{3,4},{4,5},{5,6},{6,7},{7,0},{8,9},{9,10},{10,1... | collective-permute-start | bytes 983048 | tf_op jit(solution)/shard_map/ppermute | solution.py:382
  59.3 26.7 %copy-start.6 = (bf16[80,2048]{1,0:T(8,128)(2,1)}, bf16[80,2048]{1,0:T(8,128)(2,1)S(1)}, u32[]{:S(2)}) copy-start(bf16[80,2048]{1,0:T(8,128)(2,1)S(1)} %collective-permute-done.11.refs_9_) | copy-start | bytes 983044
  59.3 14.1 %collective-permute-start.15 = (bf16[80,2048]{1,0:T(8,128)(2,1)S(1)}, bf16[80,2048]{1,0:T(8,128)(2,1)S(1)}, u32[]{:S(2)}, u32[]{:S(2)}) collective-permute-start(bf16[80,2048]{1,0:T(8,128)(2,1)S(1)} %collective-permute-done.11.refs_9_), channel_id=1, source_target_pairs={{0,7},{1,0},{2,1},{3,2},{4,3},{5,4},{6,5},{7,6},{8,15},{9,8},{10,9... | collective-permute-start | bytes 983048 | tf_op jit(solution)/shard_map/ppermute | solution.py:382
  64.3 21.7 %copy-start.7 = (bf16[80,2048]{1,0:T(8,128)(2,1)}, bf16[80,2048]{1,0:T(8,128)(2,1)S(1)}, u32[]{:S(2)}) copy-start(bf16[80,2048]{1,0:T(8,128)(2,1)S(1)} %collective-permute-done.9.refs_7_) | copy-start | bytes 983044
  64.3 14.1 %collective-permute-start.13 = (bf16[80,2048]{1,0:T(8,128)(2,1)S(1)}, bf16[80,2048]{1,0:T(8,128)(2,1)S(1)}, u32[]{:S(2)}, u32[]{:S(2)}) collective-permute-start(bf16[80,2048]{1,0:T(8,128)(2,1)S(1)} %collective-permute-done.9.refs_7_), channel_id=1, source_target_pairs={{0,1},{1,2},{2,3},{3,4},{4,5},{5,6},{6,7},{7,0},{8,9},{9,10},{10,1... | collective-permute-start | bytes 983048 | tf_op jit(solution)/shard_map/ppermute | solution.py:382
  66.3 14.1 %collective-permute-start.14 = (bf16[80,2048]{1,0:T(8,128)(2,1)S(1)}, bf16[80,2048]{1,0:T(8,128)(2,1)S(1)}, u32[]{:S(2)}, u32[]{:S(2)}) collective-permute-start(bf16[80,2048]{1,0:T(8,128)(2,1)S(1)} %collective-permute-done.10.refs_8_), channel_id=1, source_target_pairs={{0,7},{1,0},{2,1},{3,2},{4,3},{5,4},{6,5},{7,6},{8,15},{9,8},{10,9... | collective-permute-start | bytes 983048 | tf_op jit(solution)/shard_map/ppermute | solution.py:382
  71.5 14.0 %collective-permute-start.16 = (bf16[80,2048]{1,0:T(8,128)(2,1)S(1)}, bf16[80,2048]{1,0:T(8,128)(2,1)S(1)}, u32[]{:S(2)}, u32[]{:S(2)}) collective-permute-start(bf16[80,2048]{1,0:T(8,128)(2,1)S(1)} %collective-permute-done.12.refs_10_), channel_id=1, source_target_pairs={{0,1},{1,2},{2,3},{3,4},{4,5},{5,6},{6,7},{7,0},{8,9},{9,10},{10,1... | collective-permute-start | bytes 983048 | tf_op jit(solution)/shard_map/ppermute | solution.py:382
  73.5 12.6 %collective-permute-start.17 = (bf16[80,2048]{1,0:T(8,128)(2,1)S(1)}, bf16[80,2048]{1,0:T(8,128)(2,1)S(1)}, u32[]{:S(2)}, u32[]{:S(2)}) collective-permute-start(bf16[80,2048]{1,0:T(8,128)(2,1)S(1)} %collective-permute-done.15.refs_13_), channel_id=1, source_target_pairs={{0,7},{1,0},{2,1},{3,2},{4,3},{5,4},{6,5},{7,6},{8,15},{9,8},{10,9... | collective-permute-start | bytes 983048 | tf_op jit(solution)/shard_map/ppermute | solution.py:382
  91.3 16.1 %collective-permute-start.18 = (bf16[2,3,64,256]{3,2,1,0:T(8,128)(2,1)S(1)}, bf16[2,3,64,256]{3,2,1,0:T(8,128)(2,1)S(1)}, u32[]{:S(2)}, u32[]{:S(2)}) collective-permute-start(bf16[2,3,64,256]{3,2,1,0:T(8,128)(2,1)S(1)} %get-tuple-element.41), channel_id=1, source_target_pairs={{0,16},{16,32},{32,48},{48,0},{1,17},{17,33},{33,49},{49,1},{2,18}... | collective-permute-start | bytes 589832 | tf_op jit(solution)/shard_map/ppermute | solution.py:382
  92.6 14.8 %collective-permute-start.19 = (bf16[2,3,64,256]{3,2,1,0:T(8,128)(2,1)S(1)}, bf16[2,3,64,256]{3,2,1,0:T(8,128)(2,1)S(1)}, u32[]{:S(2)}, u32[]{:S(2)}) collective-permute-start(bf16[2,3,64,256]{3,2,1,0:T(8,128)(2,1)S(1)} %get-tuple-element.40), channel_id=1, source_target_pairs={{0,32},{16,48},{32,0},{48,16},{1,33},{17,49},{33,1},{49,17},{2,34}... | collective-permute-start | bytes 589832 | tf_op jit(solution)/shard_map/ppermute | solution.py:382
  95.2 12.2 %collective-permute-start.20 = (bf16[2,3,64,256]{3,2,1,0:T(8,128)(2,1)S(1)}, bf16[2,3,64,256]{3,2,1,0:T(8,128)(2,1)S(1)}, u32[]{:S(2)}, u32[]{:S(2)}) collective-permute-start(bf16[2,3,64,256]{3,2,1,0:T(8,128)(2,1)S(1)} %get-tuple-element.39), channel_id=1, source_target_pairs={{0,48},{16,0},{32,16},{48,32},{1,49},{17,1},{33,17},{49,33},{2,50}... | collective-permute-start | bytes 589832 | tf_op jit(solution)/shard_map/ppermute | solution.py:382
  110.3 113.5 %all-gather.11.cloned.1.call-start = ((), (), s32[]{:S(2)}) async-start(), calls=%async_computation.5 | async-start | bytes 8650752 | tf_op jit(solution)/shard_map/all_gather | solution.py:440
  137.4 35.9 %all-to-all-start.1 = ((bf16[16,32,2048]{2,1,0:T(8,128)(2,1)}), bf16[16,32,2048]{2,1,0:T(8,128)(2,1)S(1)}, u32[]{:S(2)}, u32[]{:S(2)}) async-start(bf16[16,32,2048]{2,1,0:T(8,128)(2,1)} %get-tuple-element.33), calls=%async_computation.1 | async-start | bytes 4194304 | tf_op jit(solution)/shard_map/all_to_all | solution.py:443
  (16 other events, 80.1 us)
Sparse Core Ops, SparseCore 0:
  27.5 60.3 all-gather.6
  110.5 41.1 all-gather.8
  154.3 69.4 all-gather.10

commit v5 on v4

--- a/solution.py
+++ b/solution.py
@@ -49,22 +49,23 @@
     return lax.dot_general(a, b, (((1,), (1,)), ((), ())), preferred_element_type=F32)
 
 
-def norm_kernel(place_ref, x_ref, gain_ref, qkv_ref, last_ref, a_ref, b_ref, rows_ref):
+def norm_kernel(place_ref, x_ref, gain_ref, qkv_ref, a_ref, b_ref, rows_ref):
     gain = gain_ref[...]
     values = jnp.transpose(x_ref[...].astype(F32), (1, 0, 2)).reshape(rows_ref.shape)
     half = rows_ref.shape[0] // 2
     rows_ref[...] = values.astype(BF)
     a_ref[:half] = normed(values[:half], gain)
     b_ref[:half] = normed(values[half:], gain)
-    shares = (qkv_ref[0], qkv_ref[1], qkv_ref[2], last_ref[...])
-    for chunk, ref in enumerate((a_ref, b_ref)):
-        for group in range(8):
-            share = shares[2 * chunk + group // 4]
-            low = 16 * (group % 4)
-            ref[half:, 256 * group : 256 * group + 256] = share[low : low + 16]
-
-
-def norm_rows(place, stream, gain, temporal_qkv, temporal_out):
+    b_ref[half:, 1024:] = jnp.zeros((16, 1024), BF)
+    for kind in range(3):
+        share = qkv_ref[kind]
+        ref = (a_ref, b_ref)[kind // 2]
+        for group in range(4):
+            low = 256 * (4 * (kind % 2) + group)
+            ref[half:, low : low + 256] = share[16 * group : 16 * group + 16]
+
+
+def norm_rows(place, stream, gain, temporal_qkv):
     patches, frames, width = stream.shape
     count = patches * frames
     half = jax.ShapeDtypeStruct((count // 2 + 16, width), BF)
@@ -77,8 +78,7 @@
             in_specs=[
                 whole(patches, frames, width),
                 whole(1, width),
-                pl.BlockSpec((3, 64, 256), lambda i, at: (0, at[2], 0)),
-                pl.BlockSpec((64, 256), lambda i, at: (at[0], at[1])),
+                pl.BlockSpec((3, 64, 256), lambda i, at: (0, at[0], 0)),
             ],
             out_specs=(
                 whole(count // 2 + 16, width),
@@ -91,42 +91,30 @@
         cost_estimate=pl.CostEstimate(
             flops=4 * count * width, bytes_accessed=6 * count * width, transcendentals=0
         ),
-    )(place, stream, gain, temporal_qkv, temporal_out)
+    )(place, stream, gain, temporal_qkv)
 
 
 def split_kernel(place_ref, *refs):
-    pieces = refs[: 2 * NZ]
-    out_ref, sends = refs[2 * NZ], refs[2 * NZ + 1 :]
+    pieces, send_ref = refs[:-1], refs[-1]
     z, y = place_ref[0], place_ref[1]
     for k in range(NZ):
         source = lax.rem(z + (OFFSETS[k] + NZ), NZ)
         step = lax.rem(source // 2 + 4 - y, 4)
         pair = lax.rem(source, 2)
-        for block in range(4):
-            ref = pieces[2 * k + block // 2]
+        for kind in range(3):
             for group in range(4):
-                low = 256 * (4 * (block % 2) + group)
-                value = ref[:, low : low + 256]
+                low = 256 * (4 * (kind % 2) + group)
                 rows = slice(16 * group, 16 * group + 16)
-                if block == 3:
-                    out_ref[source, rows] = value
-                else:
-                    sends[0][step, pair, block, rows] = value
+                send_ref[step, pair, kind, rows] = pieces[2 * k + kind // 2][:, low : low + 256]
 
 
 def split_shares(place, pieces):
     return pl.pallas_call(
         split_kernel,
         grid=(1,),
-        out_shape=(
-            jax.ShapeDtypeStruct((NZ, 64, 256), BF),
-            jax.ShapeDtypeStruct((4, 2, 3, 64, 256), BF),
-        ),
+        out_shape=jax.ShapeDtypeStruct((4, 2, 3, 64, 256), BF),
         in_specs=[smem()] + [pl.BlockSpec((16, 2048), lambda i: (4, 0))] * len(pieces),
-        out_specs=(
-            pl.BlockSpec((NZ, 64, 256), lambda i: (0, 0, 0)),
-            pl.BlockSpec((4, 2, 3, 64, 256), lambda i: (0, 0, 0, 0, 0)),
-        ),
+        out_specs=pl.BlockSpec((4, 2, 3, 64, 256), lambda i: (0, 0, 0, 0, 0)),
         compiler_params=params(),
         cost_estimate=pl.CostEstimate(flops=0, bytes_accessed=2 << 20, transcendentals=0),
     )(place, *pieces)
@@ -191,8 +179,12 @@
 
 def column_block(weight_ref, block):
     return jnp.concatenate(
-        [weight_ref[block, quarter, k] for k in range(NZ) for quarter in range(4)], axis=0
-    )
+        [weight_ref[block, head, k // 4, k % 4, 0] for k in range(NZ) for head in range(2)], axis=0
+    )
+
+
+def weight_spec(blocks, which):
+    return pl.BlockSpec((blocks, 2, 2, 4, 1, E, 256), lambda i: (i, 0, 0, 0, which, 0, 0))
 
 
 def join_blocks_kernel(z_ref, *refs):
@@ -204,7 +196,7 @@
 def join_blocks(z, parts):
     return pl.pallas_call(
         join_blocks_kernel,
-        out_shape=jax.ShapeDtypeStruct((4, 128, 256), BF),
+        out_shape=jax.ShapeDtypeStruct((4, 2, 128, 256), BF),
         in_specs=[smem()] + [vmem()] * 4,
         out_specs=vmem(),
         compiler_params=params(),
@@ -216,9 +208,7 @@
     step = pl.program_id(0)
     mix = jnp.concatenate([mix_ref[k] for k in range(NZ)], axis=1)
     for block in range(weight_ref.shape[0]):
-        weight = jnp.concatenate(
-            [weight_ref[block, head, k // 4, k % 4] for k in range(NZ) for head in range(2)], axis=0
-        )
+        weight = column_block(weight_ref, block)
         low = pl.multiple_of((step * weight_ref.shape[0] + block) * 256, 256)
         total[:, pl.ds(low, 256)] = dot(mix, weight)
 
@@ -249,7 +239,7 @@
         ),
         in_specs=[
             pl.BlockSpec((NZ, 128, 256), lambda i: (0, 0, 0)),
-            pl.BlockSpec((8 // steps, 2, 2, 4, 128, 256), lambda i: (i, 0, 0, 0, 0, 0)),
+            weight_spec(8 // steps, 0),
             pl.BlockSpec((128, width), lambda i: (0, 0)),
             pl.BlockSpec((1, width), lambda i: (0, 0)),
         ],
@@ -365,7 +355,7 @@
         out_shape=jax.ShapeDtypeStruct((32, 4, width), BF),
         in_specs=[
             pl.BlockSpec((16, 32, 512), lambda i: (0, 0, 0)),
-            pl.BlockSpec((8 // steps, 4, NZ, 64, 256), lambda i: (i, 0, 0, 0, 0)),
+            weight_spec(8 // steps, 1),
             pl.BlockSpec((128, width), lambda i: (0, 0)),
         ],
         out_specs=pl.BlockSpec((32, 4, width), lambda i: (0, 0, 0)),
@@ -382,31 +372,32 @@
     return lax.ppermute(value, axis, [(i, (i + step) % count) for i in range(count)])
 
 
-def gathered_rows(chunks):
+def gathered_rows(chunks, beside):
     up, down = list(chunks), list(chunks)
     pieces = {0: list(chunks)}
     for step in (1, 2, 3):
         up = [shifted(value, "z", 1) for value in up]
         down = [shifted(value, "z", -1) for value in down]
+        if step == 1:
+            up, down, beside = lax.optimization_barrier((up, down, beside))
         pieces[-step], pieces[step] = up, down
     pieces[4] = [shifted(up[0], "z", 1), shifted(down[1], "z", -1)]
-    return [value for offset in OFFSETS for value in pieces[offset]]
+    return [value for offset in OFFSETS for value in pieces[offset]], beside
 
 
 def local(stream, spatial_gain, spatial_qkv, spatial_out, temporal_gain, temporal_qkv, temporal_out, starts):
     patches, frames, width = stream.shape
     w, xl, y, c, z = (lax.axis_index(name) for name in ("w", "xl", "y", "c", "z"))
 
-    place = jnp.stack(
-        [
-            lax.rem(y, 2) * 2 + c,
-            (w * 2 + xl) * 2 + y // 2,
-            ((w * 2 + xl) * 2 + c) * 4 + y,
-        ]
-    ).astype(jnp.int32)
-
-    block = lax.dynamic_slice(
-        spatial_out, (lax.rem(y, 2) * 128, place[1] * 256), (128, 256)
+    place = (((w * 2 + xl) * 2 + c) * 4 + y).reshape(1)
+    first, second, rows = norm_rows(
+        place, stream, spatial_gain.reshape(1, width), jnp.transpose(temporal_qkv, (1, 0, 2))
+    )
+
+    first, spatial_out, temporal_out = lax.optimization_barrier((first, spatial_out, temporal_out))
+    low = (lax.rem(y, 2) * E, ((w * 2 + xl) * 2 + y // 2) * 256)
+    block = jnp.stack(
+        [lax.dynamic_slice(weight, low, (E, 256)) for weight in (spatial_out, temporal_out)]
     )
     parts = []
     for k in range(4):
@@ -414,37 +405,27 @@
             (a * 8 + b, (b // 4) * 8 + (b + 4 * a + k) % 8) for a in range(2) for b in range(8)
         ]
         parts.append(lax.ppermute(block, ("c", "z"), pairs))
-    gathered = join_blocks(z.reshape(1), parts)
-    whole_out = lax.all_gather(gathered, ("w", "xl", "y", "c"), axis=0, tiled=False)
-    whole_out = whole_out.reshape(8, 2, 2, 4, 128, 256)
-
-    stream, parts = lax.optimization_barrier((stream, parts))
-    first, second, rows = norm_rows(
-        place, stream, spatial_gain.reshape(1, width), jnp.transpose(temporal_qkv, (1, 0, 2)), temporal_out
-    )
-    pieces = gathered_rows((first, second))
-
-    last_share, sends = split_shares(jnp.stack([z, y]).astype(jnp.int32), pieces)
-    got = [sends[0]] + [shifted(sends[k], "y", k) for k in range(1, 4)]
+    pieces, parts = gathered_rows((first, second), parts)
+    outs = join_blocks(z.reshape(1), parts)
+    outs = lax.all_gather(outs, ("w", "xl", "y", "c"), axis=0, tiled=False)
+    outs = outs.reshape(8, 2, 2, 4, 2, E, 256)
 
     weight = jnp.transpose(spatial_qkv, (1, 0, 2))
     mix = spatial_attend(z.reshape(1), weight, pieces)
-    mix, *got = lax.optimization_barrier((mix, *got))
+    mix, *pieces = lax.optimization_barrier((mix, *pieces))
+    mix = lax.all_to_all(mix, "z", 0, 0, tiled=True)
+
+    sends = split_shares(jnp.stack([z, y]).astype(jnp.int32), pieces)
+    got = [sends[0]] + [shifted(sends[k], "y", k) for k in range(1, 4)]
     quarter = join_shares(y.reshape(1), got)
-    mix, quarter = lax.optimization_barrier((mix, quarter))
     quarter = lax.all_gather(quarter[None], ("w", "xl", "c"), axis=0, tiled=True)
-    mix = lax.all_to_all(mix, "z", 0, 0, tiled=True)
-
-    middle, send = middle_rows(mix, whole_out, rows, temporal_gain.reshape(1, width))
-    last_share, middle = lax.optimization_barrier((last_share, middle))
-    whole_last = lax.all_gather(last_share, ("w", "xl", "y", "c"), axis=0, tiled=False)
-    whole_last = whole_last.reshape(8, 4, NZ, 64, 256)
-
+
+    middle, send = middle_rows(mix, outs, rows, temporal_gain.reshape(1, width))
     window = lax.all_to_all(send, ("xl", "y", "c"), 0, 0, tiled=True)
     start = lax.dynamic_slice(starts, (w,), (1,))
     mix = temporal_attend(start, window.reshape(512, width), quarter)
     mix = lax.all_to_all(mix, ("xl", "y", "c"), 0, 0, tiled=True)
-    return last_rows(mix, whole_last, middle)
+    return last_rows(mix, outs, middle)
 
 
 def solution(mesh):

time: 237 us -> 255 us (1.076)
  waiting for transfers between devices: 76.6 us -> 99.3 us
  blocking collectives: 42.4 us -> 34.2 us
    all_gather x1, waiting for transfers between devices: 7.36 us -> 27.4 us  [local(): lax.all_gather(quarter[None], ('w', 'xl', 'c'), axis=0, tiled=True)]
    ppermute x4, waiting for transfers between devices: 3.92 us -> 18.7 us  [local(): parts.append(lax.ppermute(block, ('c', 'z'), pairs))]
    all_gather x2 -> x1, waiting for transfers between devices: 12 us -> 0.01 us  [local(): outs = lax.all_gather(outs, ('w', 'xl', 'y', 'c'), axis=0, tiled=False)]
    all_to_all x1, waiting for transfers between devices: 21.6 us -> 11 us  [local(): window = lax.all_to_all(send, ('xl', 'y', 'c'), 0, 0, tiled=True)]
    ppermute x17, waiting for transfers between devices: 31.7 us -> 42.2 us  [shifted(): lax.ppermute(value, axis, [(i, (i + step) % count) for i in range(count)])]
    all_to_all x1, blocking collectives: 22.6 us -> 15.3 us  [local(): mix = lax.all_to_all(mix, ('xl', 'y', 'c'), 0, 0, tiled=True)]
    ppermute x4, starting transfers between devices: 13.8 us -> 18.4 us  [local(): parts.append(lax.ppermute(block, ('c', 'z'), pairs))]
    ppermute x17, starting transfers between devices: 27.3 us -> 23 us  [shifted(): lax.ppermute(value, axis, [(i, (i + step) % count) for i in range(count)])]
  transfers between devices with their start and end apart: 25 -> 24, of which waited for: 15 -> 15; matrix products, arithmetic and copies ran while one was open for 2% -> 1% of each run, Pallas kernels for 17% -> 9%
where the time goes in v5:
time: 255 us; the launch traced here: 254 us
  waiting for transfers between devices  99.3 us (39%)
  starting transfers between devices  49.7 us (19%)
  Pallas kernels  49.6 us (19%)
  blocking collectives  34.2 us (13%)
  between operations  13.6 us (5%)
  local copies, waits for them, and re-layouts  7.09 us (3%)
    ppermute x17, waiting for transfers between devices, shifted(): lax.ppermute(value, axis, [(i, (i + step) % count) for i in range(count)])  42.2 us
    all_gather x1, waiting for transfers between devices, local(): lax.all_gather(quarter[None], ('w', 'xl', 'c'), axis=0, tiled=True)  27.4 us
    ppermute x17, starting transfers between devices, shifted(): lax.ppermute(value, axis, [(i, (i + step) % count) for i in range(count)])  23 us
    all_to_all x1, blocking collectives, local(): mix = lax.all_to_all(mix, 'z', 0, 0, tiled=True)  18.9 us
    ppermute x4, waiting for transfers between devices, local(): parts.append(lax.ppermute(block, ('c', 'z'), pairs))  18.7 us
    ppermute x4, starting transfers between devices, local(): parts.append(lax.ppermute(block, ('c', 'z'), pairs))  18.4 us
    all_to_all x1, blocking collectives, local(): mix = lax.all_to_all(mix, ('xl', 'y', 'c'), 0, 0, tiled=True)  15.3 us
    pallas_call x1, Pallas kernels, temporal_attend(): pl.pallas_call(temporal_kernel, grid=(6,), out_shape=jax.ShapeDtypeStruct...  14.6 us
  transfers between devices with their start and end apart: 24, of which 15 were waited for; matrix products, arithmetic and copies ran while one was open for 1% of the time, Pallas kernels for 9%

profile of v5, /device:TPU:1, one launch (start us, length us, event | category | flops | bytes accessed | tf_op | source)
XLA Modules:
  0.0 254.1 jit_solution(15503000220326783241)
XLA Ops:
  6.5 2.6 %shard_map.82 = (bf16[80,2048]{1,0:T(8,128)(2,1)}, bf16[80,2048]{1,0:T(8,128)(2,1)}, bf16[128,2048]{1,0:T(8,128)(2,1)}) custom-call(s32[1]{0:T(128)} %bitcast.2.place_ref, bf16[32,4,2048]{2,1,0:T(4,128)(2,1)} %x_ref.1, f32[1,2048]{1,0:T(1,128)} %bitcast.26, bf16[3,2048,256]{2,1,0:T(8,128)(2,1)} %bitcast.24), custom_call_target="tpu_custom_call" | custom-call | flops 1048576 | bytes 1572864 | tf_op jit(solution)/shard_map/pallas_call | solution.py:73
  10.0 10.2 %collective-permute-start.4 = (bf16[2,128,256]{2,1,0:T(8,128)(2,1)S(1)}, bf16[2,128,256]{2,1,0:T(8,128)(2,1)S(1)}, u32[]{:S(2)}, u32[]{:S(2)}) collective-permute-start(bf16[2,128,256]{2,1,0:T(8,128)(2,1)S(1)} %pad_maximum_fusion), channel_id=1, source_target_pairs={{0,0},{1,1},{2,2},{3,3},{4,12},{5,13},{6,14},{7,15},{8,4},{9,5},{1... | collective-permute-start | bytes 393224 | tf_op jit(solution)/shard_map/ppermute | solution.py:407
  21.1 1.9 collective-permute-start.2
  23.3 2.4 collective-permute-start.3
  25.8 1.8 collective-permute-done.5.refs_1_
  27.6 8.0 %collective-permute-start.6 = (bf16[2,128,256]{2,1,0:T(8,128)(2,1)S(1)}, bf16[2,128,256]{2,1,0:T(8,128)(2,1)S(1)}, u32[]{:S(2)}, u32[]{:S(2)}) collective-permute-start(bf16[2,128,256]{2,1,0:T(8,128)(2,1)S(1)} %pad_maximum_fusion), channel_id=1, source_target_pairs={{0,2},{1,3},{2,4},{3,5},{4,14},{5,15},{6,8},{7,9},{8,6},{9,7},{10,... | collective-permute-start | bytes 393224 | tf_op jit(solution)/shard_map/ppermute | solution.py:407
  35.6 9.0 %collective-permute-done.6.refs_2_ = bf16[2,128,256]{2,1,0:T(8,128)(2,1)S(1)} collective-permute-done((bf16[2,128,256]{2,1,0:T(8,128)(2,1)S(1)}, bf16[2,128,256]{2,1,0:T(8,128)(2,1)S(1)}, u32[]{:S(2)}, u32[]{:S(2)}) %collective-permute-start.6) | collective-permute-done | bytes 131104 | tf_op jit(solution)/shard_map/ppermute | solution.py:407
  44.7 7.6 %collective-permute-done.7.refs_3_ = bf16[2,128,256]{2,1,0:T(8,128)(2,1)S(1)} collective-permute-done((bf16[2,128,256]{2,1,0:T(8,128)(2,1)S(1)}, bf16[2,128,256]{2,1,0:T(8,128)(2,1)S(1)}, u32[]{:S(2)}, u32[]{:S(2)}) %collective-permute-start.7) | collective-permute-done | bytes 131104 | tf_op jit(solution)/shard_map/ppermute | solution.py:407
  53.0 1.9 shard_map.84
  54.9 2.5 collective-permute-start.8
  57.7 2.2 collective-permute-start.9
  60.4 5.6 %collective-permute-done.8.refs_6_ = bf16[80,2048]{1,0:T(8,128)(2,1)S(1)} collective-permute-done((bf16[80,2048]{1,0:T(8,128)(2,1)S(1)}, bf16[80,2048]{1,0:T(8,128)(2,1)S(1)}, u32[]{:S(2)}, u32[]{:S(2)}) %collective-permute-start.8) | collective-permute-done | bytes 327712 | tf_op jit(solution)/shard_map/ppermute | solution.py:372
  68.6 4.3 %collective-permute-done.9.refs_7_ = bf16[80,2048]{1,0:T(8,128)(2,1)S(1)} collective-permute-done((bf16[80,2048]{1,0:T(8,128)(2,1)S(1)}, bf16[80,2048]{1,0:T(8,128)(2,1)S(1)}, u32[]{:S(2)}, u32[]{:S(2)}) %collective-permute-start.9) | collective-permute-done | bytes 327712 | tf_op jit(solution)/shard_map/ppermute | solution.py:372
  73.0 1.6 collective-permute-start.13
  75.7 4.4 %collective-permute-done.12.refs_10_ = bf16[80,2048]{1,0:T(8,128)(2,1)S(1)} collective-permute-done((bf16[80,2048]{1,0:T(8,128)(2,1)S(1)}, bf16[80,2048]{1,0:T(8,128)(2,1)S(1)}, u32[]{:S(2)}, u32[]{:S(2)}) %collective-permute-start.12) | collective-permute-done | bytes 327712 | tf_op jit(solution)/shard_map/ppermute | solution.py:372
  83.4 3.6 %collective-permute-done.13.refs_11_ = bf16[80,2048]{1,0:T(8,128)(2,1)S(1)} collective-permute-done((bf16[80,2048]{1,0:T(8,128)(2,1)S(1)}, bf16[80,2048]{1,0:T(8,128)(2,1)S(1)}, u32[]{:S(2)}, u32[]{:S(2)}) %collective-permute-start.13) | collective-permute-done | bytes 327712 | tf_op jit(solution)/shard_map/ppermute | solution.py:372
  87.5 6.5 %collective-permute-done.16.refs_14_ = bf16[80,2048]{1,0:T(8,128)(2,1)S(1)} collective-permute-done((bf16[80,2048]{1,0:T(8,128)(2,1)S(1)}, bf16[80,2048]{1,0:T(8,128)(2,1)S(1)}, u32[]{:S(2)}, u32[]{:S(2)}) %collective-permute-start.16) | collective-permute-done | bytes 327712 | tf_op jit(solution)/shard_map/ppermute | solution.py:372
  94.9 12.0 %shard_map.83 = bf16[8,128,256]{2,1,0:T(8,128)(2,1)} custom-call(s32[1]{0:T(128)} %bitcast.place_ref.z_ref, bf16[3,2048,256]{2,1,0:T(8,128)(2,1)} %bitcast.29, bf16[80,2048]{1,0:T(8,128)(2,1)} %get-tuple-element.54.refs_0_, bf16[80,2048]{1,0:T(8,128)(2,1)} %get-tuple-element.55.refs_1_, bf16[80,2048]{1,0:T(8,128)(2,1)} %copy-done.2, ...), custom_call_target="tpu_custom_call" | custom-call | flops 6442450944 | bytes 8388608 | tf_op jit(solution)/shard_map/pallas_call | solution.py:168
  106.8 2.5 shard_map.86
  109.3 2.1 slice_bitcast_fusion
  112.8 2.3 collective-permute-start.19
  116.3 7.1 %collective-permute-done.18.refs_1_ = bf16[2,3,64,256]{3,2,1,0:T(8,128)(2,1)S(1)} collective-permute-done((bf16[2,3,64,256]{3,2,1,0:T(8,128)(2,1)S(1)}, bf16[2,3,64,256]{3,2,1,0:T(8,128)(2,1)S(1)}, u32[]{:S(2)}, u32[]{:S(2)}) %collective-permute-start.18) | collective-permute-done | bytes 196640 | tf_op jit(solution)/shard_map/ppermute | solution.py:372
  123.4 9.5 %collective-permute-done.19.refs_2_ = bf16[2,3,64,256]{3,2,1,0:T(8,128)(2,1)S(1)} collective-permute-done((bf16[2,3,64,256]{3,2,1,0:T(8,128)(2,1)S(1)}, bf16[2,3,64,256]{3,2,1,0:T(8,128)(2,1)S(1)}, u32[]{:S(2)}, u32[]{:S(2)}) %collective-permute-start.19) | collective-permute-done | bytes 196640 | tf_op jit(solution)/shard_map/ppermute | solution.py:372
  133.7 2.2 shard_map.87
  135.9 18.9 %all_to_all.15.mix_ref = bf16[8,128,256]{2,1,0:T(8,128)(2,1)} all-to-all(bf16[8,128,256]{2,1,0:T(8,128)(2,1)S(1)} %copy-done.1), channel_id=1, replica_groups=mesh['w'=2,'xl'=2,'y'=4,'c'=2,'z'=8] {'z'}, dimensions={0} | all-to-all | bytes 1048576 | tf_op jit(solution)/shard_map/all_to_all | solution.py:416
  154.9 7.5 %shard_map.85 = (bf16[128,2048]{1,0:T(8,128)(2,1)}, bf16[16,32,2048]{2,1,0:T(8,128)(2,1)}) custom-call(bf16[8,128,256]{2,1,0:T(8,128)(2,1)} %all_to_all.15.mix_ref, bf16[8,2,2,4,2,128,256]{6,5,4,3,2,1,0:T(8,128)(2,1)} %bitcast.22, bf16[128,2048]{1,0:T(8,128)(2,1)} %get-tuple-element.52.rows_ref, f32[1,2048]{1,0:T(1,128)} %bitcast.27), custom_call_target="tpu_custom_call" | custom-call | flops 1073741824 | bytes 12582912 | tf_op jit(solution)/shard_map/pallas_call | solution.py:233
  162.4 8.2 %all-to-all-start.1 = ((bf16[16,32,2048]{2,1,0:T(8,128)(2,1)}), bf16[16,32,2048]{2,1,0:T(8,128)(2,1)S(1)}, u32[]{:S(2)}, u32[]{:S(2)}) async-start(bf16[16,32,2048]{2,1,0:T(8,128)(2,1)} %get-tuple-element.53), calls=%async_computation.1 | async-start | bytes 4194304 | tf_op jit(solution)/shard_map/all_to_all | solution.py:424
  171.3 27.4 %all-gather.7.cloned.1.call-done = bf16[48,256,256]{2,1,0:T(8,128)(2,1)} async-done(((bf16[6,256,256]{2,1,0:T(8,128)(2,1)}), bf16[48,256,256]{2,1,0:T(8,128)(2,1)}) %all-gather.7.cloned.1.call-update) | async-done | bytes 6291472 | tf_op jit(solution)/shard_map/all_gather | solution.py:421
  198.7 11.0 %all-to-all-done.1 = bf16[16,32,2048]{2,1,0:T(8,128)(2,1)S(1)} async-done(((bf16[16,32,2048]{2,1,0:T(8,128)(2,1)}), bf16[16,32,2048]{2,1,0:T(8,128)(2,1)S(1)}, u32[]{:S(2)}, u32[]{:S(2)}) %all-to-all-start.1) | async-done | bytes 2097184 | tf_op jit(solution)/shard_map/all_to_all | solution.py:424
  211.0 14.6 %shard_map.88 = bf16[16,32,512]{2,1,0:T(8,128)(2,1)} custom-call(s32[1]{0:T(128)} %dynamic_slice.9.start_ref, bf16[512,2048]{1,0:T(8,128)(2,1)} %bitcast.25, bf16[8,6,256,256]{3,2,1,0:T(8,128)(2,1)} %bitcast.28), custom_call_target="tpu_custom_call" | custom-call | flops 3221225472 | bytes 9437184 | tf_op jit(solution)/shard_map/pallas_call | solution.py:300
  225.6 15.3 %all_to_all.16.mix_ref = bf16[16,32,512]{2,1,0:T(8,128)(2,1)} all-to-all(bf16[16,32,512]{2,1,0:T(8,128)(2,1)} %shard_map.88), channel_id=1, replica_groups=mesh['w'=2,'xl'=2,'y'=4,'c'=2,'z'=8] {'xl','y','c'}, dimensions={0} | all-to-all | bytes 1048576 | tf_op jit(solution)/shard_map/all_to_all | solution.py:427
  240.9 6.4 %shard_map.89 = bf16[32,4,2048]{2,1,0:T(4,128)(2,1)} custom-call(bf16[16,32,512]{2,1,0:T(8,128)(2,1)} %all_to_all.16.mix_ref, bf16[8,2,2,4,2,128,256]{6,5,4,3,2,1,0:T(8,128)(2,1)} %bitcast.23, bf16[128,2048]{1,0:T(8,128)(2,1)} %get-tuple-element.70.middle_ref), custom_call_target="tpu_custom_call" | custom-call | flops 1073741824 | bytes 12582912 | tf_op jit(solution)/shard_map/pallas_call | solution.py:352
  (81 shorter events, 17.2 us)
Async XLA Ops:
  6.5 148.3 %all-gather.5.cloned.1.call-start = ((), (), s32[]{:S(2)}) async-start(), calls=%async_computation.3 | async-start | bytes 17301504 | tf_op jit(solution)/shard_map/all_gather | solution.py:410
  10.0 13.3 %collective-permute-start.4 = (bf16[2,128,256]{2,1,0:T(8,128)(2,1)S(1)}, bf16[2,128,256]{2,1,0:T(8,128)(2,1)S(1)}, u32[]{:S(2)}, u32[]{:S(2)}) collective-permute-start(bf16[2,128,256]{2,1,0:T(8,128)(2,1)S(1)} %pad_maximum_fusion), channel_id=1, source_target_pairs={{0,0},{1,1},{2,2},{3,3},{4,12},{5,13},{6,14},{7,15},{8,4},{9,5},{1... | collective-permute-start | bytes 393224 | tf_op jit(solution)/shard_map/ppermute | solution.py:407
  20.2 7.4 %collective-permute-start.5 = (bf16[2,128,256]{2,1,0:T(8,128)(2,1)S(1)}, bf16[2,128,256]{2,1,0:T(8,128)(2,1)S(1)}, u32[]{:S(2)}, u32[]{:S(2)}) collective-permute-start(bf16[2,128,256]{2,1,0:T(8,128)(2,1)S(1)} %pad_maximum_fusion), channel_id=1, source_target_pairs={{0,1},{1,2},{2,3},{3,4},{4,13},{5,14},{6,15},{7,8},{8,5},{9,6},{10... | collective-permute-start | bytes 393224 | tf_op jit(solution)/shard_map/ppermute | solution.py:407
  20.3 32.0 %collective-permute-start = (bf16[80,2048]{1,0:T(8,128)(2,1)}, bf16[80,2048]{1,0:T(8,128)(2,1)S(1)}, u32[]{:S(2)}, u32[]{:S(2)}) collective-permute-start(bf16[80,2048]{1,0:T(8,128)(2,1)} %get-tuple-element.54.refs_0_), channel_id=1, source_target_pairs={{0,1},{1,2},{2,3},{3,4},{4,5},{5,6},{6,7},{7,0},{8,9},{9,10},{10,1... | collective-permute-start | bytes 983048 | tf_op jit(solution)/shard_map/ppermute | solution.py:372
  21.1 31.2 %collective-permute-start.2 = (bf16[80,2048]{1,0:T(8,128)(2,1)}, bf16[80,2048]{1,0:T(8,128)(2,1)S(1)}, u32[]{:S(2)}, u32[]{:S(2)}) collective-permute-start(bf16[80,2048]{1,0:T(8,128)(2,1)} %get-tuple-element.54.refs_0_), channel_id=1, source_target_pairs={{0,7},{1,0},{2,1},{3,2},{4,3},{5,4},{6,5},{7,6},{8,15},{9,8},{10,9... | collective-permute-start | bytes 983048 | tf_op jit(solution)/shard_map/ppermute | solution.py:372
  23.1 29.2 %collective-permute-start.1 = (bf16[80,2048]{1,0:T(8,128)(2,1)}, bf16[80,2048]{1,0:T(8,128)(2,1)S(1)}, u32[]{:S(2)}, u32[]{:S(2)}) collective-permute-start(bf16[80,2048]{1,0:T(8,128)(2,1)} %get-tuple-element.55.refs_1_), channel_id=1, source_target_pairs={{0,1},{1,2},{2,3},{3,4},{4,5},{5,6},{6,7},{7,0},{8,9},{9,10},{10,1... | collective-permute-start | bytes 983048 | tf_op jit(solution)/shard_map/ppermute | solution.py:372
  23.3 29.0 %copy-start.19 = (bf16[2,128,256]{2,1,0:T(8,128)(2,1)}, bf16[2,128,256]{2,1,0:T(8,128)(2,1)S(1)}, u32[]{:S(2)}) copy-start(bf16[2,128,256]{2,1,0:T(8,128)(2,1)S(1)} %collective-permute-done.4.refs_0_) | copy-start | bytes 393220
  23.3 29.0 %collective-permute-start.3 = (bf16[80,2048]{1,0:T(8,128)(2,1)}, bf16[80,2048]{1,0:T(8,128)(2,1)S(1)}, u32[]{:S(2)}, u32[]{:S(2)}) collective-permute-start(bf16[80,2048]{1,0:T(8,128)(2,1)} %get-tuple-element.55.refs_1_), channel_id=1, source_target_pairs={{0,7},{1,0},{2,1},{3,2},{4,3},{5,4},{6,5},{7,6},{8,15},{9,8},{10,9... | collective-permute-start | bytes 983048 | tf_op jit(solution)/shard_map/ppermute | solution.py:372
  27.6 17.1 %collective-permute-start.6 = (bf16[2,128,256]{2,1,0:T(8,128)(2,1)S(1)}, bf16[2,128,256]{2,1,0:T(8,128)(2,1)S(1)}, u32[]{:S(2)}, u32[]{:S(2)}) collective-permute-start(bf16[2,128,256]{2,1,0:T(8,128)(2,1)S(1)} %pad_maximum_fusion), channel_id=1, source_target_pairs={{0,2},{1,3},{2,4},{3,5},{4,14},{5,15},{6,8},{7,9},{8,6},{9,7},{10,... | collective-permute-start | bytes 393224 | tf_op jit(solution)/shard_map/ppermute | solution.py:407
  44.7 7.6 %collective-permute-start.7 = (bf16[2,128,256]{2,1,0:T(8,128)(2,1)S(1)}, bf16[2,128,256]{2,1,0:T(8,128)(2,1)S(1)}, u32[]{:S(2)}, u32[]{:S(2)}) collective-permute-start(bf16[2,128,256]{2,1,0:T(8,128)(2,1)S(1)} %pad_maximum_fusion), channel_id=1, source_target_pairs={{0,3},{1,4},{2,5},{3,6},{4,15},{5,8},{6,9},{7,10},{8,7},{9,0},{10,... | collective-permute-start | bytes 393224 | tf_op jit(solution)/shard_map/ppermute | solution.py:407
  52.3 41.7 %copy-start.2 = (bf16[80,2048]{1,0:T(8,128)(2,1)}, bf16[80,2048]{1,0:T(8,128)(2,1)S(1)}, u32[]{:S(2)}) copy-start(bf16[80,2048]{1,0:T(8,128)(2,1)S(1)} %collective-permute-done.refs_2_) | copy-start | bytes 983044
  52.3 41.7 %copy-start.4 = (bf16[80,2048]{1,0:T(8,128)(2,1)}, bf16[80,2048]{1,0:T(8,128)(2,1)S(1)}, u32[]{:S(2)}) copy-start(bf16[80,2048]{1,0:T(8,128)(2,1)S(1)} %collective-permute-done.1.refs_3_) | copy-start | bytes 983044
  52.3 41.7 %copy-start.3 = (bf16[80,2048]{1,0:T(8,128)(2,1)}, bf16[80,2048]{1,0:T(8,128)(2,1)S(1)}, u32[]{:S(2)}) copy-start(bf16[80,2048]{1,0:T(8,128)(2,1)S(1)} %collective-permute-done.2.refs_4_) | copy-start | bytes 983044
  52.4 41.7 %copy-start.5 = (bf16[80,2048]{1,0:T(8,128)(2,1)}, bf16[80,2048]{1,0:T(8,128)(2,1)S(1)}, u32[]{:S(2)}) copy-start(bf16[80,2048]{1,0:T(8,128)(2,1)S(1)} %collective-permute-done.3.refs_5_) | copy-start | bytes 983044
  54.9 143.8 %all-gather.7.cloned.1.call-start = ((), (), s32[]{:S(2)}) async-start(), calls=%async_computation.4 | async-start | bytes 7077888 | tf_op jit(solution)/shard_map/all_gather | solution.py:421
  54.9 11.0 %collective-permute-start.8 = (bf16[80,2048]{1,0:T(8,128)(2,1)S(1)}, bf16[80,2048]{1,0:T(8,128)(2,1)S(1)}, u32[]{:S(2)}, u32[]{:S(2)}) collective-permute-start(bf16[80,2048]{1,0:T(8,128)(2,1)S(1)} %collective-permute-done.refs_2_), channel_id=1, source_target_pairs={{0,1},{1,2},{2,3},{3,4},{4,5},{5,6},{6,7},{7,0},{8,9},{9,10},{10,1... | collective-permute-start | bytes 983048 | tf_op jit(solution)/shard_map/ppermute | solution.py:372
  57.4 10.6 %collective-permute-start.11 = (bf16[80,2048]{1,0:T(8,128)(2,1)S(1)}, bf16[80,2048]{1,0:T(8,128)(2,1)S(1)}, u32[]{:S(2)}, u32[]{:S(2)}) collective-permute-start(bf16[80,2048]{1,0:T(8,128)(2,1)S(1)} %collective-permute-done.3.refs_5_), channel_id=1, source_target_pairs={{0,7},{1,0},{2,1},{3,2},{4,3},{5,4},{6,5},{7,6},{8,15},{9,8},{10,9... | collective-permute-start | bytes 983048 | tf_op jit(solution)/shard_map/ppermute | solution.py:372
  57.7 15.3 %collective-permute-start.9 = (bf16[80,2048]{1,0:T(8,128)(2,1)S(1)}, bf16[80,2048]{1,0:T(8,128)(2,1)S(1)}, u32[]{:S(2)}, u32[]{:S(2)}) collective-permute-start(bf16[80,2048]{1,0:T(8,128)(2,1)S(1)} %collective-permute-done.1.refs_3_), channel_id=1, source_target_pairs={{0,1},{1,2},{2,3},{3,4},{4,5},{5,6},{6,7},{7,0},{8,9},{9,10},{10,1... | collective-permute-start | bytes 983048 | tf_op jit(solution)/shard_map/ppermute | solution.py:372
  59.9 14.6 %collective-permute-start.10 = (bf16[80,2048]{1,0:T(8,128)(2,1)S(1)}, bf16[80,2048]{1,0:T(8,128)(2,1)S(1)}, u32[]{:S(2)}, u32[]{:S(2)}) collective-permute-start(bf16[80,2048]{1,0:T(8,128)(2,1)S(1)} %collective-permute-done.2.refs_4_), channel_id=1, source_target_pairs={{0,7},{1,0},{2,1},{3,2},{4,3},{5,4},{6,5},{7,6},{8,15},{9,8},{10,9... | collective-permute-start | bytes 983048 | tf_op jit(solution)/shard_map/ppermute | solution.py:372
  65.9 28.1 %copy-start.6 = (bf16[80,2048]{1,0:T(8,128)(2,1)}, bf16[80,2048]{1,0:T(8,128)(2,1)S(1)}, u32[]{:S(2)}) copy-start(bf16[80,2048]{1,0:T(8,128)(2,1)S(1)} %collective-permute-done.8.refs_6_) | copy-start | bytes 983044
  65.9 14.1 %collective-permute-start.12 = (bf16[80,2048]{1,0:T(8,128)(2,1)S(1)}, bf16[80,2048]{1,0:T(8,128)(2,1)S(1)}, u32[]{:S(2)}, u32[]{:S(2)}) collective-permute-start(bf16[80,2048]{1,0:T(8,128)(2,1)S(1)} %collective-permute-done.8.refs_6_), channel_id=1, source_target_pairs={{0,1},{1,2},{2,3},{3,4},{4,5},{5,6},{6,7},{7,0},{8,9},{9,10},{10,1... | collective-permute-start | bytes 983048 | tf_op jit(solution)/shard_map/ppermute | solution.py:372
  68.1 26.0 %copy-start.7 = (bf16[80,2048]{1,0:T(8,128)(2,1)}, bf16[80,2048]{1,0:T(8,128)(2,1)S(1)}, u32[]{:S(2)}) copy-start(bf16[80,2048]{1,0:T(8,128)(2,1)S(1)} %collective-permute-done.11.refs_9_) | copy-start | bytes 983044
  68.1 13.5 %collective-permute-start.15 = (bf16[80,2048]{1,0:T(8,128)(2,1)S(1)}, bf16[80,2048]{1,0:T(8,128)(2,1)S(1)}, u32[]{:S(2)}, u32[]{:S(2)}) collective-permute-start(bf16[80,2048]{1,0:T(8,128)(2,1)S(1)} %collective-permute-done.11.refs_9_), channel_id=1, source_target_pairs={{0,7},{1,0},{2,1},{3,2},{4,3},{5,4},{6,5},{7,6},{8,15},{9,8},{10,9... | collective-permute-start | bytes 983048 | tf_op jit(solution)/shard_map/ppermute | solution.py:372
  73.0 14.0 %collective-permute-start.13 = (bf16[80,2048]{1,0:T(8,128)(2,1)S(1)}, bf16[80,2048]{1,0:T(8,128)(2,1)S(1)}, u32[]{:S(2)}, u32[]{:S(2)}) collective-permute-start(bf16[80,2048]{1,0:T(8,128)(2,1)S(1)} %collective-permute-done.9.refs_7_), channel_id=1, source_target_pairs={{0,1},{1,2},{2,3},{3,4},{4,5},{5,6},{6,7},{7,0},{8,9},{9,10},{10,1... | collective-permute-start | bytes 983048 | tf_op jit(solution)/shard_map/ppermute | solution.py:372
  74.6 13.0 %collective-permute-start.14 = (bf16[80,2048]{1,0:T(8,128)(2,1)S(1)}, bf16[80,2048]{1,0:T(8,128)(2,1)S(1)}, u32[]{:S(2)}, u32[]{:S(2)}) collective-permute-start(bf16[80,2048]{1,0:T(8,128)(2,1)S(1)} %collective-permute-done.10.refs_8_), channel_id=1, source_target_pairs={{0,7},{1,0},{2,1},{3,2},{4,3},{5,4},{6,5},{7,6},{8,15},{9,8},{10,9... | collective-permute-start | bytes 983048 | tf_op jit(solution)/shard_map/ppermute | solution.py:372
  80.1 13.9 %collective-permute-start.16 = (bf16[80,2048]{1,0:T(8,128)(2,1)S(1)}, bf16[80,2048]{1,0:T(8,128)(2,1)S(1)}, u32[]{:S(2)}, u32[]{:S(2)}) collective-permute-start(bf16[80,2048]{1,0:T(8,128)(2,1)S(1)} %collective-permute-done.12.refs_10_), channel_id=1, source_target_pairs={{0,1},{1,2},{2,3},{3,4},{4,5},{5,6},{6,7},{7,0},{8,9},{9,10},{10,1... | collective-permute-start | bytes 983048 | tf_op jit(solution)/shard_map/ppermute | solution.py:372
  81.6 12.5 %collective-permute-start.17 = (bf16[80,2048]{1,0:T(8,128)(2,1)S(1)}, bf16[80,2048]{1,0:T(8,128)(2,1)S(1)}, u32[]{:S(2)}, u32[]{:S(2)}) collective-permute-start(bf16[80,2048]{1,0:T(8,128)(2,1)S(1)} %collective-permute-done.15.refs_13_), channel_id=1, source_target_pairs={{0,7},{1,0},{2,1},{3,2},{4,3},{5,4},{6,5},{7,6},{8,15},{9,8},{10,9... | collective-permute-start | bytes 983048 | tf_op jit(solution)/shard_map/ppermute | solution.py:372
  109.3 26.6 %copy-start.1 = (bf16[8,128,256]{2,1,0:T(8,128)(2,1)S(1)}, bf16[8,128,256]{2,1,0:T(8,128)(2,1)}, u32[]{:S(2)}) copy-start(bf16[8,128,256]{2,1,0:T(8,128)(2,1)} %shard_map.83) | copy-start | bytes 1572868
  111.4 12.0 %collective-permute-start.18 = (bf16[2,3,64,256]{3,2,1,0:T(8,128)(2,1)S(1)}, bf16[2,3,64,256]{3,2,1,0:T(8,128)(2,1)S(1)}, u32[]{:S(2)}, u32[]{:S(2)}) collective-permute-start(bf16[2,3,64,256]{3,2,1,0:T(8,128)(2,1)S(1)} %get-tuple-element.73), channel_id=1, source_target_pairs={{0,16},{16,32},{32,48},{48,0},{1,17},{17,33},{33,49},{49,1},{2,18}... | collective-permute-start | bytes 589832 | tf_op jit(solution)/shard_map/ppermute | solution.py:372
  112.8 20.1 %collective-permute-start.19 = (bf16[2,3,64,256]{3,2,1,0:T(8,128)(2,1)S(1)}, bf16[2,3,64,256]{3,2,1,0:T(8,128)(2,1)S(1)}, u32[]{:S(2)}, u32[]{:S(2)}) collective-permute-start(bf16[2,3,64,256]{3,2,1,0:T(8,128)(2,1)S(1)} %get-tuple-element.72), channel_id=1, source_target_pairs={{0,32},{16,48},{32,0},{48,16},{1,33},{17,49},{33,1},{49,17},{2,34}... | collective-permute-start | bytes 589832 | tf_op jit(solution)/shard_map/ppermute | solution.py:372
  115.1 17.8 %collective-permute-start.20 = (bf16[2,3,64,256]{3,2,1,0:T(8,128)(2,1)S(1)}, bf16[2,3,64,256]{3,2,1,0:T(8,128)(2,1)S(1)}, u32[]{:S(2)}, u32[]{:S(2)}) collective-permute-start(bf16[2,3,64,256]{3,2,1,0:T(8,128)(2,1)S(1)} %get-tuple-element.71), channel_id=1, source_target_pairs={{0,48},{16,0},{32,16},{48,32},{1,49},{17,1},{33,17},{49,33},{2,50}... | collective-permute-start | bytes 589832 | tf_op jit(solution)/shard_map/ppermute | solution.py:372
  162.4 47.2 %all-to-all-start.1 = ((bf16[16,32,2048]{2,1,0:T(8,128)(2,1)}), bf16[16,32,2048]{2,1,0:T(8,128)(2,1)S(1)}, u32[]{:S(2)}, u32[]{:S(2)}) async-start(bf16[16,32,2048]{2,1,0:T(8,128)(2,1)} %get-tuple-element.53), calls=%async_computation.1 | async-start | bytes 4194304 | tf_op jit(solution)/shard_map/all_to_all | solution.py:424
  (16 other events, 136.3 us)
Sparse Core Ops, SparseCore 0:
  55.0 87.8 all-gather.4
  144.7 53.8 all-gather.6

commit v6 on v5

v6 whole, which is shorter than its diff:
```python
import functools
import math

import jax
import jax.numpy as jnp
from jax import lax
from jax.experimental import pallas as pl
from jax.experimental.pallas import tpu as pltpu
from jax.sharding import Mesh
from jax.sharding import PartitionSpec as P

E = 128
SEQ = 64
SCALE = 1.0 / math.sqrt(E)
BF = jnp.bfloat16
F32 = jnp.float32
NZ = 8
VMEM_LIMIT = 28 * 1024 * 1024
OFFSETS = (0, -1, 1, -2, 2, -3, 3, 4)


def params():
    return pltpu.CompilerParams(vmem_limit_bytes=VMEM_LIMIT)


def vmem():
    return pl.BlockSpec(memory_space=pltpu.VMEM)


def smem():
    return pl.BlockSpec(memory_space=pltpu.SMEM)


def normed(values, gain):
    scaled = values * lax.rsqrt(jnp.mean(values * values, axis=-1, keepdims=True) + 1e-05)
    return (scaled * gain).astype(BF)


def softmax(scores):
    top = jnp.max(scores, axis=-1, keepdims=True)
    shifted = jnp.exp2((scores - top) * (SCALE * math.log2(math.e)))
    return (shifted * (1.0 / jnp.sum(shifted, axis=-1, keepdims=True))).astype(BF)


def dot(a, b):
    return jnp.dot(a, b, preferred_element_type=F32)


def dot_t(a, b):
    return lax.dot_general(a, b, (((1,), (1,)), ((), ())), preferred_element_type=F32)


def norm_kernel(place_ref, x_ref, gain_ref, qkv_ref, a_ref, b_ref, rows_ref):
    gain = gain_ref[...]
    values = jnp.transpose(x_ref[...].astype(F32), (1, 0, 2)).reshape(rows_ref.shape)
    half = rows_ref.shape[0] // 2
    rows_ref[...] = values.astype(BF)
    a_ref[:half] = normed(values[:half], gain)
    b_ref[:half] = normed(values[half:], gain)
    b_ref[half:, 1024:] = jnp.zeros((16, 1024), BF)
    for kind in range(3):
        share = qkv_ref[kind]
        ref = (a_ref, b_ref)[kind // 2]
        for group in range(4):
            low = 256 * (4 * (kind % 2) + group)
            ref[half:, low : low + 256] = share[16 * group : 16 * group + 16]


def norm_rows(place, stream, gain, temporal_qkv):
    patches, frames, width = stream.shape
    count = patches * frames
    half = jax.ShapeDtypeStruct((count // 2 + 16, width), BF)
    whole = lambda *shape: pl.BlockSpec(shape, lambda i, at: (0,) * len(shape))
    return pl.pallas_call(
        norm_kernel,
        grid_spec=pltpu.PrefetchScalarGridSpec(
            num_scalar_prefetch=1,
            grid=(1,),
            in_specs=[
                whole(patches, frames, width),
                whole(1, width),
                pl.BlockSpec((3, 64, 256), lambda i, at: (0, at[0], 0)),
            ],
            out_specs=(
                whole(count // 2 + 16, width),
                whole(count // 2 + 16, width),
                whole(count, width),
            ),
        ),
        out_shape=(half, half, jax.ShapeDtypeStruct((count, width), BF)),
        compiler_params=params(),
        cost_estimate=pl.CostEstimate(
            flops=4 * count * width, bytes_accessed=6 * count * width, transcendentals=0
        ),
    )(place, stream, gain, temporal_qkv)


def split_kernel(place_ref, *refs):
    pieces, sends = refs[:-4], refs[-4:]
    z, y = place_ref[0], place_ref[1]
    for k in range(NZ):
        source = lax.rem(z + (OFFSETS[k] + NZ), NZ)
        step = lax.rem(source // 2 + 4 - y, 4)
        pair = lax.rem(source, 2)
        for index, send_ref in enumerate(sends):

            @pl.when(step == index)
            def _():
                for kind in range(3):
                    for group in range(4):
                        low = 256 * (4 * (kind % 2) + group)
                        rows = slice(16 * group, 16 * group + 16)
                        value = pieces[2 * k + kind // 2][:, low : low + 256]
                        send_ref[pair, kind, rows] = value


def split_shares(place, pieces):
    return pl.pallas_call(
        split_kernel,
        grid=(1,),
        out_shape=(jax.ShapeDtypeStruct((2, 3, 64, 256), BF),) * 4,
        in_specs=[smem()] + [pl.BlockSpec((16, 2048), lambda i: (4, 0))] * len(pieces),
        out_specs=(pl.BlockSpec((2, 3, 64, 256), lambda i: (0, 0, 0, 0)),) * 4,
        compiler_params=params(),
        cost_estimate=pl.CostEstimate(flops=0, bytes_accessed=2 << 20, transcendentals=0),
    )(place, *pieces)


def join_kernel(y_ref, *refs):
    out_ref = refs[-1]
    for step in range(4):
        low = pl.multiple_of(64 * lax.rem(y_ref[0] + (4 - step), 4), 64)
        for pair in range(2):
            for kind in range(3):
                out_ref[3 * pair + kind, pl.ds(low, 64), :] = refs[step][pair, kind]


def join_shares(y, got):
    return pl.pallas_call(
        join_kernel,
        out_shape=jax.ShapeDtypeStruct((6, 256, 256), BF),
        in_specs=[smem()] + [vmem()] * 4,
        out_specs=vmem(),
        compiler_params=params(),
        cost_estimate=pl.CostEstimate(flops=0, bytes_accessed=2 << 20, transcendentals=0),
    )(y, *got)


def attend(chains):
    scores = [dot_t(query, key) for query, key, _, _ in chains]
    scores = [
        one if chain[3] is None else jnp.where(chain[3] < 0.0, chain[3], one)
        for one, chain in zip(scores, chains)
    ]
    weights = [softmax(one) for one in scores]
    return [dot(one, chain[2]).astype(BF) for one, chain in zip(weights, chains)]


def spatial_kernel(place_ref, weight_ref, *refs):
    pieces, out_ref, qkv = refs[: 2 * NZ], refs[2 * NZ], refs[2 * NZ + 1]
    place = place_ref[0]
    for frame in range(4):
        low = 32 * (frame % 2)
        rows = jnp.concatenate(
            [pieces[2 * k + frame // 2][low : low + 32, :] for k in range(NZ)], axis=0
        )
        for kind in range(3):
            qkv[kind, 256 * frame : 256 * frame + 256] = dot(rows, weight_ref[kind]).astype(BF)
    for frames in ((0, 1), (2, 3)):
        spots = [(frame, head * E) for frame in frames for head in range(2)]
        chains = []
        for frame, low in spots:
            at, cols = slice(256 * frame, 256 * frame + 256), slice(low, low + E)
            chains.append((qkv[0, at, cols], qkv[1, at, cols], qkv[2, at, cols], None))
        for (frame, low), mixed in zip(spots, attend(chains)):
            for k in range(NZ):
                target = lax.rem(place + (OFFSETS[k] + NZ), NZ)
                out_ref[target, 32 * frame : 32 * frame + 32, low : low + E] = mixed[
                    32 * k : 32 * k + 32
                ]


def spatial_attend(place, weight, pieces):
    return pl.pallas_call(
        spatial_kernel,
        out_shape=jax.ShapeDtypeStruct((NZ, 128, 256), BF),
        in_specs=[smem(), vmem()] + [vmem()] * len(pieces),
        out_specs=vmem(),
        scratch_shapes=[pltpu.VMEM((3, 1024, 256), BF)],
        compiler_params=params(),
        cost_estimate=pl.CostEstimate(
            flops=2 * 1024 * 2048 * 768 * 2, bytes_accessed=8 << 20, transcendentals=8 * 65536
        ),
    )(place, weight, *pieces)


def column_block(read):
    return jnp.concatenate([read(head, k // 4, k % 4) for k in range(NZ) for head in range(2)], axis=0)


def join_blocks_kernel(z_ref, *refs):
    out_ref = refs[-1]
    for step in range(4):
        out_ref[lax.rem(z_ref[0] + (4 - step), 4)] = refs[step][...]


def join_blocks(z, parts):
    return pl.pallas_call(
        join_blocks_kernel,
        out_shape=jax.ShapeDtypeStruct((4, 2, 128, 256), BF),
        in_specs=[smem()] + [vmem()] * 4,
        out_specs=vmem(),
        compiler_params=params(),
        cost_estimate=pl.CostEstimate(flops=0, bytes_accessed=512 << 10, transcendentals=0),
    )(z, *parts)


def middle_kernel(mix_ref, weight_ref, rows_ref, gain_ref, middle_ref, send_ref, weight, total, sems):
    copies = [
        pltpu.make_async_copy(weight_ref.at[block, :, :, :, 0], weight.at[block], sems.at[block])
        for block in range(8)
    ]
    for copy in copies:
        copy.start()
    mix = jnp.concatenate([mix_ref[k] for k in range(NZ)], axis=1)
    for block in range(8):
        copies[block].wait()
        part = column_block(lambda *at: weight[(block, *at)])
        total[:, 256 * block : 256 * block + 256] = dot(mix, part)
    middle = (total[...] + rows_ref[...].astype(F32)).astype(BF)
    middle_ref[...] = middle
    values = middle.astype(F32)
    scaled = values * lax.rsqrt(jnp.mean(values * values, axis=-1, keepdims=True) + 1e-05)
    scaled = scaled * gain_ref[...]
    for group in range(4):
        chunk = jnp.concatenate(
            [scaled[32 * f + 8 * group : 32 * f + 8 * group + 8] for f in range(4)], axis=0
        ).astype(BF)
        for y in range(4):
            send_ref[(group // 2) * 8 + y * 2 + group % 2] = chunk


def middle_rows(mix, weight, rows, gain):
    width = rows.shape[1]
    return pl.pallas_call(
        middle_kernel,
        out_shape=(
            jax.ShapeDtypeStruct((128, width), BF),
            jax.ShapeDtypeStruct((16, 32, width), BF),
        ),
        in_specs=[vmem(), pl.BlockSpec(memory_space=pl.ANY), vmem(), vmem()],
        out_specs=(vmem(), vmem()),
        scratch_shapes=[
            pltpu.VMEM((8, 2, 2, 4, E, 256), BF),
            pltpu.VMEM((128, width), F32),
            pltpu.SemaphoreType.DMA((8,)),
        ],
        compiler_params=params(),
        cost_estimate=pl.CostEstimate(
            flops=2 * 128 * 2048 * 2048, bytes_accessed=12 << 20, transcendentals=0
        ),
    )(mix, weight, rows, gain)


def temporal_kernel(start_ref, rows_ref, weight_ref, out_ref, qkv, bias):
    count = rows_ref.shape[0]
    start = start_ref[0]
    late = lax.broadcasted_iota(jnp.int32, (count, count), 0)
    early = lax.broadcasted_iota(jnp.int32, (count, count), 1)
    same = (late & 7) == (early & 7)
    allowed = same & (early <= late) & ((early >= 8 * start) == (late >= 8 * start))
    bias[...] = jnp.where(allowed, 0.0, -1e30)
    for block in range(6):
        qkv[block] = dot(rows_ref[...], weight_ref[:, block].reshape(2048, 256)).astype(BF)
    size = 256
    for pair in range(2):
        for low in range(0, count, size):
            chains = []
            high = low + size
            for head in range(2):
                cols = slice(head * E, head * E + E)
                chains.append(
                    (
                        qkv[3 * pair, low:high, cols],
                        qkv[3 * pair + 1, :high, cols],
                        qkv[3 * pair + 2, :high, cols],
                        bias[low:high, :high],
                    )
                )
            for head, mixed in enumerate(attend(chains)):
                at = 256 * pair + head * E
                out_ref[low // 32 : high // 32, :, at : at + E] = mixed.reshape(size // 32, 32, E)


def temporal_attend(start, rows, weight):
    count, width = rows.shape
    return pl.pallas_call(
        temporal_kernel,
        out_shape=jax.ShapeDtypeStruct((16, 32, 512), BF),
        in_specs=[smem(), vmem(), vmem()],
        out_specs=vmem(),
        scratch_shapes=[
            pltpu.VMEM((6, count, 256), BF),
            pltpu.VMEM((count, count), F32),
        ],
        compiler_params=params(),
        cost_estimate=pl.CostEstimate(
            flops=2 * 512 * 2048 * 1536, bytes_accessed=9 << 20, transcendentals=131072
        ),
    )(start, rows, weight)


def last_kernel(mix_ref, weight_ref, middle_ref, out_ref, total):
    mix = jnp.concatenate(
        [
            jnp.concatenate([mix_ref[xl * 8 + y * 2 + c] for xl in range(2) for c in range(2)], axis=0)
            for y in range(4)
        ],
        axis=1,
    )
    for block in range(8):
        part = column_block(lambda *at: weight_ref[(block, *at, 1)])
        total[:, 256 * block : 256 * block + 256] = dot(mix, part)
    for group in range(4):
        rows = total[32 * group : 32 * group + 32].reshape(4, 8, -1)
        middle = jnp.stack(
            [
                middle_ref[32 * f : 32 * f + 32].astype(F32)[8 * group : 8 * group + 8]
                for f in range(4)
            ],
            axis=0,
        )
        out = jnp.transpose(rows + middle, (1, 0, 2)).astype(BF)
        out_ref[8 * group : 8 * group + 8] = out


def last_rows(mix, weight, middle):
    width = middle.shape[1]
    return pl.pallas_call(
        last_kernel,
        out_shape=jax.ShapeDtypeStruct((32, 4, width), BF),
        in_specs=[vmem()] * 3,
        out_specs=vmem(),
        scratch_shapes=[pltpu.VMEM((128, width), F32)],
        compiler_params=params(),
        cost_estimate=pl.CostEstimate(
            flops=2 * 128 * 2048 * 2048, bytes_accessed=12 << 20, transcendentals=0
        ),
    )(mix, weight, middle)


def shifted(value, axis, step):
    count = lax.axis_size(axis)
    return lax.ppermute(value, axis, [(i, (i + step) % count) for i in range(count)])


def gathered_rows(chunks):
    up, down = list(chunks), list(chunks)
    pieces = {0: list(chunks)}
    for step in (1, 2, 3):
        up = [shifted(value, "z", 1) for value in up]
        down = [shifted(value, "z", -1) for value in down]
        pieces[-step], pieces[step] = up, down
    pieces[4] = [shifted(up[0], "z", 1), shifted(down[1], "z", -1)]
    return [value for offset in OFFSETS for value in pieces[offset]]


def local(stream, spatial_gain, spatial_qkv, spatial_out, temporal_gain, temporal_qkv, temporal_out, starts):
    patches, frames, width = stream.shape
    w, xl, y, c, z = (lax.axis_index(name) for name in ("w", "xl", "y", "c", "z"))

    place = (((w * 2 + xl) * 2 + c) * 4 + y).reshape(1)
    first, second, rows = norm_rows(
        place, stream, spatial_gain.reshape(1, width), jnp.transpose(temporal_qkv, (1, 0, 2))
    )

    low = (lax.rem(y, 2) * E, ((w * 2 + xl) * 2 + y // 2) * 256)
    block = jnp.stack(
        [lax.dynamic_slice(weight, low, (E, 256)) for weight in (spatial_out, temporal_out)]
    )
    parts = []
    for k in range(4):
        pairs = [
            (a * 8 + b, (b // 4) * 8 + (b + 4 * a + k) % 8) for a in range(2) for b in range(8)
        ]
        parts.append(lax.ppermute(block, ("c", "z"), pairs))
    first, second, parts = lax.optimization_barrier((first, second, parts))
    outs = join_blocks(z.reshape(1), parts)
    outs = lax.all_gather(outs, ("w", "xl", "y", "c"), axis=0, tiled=False)
    outs = outs.reshape(8, 2, 2, 4, 2, E, 256)

    pieces = gathered_rows((first, second))

    sends = split_shares(jnp.stack([z, y]).astype(jnp.int32), pieces)
    got = [sends[0]] + [shifted(sends[k], "y", k) for k in range(1, 4)]

    weight = jnp.transpose(spatial_qkv, (1, 0, 2))
    mix = spatial_attend(z.reshape(1), weight, pieces)
    mix, *got = lax.optimization_barrier((mix, *got))
    quarter = join_shares(y.reshape(1), got)
    mix, quarter = lax.optimization_barrier((mix, quarter))
    quarter = lax.all_gather(quarter[None], ("w", "xl", "c"), axis=0, tiled=True)
    mix = lax.all_to_all(mix, "z", 0, 0, tiled=True)

    middle, send = middle_rows(mix, outs, rows, temporal_gain.reshape(1, width))
    window = lax.all_to_all(send, ("xl", "y", "c"), 0, 0, tiled=True)
    start = lax.dynamic_slice(starts, (w,), (1,))
    mix = temporal_attend(start, window.reshape(512, width), quarter)
    mix = lax.all_to_all(mix, ("xl", "y", "c"), 0, 0, tiled=True)
    return last_rows(mix, outs, middle)


def solution(mesh):
    names = ("w", "xl", "y", "c", "z")
    fine = Mesh(mesh.devices.reshape(2, 2, 4, 2, NZ), names)
    tm = ("w", "xl", "y", "c")
    placed = (
        P("z", tm, None),
        P(),
        P(None, None, "z"),
        P("z", None),
        P(),
        P(None, None, "z"),
        P("z", None),
        P(),
    )
    return jax.shard_map(
        local, mesh=fine, in_specs=placed, out_specs=P("z", tm, None), check_vma=False
    )
```

time: 255 us -> 222 us (0.87)
  Pallas kernels: 49.6 us -> 20.3 us
  local copies, waits for them, and re-layouts: 7.09 us -> 21.1 us
  waiting for transfers between devices: 99.3 us -> 87.4 us
  starting transfers between devices: 49.7 us -> 47.1 us
    pallas_call x4, Pallas kernels: 31 us -> 13.3 us  [the longest x1 6.01 us: temporal_attend(): pl.pallas_call(temporal_kernel, out_shape=jax.ShapeDtypeStruct((16, 32, 5...]
    unnamed x48 -> x20, local copies, waits for them, and re-layouts: 3.48 us -> 19.7 us
    ppermute x4, waiting for transfers between devices: 18.7 us -> 4.04 us  [local(): parts.append(lax.ppermute(block, ('c', 'z'), pairs))]
    pallas_call x1, Pallas kernels: 12 us -> 4.47 us  [spatial_attend(): pl.pallas_call(spatial_kernel, out_shape=jax.ShapeDtypeStruct((NZ, 128, 2...]
    ppermute x4, starting transfers between devices: 18.4 us -> 13.8 us  [local(): parts.append(lax.ppermute(block, ('c', 'z'), pairs))]
    ppermute x17, waiting for transfers between devices: 42.2 us -> 46.3 us  [shifted(): lax.ppermute(value, axis, [(i, (i + step) % count) for i in range(count)])]
    all_gather x1, waiting for transfers between devices: 27.4 us -> 24.7 us  [local(): lax.all_gather(quarter[None], ('w', 'xl', 'c'), axis=0, tiled=True)]
  transfers between devices with their start and end apart: 24 -> 24, of which waited for: 15 -> 18; matrix products, arithmetic and copies ran while one was open for 1% -> 0% of each run, Pallas kernels for 9% -> 5%
where the time goes in v6:
time: 222 us
  waiting for transfers between devices  87.4 us (39%)
  starting transfers between devices  47.1 us (21%)
  blocking collectives  32.4 us (15%)
  local copies, waits for them, and re-layouts  21.1 us (10%)
  Pallas kernels  20.3 us (9%)
  between operations  13.5 us (6%)
    ppermute x17, waiting for transfers between devices, shifted(): lax.ppermute(value, axis, [(i, (i + step) % count) for i in range(count)])  46.3 us
    all_gather x1, waiting for transfers between devices, local(): lax.all_gather(quarter[None], ('w', 'xl', 'c'), axis=0, tiled=True)  24.7 us
    ppermute x17, starting transfers between devices, shifted(): lax.ppermute(value, axis, [(i, (i + step) % count) for i in range(count)])  23.7 us
    unnamed x20, local copies, waits for them, and re-layouts  19.7 us
    all_to_all x1, blocking collectives, local(): mix = lax.all_to_all(mix, 'z', 0, 0, tiled=True)  17.5 us
    all_to_all x1, blocking collectives, local(): mix = lax.all_to_all(mix, ('xl', 'y', 'c'), 0, 0, tiled=True)  14.9 us
    ppermute x4, starting transfers between devices, local(): parts.append(lax.ppermute(block, ('c', 'z'), pairs))  13.8 us
    all_to_all x1, waiting for transfers between devices, local(): window = lax.all_to_all(send, ('xl', 'y', 'c'), 0, 0, tiled=True)  12.3 us
  transfers between devices with their start and end apart: 24, of which 18 were waited for; matrix products, arithmetic and copies ran while one was open for 0% of the time, Pallas kernels for 5%

profile of v6, /device:TPU:1, one launch (start us, length us, event | category | flops | bytes accessed | tf_op | source)
XLA Modules:
  0.0 221.9 jit_solution(16595207704005869199)
XLA Ops:
  7.4 10.2 %collective-permute-start = (bf16[2,128,256]{2,1,0:T(8,128)(2,1)S(1)}, bf16[2,128,256]{2,1,0:T(8,128)(2,1)S(1)}, u32[]{:S(2)}, u32[]{:S(2)}) collective-permute-start(bf16[2,128,256]{2,1,0:T(8,128)(2,1)S(1)} %pad_maximum_fusion), channel_id=1, source_target_pairs={{0,0},{1,1},{2,2},{3,3},{4,12},{5,13},{6,14},{7,15},{8,4},{9,5},{1... | collective-permute-start | bytes 393224 | tf_op jit(solution)/shard_map/ppermute | solution.py:386
  18.5 2.8 %collective-permute-start.3 = (bf16[2,128,256]{2,1,0:T(8,128)(2,1)S(1)}, bf16[2,128,256]{2,1,0:T(8,128)(2,1)S(1)}, u32[]{:S(2)}, u32[]{:S(2)}) collective-permute-start(bf16[2,128,256]{2,1,0:T(8,128)(2,1)S(1)} %pad_maximum_fusion), channel_id=1, source_target_pairs={{0,3},{1,4},{2,5},{3,6},{4,15},{5,8},{6,9},{7,10},{8,7},{9,0},{10,... | collective-permute-start | bytes 393224 | tf_op jit(solution)/shard_map/ppermute | solution.py:386
  26.5 3.1 %collective-permute-done.3.refs_3_ = bf16[2,128,256]{2,1,0:T(8,128)(2,1)S(1)} collective-permute-done((bf16[2,128,256]{2,1,0:T(8,128)(2,1)S(1)}, bf16[2,128,256]{2,1,0:T(8,128)(2,1)S(1)}, u32[]{:S(2)}, u32[]{:S(2)}) %collective-permute-start.3) | collective-permute-done | bytes 131104 | tf_op jit(solution)/shard_map/ppermute | solution.py:386
  33.7 2.2 collective-permute-start.6
  35.9 3.2 %collective-permute-done.4.refs_2_ = bf16[80,2048]{1,0:T(8,128)(2,1)S(1)} collective-permute-done((bf16[80,2048]{1,0:T(8,128)(2,1)S(1)}, bf16[80,2048]{1,0:T(8,128)(2,1)S(1)}, u32[]{:S(2)}, u32[]{:S(2)}) %collective-permute-start.4) | collective-permute-done | bytes 327712 | tf_op jit(solution)/shard_map/ppermute | solution.py:354
  39.1 2.2 %collective-permute-start.8 = (bf16[80,2048]{1,0:T(8,128)(2,1)S(1)}, bf16[80,2048]{1,0:T(8,128)(2,1)S(1)}, u32[]{:S(2)}, u32[]{:S(2)}) collective-permute-start(bf16[80,2048]{1,0:T(8,128)(2,1)S(1)} %collective-permute-done.4.refs_2_), channel_id=1, source_target_pairs={{0,1},{1,2},{2,3},{3,4},{4,5},{5,6},{6,7},{7,0},{8,9},{9,10},{10,1... | collective-permute-start | bytes 983048 | tf_op jit(solution)/shard_map/ppermute | solution.py:354
  41.8 4.3 %collective-permute-done.5.refs_3_ = bf16[80,2048]{1,0:T(8,128)(2,1)S(1)} collective-permute-done((bf16[80,2048]{1,0:T(8,128)(2,1)S(1)}, bf16[80,2048]{1,0:T(8,128)(2,1)S(1)}, u32[]{:S(2)}, u32[]{:S(2)}) %collective-permute-start.5) | collective-permute-done | bytes 327712 | tf_op jit(solution)/shard_map/ppermute | solution.py:354
  46.1 2.2 %collective-permute-start.9 = (bf16[80,2048]{1,0:T(8,128)(2,1)S(1)}, bf16[80,2048]{1,0:T(8,128)(2,1)S(1)}, u32[]{:S(2)}, u32[]{:S(2)}) collective-permute-start(bf16[80,2048]{1,0:T(8,128)(2,1)S(1)} %collective-permute-done.5.refs_3_), channel_id=1, source_target_pairs={{0,1},{1,2},{2,3},{3,4},{4,5},{5,6},{6,7},{7,0},{8,9},{9,10},{10,1... | collective-permute-start | bytes 983048 | tf_op jit(solution)/shard_map/ppermute | solution.py:354
  48.8 4.4 %collective-permute-done.8.refs_6_ = bf16[80,2048]{1,0:T(8,128)(2,1)S(1)} collective-permute-done((bf16[80,2048]{1,0:T(8,128)(2,1)S(1)}, bf16[80,2048]{1,0:T(8,128)(2,1)S(1)}, u32[]{:S(2)}, u32[]{:S(2)}) %collective-permute-start.8) | collective-permute-done | bytes 327712 | tf_op jit(solution)/shard_map/ppermute | solution.py:354
  55.9 4.2 %collective-permute-done.9.refs_7_ = bf16[80,2048]{1,0:T(8,128)(2,1)S(1)} collective-permute-done((bf16[80,2048]{1,0:T(8,128)(2,1)S(1)}, bf16[80,2048]{1,0:T(8,128)(2,1)S(1)}, u32[]{:S(2)}, u32[]{:S(2)}) %collective-permute-start.9) | collective-permute-done | bytes 327712 | tf_op jit(solution)/shard_map/ppermute | solution.py:354
  60.2 2.2 %collective-permute-start.13 = (bf16[80,2048]{1,0:T(8,128)(2,1)S(1)}, bf16[80,2048]{1,0:T(8,128)(2,1)S(1)}, u32[]{:S(2)}, u32[]{:S(2)}) collective-permute-start(bf16[80,2048]{1,0:T(8,128)(2,1)S(1)} %collective-permute-done.9.refs_7_), channel_id=1, source_target_pairs={{0,1},{1,2},{2,3},{3,4},{4,5},{5,6},{6,7},{7,0},{8,9},{9,10},{10,1... | collective-permute-start | bytes 983048 | tf_op jit(solution)/shard_map/ppermute | solution.py:354
  62.9 4.3 %collective-permute-done.12.refs_10_ = bf16[80,2048]{1,0:T(8,128)(2,1)S(1)} collective-permute-done((bf16[80,2048]{1,0:T(8,128)(2,1)S(1)}, bf16[80,2048]{1,0:T(8,128)(2,1)S(1)}, u32[]{:S(2)}, u32[]{:S(2)}) %collective-permute-start.12) | collective-permute-done | bytes 327712 | tf_op jit(solution)/shard_map/ppermute | solution.py:354
  67.2 2.2 %collective-permute-start.16 = (bf16[80,2048]{1,0:T(8,128)(2,1)S(1)}, bf16[80,2048]{1,0:T(8,128)(2,1)S(1)}, u32[]{:S(2)}, u32[]{:S(2)}) collective-permute-start(bf16[80,2048]{1,0:T(8,128)(2,1)S(1)} %collective-permute-done.12.refs_10_), channel_id=1, source_target_pairs={{0,1},{1,2},{2,3},{3,4},{4,5},{5,6},{6,7},{7,0},{8,9},{9,10},{10,1... | collective-permute-start | bytes 983048 | tf_op jit(solution)/shard_map/ppermute | solution.py:354
  69.9 4.4 %collective-permute-done.13.refs_11_ = bf16[80,2048]{1,0:T(8,128)(2,1)S(1)} collective-permute-done((bf16[80,2048]{1,0:T(8,128)(2,1)S(1)}, bf16[80,2048]{1,0:T(8,128)(2,1)S(1)}, u32[]{:S(2)}, u32[]{:S(2)}) %collective-permute-start.13) | collective-permute-done | bytes 327712 | tf_op jit(solution)/shard_map/ppermute | solution.py:354
  74.3 2.2 collective-permute-done.14.refs_12_
  76.5 4.8 %collective-permute-done.16.refs_14_ = bf16[80,2048]{1,0:T(8,128)(2,1)S(1)} collective-permute-done((bf16[80,2048]{1,0:T(8,128)(2,1)S(1)}, bf16[80,2048]{1,0:T(8,128)(2,1)S(1)}, u32[]{:S(2)}, u32[]{:S(2)}) %collective-permute-start.16) | collective-permute-done | bytes 327712 | tf_op jit(solution)/shard_map/ppermute | solution.py:354
  81.3 2.2 collective-permute-done.17.refs_15_
  85.8 2.6 %collective-permute-start.19 = (bf16[2,3,64,256]{3,2,1,0:T(8,128)(2,1)S(1)}, bf16[2,3,64,256]{3,2,1,0:T(8,128)(2,1)S(1)}, u32[]{:S(2)}, u32[]{:S(2)}) collective-permute-start(bf16[2,3,64,256]{3,2,1,0:T(8,128)(2,1)S(1)} %get-tuple-element.33), channel_id=1, source_target_pairs={{0,32},{16,48},{32,0},{48,16},{1,33},{17,49},{33,1},{49,17},{2,34}... | collective-permute-start | bytes 589832 | tf_op jit(solution)/shard_map/ppermute | solution.py:354
  89.5 4.5 %shard_map.83 = bf16[8,128,256]{2,1,0:T(8,128)(2,1)S(1)} custom-call(s32[1]{0:T(128)} %bitcast.place_ref.z_ref, bf16[3,2048,256]{2,1,0:T(8,128)(2,1)S(1)} %bitcast.21, bf16[80,2048]{1,0:T(8,128)(2,1)S(1)} %get-tuple-element.29.refs_0_, bf16[80,2048]{1,0:T(8,128)(2,1)S(1)} %get-tuple-element.30.refs_1_, bf16[80,2048]{1,0:T(8,128)(2,1)S(1)} %collective-permute-done.4.refs_2_, ...), custom_call_target="tpu_custom_call" | custom-call | flops 6442450944 | bytes 8388608 | tf_op jit(solution)/shard_map/pallas_call | solution.py:184
  93.9 2.5 %collective-permute-done.18.refs_1_ = bf16[2,3,64,256]{3,2,1,0:T(8,128)(2,1)S(1)} collective-permute-done((bf16[2,3,64,256]{3,2,1,0:T(8,128)(2,1)S(1)}, bf16[2,3,64,256]{3,2,1,0:T(8,128)(2,1)S(1)}, u32[]{:S(2)}, u32[]{:S(2)}) %collective-permute-start.18) | collective-permute-done | bytes 196640 | tf_op jit(solution)/shard_map/ppermute | solution.py:354
  96.5 9.5 %collective-permute-done.19.refs_2_ = bf16[2,3,64,256]{3,2,1,0:T(8,128)(2,1)S(1)} collective-permute-done((bf16[2,3,64,256]{3,2,1,0:T(8,128)(2,1)S(1)}, bf16[2,3,64,256]{3,2,1,0:T(8,128)(2,1)S(1)}, u32[]{:S(2)}, u32[]{:S(2)}) %collective-permute-start.19) | collective-permute-done | bytes 196640 | tf_op jit(solution)/shard_map/ppermute | solution.py:354
  107.0 17.5 %all_to_all.15.mix_ref = bf16[8,128,256]{2,1,0:T(8,128)(2,1)S(1)} all-to-all(bf16[8,128,256]{2,1,0:T(8,128)(2,1)S(1)} %shard_map.83), channel_id=1, replica_groups=mesh['w'=2,'xl'=2,'y'=4,'c'=2,'z'=8] {'z'}, dimensions={0} | all-to-all | bytes 1048576 | tf_op jit(solution)/shard_map/all_to_all | solution.py:403
  124.5 6.1 %copy-done = bf16[128,2,128,256]{3,2,1,0:T(8,128)(2,1)S(1)} copy-done((bf16[128,2,128,256]{3,2,1,0:T(8,128)(2,1)S(1)}, bf16[128,2,128,256]{3,2,1,0:T(8,128)(2,1)}, u32[]{:S(2)}) %copy-start) | copy-done | bytes 16777240
  130.6 4.3 %shard_map.87 = (bf16[128,2048]{1,0:T(8,128)(2,1)S(1)}, bf16[16,32,2048]{2,1,0:T(8,128)(2,1)S(1)}) custom-call(bf16[8,128,256]{2,1,0:T(8,128)(2,1)S(1)} %all_to_all.15.mix_ref, bf16[8,2,2,4,2,128,256]{6,5,4,3,2,1,0:T(8,128)(2,1)S(1)} %bitcast.14, bf16[128,2048]{1,0:T(8,128)(2,1)S(1)} %get-tuple-element.45.rows_ref, f32[1,2048]{1,0:T(1,128)S(1)} %bitcast.19), custom_call_target="tpu_custom_call" | custom-call | flops 1073741824 | bytes 12582912 | tf_op jit(solution)/shard_map/pallas_call | solution.py:245
  136.2 9.5 %all-to-all-start.1 = ((bf16[16,32,2048]{2,1,0:T(8,128)(2,1)}), bf16[16,32,2048]{2,1,0:T(8,128)(2,1)S(1)}, u32[]{:S(2)}, u32[]{:S(2)}) async-start(bf16[16,32,2048]{2,1,0:T(8,128)(2,1)} %copy-done.3), calls=%async_computation.1 | async-start | bytes 4194304 | tf_op jit(solution)/shard_map/all_to_all | solution.py:406
  146.4 24.7 %all-gather.7.cloned.1.call-done = bf16[48,256,256]{2,1,0:T(8,128)(2,1)} async-done(((bf16[6,256,256]{2,1,0:T(8,128)(2,1)}), bf16[48,256,256]{2,1,0:T(8,128)(2,1)}) %all-gather.7.cloned.1.call-update) | async-done | bytes 6291472 | tf_op jit(solution)/shard_map/all_gather | solution.py:402
  171.0 12.3 %all-to-all-done.1 = bf16[16,32,2048]{2,1,0:T(8,128)(2,1)S(1)} async-done(((bf16[16,32,2048]{2,1,0:T(8,128)(2,1)}), bf16[16,32,2048]{2,1,0:T(8,128)(2,1)S(1)}, u32[]{:S(2)}, u32[]{:S(2)}) %all-to-all-start.1) | async-done | bytes 2097184 | tf_op jit(solution)/shard_map/all_to_all | solution.py:406
  183.4 2.8 %copy-done.7 = bf16[48,256,256]{2,1,0:T(8,128)(2,1)S(1)} copy-done((bf16[48,256,256]{2,1,0:T(8,128)(2,1)S(1)}, bf16[48,256,256]{2,1,0:T(8,128)(2,1)}, u32[]{:S(2)}) %copy-start.7) | copy-done | bytes 6291480
  186.2 6.0 %shard_map.88 = bf16[16,32,512]{2,1,0:T(8,128)(2,1)S(1)} custom-call(s32[1]{0:T(128)} %dynamic_slice.9.start_ref, bf16[512,2048]{1,0:T(8,128)(2,1)S(1)} %bitcast.17, bf16[8,6,256,256]{3,2,1,0:T(8,128)(2,1)S(1)} %bitcast.20), custom_call_target="tpu_custom_call" | custom-call | flops 3221225472 | bytes 9437184 | tf_op jit(solution)/shard_map/pallas_call | solution.py:297
  192.2 14.9 %all_to_all.16.mix_ref = bf16[16,32,512]{2,1,0:T(8,128)(2,1)S(1)} all-to-all(bf16[16,32,512]{2,1,0:T(8,128)(2,1)S(1)} %shard_map.88), channel_id=1, replica_groups=mesh['w'=2,'xl'=2,'y'=4,'c'=2,'z'=8] {'xl','y','c'}, dimensions={0} | all-to-all | bytes 1048576 | tf_op jit(solution)/shard_map/all_to_all | solution.py:409
  207.1 5.8 %copy-done.1 = bf16[128,2,128,256]{3,2,1,0:T(8,128)(2,1)S(1)} copy-done((bf16[128,2,128,256]{3,2,1,0:T(8,128)(2,1)S(1)}, bf16[128,2,128,256]{3,2,1,0:T(8,128)(2,1)}, u32[]{:S(2)}) %copy-start.1) | copy-done | bytes 16777240
  212.9 2.2 shard_map.89
  (52 shorter events, 22.0 us)
Async XLA Ops:
  6.5 117.9 %all-gather.5.cloned.1.call-start = ((), (), s32[]{:S(2)}) async-start(), calls=%async_computation.3 | async-start | bytes 17301504 | tf_op jit(solution)/shard_map/all_gather | solution.py:389
  7.4 18.1 %collective-permute-start = (bf16[2,128,256]{2,1,0:T(8,128)(2,1)S(1)}, bf16[2,128,256]{2,1,0:T(8,128)(2,1)S(1)}, u32[]{:S(2)}, u32[]{:S(2)}) collective-permute-start(bf16[2,128,256]{2,1,0:T(8,128)(2,1)S(1)} %pad_maximum_fusion), channel_id=1, source_target_pairs={{0,0},{1,1},{2,2},{3,3},{4,12},{5,13},{6,14},{7,15},{8,4},{9,5},{1... | collective-permute-start | bytes 393224 | tf_op jit(solution)/shard_map/ppermute | solution.py:386
  17.7 8.0 %collective-permute-start.1 = (bf16[2,128,256]{2,1,0:T(8,128)(2,1)S(1)}, bf16[2,128,256]{2,1,0:T(8,128)(2,1)S(1)}, u32[]{:S(2)}, u32[]{:S(2)}) collective-permute-start(bf16[2,128,256]{2,1,0:T(8,128)(2,1)S(1)} %pad_maximum_fusion), channel_id=1, source_target_pairs={{0,1},{1,2},{2,3},{3,4},{4,13},{5,14},{6,15},{7,8},{8,5},{9,6},{10... | collective-permute-start | bytes 393224 | tf_op jit(solution)/shard_map/ppermute | solution.py:386
  17.8 8.8 %collective-permute-start.2 = (bf16[2,128,256]{2,1,0:T(8,128)(2,1)S(1)}, bf16[2,128,256]{2,1,0:T(8,128)(2,1)S(1)}, u32[]{:S(2)}, u32[]{:S(2)}) collective-permute-start(bf16[2,128,256]{2,1,0:T(8,128)(2,1)S(1)} %pad_maximum_fusion), channel_id=1, source_target_pairs={{0,2},{1,3},{2,4},{3,5},{4,14},{5,15},{6,8},{7,9},{8,6},{9,7},{10,... | collective-permute-start | bytes 393224 | tf_op jit(solution)/shard_map/ppermute | solution.py:386
  18.5 11.1 %collective-permute-start.3 = (bf16[2,128,256]{2,1,0:T(8,128)(2,1)S(1)}, bf16[2,128,256]{2,1,0:T(8,128)(2,1)S(1)}, u32[]{:S(2)}, u32[]{:S(2)}) collective-permute-start(bf16[2,128,256]{2,1,0:T(8,128)(2,1)S(1)} %pad_maximum_fusion), channel_id=1, source_target_pairs={{0,3},{1,4},{2,5},{3,6},{4,15},{5,8},{6,9},{7,10},{8,7},{9,0},{10,... | collective-permute-start | bytes 393224 | tf_op jit(solution)/shard_map/ppermute | solution.py:386
  21.2 1.9 copy-start.2
  30.4 140.6 %all-gather.7.cloned.1.call-start = ((), (), s32[]{:S(2)}) async-start(), calls=%async_computation.4 | async-start | bytes 7077888 | tf_op jit(solution)/shard_map/all_gather | solution.py:402
  30.5 59.0 %copy-start.8 = (bf16[2048,3,256]{2,0,1:T(8,128)(2,1)S(1)}, bf16[2048,3,256]{2,0,1:T(8,128)(2,1)}, u32[]{:S(2)}) copy-start(bf16[2048,3,256]{2,0,1:T(8,128)(2,1)} %param.10) | copy-start | bytes 9437188
  30.5 8.6 %collective-permute-start.4 = (bf16[80,2048]{1,0:T(8,128)(2,1)S(1)}, bf16[80,2048]{1,0:T(8,128)(2,1)S(1)}, u32[]{:S(2)}, u32[]{:S(2)}) collective-permute-start(bf16[80,2048]{1,0:T(8,128)(2,1)S(1)} %get-tuple-element.29.refs_0_), channel_id=1, source_target_pairs={{0,1},{1,2},{2,3},{3,4},{4,5},{5,6},{6,7},{7,0},{8,9},{9,10},{10,1... | collective-permute-start | bytes 983048 | tf_op jit(solution)/shard_map/ppermute | solution.py:354
  31.3 10.0 %collective-permute-start.7 = (bf16[80,2048]{1,0:T(8,128)(2,1)S(1)}, bf16[80,2048]{1,0:T(8,128)(2,1)S(1)}, u32[]{:S(2)}, u32[]{:S(2)}) collective-permute-start(bf16[80,2048]{1,0:T(8,128)(2,1)S(1)} %get-tuple-element.30.refs_1_), channel_id=1, source_target_pairs={{0,7},{1,0},{2,1},{3,2},{4,3},{5,4},{6,5},{7,6},{8,15},{9,8},{10,9... | collective-permute-start | bytes 983048 | tf_op jit(solution)/shard_map/ppermute | solution.py:354
  33.3 12.9 %collective-permute-start.5 = (bf16[80,2048]{1,0:T(8,128)(2,1)S(1)}, bf16[80,2048]{1,0:T(8,128)(2,1)S(1)}, u32[]{:S(2)}, u32[]{:S(2)}) collective-permute-start(bf16[80,2048]{1,0:T(8,128)(2,1)S(1)} %get-tuple-element.30.refs_1_), channel_id=1, source_target_pairs={{0,1},{1,2},{2,3},{3,4},{4,5},{5,6},{6,7},{7,0},{8,9},{9,10},{10,1... | collective-permute-start | bytes 983048 | tf_op jit(solution)/shard_map/ppermute | solution.py:354
  33.7 14.7 %collective-permute-start.6 = (bf16[80,2048]{1,0:T(8,128)(2,1)S(1)}, bf16[80,2048]{1,0:T(8,128)(2,1)S(1)}, u32[]{:S(2)}, u32[]{:S(2)}) collective-permute-start(bf16[80,2048]{1,0:T(8,128)(2,1)S(1)} %get-tuple-element.29.refs_0_), channel_id=1, source_target_pairs={{0,7},{1,0},{2,1},{3,2},{4,3},{5,4},{6,5},{7,6},{8,15},{9,8},{10,9... | collective-permute-start | bytes 983048 | tf_op jit(solution)/shard_map/ppermute | solution.py:354
  39.1 14.1 %collective-permute-start.8 = (bf16[80,2048]{1,0:T(8,128)(2,1)S(1)}, bf16[80,2048]{1,0:T(8,128)(2,1)S(1)}, u32[]{:S(2)}, u32[]{:S(2)}) collective-permute-start(bf16[80,2048]{1,0:T(8,128)(2,1)S(1)} %collective-permute-done.4.refs_2_), channel_id=1, source_target_pairs={{0,1},{1,2},{2,3},{3,4},{4,5},{5,6},{6,7},{7,0},{8,9},{9,10},{10,1... | collective-permute-start | bytes 983048 | tf_op jit(solution)/shard_map/ppermute | solution.py:354
  41.3 14.1 %collective-permute-start.11 = (bf16[80,2048]{1,0:T(8,128)(2,1)S(1)}, bf16[80,2048]{1,0:T(8,128)(2,1)S(1)}, u32[]{:S(2)}, u32[]{:S(2)}) collective-permute-start(bf16[80,2048]{1,0:T(8,128)(2,1)S(1)} %collective-permute-done.7.refs_5_), channel_id=1, source_target_pairs={{0,7},{1,0},{2,1},{3,2},{4,3},{5,4},{6,5},{7,6},{8,15},{9,8},{10,9... | collective-permute-start | bytes 983048 | tf_op jit(solution)/shard_map/ppermute | solution.py:354
  46.1 14.0 %collective-permute-start.9 = (bf16[80,2048]{1,0:T(8,128)(2,1)S(1)}, bf16[80,2048]{1,0:T(8,128)(2,1)S(1)}, u32[]{:S(2)}, u32[]{:S(2)}) collective-permute-start(bf16[80,2048]{1,0:T(8,128)(2,1)S(1)} %collective-permute-done.5.refs_3_), channel_id=1, source_target_pairs={{0,1},{1,2},{2,3},{3,4},{4,5},{5,6},{6,7},{7,0},{8,9},{9,10},{10,1... | collective-permute-start | bytes 983048 | tf_op jit(solution)/shard_map/ppermute | solution.py:354
  48.4 14.0 %collective-permute-start.10 = (bf16[80,2048]{1,0:T(8,128)(2,1)S(1)}, bf16[80,2048]{1,0:T(8,128)(2,1)S(1)}, u32[]{:S(2)}, u32[]{:S(2)}) collective-permute-start(bf16[80,2048]{1,0:T(8,128)(2,1)S(1)} %collective-permute-done.6.refs_4_), channel_id=1, source_target_pairs={{0,7},{1,0},{2,1},{3,2},{4,3},{5,4},{6,5},{7,6},{8,15},{9,8},{10,9... | collective-permute-start | bytes 983048 | tf_op jit(solution)/shard_map/ppermute | solution.py:354
  53.3 13.9 %collective-permute-start.12 = (bf16[80,2048]{1,0:T(8,128)(2,1)S(1)}, bf16[80,2048]{1,0:T(8,128)(2,1)S(1)}, u32[]{:S(2)}, u32[]{:S(2)}) collective-permute-start(bf16[80,2048]{1,0:T(8,128)(2,1)S(1)} %collective-permute-done.8.refs_6_), channel_id=1, source_target_pairs={{0,1},{1,2},{2,3},{3,4},{4,5},{5,6},{6,7},{7,0},{8,9},{9,10},{10,1... | collective-permute-start | bytes 983048 | tf_op jit(solution)/shard_map/ppermute | solution.py:354
  55.4 14.0 %collective-permute-start.15 = (bf16[80,2048]{1,0:T(8,128)(2,1)S(1)}, bf16[80,2048]{1,0:T(8,128)(2,1)S(1)}, u32[]{:S(2)}, u32[]{:S(2)}) collective-permute-start(bf16[80,2048]{1,0:T(8,128)(2,1)S(1)} %collective-permute-done.11.refs_9_), channel_id=1, source_target_pairs={{0,7},{1,0},{2,1},{3,2},{4,3},{5,4},{6,5},{7,6},{8,15},{9,8},{10,9... | collective-permute-start | bytes 983048 | tf_op jit(solution)/shard_map/ppermute | solution.py:354
  60.2 14.1 %collective-permute-start.13 = (bf16[80,2048]{1,0:T(8,128)(2,1)S(1)}, bf16[80,2048]{1,0:T(8,128)(2,1)S(1)}, u32[]{:S(2)}, u32[]{:S(2)}) collective-permute-start(bf16[80,2048]{1,0:T(8,128)(2,1)S(1)} %collective-permute-done.9.refs_7_), channel_id=1, source_target_pairs={{0,1},{1,2},{2,3},{3,4},{4,5},{5,6},{6,7},{7,0},{8,9},{9,10},{10,1... | collective-permute-start | bytes 983048 | tf_op jit(solution)/shard_map/ppermute | solution.py:354
  62.4 14.1 %collective-permute-start.14 = (bf16[80,2048]{1,0:T(8,128)(2,1)S(1)}, bf16[80,2048]{1,0:T(8,128)(2,1)S(1)}, u32[]{:S(2)}, u32[]{:S(2)}) collective-permute-start(bf16[80,2048]{1,0:T(8,128)(2,1)S(1)} %collective-permute-done.10.refs_8_), channel_id=1, source_target_pairs={{0,7},{1,0},{2,1},{3,2},{4,3},{5,4},{6,5},{7,6},{8,15},{9,8},{10,9... | collective-permute-start | bytes 983048 | tf_op jit(solution)/shard_map/ppermute | solution.py:354
  67.2 14.1 %collective-permute-start.16 = (bf16[80,2048]{1,0:T(8,128)(2,1)S(1)}, bf16[80,2048]{1,0:T(8,128)(2,1)S(1)}, u32[]{:S(2)}, u32[]{:S(2)}) collective-permute-start(bf16[80,2048]{1,0:T(8,128)(2,1)S(1)} %collective-permute-done.12.refs_10_), channel_id=1, source_target_pairs={{0,1},{1,2},{2,3},{3,4},{4,5},{5,6},{6,7},{7,0},{8,9},{9,10},{10,1... | collective-permute-start | bytes 983048 | tf_op jit(solution)/shard_map/ppermute | solution.py:354
  69.4 14.1 %collective-permute-start.17 = (bf16[80,2048]{1,0:T(8,128)(2,1)S(1)}, bf16[80,2048]{1,0:T(8,128)(2,1)S(1)}, u32[]{:S(2)}, u32[]{:S(2)}) collective-permute-start(bf16[80,2048]{1,0:T(8,128)(2,1)S(1)} %collective-permute-done.15.refs_13_), channel_id=1, source_target_pairs={{0,7},{1,0},{2,1},{3,2},{4,3},{5,4},{6,5},{7,6},{8,15},{9,8},{10,9... | collective-permute-start | bytes 983048 | tf_op jit(solution)/shard_map/ppermute | solution.py:354
  84.4 12.1 %collective-permute-start.18 = (bf16[2,3,64,256]{3,2,1,0:T(8,128)(2,1)S(1)}, bf16[2,3,64,256]{3,2,1,0:T(8,128)(2,1)S(1)}, u32[]{:S(2)}, u32[]{:S(2)}) collective-permute-start(bf16[2,3,64,256]{3,2,1,0:T(8,128)(2,1)S(1)} %get-tuple-element.32), channel_id=1, source_target_pairs={{0,16},{16,32},{32,48},{48,0},{1,17},{17,33},{33,49},{49,1},{2,18}... | collective-permute-start | bytes 589832 | tf_op jit(solution)/shard_map/ppermute | solution.py:354
  85.8 20.2 %collective-permute-start.19 = (bf16[2,3,64,256]{3,2,1,0:T(8,128)(2,1)S(1)}, bf16[2,3,64,256]{3,2,1,0:T(8,128)(2,1)S(1)}, u32[]{:S(2)}, u32[]{:S(2)}) collective-permute-start(bf16[2,3,64,256]{3,2,1,0:T(8,128)(2,1)S(1)} %get-tuple-element.33), channel_id=1, source_target_pairs={{0,32},{16,48},{32,0},{48,16},{1,33},{17,49},{33,1},{49,17},{2,34}... | collective-permute-start | bytes 589832 | tf_op jit(solution)/shard_map/ppermute | solution.py:354
  88.4 17.6 %collective-permute-start.20 = (bf16[2,3,64,256]{3,2,1,0:T(8,128)(2,1)S(1)}, bf16[2,3,64,256]{3,2,1,0:T(8,128)(2,1)S(1)}, u32[]{:S(2)}, u32[]{:S(2)}) collective-permute-start(bf16[2,3,64,256]{3,2,1,0:T(8,128)(2,1)S(1)} %get-tuple-element.34), channel_id=1, source_target_pairs={{0,48},{16,0},{32,16},{48,32},{1,49},{17,1},{33,17},{49,33},{2,50}... | collective-permute-start | bytes 589832 | tf_op jit(solution)/shard_map/ppermute | solution.py:354
  93.9 30.5 %copy-start.6 = (f32[2048]{0:T(1024)S(1)}, f32[2048]{0:T(1024)}, u32[]{:S(2)}) copy-start(f32[2048]{0:T(1024)} %param.12) | copy-start | bytes 24580
  124.5 6.1 %copy-start = (bf16[128,2,128,256]{3,2,1,0:T(8,128)(2,1)S(1)}, bf16[128,2,128,256]{3,2,1,0:T(8,128)(2,1)}, u32[]{:S(2)}) copy-start(bf16[128,2,128,256]{3,2,1,0:T(8,128)(2,1)} %all-gather.5.cloned.1.call-done) | copy-start | bytes 50331652
  134.8 1.4 copy-start.3
  136.2 9.5 %copy-start.9 = (s32[2]{0:T(128)S(1)}, s32[2]{0:T(128)}, u32[]{:S(2)}) copy-start(s32[2]{0:T(128)} %param.15) | copy-start | bytes 28
  136.2 47.1 %all-to-all-start.1 = ((bf16[16,32,2048]{2,1,0:T(8,128)(2,1)}), bf16[16,32,2048]{2,1,0:T(8,128)(2,1)S(1)}, u32[]{:S(2)}, u32[]{:S(2)}) async-start(bf16[16,32,2048]{2,1,0:T(8,128)(2,1)} %copy-done.3), calls=%async_computation.1 | async-start | bytes 4194304 | tf_op jit(solution)/shard_map/all_to_all | solution.py:406
  183.4 2.8 %copy-start.7 = (bf16[48,256,256]{2,1,0:T(8,128)(2,1)S(1)}, bf16[48,256,256]{2,1,0:T(8,128)(2,1)}, u32[]{:S(2)}) copy-start(bf16[48,256,256]{2,1,0:T(8,128)(2,1)} %all-gather.7.cloned.1.call-done) | copy-start | bytes 18874372
  207.1 5.8 %copy-start.1 = (bf16[128,2,128,256]{3,2,1,0:T(8,128)(2,1)S(1)}, bf16[128,2,128,256]{3,2,1,0:T(8,128)(2,1)}, u32[]{:S(2)}) copy-start(bf16[128,2,128,256]{3,2,1,0:T(8,128)(2,1)} %all-gather.5.cloned.1.call-done) | copy-start | bytes 50331652
  (2 other events, 1.7 us)
Sparse Core Ops, SparseCore 0:
  30.6 86.0 all-gather.4
  118.5 52.5 all-gather.6

commit v7 on v6

--- a/solution.py
+++ b/solution.py
@@ -207,7 +207,7 @@
 def join_blocks(z, parts):
     return pl.pallas_call(
         join_blocks_kernel,
-        out_shape=jax.ShapeDtypeStruct((4, 2, 128, 256), BF),
+        out_shape=jax.ShapeDtypeStruct((4, 128, 256), BF),
         in_specs=[smem()] + [vmem()] * 4,
         out_specs=vmem(),
         compiler_params=params(),
@@ -215,17 +215,10 @@
     )(z, *parts)
 
 
-def middle_kernel(mix_ref, weight_ref, rows_ref, gain_ref, middle_ref, send_ref, weight, total, sems):
-    copies = [
-        pltpu.make_async_copy(weight_ref.at[block, :, :, :, 0], weight.at[block], sems.at[block])
-        for block in range(8)
-    ]
-    for copy in copies:
-        copy.start()
+def middle_kernel(mix_ref, weight_ref, rows_ref, gain_ref, middle_ref, send_ref, total):
     mix = jnp.concatenate([mix_ref[k] for k in range(NZ)], axis=1)
     for block in range(8):
-        copies[block].wait()
-        part = column_block(lambda *at: weight[(block, *at)])
+        part = column_block(lambda *at: weight_ref[(block, *at)])
         total[:, 256 * block : 256 * block + 256] = dot(mix, part)
     middle = (total[...] + rows_ref[...].astype(F32)).astype(BF)
     middle_ref[...] = middle
@@ -248,13 +241,9 @@
             jax.ShapeDtypeStruct((128, width), BF),
             jax.ShapeDtypeStruct((16, 32, width), BF),
         ),
-        in_specs=[vmem(), pl.BlockSpec(memory_space=pl.ANY), vmem(), vmem()],
+        in_specs=[vmem()] * 4,
         out_specs=(vmem(), vmem()),
-        scratch_shapes=[
-            pltpu.VMEM((8, 2, 2, 4, E, 256), BF),
-            pltpu.VMEM((128, width), F32),
-            pltpu.SemaphoreType.DMA((8,)),
-        ],
+        scratch_shapes=[pltpu.VMEM((128, width), F32)],
         compiler_params=params(),
         cost_estimate=pl.CostEstimate(
             flops=2 * 128 * 2048 * 2048, bytes_accessed=12 << 20, transcendentals=0
@@ -288,15 +277,17 @@
                     )
                 )
             for head, mixed in enumerate(attend(chains)):
-                at = 256 * pair + head * E
-                out_ref[low // 32 : high // 32, :, at : at + E] = mixed.reshape(size // 32, 32, E)
+                for spot in range(low // 32, high // 32):
+                    rows = mixed[32 * spot - low : 32 * spot - low + 32]
+                    at = (spot // 2 * 2 + head, spot % 2, slice(None), slice(E * pair, E * pair + E))
+                    out_ref[at] = rows
 
 
 def temporal_attend(start, rows, weight):
     count, width = rows.shape
     return pl.pallas_call(
         temporal_kernel,
-        out_shape=jax.ShapeDtypeStruct((16, 32, 512), BF),
+        out_shape=jax.ShapeDtypeStruct((16, 2, 32, 256), BF),
         in_specs=[smem(), vmem(), vmem()],
         out_specs=vmem(),
         scratch_shapes=[
@@ -310,19 +301,54 @@
     )(start, rows, weight)
 
 
-def last_kernel(mix_ref, weight_ref, middle_ref, out_ref, total):
-    mix = jnp.concatenate(
-        [
-            jnp.concatenate([mix_ref[xl * 8 + y * 2 + c] for xl in range(2) for c in range(2)], axis=0)
-            for y in range(4)
-        ],
-        axis=1,
-    )
-    for block in range(8):
-        part = column_block(lambda *at: weight_ref[(block, *at, 1)])
-        total[:, 256 * block : 256 * block + 256] = dot(mix, part)
+def last_kernel(place_ref, mix_ref, *refs):
+    pieces, (keep_ref, give_ref, total) = refs[: NZ + 1], refs[NZ + 1 :]
+    z, c = place_ref[0], place_ref[1]
+    blocks = []
+    for k in range(NZ):
+        source = lax.rem(z + (OFFSETS[k] + NZ), NZ)
+        cols = pl.ds(pl.multiple_of(lax.rem(source, 2) * E, E), E)
+        blocks.append(
+            jnp.concatenate(
+                [
+                    mix_ref[xl * 8 + source // 2 * 2 + core, frames, :, cols]
+                    for frames in range(2)
+                    for xl in range(2)
+                    for core in range(2)
+                ],
+                axis=0,
+            )
+        )
+    mix = jnp.concatenate(blocks, axis=1)
+    for low in range(0, 2048, 512):
+        part = jnp.concatenate([piece[:, low : low + 512] for piece in pieces], axis=0)
+        total[:, :, low : low + 512] = dot(mix, part).reshape(2, 128, 512)
+    keep_ref[...] = total[c]
+    give_ref[...] = total[1 - c].astype(BF)
+
+
+def last_sums(place, mix, pieces):
+    width = pieces[0].shape[1]
+    return pl.pallas_call(
+        last_kernel,
+        out_shape=(
+            jax.ShapeDtypeStruct((128, width), F32),
+            jax.ShapeDtypeStruct((128, width), BF),
+        ),
+        in_specs=[smem()] + [vmem()] * (NZ + 2),
+        out_specs=(vmem(), vmem()),
+        scratch_shapes=[pltpu.VMEM((2, 128, width), F32)],
+        compiler_params=params(),
+        cost_estimate=pl.CostEstimate(
+            flops=2 * 128 * 2048 * 2048, bytes_accessed=8 << 20, transcendentals=0
+        ),
+    )(place, mix, *pieces)
+
+
+def end_kernel(keep_ref, got_ref, middle_ref, out_ref):
     for group in range(4):
-        rows = total[32 * group : 32 * group + 32].reshape(4, 8, -1)
+        at = slice(32 * group, 32 * group + 32)
+        rows = (keep_ref[at] + got_ref[at].astype(F32)).reshape(4, 8, -1)
         middle = jnp.stack(
             [
                 middle_ref[32 * f : 32 * f + 32].astype(F32)[8 * group : 8 * group + 8]
@@ -334,19 +360,15 @@
         out_ref[8 * group : 8 * group + 8] = out
 
 
-def last_rows(mix, weight, middle):
-    width = middle.shape[1]
-    return pl.pallas_call(
-        last_kernel,
-        out_shape=jax.ShapeDtypeStruct((32, 4, width), BF),
+def end_rows(keep, got, middle):
+    return pl.pallas_call(
+        end_kernel,
+        out_shape=jax.ShapeDtypeStruct((32, 4, middle.shape[1]), BF),
         in_specs=[vmem()] * 3,
         out_specs=vmem(),
-        scratch_shapes=[pltpu.VMEM((128, width), F32)],
-        compiler_params=params(),
-        cost_estimate=pl.CostEstimate(
-            flops=2 * 128 * 2048 * 2048, bytes_accessed=12 << 20, transcendentals=0
-        ),
-    )(mix, weight, middle)
+        compiler_params=params(),
+        cost_estimate=pl.CostEstimate(flops=1 << 20, bytes_accessed=3 << 20, transcendentals=0),
+    )(keep, got, middle)
 
 
 def shifted(value, axis, step):
@@ -375,9 +397,7 @@
     )
 
     low = (lax.rem(y, 2) * E, ((w * 2 + xl) * 2 + y // 2) * 256)
-    block = jnp.stack(
-        [lax.dynamic_slice(weight, low, (E, 256)) for weight in (spatial_out, temporal_out)]
-    )
+    block = lax.dynamic_slice(spatial_out, low, (E, 256))
     parts = []
     for k in range(4):
         pairs = [
@@ -385,9 +405,9 @@
         ]
         parts.append(lax.ppermute(block, ("c", "z"), pairs))
     first, second, parts = lax.optimization_barrier((first, second, parts))
-    outs = join_blocks(z.reshape(1), parts)
-    outs = lax.all_gather(outs, ("w", "xl", "y", "c"), axis=0, tiled=False)
-    outs = outs.reshape(8, 2, 2, 4, 2, E, 256)
+    whole_out = join_blocks(z.reshape(1), parts)
+    whole_out = lax.all_gather(whole_out, ("w", "xl", "y", "c"), axis=0, tiled=False)
+    whole_out = whole_out.reshape(8, 2, 2, 4, E, 256)
 
     pieces = gathered_rows((first, second))
 
@@ -398,16 +418,28 @@
     mix = spatial_attend(z.reshape(1), weight, pieces)
     mix, *got = lax.optimization_barrier((mix, *got))
     quarter = join_shares(y.reshape(1), got)
-    mix, quarter = lax.optimization_barrier((mix, quarter))
+    mix, quarter, whole_out = lax.optimization_barrier((mix, quarter, whole_out))
     quarter = lax.all_gather(quarter[None], ("w", "xl", "c"), axis=0, tiled=True)
     mix = lax.all_to_all(mix, "z", 0, 0, tiled=True)
 
-    middle, send = middle_rows(mix, outs, rows, temporal_gain.reshape(1, width))
+    middle, send = middle_rows(mix, whole_out, rows, temporal_gain.reshape(1, width))
+
+    half = lax.dynamic_slice(temporal_out, (c * E, 0), (E, width))
+    send, half = lax.optimization_barrier((send, half))
+    up, down = half, half
+    halves = [half]
+    for step in (1, 2, 3):
+        up, down = shifted(up, "z", 1), shifted(down, "z", -1)
+        halves += [up, down]
+    halves += [shifted(up[:64], "z", 1), shifted(down[64:], "z", -1)]
+
     window = lax.all_to_all(send, ("xl", "y", "c"), 0, 0, tiled=True)
+    window, *halves[1:5] = lax.optimization_barrier((window, *halves[1:5]))
     start = lax.dynamic_slice(starts, (w,), (1,))
     mix = temporal_attend(start, window.reshape(512, width), quarter)
     mix = lax.all_to_all(mix, ("xl", "y", "c"), 0, 0, tiled=True)
-    return last_rows(mix, outs, middle)
+    keep, give = last_sums(jnp.stack([z, c]).astype(jnp.int32), mix, halves)
+    return end_rows(keep, shifted(give, "c", 1), middle)
 
 
 def solution(mesh):

time: 222 us -> 206 us (0.928)
  blocking collectives: 32.4 us -> 0 us
  starting transfers between devices: 47.1 us -> 70 us
  waiting for transfers between devices: 87.4 us -> 81.5 us
    all_to_all x2 -> x0, blocking collectives: 32.4 us -> none  [the longest x1 17.5 us: local(): mix = lax.all_to_all(mix, 'z', 0, 0, tiled=True)]
    all_gather x1, waiting for transfers between devices: 24.7 us -> 0.01 us  [local(): lax.all_gather(quarter[None], ('w', 'xl', 'c'), axis=0, tiled=True)]
    ppermute x17 -> x26, waiting for transfers between devices: 46.3 us -> 65.8 us  [shifted(): lax.ppermute(value, axis, [(i, (i + step) % count) for i in range(count)])]
    all_to_all x0 -> x2, waiting for transfers between devices: none -> 15.6 us  [the longest x1 15.6 us: local(): mix = lax.all_to_all(mix, 'z', 0, 0, tiled=True)]
    ppermute x17 -> x26, starting transfers between devices: 23.7 us -> 36.9 us  [shifted(): lax.ppermute(value, axis, [(i, (i + step) % count) for i in range(count)])]
    all_to_all x1, waiting for transfers between devices: 12.3 us -> 0.01 us  [local(): window = lax.all_to_all(send, ('xl', 'y', 'c'), 0, 0, tiled=True)]
    all_to_all x0 -> x2, starting transfers between devices: none -> 12.1 us  [the longest x1 7.78 us: local(): mix = lax.all_to_all(mix, ('xl', 'y', 'c'), 0, 0, tiled=True)]
    ppermute x4, waiting for transfers between devices: 4.04 us -> 0.01 us  [local(): parts.append(lax.ppermute(block, ('c', 'z'), pairs))]
  transfers between devices with their start and end apart: 24 -> 35, of which waited for: 18 -> 15; matrix products, arithmetic and copies ran while one was open for 0% -> 0% of each run, Pallas kernels for 5% -> 8%
where the time goes in v7:
time: 206 us
  waiting for transfers between devices  81.5 us (40%)
  starting transfers between devices  70 us (34%)
  Pallas kernels  21.4 us (10%)
  local copies, waits for them, and re-layouts  19 us (9%)
  between operations  13.6 us (7%)
    ppermute x26, waiting for transfers between devices, shifted(): lax.ppermute(value, axis, [(i, (i + step) % count) for i in range(count)])  65.8 us
    ppermute x26, starting transfers between devices, shifted(): lax.ppermute(value, axis, [(i, (i + step) % count) for i in range(count)])  36.9 us
    unnamed x38, local copies, waits for them, and re-layouts  17.4 us
    all_to_all x1, waiting for transfers between devices, local(): mix = lax.all_to_all(mix, 'z', 0, 0, tiled=True)  15.6 us
    ppermute x4, starting transfers between devices, local(): parts.append(lax.ppermute(block, ('c', 'z'), pairs))  13.8 us
    all_to_all x1, starting transfers between devices, local(): mix = lax.all_to_all(mix, ('xl', 'y', 'c'), 0, 0, tiled=True)  7.78 us
    pallas_call x1, Pallas kernels, temporal_attend(): pl.pallas_call(temporal_kernel, out_shape=jax.ShapeDtypeStruct((16, 2, 32...  7.6 us
    all_to_all x1, starting transfers between devices, local(): window = lax.all_to_all(send, ('xl', 'y', 'c'), 0, 0, tiled=True)  7.14 us
  transfers between devices with their start and end apart: 35, of which 15 were waited for; matrix products, arithmetic and copies ran while one was open for 0% of the time, Pallas kernels for 8%

profile of v7, /device:TPU:1, one launch (start us, length us, event | category | flops | bytes accessed | tf_op | source)
XLA Modules:
  0.0 205.7 jit_solution(2119877752043647681)
XLA Ops:
  7.5 10.2 %collective-permute-start = (bf16[128,256]{1,0:T(8,128)(2,1)S(1)}, bf16[128,256]{1,0:T(8,128)(2,1)S(1)}, u32[]{:S(2)}, u32[]{:S(2)}) collective-permute-start(bf16[128,256]{1,0:T(8,128)(2,1)S(1)} %dynamic_slice.10), channel_id=1, source_target_pairs={{0,0},{1,1},{2,2},{3,3},{4,12},{5,13},{6,14},{7,15},{8,4},{9,5},{1... | collective-permute-start | bytes 196616 | tf_op jit(solution)/shard_map/ppermute | solution.py:406
  18.5 2.8 %collective-permute-start.3 = (bf16[128,256]{1,0:T(8,128)(2,1)S(1)}, bf16[128,256]{1,0:T(8,128)(2,1)S(1)}, u32[]{:S(2)}, u32[]{:S(2)}) collective-permute-start(bf16[128,256]{1,0:T(8,128)(2,1)S(1)} %dynamic_slice.10), channel_id=1, source_target_pairs={{0,3},{1,4},{2,5},{3,6},{4,15},{5,8},{6,9},{7,10},{8,7},{9,0},{10,... | collective-permute-start | bytes 196616 | tf_op jit(solution)/shard_map/ppermute | solution.py:406
  21.3 1.9 copy-done.2
  26.4 3.6 %collective-permute-start.4 = (bf16[80,2048]{1,0:T(8,128)(2,1)S(1)}, bf16[80,2048]{1,0:T(8,128)(2,1)S(1)}, u32[]{:S(2)}, u32[]{:S(2)}) collective-permute-start(bf16[80,2048]{1,0:T(8,128)(2,1)S(1)} %get-tuple-element.39.refs_0_), channel_id=1, source_target_pairs={{0,1},{1,2},{2,3},{3,4},{4,5},{5,6},{6,7},{7,0},{8,9},{9,10},{10,1... | collective-permute-start | bytes 983048 | tf_op jit(solution)/shard_map/ppermute | solution.py:376
  32.7 5.1 %collective-permute-done.4.refs_2_ = bf16[80,2048]{1,0:T(8,128)(2,1)S(1)} collective-permute-done((bf16[80,2048]{1,0:T(8,128)(2,1)S(1)}, bf16[80,2048]{1,0:T(8,128)(2,1)S(1)}, u32[]{:S(2)}, u32[]{:S(2)}) %collective-permute-start.4) | collective-permute-done | bytes 327712 | tf_op jit(solution)/shard_map/ppermute | solution.py:376
  37.8 1.5 collective-permute-start.8
  40.5 4.3 %collective-permute-done.5.refs_3_ = bf16[80,2048]{1,0:T(8,128)(2,1)S(1)} collective-permute-done((bf16[80,2048]{1,0:T(8,128)(2,1)S(1)}, bf16[80,2048]{1,0:T(8,128)(2,1)S(1)}, u32[]{:S(2)}, u32[]{:S(2)}) %collective-permute-start.5) | collective-permute-done | bytes 327712 | tf_op jit(solution)/shard_map/ppermute | solution.py:376
  44.8 1.6 collective-permute-start.9
  47.5 4.3 %collective-permute-done.8.refs_6_ = bf16[80,2048]{1,0:T(8,128)(2,1)S(1)} collective-permute-done((bf16[80,2048]{1,0:T(8,128)(2,1)S(1)}, bf16[80,2048]{1,0:T(8,128)(2,1)S(1)}, u32[]{:S(2)}, u32[]{:S(2)}) %collective-permute-start.8) | collective-permute-done | bytes 327712 | tf_op jit(solution)/shard_map/ppermute | solution.py:376
  54.5 4.3 %collective-permute-done.9.refs_7_ = bf16[80,2048]{1,0:T(8,128)(2,1)S(1)} collective-permute-done((bf16[80,2048]{1,0:T(8,128)(2,1)S(1)}, bf16[80,2048]{1,0:T(8,128)(2,1)S(1)}, u32[]{:S(2)}, u32[]{:S(2)}) %collective-permute-start.9) | collective-permute-done | bytes 327712 | tf_op jit(solution)/shard_map/ppermute | solution.py:376
  61.6 4.3 %collective-permute-done.12.refs_10_ = bf16[80,2048]{1,0:T(8,128)(2,1)S(1)} collective-permute-done((bf16[80,2048]{1,0:T(8,128)(2,1)S(1)}, bf16[80,2048]{1,0:T(8,128)(2,1)S(1)}, u32[]{:S(2)}, u32[]{:S(2)}) %collective-permute-start.12) | collective-permute-done | bytes 327712 | tf_op jit(solution)/shard_map/ppermute | solution.py:376
  68.7 4.3 %collective-permute-done.13.refs_11_ = bf16[80,2048]{1,0:T(8,128)(2,1)S(1)} collective-permute-done((bf16[80,2048]{1,0:T(8,128)(2,1)S(1)}, bf16[80,2048]{1,0:T(8,128)(2,1)S(1)}, u32[]{:S(2)}, u32[]{:S(2)}) %collective-permute-start.13) | collective-permute-done | bytes 327712 | tf_op jit(solution)/shard_map/ppermute | solution.py:376
  74.2 5.8 %collective-permute-done.16.refs_14_ = bf16[80,2048]{1,0:T(8,128)(2,1)S(1)} collective-permute-done((bf16[80,2048]{1,0:T(8,128)(2,1)S(1)}, bf16[80,2048]{1,0:T(8,128)(2,1)S(1)}, u32[]{:S(2)}, u32[]{:S(2)}) %collective-permute-start.16) | collective-permute-done | bytes 327712 | tf_op jit(solution)/shard_map/ppermute | solution.py:376
  83.4 2.6 %collective-permute-start.19 = (bf16[2,3,64,256]{3,2,1,0:T(8,128)(2,1)S(1)}, bf16[2,3,64,256]{3,2,1,0:T(8,128)(2,1)S(1)}, u32[]{:S(2)}, u32[]{:S(2)}) collective-permute-start(bf16[2,3,64,256]{3,2,1,0:T(8,128)(2,1)S(1)} %get-tuple-element.43), channel_id=1, source_target_pairs={{0,32},{16,48},{32,0},{48,16},{1,33},{17,49},{33,1},{49,17},{2,34}... | collective-permute-start | bytes 589832 | tf_op jit(solution)/shard_map/ppermute | solution.py:376
  87.1 5.3 %shard_map.83 = bf16[8,128,256]{2,1,0:T(8,128)(2,1)} custom-call(s32[1]{0:T(128)} %bitcast.place_ref.z_ref, bf16[3,2048,256]{2,1,0:T(8,128)(2,1)S(1)} %bitcast.16, bf16[80,2048]{1,0:T(8,128)(2,1)S(1)} %get-tuple-element.39.refs_0_, bf16[80,2048]{1,0:T(8,128)(2,1)S(1)} %get-tuple-element.40.refs_1_, bf16[80,2048]{1,0:T(8,128)(2,1)S(1)} %collective-permute-done.4.refs_2_, ...), custom_call_target="tpu_custom_call" | custom-call | flops 6442450944 | bytes 8388608 | tf_op jit(solution)/shard_map/pallas_call | solution.py:184
  92.4 1.7 collective-permute-done.19.refs_2_
  95.1 4.4 %all-to-all-start = ((bf16[8,128,256]{2,1,0:T(8,128)(2,1)}), bf16[8,128,256]{2,1,0:T(8,128)(2,1)S(1)}, u32[]{:S(2)}, u32[]{:S(2)}) async-start(bf16[8,128,256]{2,1,0:T(8,128)(2,1)} %shard_map.83), calls=%async_computation | async-start | bytes 1048576 | tf_op jit(solution)/shard_map/all_to_all | solution.py:423
  99.5 15.6 %all-to-all-done.mix_ref = bf16[8,128,256]{2,1,0:T(8,128)(2,1)S(1)} async-done(((bf16[8,128,256]{2,1,0:T(8,128)(2,1)}), bf16[8,128,256]{2,1,0:T(8,128)(2,1)S(1)}, u32[]{:S(2)}, u32[]{:S(2)}) %all-to-all-start) | async-done | bytes 524320 | tf_op jit(solution)/shard_map/all_to_all | solution.py:423
  115.2 3.5 %copy-done.1 = bf16[128,128,256]{2,1,0:T(8,128)(2,1)S(1)} copy-done((bf16[128,128,256]{2,1,0:T(8,128)(2,1)S(1)}, bf16[128,128,256]{2,1,0:T(8,128)(2,1)}, u32[]{:S(2)}) %copy-start.1) | copy-done | bytes 8388632
  122.4 7.1 %all-to-all-start.1 = ((bf16[16,32,2048]{2,1,0:T(8,128)(2,1)}), bf16[16,32,2048]{2,1,0:T(8,128)(2,1)}, u32[]{:S(2)}, u32[]{:S(2)}) async-start(bf16[16,32,2048]{2,1,0:T(8,128)(2,1)} %copy-done.3), calls=%async_computation.1 | async-start | bytes 4194304 | tf_op jit(solution)/shard_map/all_to_all | solution.py:436
  129.8 2.4 %collective-permute-start.22 = (bf16[128,2048]{1,0:T(8,128)(2,1)S(1)}, bf16[128,2048]{1,0:T(8,128)(2,1)S(1)}, u32[]{:S(2)}, u32[]{:S(2)}) collective-permute-start(bf16[128,2048]{1,0:T(8,128)(2,1)S(1)} %constant_dynamic-slice_fusion.refs_0_), channel_id=1, source_target_pairs={{0,7},{1,0},{2,1},{3,2},{4,3},{5,4},{6,5},{7,6},{8,15},{9,8},{10,9... | collective-permute-start | bytes 1572872 | tf_op jit(solution)/shard_map/ppermute | solution.py:376
  132.2 11.8 %collective-permute-done.21.refs_1_ = bf16[128,2048]{1,0:T(8,128)(2,1)S(1)} collective-permute-done((bf16[128,2048]{1,0:T(8,128)(2,1)S(1)}, bf16[128,2048]{1,0:T(8,128)(2,1)S(1)}, u32[]{:S(2)}, u32[]{:S(2)}) %collective-permute-start.21) | collective-permute-done | bytes 524320 | tf_op jit(solution)/shard_map/ppermute | solution.py:376
  144.0 2.7 %collective-permute-start.24 = (bf16[128,2048]{1,0:T(8,128)(2,1)S(1)}, bf16[128,2048]{1,0:T(8,128)(2,1)}, u32[]{:S(2)}, u32[]{:S(2)}) collective-permute-start(bf16[128,2048]{1,0:T(8,128)(2,1)S(1)} %collective-permute-done.22.refs_2_), channel_id=1, source_target_pairs={{0,7},{1,0},{2,1},{3,2},{4,3},{5,4},{6,5},{7,6},{8,15},{9,8},{10,9... | collective-permute-start | bytes 1572872 | tf_op jit(solution)/shard_map/ppermute | solution.py:376
  148.1 9.6 %collective-permute-done.23.refs_3_ = bf16[128,2048]{1,0:T(8,128)(2,1)} collective-permute-done((bf16[128,2048]{1,0:T(8,128)(2,1)S(1)}, bf16[128,2048]{1,0:T(8,128)(2,1)}, u32[]{:S(2)}, u32[]{:S(2)}) %collective-permute-start.23) | collective-permute-done | bytes 524320 | tf_op jit(solution)/shard_map/ppermute | solution.py:376
  157.7 2.7 %collective-permute-start.26 = (bf16[128,2048]{1,0:T(8,128)(2,1)}, bf16[128,2048]{1,0:T(8,128)(2,1)S(1)}, u32[]{:S(2)}, u32[]{:S(2)}) collective-permute-start(bf16[128,2048]{1,0:T(8,128)(2,1)} %collective-permute-done.24.refs_4_), channel_id=1, source_target_pairs={{0,7},{1,0},{2,1},{3,2},{4,3},{5,4},{6,5},{7,6},{8,15},{9,8},{10,9... | collective-permute-start | bytes 1572872 | tf_op jit(solution)/shard_map/ppermute | solution.py:376
  160.4 2.8 %copy-done.16 = bf16[48,256,256]{2,1,0:T(8,128)(2,1)S(1)} copy-done((bf16[48,256,256]{2,1,0:T(8,128)(2,1)S(1)}, bf16[48,256,256]{2,1,0:T(8,128)(2,1)}, u32[]{:S(2)}) %copy-start.16) | copy-done | bytes 6291480
  163.2 7.6 %shard_map.88 = bf16[16,2,32,256]{3,2,1,0:T(8,128)(2,1)S(1)} custom-call(s32[1]{0:T(128)} %dynamic_slice.9.start_ref, bf16[512,2048]{1,0:T(8,128)(2,1)} %bitcast.9.rows_ref, bf16[8,6,256,256]{3,2,1,0:T(8,128)(2,1)S(1)} %bitcast.15), custom_call_target="tpu_custom_call" | custom-call | flops 3221225472 | bytes 9437184 | tf_op jit(solution)/shard_map/pallas_call | solution.py:288
  171.6 7.8 %all-to-all-start.2 = ((bf16[16,2,32,256]{3,2,1,0:T(8,128)(2,1)}), bf16[16,2,32,256]{3,2,1,0:T(8,128)(2,1)S(1)}, u32[]{:S(2)}, u32[]{:S(2)}) async-start(bf16[16,2,32,256]{3,2,1,0:T(8,128)(2,1)} %copy-done.10), calls=%async_computation.2 | async-start | bytes 1048576 | tf_op jit(solution)/shard_map/all_to_all | solution.py:440
  179.5 2.8 %collective-permute-start.28 = (bf16[64,2048]{1,0:T(8,128)(2,1)S(1)}, bf16[64,2048]{1,0:T(8,128)(2,1)S(1)}, u32[]{:S(2)}, u32[]{:S(2)}) collective-permute-start(bf16[64,2048]{1,0:T(8,128)(2,1)S(1)} %slice.9), channel_id=1, source_target_pairs={{0,7},{1,0},{2,1},{3,2},{4,3},{5,4},{6,5},{7,6},{8,15},{9,8},{10,9... | collective-permute-start | bytes 786440 | tf_op jit(solution)/shard_map/ppermute | solution.py:376
  182.4 6.2 %collective-permute-done.27.refs_7_ = bf16[64,2048]{1,0:T(8,128)(2,1)S(1)} collective-permute-done((bf16[64,2048]{1,0:T(8,128)(2,1)S(1)}, bf16[64,2048]{1,0:T(8,128)(2,1)S(1)}, u32[]{:S(2)}, u32[]{:S(2)}) %collective-permute-start.27) | collective-permute-done | bytes 262176 | tf_op jit(solution)/shard_map/ppermute | solution.py:376
  192.3 2.6 %shard_map.89 = (f32[128,2048]{1,0:T(8,128)S(1)}, bf16[128,2048]{1,0:T(8,128)(2,1)S(1)}) custom-call(s32[2]{0:T(128)S(1)} %pad_add_fusion.place_ref, bf16[16,2,32,256]{3,2,1,0:T(8,128)(2,1)S(1)} %all-to-all-done.2.mix_ref, bf16[128,2048]{1,0:T(8,128)(2,1)S(1)} %constant_dynamic-slice_fusion.refs_0_, bf16[128,2048]{1,0:T(8,128)(2,1)S(1)} %copy-done.7, ...), custom_call_target="tpu_custom_call" | custom-call | flops 1073741824 | bytes 8388608 | tf_op jit(solution)/shard_map/pallas_call | solution.py:332
  196.1 1.5 collective-permute-done.29.got_ref
  (94 shorter events, 37.3 us)
Async XLA Ops:
  6.5 88.5 %all-gather.5.cloned.1.call-start = ((), (), s32[]{:S(2)}) async-start(), calls=%async_computation.3 | async-start | bytes 8650752 | tf_op jit(solution)/shard_map/all_gather | solution.py:409
  7.5 18.1 %collective-permute-start = (bf16[128,256]{1,0:T(8,128)(2,1)S(1)}, bf16[128,256]{1,0:T(8,128)(2,1)S(1)}, u32[]{:S(2)}, u32[]{:S(2)}) collective-permute-start(bf16[128,256]{1,0:T(8,128)(2,1)S(1)} %dynamic_slice.10), channel_id=1, source_target_pairs={{0,0},{1,1},{2,2},{3,3},{4,12},{5,13},{6,14},{7,15},{8,4},{9,5},{1... | collective-permute-start | bytes 196616 | tf_op jit(solution)/shard_map/ppermute | solution.py:406
  17.7 7.9 %collective-permute-start.1 = (bf16[128,256]{1,0:T(8,128)(2,1)S(1)}, bf16[128,256]{1,0:T(8,128)(2,1)S(1)}, u32[]{:S(2)}, u32[]{:S(2)}) collective-permute-start(bf16[128,256]{1,0:T(8,128)(2,1)S(1)} %dynamic_slice.10), channel_id=1, source_target_pairs={{0,1},{1,2},{2,3},{3,4},{4,13},{5,14},{6,15},{7,8},{8,5},{9,6},{10... | collective-permute-start | bytes 196616 | tf_op jit(solution)/shard_map/ppermute | solution.py:406
  26.4 134.0 %all-gather.7.cloned.1.call-start = ((), (), s32[]{:S(2)}) async-start(), calls=%async_computation.4 | async-start | bytes 7077888 | tf_op jit(solution)/shard_map/all_gather | solution.py:422
  26.4 11.4 %collective-permute-start.4 = (bf16[80,2048]{1,0:T(8,128)(2,1)S(1)}, bf16[80,2048]{1,0:T(8,128)(2,1)S(1)}, u32[]{:S(2)}, u32[]{:S(2)}) collective-permute-start(bf16[80,2048]{1,0:T(8,128)(2,1)S(1)} %get-tuple-element.39.refs_0_), channel_id=1, source_target_pairs={{0,1},{1,2},{2,3},{3,4},{4,5},{5,6},{6,7},{7,0},{8,9},{9,10},{10,1... | collective-permute-start | bytes 983048 | tf_op jit(solution)/shard_map/ppermute | solution.py:376
  30.0 9.3 %collective-permute-start.7 = (bf16[80,2048]{1,0:T(8,128)(2,1)S(1)}, bf16[80,2048]{1,0:T(8,128)(2,1)S(1)}, u32[]{:S(2)}, u32[]{:S(2)}) collective-permute-start(bf16[80,2048]{1,0:T(8,128)(2,1)S(1)} %get-tuple-element.40.refs_1_), channel_id=1, source_target_pairs={{0,7},{1,0},{2,1},{3,2},{4,3},{5,4},{6,5},{7,6},{8,15},{9,8},{10,9... | collective-permute-start | bytes 983048 | tf_op jit(solution)/shard_map/ppermute | solution.py:376
  30.0 14.8 %collective-permute-start.5 = (bf16[80,2048]{1,0:T(8,128)(2,1)S(1)}, bf16[80,2048]{1,0:T(8,128)(2,1)S(1)}, u32[]{:S(2)}, u32[]{:S(2)}) collective-permute-start(bf16[80,2048]{1,0:T(8,128)(2,1)S(1)} %get-tuple-element.40.refs_1_), channel_id=1, source_target_pairs={{0,1},{1,2},{2,3},{3,4},{4,5},{5,6},{6,7},{7,0},{8,9},{9,10},{10,1... | collective-permute-start | bytes 983048 | tf_op jit(solution)/shard_map/ppermute | solution.py:376
  31.5 14.9 %collective-permute-start.6 = (bf16[80,2048]{1,0:T(8,128)(2,1)S(1)}, bf16[80,2048]{1,0:T(8,128)(2,1)S(1)}, u32[]{:S(2)}, u32[]{:S(2)}) collective-permute-start(bf16[80,2048]{1,0:T(8,128)(2,1)S(1)} %get-tuple-element.39.refs_0_), channel_id=1, source_target_pairs={{0,7},{1,0},{2,1},{3,2},{4,3},{5,4},{6,5},{7,6},{8,15},{9,8},{10,9... | collective-permute-start | bytes 983048 | tf_op jit(solution)/shard_map/ppermute | solution.py:376
  37.8 14.0 %collective-permute-start.8 = (bf16[80,2048]{1,0:T(8,128)(2,1)S(1)}, bf16[80,2048]{1,0:T(8,128)(2,1)S(1)}, u32[]{:S(2)}, u32[]{:S(2)}) collective-permute-start(bf16[80,2048]{1,0:T(8,128)(2,1)S(1)} %collective-permute-done.4.refs_2_), channel_id=1, source_target_pairs={{0,1},{1,2},{2,3},{3,4},{4,5},{5,6},{6,7},{7,0},{8,9},{9,10},{10,1... | collective-permute-start | bytes 983048 | tf_op jit(solution)/shard_map/ppermute | solution.py:376
  39.3 14.0 %collective-permute-start.11 = (bf16[80,2048]{1,0:T(8,128)(2,1)S(1)}, bf16[80,2048]{1,0:T(8,128)(2,1)S(1)}, u32[]{:S(2)}, u32[]{:S(2)}) collective-permute-start(bf16[80,2048]{1,0:T(8,128)(2,1)S(1)} %collective-permute-done.7.refs_5_), channel_id=1, source_target_pairs={{0,7},{1,0},{2,1},{3,2},{4,3},{5,4},{6,5},{7,6},{8,15},{9,8},{10,9... | collective-permute-start | bytes 983048 | tf_op jit(solution)/shard_map/ppermute | solution.py:376
  44.8 14.0 %collective-permute-start.9 = (bf16[80,2048]{1,0:T(8,128)(2,1)S(1)}, bf16[80,2048]{1,0:T(8,128)(2,1)S(1)}, u32[]{:S(2)}, u32[]{:S(2)}) collective-permute-start(bf16[80,2048]{1,0:T(8,128)(2,1)S(1)} %collective-permute-done.5.refs_3_), channel_id=1, source_target_pairs={{0,1},{1,2},{2,3},{3,4},{4,5},{5,6},{6,7},{7,0},{8,9},{9,10},{10,1... | collective-permute-start | bytes 983048 | tf_op jit(solution)/shard_map/ppermute | solution.py:376
  46.4 13.9 %collective-permute-start.10 = (bf16[80,2048]{1,0:T(8,128)(2,1)S(1)}, bf16[80,2048]{1,0:T(8,128)(2,1)S(1)}, u32[]{:S(2)}, u32[]{:S(2)}) collective-permute-start(bf16[80,2048]{1,0:T(8,128)(2,1)S(1)} %collective-permute-done.6.refs_4_), channel_id=1, source_target_pairs={{0,7},{1,0},{2,1},{3,2},{4,3},{5,4},{6,5},{7,6},{8,15},{9,8},{10,9... | collective-permute-start | bytes 983048 | tf_op jit(solution)/shard_map/ppermute | solution.py:376
  51.8 14.0 %collective-permute-start.12 = (bf16[80,2048]{1,0:T(8,128)(2,1)S(1)}, bf16[80,2048]{1,0:T(8,128)(2,1)S(1)}, u32[]{:S(2)}, u32[]{:S(2)}) collective-permute-start(bf16[80,2048]{1,0:T(8,128)(2,1)S(1)} %collective-permute-done.8.refs_6_), channel_id=1, source_target_pairs={{0,1},{1,2},{2,3},{3,4},{4,5},{5,6},{6,7},{7,0},{8,9},{9,10},{10,1... | collective-permute-start | bytes 983048 | tf_op jit(solution)/shard_map/ppermute | solution.py:376
  53.3 14.0 %collective-permute-start.15 = (bf16[80,2048]{1,0:T(8,128)(2,1)S(1)}, bf16[80,2048]{1,0:T(8,128)(2,1)S(1)}, u32[]{:S(2)}, u32[]{:S(2)}) collective-permute-start(bf16[80,2048]{1,0:T(8,128)(2,1)S(1)} %collective-permute-done.11.refs_9_), channel_id=1, source_target_pairs={{0,7},{1,0},{2,1},{3,2},{4,3},{5,4},{6,5},{7,6},{8,15},{9,8},{10,9... | collective-permute-start | bytes 983048 | tf_op jit(solution)/shard_map/ppermute | solution.py:376
  58.8 14.1 %collective-permute-start.13 = (bf16[80,2048]{1,0:T(8,128)(2,1)S(1)}, bf16[80,2048]{1,0:T(8,128)(2,1)S(1)}, u32[]{:S(2)}, u32[]{:S(2)}) collective-permute-start(bf16[80,2048]{1,0:T(8,128)(2,1)S(1)} %collective-permute-done.9.refs_7_), channel_id=1, source_target_pairs={{0,1},{1,2},{2,3},{3,4},{4,5},{5,6},{6,7},{7,0},{8,9},{9,10},{10,1... | collective-permute-start | bytes 983048 | tf_op jit(solution)/shard_map/ppermute | solution.py:376
  60.4 13.8 %collective-permute-start.14 = (bf16[80,2048]{1,0:T(8,128)(2,1)S(1)}, bf16[80,2048]{1,0:T(8,128)(2,1)S(1)}, u32[]{:S(2)}, u32[]{:S(2)}) collective-permute-start(bf16[80,2048]{1,0:T(8,128)(2,1)S(1)} %collective-permute-done.10.refs_8_), channel_id=1, source_target_pairs={{0,7},{1,0},{2,1},{3,2},{4,3},{5,4},{6,5},{7,6},{8,15},{9,8},{10,9... | collective-permute-start | bytes 983048 | tf_op jit(solution)/shard_map/ppermute | solution.py:376
  65.9 14.1 %collective-permute-start.16 = (bf16[80,2048]{1,0:T(8,128)(2,1)S(1)}, bf16[80,2048]{1,0:T(8,128)(2,1)S(1)}, u32[]{:S(2)}, u32[]{:S(2)}) collective-permute-start(bf16[80,2048]{1,0:T(8,128)(2,1)S(1)} %collective-permute-done.12.refs_10_), channel_id=1, source_target_pairs={{0,1},{1,2},{2,3},{3,4},{4,5},{5,6},{6,7},{7,0},{8,9},{9,10},{10,1... | collective-permute-start | bytes 983048 | tf_op jit(solution)/shard_map/ppermute | solution.py:376
  67.4 13.8 %collective-permute-start.17 = (bf16[80,2048]{1,0:T(8,128)(2,1)S(1)}, bf16[80,2048]{1,0:T(8,128)(2,1)S(1)}, u32[]{:S(2)}, u32[]{:S(2)}) collective-permute-start(bf16[80,2048]{1,0:T(8,128)(2,1)S(1)} %collective-permute-done.15.refs_13_), channel_id=1, source_target_pairs={{0,7},{1,0},{2,1},{3,2},{4,3},{5,4},{6,5},{7,6},{8,15},{9,8},{10,9... | collective-permute-start | bytes 983048 | tf_op jit(solution)/shard_map/ppermute | solution.py:376
  82.1 10.3 %collective-permute-start.18 = (bf16[2,3,64,256]{3,2,1,0:T(8,128)(2,1)S(1)}, bf16[2,3,64,256]{3,2,1,0:T(8,128)(2,1)S(1)}, u32[]{:S(2)}, u32[]{:S(2)}) collective-permute-start(bf16[2,3,64,256]{3,2,1,0:T(8,128)(2,1)S(1)} %get-tuple-element.42), channel_id=1, source_target_pairs={{0,16},{16,32},{32,48},{48,0},{1,17},{17,33},{33,49},{49,1},{2,18}... | collective-permute-start | bytes 589832 | tf_op jit(solution)/shard_map/ppermute | solution.py:376
  83.4 10.7 %collective-permute-start.19 = (bf16[2,3,64,256]{3,2,1,0:T(8,128)(2,1)S(1)}, bf16[2,3,64,256]{3,2,1,0:T(8,128)(2,1)S(1)}, u32[]{:S(2)}, u32[]{:S(2)}) collective-permute-start(bf16[2,3,64,256]{3,2,1,0:T(8,128)(2,1)S(1)} %get-tuple-element.43), channel_id=1, source_target_pairs={{0,32},{16,48},{32,0},{48,16},{1,33},{17,49},{33,1},{49,17},{2,34}... | collective-permute-start | bytes 589832 | tf_op jit(solution)/shard_map/ppermute | solution.py:376
  86.0 8.1 %collective-permute-start.20 = (bf16[2,3,64,256]{3,2,1,0:T(8,128)(2,1)S(1)}, bf16[2,3,64,256]{3,2,1,0:T(8,128)(2,1)S(1)}, u32[]{:S(2)}, u32[]{:S(2)}) collective-permute-start(bf16[2,3,64,256]{3,2,1,0:T(8,128)(2,1)S(1)} %get-tuple-element.44), channel_id=1, source_target_pairs={{0,48},{16,0},{32,16},{48,32},{1,49},{17,1},{33,17},{49,33},{2,50}... | collective-permute-start | bytes 589832 | tf_op jit(solution)/shard_map/ppermute | solution.py:376
  95.1 20.0 %all-to-all-start = ((bf16[8,128,256]{2,1,0:T(8,128)(2,1)}), bf16[8,128,256]{2,1,0:T(8,128)(2,1)S(1)}, u32[]{:S(2)}, u32[]{:S(2)}) async-start(bf16[8,128,256]{2,1,0:T(8,128)(2,1)} %shard_map.83), calls=%async_computation | async-start | bytes 1048576 | tf_op jit(solution)/shard_map/all_to_all | solution.py:423
  122.4 38.0 %all-to-all-start.1 = ((bf16[16,32,2048]{2,1,0:T(8,128)(2,1)}), bf16[16,32,2048]{2,1,0:T(8,128)(2,1)}, u32[]{:S(2)}, u32[]{:S(2)}) async-start(bf16[16,32,2048]{2,1,0:T(8,128)(2,1)} %copy-done.3), calls=%async_computation.1 | async-start | bytes 4194304 | tf_op jit(solution)/shard_map/all_to_all | solution.py:436
  129.5 14.5 %collective-permute-start.21 = (bf16[128,2048]{1,0:T(8,128)(2,1)S(1)}, bf16[128,2048]{1,0:T(8,128)(2,1)S(1)}, u32[]{:S(2)}, u32[]{:S(2)}) collective-permute-start(bf16[128,2048]{1,0:T(8,128)(2,1)S(1)} %constant_dynamic-slice_fusion.refs_0_), channel_id=1, source_target_pairs={{0,1},{1,2},{2,3},{3,4},{4,5},{5,6},{6,7},{7,0},{8,9},{9,10},{10,1... | collective-permute-start | bytes 1572872 | tf_op jit(solution)/shard_map/ppermute | solution.py:376
  129.8 14.2 %collective-permute-start.22 = (bf16[128,2048]{1,0:T(8,128)(2,1)S(1)}, bf16[128,2048]{1,0:T(8,128)(2,1)S(1)}, u32[]{:S(2)}, u32[]{:S(2)}) collective-permute-start(bf16[128,2048]{1,0:T(8,128)(2,1)S(1)} %constant_dynamic-slice_fusion.refs_0_), channel_id=1, source_target_pairs={{0,7},{1,0},{2,1},{3,2},{4,3},{5,4},{6,5},{7,6},{8,15},{9,8},{10,9... | collective-permute-start | bytes 1572872 | tf_op jit(solution)/shard_map/ppermute | solution.py:376
  144.0 13.7 %collective-permute-start.23 = (bf16[128,2048]{1,0:T(8,128)(2,1)S(1)}, bf16[128,2048]{1,0:T(8,128)(2,1)}, u32[]{:S(2)}, u32[]{:S(2)}) collective-permute-start(bf16[128,2048]{1,0:T(8,128)(2,1)S(1)} %collective-permute-done.21.refs_1_), channel_id=1, source_target_pairs={{0,1},{1,2},{2,3},{3,4},{4,5},{5,6},{6,7},{7,0},{8,9},{9,10},{10,1... | collective-permute-start | bytes 1572872 | tf_op jit(solution)/shard_map/ppermute | solution.py:376
  144.0 13.7 %collective-permute-start.24 = (bf16[128,2048]{1,0:T(8,128)(2,1)S(1)}, bf16[128,2048]{1,0:T(8,128)(2,1)}, u32[]{:S(2)}, u32[]{:S(2)}) collective-permute-start(bf16[128,2048]{1,0:T(8,128)(2,1)S(1)} %collective-permute-done.22.refs_2_), channel_id=1, source_target_pairs={{0,7},{1,0},{2,1},{3,2},{4,3},{5,4},{6,5},{7,6},{8,15},{9,8},{10,9... | collective-permute-start | bytes 1572872 | tf_op jit(solution)/shard_map/ppermute | solution.py:376
  157.7 21.7 %collective-permute-start.25 = (bf16[128,2048]{1,0:T(8,128)(2,1)}, bf16[128,2048]{1,0:T(8,128)(2,1)S(1)}, u32[]{:S(2)}, u32[]{:S(2)}) collective-permute-start(bf16[128,2048]{1,0:T(8,128)(2,1)} %collective-permute-done.23.refs_3_), channel_id=1, source_target_pairs={{0,1},{1,2},{2,3},{3,4},{4,5},{5,6},{6,7},{7,0},{8,9},{9,10},{10,1... | collective-permute-start | bytes 1572872 | tf_op jit(solution)/shard_map/ppermute | solution.py:376
  157.7 21.8 %collective-permute-start.26 = (bf16[128,2048]{1,0:T(8,128)(2,1)}, bf16[128,2048]{1,0:T(8,128)(2,1)S(1)}, u32[]{:S(2)}, u32[]{:S(2)}) collective-permute-start(bf16[128,2048]{1,0:T(8,128)(2,1)} %collective-permute-done.24.refs_4_), channel_id=1, source_target_pairs={{0,7},{1,0},{2,1},{3,2},{4,3},{5,4},{6,5},{7,6},{8,15},{9,8},{10,9... | collective-permute-start | bytes 1572872 | tf_op jit(solution)/shard_map/ppermute | solution.py:376
  171.6 17.7 %all-to-all-start.2 = ((bf16[16,2,32,256]{3,2,1,0:T(8,128)(2,1)}), bf16[16,2,32,256]{3,2,1,0:T(8,128)(2,1)S(1)}, u32[]{:S(2)}, u32[]{:S(2)}) async-start(bf16[16,2,32,256]{3,2,1,0:T(8,128)(2,1)} %copy-done.10), calls=%async_computation.2 | async-start | bytes 1048576 | tf_op jit(solution)/shard_map/all_to_all | solution.py:440
  179.4 9.2 %collective-permute-start.27 = (bf16[64,2048]{1,0:T(8,128)(2,1)S(1)}, bf16[64,2048]{1,0:T(8,128)(2,1)S(1)}, u32[]{:S(2)}, u32[]{:S(2)}) collective-permute-start(bf16[64,2048]{1,0:T(8,128)(2,1)S(1)} %slice.8), channel_id=1, source_target_pairs={{0,1},{1,2},{2,3},{3,4},{4,5},{5,6},{6,7},{7,0},{8,9},{9,10},{10,1... | collective-permute-start | bytes 786440 | tf_op jit(solution)/shard_map/ppermute | solution.py:376
  179.5 9.0 %collective-permute-start.28 = (bf16[64,2048]{1,0:T(8,128)(2,1)S(1)}, bf16[64,2048]{1,0:T(8,128)(2,1)S(1)}, u32[]{:S(2)}, u32[]{:S(2)}) collective-permute-start(bf16[64,2048]{1,0:T(8,128)(2,1)S(1)} %slice.9), channel_id=1, source_target_pairs={{0,7},{1,0},{2,1},{3,2},{4,3},{5,4},{6,5},{7,6},{8,15},{9,8},{10,9... | collective-permute-start | bytes 786440 | tf_op jit(solution)/shard_map/ppermute | solution.py:376
  (22 other events, 268.7 us)
Sparse Core Ops, SparseCore 0:
  26.5 59.9 all-gather.4
  95.2 44.2 all-gather.6

commit v8 on v7

--- a/solution.py
+++ b/solution.py
@@ -50,11 +50,12 @@
     return lax.dot_general(a, b, (((1,), (1,)), ((), ())), preferred_element_type=F32)
 
 
-def norm_kernel(place_ref, x_ref, gain_ref, qkv_ref, a_ref, b_ref, rows_ref):
+def norm_kernel(place_ref, x_ref, gain_ref, qkv_ref, a_ref, b_ref, rows_a_ref, rows_b_ref):
     gain = gain_ref[...]
-    values = jnp.transpose(x_ref[...].astype(F32), (1, 0, 2)).reshape(rows_ref.shape)
-    half = rows_ref.shape[0] // 2
-    rows_ref[...] = values.astype(BF)
+    half = rows_a_ref.shape[0]
+    values = jnp.transpose(x_ref[...].astype(F32), (1, 0, 2)).reshape(2 * half, -1)
+    rows_a_ref[...] = values[:half].astype(BF)
+    rows_b_ref[...] = values[half:].astype(BF)
     a_ref[:half] = normed(values[:half], gain)
     b_ref[:half] = normed(values[half:], gain)
     b_ref[half:, 1024:] = jnp.zeros((16, 1024), BF)
@@ -84,10 +85,11 @@
             out_specs=(
                 whole(count // 2 + 16, width),
                 whole(count // 2 + 16, width),
-                whole(count, width),
+                whole(count // 2, width),
+                whole(count // 2, width),
             ),
         ),
-        out_shape=(half, half, jax.ShapeDtypeStruct((count, width), BF)),
+        out_shape=(half, half) + (jax.ShapeDtypeStruct((count // 2, width), BF),) * 2,
         compiler_params=params(),
         cost_estimate=pl.CostEstimate(
             flops=4 * count * width, bytes_accessed=6 * count * width, transcendentals=0
@@ -157,39 +159,36 @@
 
 
 def spatial_kernel(place_ref, weight_ref, *refs):
-    pieces, out_ref, qkv = refs[: 2 * NZ], refs[2 * NZ], refs[2 * NZ + 1]
+    pieces, out_ref, qkv = refs[:NZ], refs[NZ], refs[NZ + 1]
     place = place_ref[0]
-    for frame in range(4):
-        low = 32 * (frame % 2)
-        rows = jnp.concatenate(
-            [pieces[2 * k + frame // 2][low : low + 32, :] for k in range(NZ)], axis=0
-        )
+    for frame in range(2):
+        low = 32 * frame
+        rows = jnp.concatenate([piece[low : low + 32, :] for piece in pieces], axis=0)
         for kind in range(3):
             qkv[kind, 256 * frame : 256 * frame + 256] = dot(rows, weight_ref[kind]).astype(BF)
-    for frames in ((0, 1), (2, 3)):
-        spots = [(frame, head * E) for frame in frames for head in range(2)]
-        chains = []
-        for frame, low in spots:
-            at, cols = slice(256 * frame, 256 * frame + 256), slice(low, low + E)
-            chains.append((qkv[0, at, cols], qkv[1, at, cols], qkv[2, at, cols], None))
-        for (frame, low), mixed in zip(spots, attend(chains)):
-            for k in range(NZ):
-                target = lax.rem(place + (OFFSETS[k] + NZ), NZ)
-                out_ref[target, 32 * frame : 32 * frame + 32, low : low + E] = mixed[
-                    32 * k : 32 * k + 32
-                ]
+    spots = [(frame, head * E) for frame in range(2) for head in range(2)]
+    chains = []
+    for frame, low in spots:
+        at, cols = slice(256 * frame, 256 * frame + 256), slice(low, low + E)
+        chains.append((qkv[0, at, cols], qkv[1, at, cols], qkv[2, at, cols], None))
+    for (frame, low), mixed in zip(spots, attend(chains)):
+        for k in range(NZ):
+            target = lax.rem(place + (OFFSETS[k] + NZ), NZ)
+            out_ref[target, 32 * frame : 32 * frame + 32, low : low + E] = mixed[
+                32 * k : 32 * k + 32
+            ]
 
 
 def spatial_attend(place, weight, pieces):
     return pl.pallas_call(
         spatial_kernel,
-        out_shape=jax.ShapeDtypeStruct((NZ, 128, 256), BF),
+        out_shape=jax.ShapeDtypeStruct((NZ, 64, 256), BF),
         in_specs=[smem(), vmem()] + [vmem()] * len(pieces),
         out_specs=vmem(),
-        scratch_shapes=[pltpu.VMEM((3, 1024, 256), BF)],
+        scratch_shapes=[pltpu.VMEM((3, 512, 256), BF)],
         compiler_params=params(),
         cost_estimate=pl.CostEstimate(
-            flops=2 * 1024 * 2048 * 768 * 2, bytes_accessed=8 << 20, transcendentals=8 * 65536
+            flops=2 * 1024 * 2048 * 768, bytes_accessed=6 << 20, transcendentals=4 * 65536
         ),
     )(place, weight, *pieces)
 
@@ -227,32 +226,35 @@
     scaled = scaled * gain_ref[...]
     for group in range(4):
         chunk = jnp.concatenate(
-            [scaled[32 * f + 8 * group : 32 * f + 8 * group + 8] for f in range(4)], axis=0
+            [scaled[32 * f + 8 * group : 32 * f + 8 * group + 8] for f in range(2)], axis=0
         ).astype(BF)
         for y in range(4):
             send_ref[(group // 2) * 8 + y * 2 + group % 2] = chunk
 
 
 def middle_rows(mix, weight, rows, gain):
-    width = rows.shape[1]
+    count, width = rows.shape
     return pl.pallas_call(
         middle_kernel,
         out_shape=(
-            jax.ShapeDtypeStruct((128, width), BF),
-            jax.ShapeDtypeStruct((16, 32, width), BF),
+            jax.ShapeDtypeStruct((count, width), BF),
+            jax.ShapeDtypeStruct((16, count // 4, width), BF),
         ),
         in_specs=[vmem()] * 4,
         out_specs=(vmem(), vmem()),
-        scratch_shapes=[pltpu.VMEM((128, width), F32)],
+        scratch_shapes=[pltpu.VMEM((count, width), F32)],
         compiler_params=params(),
         cost_estimate=pl.CostEstimate(
-            flops=2 * 128 * 2048 * 2048, bytes_accessed=12 << 20, transcendentals=0
+            flops=2 * 64 * 2048 * 2048, bytes_accessed=10 << 20, transcendentals=0
         ),
     )(mix, weight, rows, gain)
 
 
-def temporal_kernel(start_ref, rows_ref, weight_ref, out_ref, qkv, bias):
-    count = rows_ref.shape[0]
+def temporal_kernel(start_ref, first_ref, second_ref, weight_ref, out_ref, rows, qkv, bias):
+    count = rows.shape[0]
+    for spot in range(16):
+        rows[32 * spot : 32 * spot + 16] = first_ref[spot]
+        rows[32 * spot + 16 : 32 * spot + 32] = second_ref[spot]
     start = start_ref[0]
     late = lax.broadcasted_iota(jnp.int32, (count, count), 0)
     early = lax.broadcasted_iota(jnp.int32, (count, count), 1)
@@ -260,7 +262,7 @@
     allowed = same & (early <= late) & ((early >= 8 * start) == (late >= 8 * start))
     bias[...] = jnp.where(allowed, 0.0, -1e30)
     for block in range(6):
-        qkv[block] = dot(rows_ref[...], weight_ref[:, block].reshape(2048, 256)).astype(BF)
+        qkv[block] = dot(rows[...], weight_ref[:, block].reshape(2048, 256)).astype(BF)
     size = 256
     for pair in range(2):
         for low in range(0, count, size):
@@ -283,14 +285,15 @@
                     out_ref[at] = rows
 
 
-def temporal_attend(start, rows, weight):
-    count, width = rows.shape
+def temporal_attend(start, first, second, weight):
+    count, width = 2 * 16 * first.shape[1], first.shape[2]
     return pl.pallas_call(
         temporal_kernel,
         out_shape=jax.ShapeDtypeStruct((16, 2, 32, 256), BF),
-        in_specs=[smem(), vmem(), vmem()],
+        in_specs=[smem(), vmem(), vmem(), vmem()],
         out_specs=vmem(),
         scratch_shapes=[
+            pltpu.VMEM((count, width), BF),
             pltpu.VMEM((6, count, 256), BF),
             pltpu.VMEM((count, count), F32),
         ],
@@ -298,7 +301,7 @@
         cost_estimate=pl.CostEstimate(
             flops=2 * 512 * 2048 * 1536, bytes_accessed=9 << 20, transcendentals=131072
         ),
-    )(start, rows, weight)
+    )(start, first, second, weight)
 
 
 def last_kernel(place_ref, mix_ref, *refs):
@@ -345,14 +348,15 @@
     )(place, mix, *pieces)
 
 
-def end_kernel(keep_ref, got_ref, middle_ref, out_ref):
+def end_kernel(keep_ref, got_ref, first_ref, second_ref, out_ref):
     for group in range(4):
         at = slice(32 * group, 32 * group + 32)
         rows = (keep_ref[at] + got_ref[at].astype(F32)).reshape(4, 8, -1)
         middle = jnp.stack(
             [
-                middle_ref[32 * f : 32 * f + 32].astype(F32)[8 * group : 8 * group + 8]
-                for f in range(4)
+                ref[32 * f : 32 * f + 32].astype(F32)[8 * group : 8 * group + 8]
+                for ref in (first_ref, second_ref)
+                for f in range(2)
             ],
             axis=0,
         )
@@ -360,15 +364,15 @@
         out_ref[8 * group : 8 * group + 8] = out
 
 
-def end_rows(keep, got, middle):
+def end_rows(keep, got, first, second):
     return pl.pallas_call(
         end_kernel,
-        out_shape=jax.ShapeDtypeStruct((32, 4, middle.shape[1]), BF),
-        in_specs=[vmem()] * 3,
+        out_shape=jax.ShapeDtypeStruct((32, 4, first.shape[1]), BF),
+        in_specs=[vmem()] * 4,
         out_specs=vmem(),
         compiler_params=params(),
         cost_estimate=pl.CostEstimate(flops=1 << 20, bytes_accessed=3 << 20, transcendentals=0),
-    )(keep, got, middle)
+    )(keep, got, first, second)
 
 
 def shifted(value, axis, step):
@@ -392,7 +396,7 @@
     w, xl, y, c, z = (lax.axis_index(name) for name in ("w", "xl", "y", "c", "z"))
 
     place = (((w * 2 + xl) * 2 + c) * 4 + y).reshape(1)
-    first, second, rows = norm_rows(
+    first, second, *rows = norm_rows(
         place, stream, spatial_gain.reshape(1, width), jnp.transpose(temporal_qkv, (1, 0, 2))
     )
 
@@ -415,31 +419,43 @@
     got = [sends[0]] + [shifted(sends[k], "y", k) for k in range(1, 4)]
 
     weight = jnp.transpose(spatial_qkv, (1, 0, 2))
-    mix = spatial_attend(z.reshape(1), weight, pieces)
-    mix, *got = lax.optimization_barrier((mix, *got))
+    mixes = [spatial_attend(z.reshape(1), weight, pieces[0::2])]
+    mixes[0], later = lax.optimization_barrier((mixes[0], pieces[1::2]))
+    mixes.append(spatial_attend(z.reshape(1), weight, later))
+    mixes[1], got = lax.optimization_barrier((mixes[1], got))
     quarter = join_shares(y.reshape(1), got)
-    mix, quarter, whole_out = lax.optimization_barrier((mix, quarter, whole_out))
+    mixes[1], quarter = lax.optimization_barrier((mixes[1], quarter))
     quarter = lax.all_gather(quarter[None], ("w", "xl", "c"), axis=0, tiled=True)
-    mix = lax.all_to_all(mix, "z", 0, 0, tiled=True)
-
-    middle, send = middle_rows(mix, whole_out, rows, temporal_gain.reshape(1, width))
-
+
+    gain = temporal_gain.reshape(1, width)
     half = lax.dynamic_slice(temporal_out, (c * E, 0), (E, width))
-    send, half = lax.optimization_barrier((send, half))
+    middles, sends, windows = [], [], []
+    for part in range(2):
+        mix = lax.all_to_all(mixes[part], "z", 0, 0, tiled=True)
+        if part == 1:
+            mix, half, _ = lax.optimization_barrier((mix, half, sends[0]))
+        middle, send = middle_rows(mix, whole_out, rows[part], gain)
+        middles.append(middle)
+        sends.append(send)
+        windows.append(lax.all_to_all(send, ("xl", "y", "c"), 0, 0, tiled=True))
+
     up, down = half, half
     halves = [half]
     for step in (1, 2, 3):
         up, down = shifted(up, "z", 1), shifted(down, "z", -1)
+        if step == 1:
+            up, down, _ = lax.optimization_barrier((up, down, sends[1]))
+        if step == 2:
+            up, down, quarter = lax.optimization_barrier((up, down, quarter))
         halves += [up, down]
     halves += [shifted(up[:64], "z", 1), shifted(down[64:], "z", -1)]
 
-    window = lax.all_to_all(send, ("xl", "y", "c"), 0, 0, tiled=True)
-    window, *halves[1:5] = lax.optimization_barrier((window, *halves[1:5]))
+    windows, halves[1:3] = lax.optimization_barrier((windows, halves[1:3]))
     start = lax.dynamic_slice(starts, (w,), (1,))
-    mix = temporal_attend(start, window.reshape(512, width), quarter)
+    mix = temporal_attend(start, *windows, quarter)
     mix = lax.all_to_all(mix, ("xl", "y", "c"), 0, 0, tiled=True)
     keep, give = last_sums(jnp.stack([z, c]).astype(jnp.int32), mix, halves)
-    return end_rows(keep, shifted(give, "c", 1), middle)
+    return end_rows(keep, shifted(give, "c", 1), *middles)
 
 
 def solution(mesh):

time: 206 us -> 221 us (1.073)
  blocking collectives: 0 us -> 12.9 us
  waiting for transfers between devices: 81.5 us -> 71.3 us
  local copies, waits for them, and re-layouts: 19 us -> 25.1 us
  starting transfers between devices: 70 us -> 73 us
    ppermute x26, waiting for transfers between devices: 65.8 us -> 36.8 us  [shifted(): lax.ppermute(value, axis, [(i, (i + step) % count) for i in range(count)])]
    all_to_all x2 -> x3, waiting for transfers between devices: 15.6 us -> 28.9 us  [the longest x2 25.8 us: local(): windows.append(lax.all_to_all(send, ('xl', 'y', 'c'), 0, 0, tiled=True))]
    all_to_all x0 -> x1, blocking collectives: none -> 12.9 us  [local(): mix = lax.all_to_all(mixes[part], 'z', 0, 0, tiled=True)]
    all_to_all x1, waiting for transfers between devices: 0.01 us -> 5.57 us  [local(): mix = lax.all_to_all(mix, ('xl', 'y', 'c'), 0, 0, tiled=True)]
    all_to_all x2 -> x3, starting transfers between devices: 11.5 us -> 16.9 us  [the longest x2 13.5 us: local(): windows.append(lax.all_to_all(send, ('xl', 'y', 'c'), 0, 0, tiled=True))]
    unnamed x38, local copies, waits for them, and re-layouts: 17.4 us -> 22.1 us
    pallas_call x3 -> x5, Pallas kernels: 7.96 us -> 10.2 us  [the longest x2 5.52 us: spatial_attend(): pl.pallas_call(spatial_kernel, out_shape=jax.ShapeDtypeStruct((NZ, 64, 25...]
  transfers between devices with their start and end apart: 35 -> 36, of which waited for: 15 -> 15; matrix products, arithmetic and copies ran while one was open for 0% -> 1% of each run, Pallas kernels for 8% -> 8%
where the time goes in v8:
time: 221 us; the launch traced here: 220 us
  starting transfers between devices  73 us (33%)
  waiting for transfers between devices  71.3 us (32%)
  local copies, waits for them, and re-layouts  25.1 us (11%)
  Pallas kernels  23.5 us (11%)
  between operations  13.7 us (6%)
  blocking collectives  12.9 us (6%)
    ppermute x26, waiting for transfers between devices, shifted(): lax.ppermute(value, axis, [(i, (i + step) % count) for i in range(count)])  36.8 us
    ppermute x26, starting transfers between devices, shifted(): lax.ppermute(value, axis, [(i, (i + step) % count) for i in range(count)])  36.7 us
    all_to_all x2, waiting for transfers between devices, local(): windows.append(lax.all_to_all(send, ('xl', 'y', 'c'), 0, 0, tiled=True))  25.8 us
    unnamed x38, local copies, waits for them, and re-layouts  22.1 us
    ppermute x4, starting transfers between devices, local(): parts.append(lax.ppermute(block, ('c', 'z'), pairs))  13.8 us
    all_to_all x2, starting transfers between devices, local(): windows.append(lax.all_to_all(send, ('xl', 'y', 'c'), 0, 0, tiled=True))  13.5 us
    all_to_all x1, blocking collectives, local(): mix = lax.all_to_all(mixes[part], 'z', 0, 0, tiled=True)  12.9 us
    pallas_call x1, Pallas kernels, temporal_attend(): pl.pallas_call(temporal_kernel, out_shape=jax.ShapeDtypeStruct((16, 2, 32...  7.23 us
  transfers between devices with their start and end apart: 36, of which 15 were waited for; matrix products, arithmetic and copies ran while one was open for 1% of the time, Pallas kernels for 8%

profile of v8, /device:TPU:1, one launch (start us, length us, event | category | flops | bytes accessed | tf_op | source)
XLA Modules:
  0.0 219.6 jit_solution(12337531564337229515)
XLA Ops:
  7.5 10.2 %collective-permute-start = (bf16[128,256]{1,0:T(8,128)(2,1)S(1)}, bf16[128,256]{1,0:T(8,128)(2,1)S(1)}, u32[]{:S(2)}, u32[]{:S(2)}) collective-permute-start(bf16[128,256]{1,0:T(8,128)(2,1)S(1)} %dynamic_slice.10), channel_id=1, source_target_pairs={{0,0},{1,1},{2,2},{3,3},{4,12},{5,13},{6,14},{7,15},{8,4},{9,5},{1... | collective-permute-start | bytes 196616 | tf_op jit(solution)/shard_map/ppermute | solution.py:410
  18.5 2.8 %collective-permute-start.3 = (bf16[128,256]{1,0:T(8,128)(2,1)S(1)}, bf16[128,256]{1,0:T(8,128)(2,1)S(1)}, u32[]{:S(2)}, u32[]{:S(2)}) collective-permute-start(bf16[128,256]{1,0:T(8,128)(2,1)S(1)} %dynamic_slice.10), channel_id=1, source_target_pairs={{0,3},{1,4},{2,5},{3,6},{4,15},{5,8},{6,9},{7,10},{8,7},{9,0},{10,... | collective-permute-start | bytes 196616 | tf_op jit(solution)/shard_map/ppermute | solution.py:410
  21.3 1.9 copy-done.3
  26.4 3.6 %collective-permute-start.4 = (bf16[80,2048]{1,0:T(8,128)(2,1)S(1)}, bf16[80,2048]{1,0:T(8,128)(2,1)S(1)}, u32[]{:S(2)}, u32[]{:S(2)}) collective-permute-start(bf16[80,2048]{1,0:T(8,128)(2,1)S(1)} %get-tuple-element.54.refs_0_), channel_id=1, source_target_pairs={{0,1},{1,2},{2,3},{3,4},{4,5},{5,6},{6,7},{7,0},{8,9},{9,10},{10,1... | collective-permute-start | bytes 983048 | tf_op jit(solution)/shard_map/ppermute | solution.py:380
  32.7 5.1 %collective-permute-done.4.refs_1_.refs_2_ = bf16[80,2048]{1,0:T(8,128)(2,1)S(1)} collective-permute-done((bf16[80,2048]{1,0:T(8,128)(2,1)S(1)}, bf16[80,2048]{1,0:T(8,128)(2,1)S(1)}, u32[]{:S(2)}, u32[]{:S(2)}) %collective-permute-start.4) | collective-permute-done | bytes 327712 | tf_op jit(solution)/shard_map/ppermute | solution.py:380
  40.5 4.3 %collective-permute-done.11.refs_1_.refs_3_ = bf16[80,2048]{1,0:T(8,128)(2,1)S(1)} collective-permute-done((bf16[80,2048]{1,0:T(8,128)(2,1)S(1)}, bf16[80,2048]{1,0:T(8,128)(2,1)S(1)}, u32[]{:S(2)}, u32[]{:S(2)}) %collective-permute-start.11) | collective-permute-done | bytes 327712 | tf_op jit(solution)/shard_map/ppermute | solution.py:380
  47.5 4.3 %collective-permute-done.6.refs_3_.refs_6_ = bf16[80,2048]{1,0:T(8,128)(2,1)S(1)} collective-permute-done((bf16[80,2048]{1,0:T(8,128)(2,1)S(1)}, bf16[80,2048]{1,0:T(8,128)(2,1)S(1)}, u32[]{:S(2)}, u32[]{:S(2)}) %collective-permute-start.6) | collective-permute-done | bytes 327712 | tf_op jit(solution)/shard_map/ppermute | solution.py:380
  54.5 4.3 %collective-permute-done.13.refs_3_.refs_7_ = bf16[80,2048]{1,0:T(8,128)(2,1)S(1)} collective-permute-done((bf16[80,2048]{1,0:T(8,128)(2,1)S(1)}, bf16[80,2048]{1,0:T(8,128)(2,1)S(1)}, u32[]{:S(2)}, u32[]{:S(2)}) %collective-permute-start.13) | collective-permute-done | bytes 327712 | tf_op jit(solution)/shard_map/ppermute | solution.py:380
  61.5 4.3 %collective-permute-done.8.refs_5_.refs_10_ = bf16[80,2048]{1,0:T(8,128)(2,1)S(1)} collective-permute-done((bf16[80,2048]{1,0:T(8,128)(2,1)S(1)}, bf16[80,2048]{1,0:T(8,128)(2,1)S(1)}, u32[]{:S(2)}, u32[]{:S(2)}) %collective-permute-start.8) | collective-permute-done | bytes 327712 | tf_op jit(solution)/shard_map/ppermute | solution.py:380
  68.6 4.3 %collective-permute-done.15.refs_5_.refs_11_ = bf16[80,2048]{1,0:T(8,128)(2,1)S(1)} collective-permute-done((bf16[80,2048]{1,0:T(8,128)(2,1)S(1)}, bf16[80,2048]{1,0:T(8,128)(2,1)S(1)}, u32[]{:S(2)}, u32[]{:S(2)}) %collective-permute-start.15) | collective-permute-done | bytes 327712 | tf_op jit(solution)/shard_map/ppermute | solution.py:380
  74.1 5.9 %collective-permute-done.10.refs_7_.refs_14_ = bf16[80,2048]{1,0:T(8,128)(2,1)S(1)} collective-permute-done((bf16[80,2048]{1,0:T(8,128)(2,1)S(1)}, bf16[80,2048]{1,0:T(8,128)(2,1)S(1)}, u32[]{:S(2)}, u32[]{:S(2)}) %collective-permute-start.10) | collective-permute-done | bytes 327712 | tf_op jit(solution)/shard_map/ppermute | solution.py:380
  83.4 2.6 %collective-permute-start.19 = (bf16[2,3,64,256]{3,2,1,0:T(8,128)(2,1)S(1)}, bf16[2,3,64,256]{3,2,1,0:T(8,128)(2,1)S(1)}, u32[]{:S(2)}, u32[]{:S(2)}) collective-permute-start(bf16[2,3,64,256]{3,2,1,0:T(8,128)(2,1)S(1)} %get-tuple-element.73), channel_id=1, source_target_pairs={{0,32},{16,48},{32,0},{48,16},{1,33},{17,49},{33,1},{49,17},{2,34}... | collective-permute-start | bytes 589832 | tf_op jit(solution)/shard_map/ppermute | solution.py:380
  89.0 2.4 %shard_map.83 = bf16[8,64,256]{2,1,0:T(8,128)(2,1)S(1)} custom-call(s32[1]{0:T(128)} %bitcast.place_ref.z_ref, bf16[3,2048,256]{2,1,0:T(8,128)(2,1)S(1)} %bitcast.17, bf16[80,2048]{1,0:T(8,128)(2,1)S(1)} %get-tuple-element.54.refs_0_, bf16[80,2048]{1,0:T(8,128)(2,1)S(1)} %collective-permute-done.4.refs_1_.refs_2_, ...), custom_call_target="tpu_custom_call" | custom-call | flops 3221225472 | bytes 6291456 | tf_op jit(solution)/shard_map/pallas_call | solution.py:183
  91.4 3.1 %shard_map.86 = bf16[8,64,256]{2,1,0:T(8,128)(2,1)} custom-call(s32[1]{0:T(128)} %bitcast.place_ref.z_ref, bf16[3,2048,256]{2,1,0:T(8,128)(2,1)S(1)} %bitcast.18, bf16[80,2048]{1,0:T(8,128)(2,1)S(1)} %get-tuple-element.63.refs_0_.refs_1_, bf16[80,2048]{1,0:T(8,128)(2,1)S(1)} %collective-permute-done.11.refs_1_.refs_3_, ...), custom_call_target="tpu_custom_call" | custom-call | flops 3221225472 | bytes 6291456 | tf_op jit(solution)/shard_map/pallas_call | solution.py:183
  95.5 12.9 %all_to_all.25.mix_ref = bf16[8,64,256]{2,1,0:T(8,128)(2,1)S(1)} all-to-all(bf16[8,64,256]{2,1,0:T(8,128)(2,1)S(1)} %shard_map.83), channel_id=1, replica_groups=mesh['w'=2,'xl'=2,'y'=4,'c'=2,'z'=8] {'z'}, dimensions={0} | all-to-all | bytes 524288 | tf_op jit(solution)/shard_map/all_to_all | solution.py:434
  108.5 3.4 %all-to-all-start.2 = ((bf16[8,64,256]{2,1,0:T(8,128)(2,1)}), bf16[8,64,256]{2,1,0:T(8,128)(2,1)S(1)}, u32[]{:S(2)}, u32[]{:S(2)}) async-start(bf16[8,64,256]{2,1,0:T(8,128)(2,1)} %shard_map.86), calls=%async_computation.2 | async-start | bytes 524288 | tf_op jit(solution)/shard_map/all_to_all | solution.py:434
  112.0 3.5 %copy-done.1 = bf16[128,128,256]{2,1,0:T(8,128)(2,1)S(1)} copy-done((bf16[128,128,256]{2,1,0:T(8,128)(2,1)S(1)}, bf16[128,128,256]{2,1,0:T(8,128)(2,1)}, u32[]{:S(2)}) %copy-start.1) | copy-done | bytes 8388632
  118.2 3.1 %all-to-all-done.2.mix_ref = bf16[8,64,256]{2,1,0:T(8,128)(2,1)S(1)} async-done(((bf16[8,64,256]{2,1,0:T(8,128)(2,1)}), bf16[8,64,256]{2,1,0:T(8,128)(2,1)S(1)}, u32[]{:S(2)}, u32[]{:S(2)}) %all-to-all-start.2) | async-done | bytes 262176 | tf_op jit(solution)/shard_map/all_to_all | solution.py:434
  121.3 3.5 %copy-done.2 = bf16[128,128,256]{2,1,0:T(8,128)(2,1)S(1)} copy-done((bf16[128,128,256]{2,1,0:T(8,128)(2,1)S(1)}, bf16[128,128,256]{2,1,0:T(8,128)(2,1)}, u32[]{:S(2)}) %copy-start.2) | copy-done | bytes 8388632
  128.3 8.5 %all-to-all-start.3 = ((bf16[16,16,2048]{2,1,0:T(8,128)(2,1)}), bf16[16,16,2048]{2,1,0:T(8,128)(2,1)S(1)}, u32[]{:S(2)}, u32[]{:S(2)}) async-start(bf16[16,16,2048]{2,1,0:T(8,128)(2,1)} %copy-done.7), calls=%async_computation.3 | async-start | bytes 2097152 | tf_op jit(solution)/shard_map/all_to_all | solution.py:440
  137.1 2.3 %collective-permute-start.22 = (bf16[128,2048]{1,0:T(8,128)(2,1)S(1)}, bf16[128,2048]{1,0:T(8,128)(2,1)}, u32[]{:S(2)}, u32[]{:S(2)}) collective-permute-start(bf16[128,2048]{1,0:T(8,128)(2,1)S(1)} %constant_dynamic-slice_fusion.refs_0_), channel_id=1, source_target_pairs={{0,7},{1,0},{2,1},{3,2},{4,3},{5,4},{6,5},{7,6},{8,15},{9,8},{10,9... | collective-permute-start | bytes 1572872 | tf_op jit(solution)/shard_map/ppermute | solution.py:380
  139.5 13.2 %all-to-all-done.3.second_ref = bf16[16,16,2048]{2,1,0:T(8,128)(2,1)S(1)} async-done(((bf16[16,16,2048]{2,1,0:T(8,128)(2,1)}), bf16[16,16,2048]{2,1,0:T(8,128)(2,1)S(1)}, u32[]{:S(2)}, u32[]{:S(2)}) %all-to-all-start.3) | async-done | bytes 1048608 | tf_op jit(solution)/shard_map/all_to_all | solution.py:440
  152.6 4.9 %all-to-all-start.1 = ((bf16[16,16,2048]{2,1,0:T(8,128)(2,1)}), bf16[16,16,2048]{2,1,0:T(8,128)(2,1)}, u32[]{:S(2)}, u32[]{:S(2)}) async-start(bf16[16,16,2048]{2,1,0:T(8,128)(2,1)} %copy-done.6), calls=%async_computation.1 | async-start | bytes 2097152 | tf_op jit(solution)/shard_map/all_to_all | solution.py:440
  158.0 2.3 %collective-permute-start.24 = (bf16[128,2048]{1,0:T(8,128)(2,1)}, bf16[128,2048]{1,0:T(8,128)(2,1)}, u32[]{:S(2)}, u32[]{:S(2)}) collective-permute-start(bf16[128,2048]{1,0:T(8,128)(2,1)} %collective-permute-done.22.refs_2_), channel_id=1, source_target_pairs={{0,7},{1,0},{2,1},{3,2},{4,3},{5,4},{6,5},{7,6},{8,15},{9,8},{10,9... | collective-permute-start | bytes 1572872 | tf_op jit(solution)/shard_map/ppermute | solution.py:380
  160.9 12.6 %all-to-all-done.1.first_ref = bf16[16,16,2048]{2,1,0:T(8,128)(2,1)} async-done(((bf16[16,16,2048]{2,1,0:T(8,128)(2,1)}), bf16[16,16,2048]{2,1,0:T(8,128)(2,1)}, u32[]{:S(2)}, u32[]{:S(2)}) %all-to-all-start.1) | async-done | bytes 1048608 | tf_op jit(solution)/shard_map/all_to_all | solution.py:440
  174.0 2.3 %collective-permute-start.26 = (bf16[128,2048]{1,0:T(8,128)(2,1)}, bf16[128,2048]{1,0:T(8,128)(2,1)S(1)}, u32[]{:S(2)}, u32[]{:S(2)}) collective-permute-start(bf16[128,2048]{1,0:T(8,128)(2,1)} %collective-permute-done.24.refs_4_), channel_id=1, source_target_pairs={{0,7},{1,0},{2,1},{3,2},{4,3},{5,4},{6,5},{7,6},{8,15},{9,8},{10,9... | collective-permute-start | bytes 1572872 | tf_op jit(solution)/shard_map/ppermute | solution.py:380
  177.6 2.8 %copy-done.16 = bf16[48,256,256]{2,1,0:T(8,128)(2,1)S(1)} copy-done((bf16[48,256,256]{2,1,0:T(8,128)(2,1)S(1)}, bf16[48,256,256]{2,1,0:T(8,128)(2,1)}, u32[]{:S(2)}) %copy-start.16) | copy-done | bytes 6291480
  180.4 7.2 %shard_map.90 = bf16[16,2,32,256]{3,2,1,0:T(8,128)(2,1)S(1)} custom-call(s32[1]{0:T(128)} %dynamic_slice.9.start_ref, bf16[16,16,2048]{2,1,0:T(8,128)(2,1)} %all-to-all-done.1.first_ref, bf16[16,16,2048]{2,1,0:T(8,128)(2,1)S(1)} %copy-done.5, bf16[8,6,256,256]{3,2,1,0:T(8,128)(2,1)S(1)} %bitcast.16), custom_call_target="tpu_custom_call" | custom-call | flops 3221225472 | bytes 9437184 | tf_op jit(solution)/shard_map/pallas_call | solution.py:290
  188.4 5.6 %all-to-all-start.4 = ((bf16[16,2,32,256]{3,2,1,0:T(8,128)(2,1)}), bf16[16,2,32,256]{3,2,1,0:T(8,128)(2,1)S(1)}, u32[]{:S(2)}, u32[]{:S(2)}) async-start(bf16[16,2,32,256]{3,2,1,0:T(8,128)(2,1)} %copy-done.10), calls=%async_computation.4 | async-start | bytes 1048576 | tf_op jit(solution)/shard_map/all_to_all | solution.py:456
  195.5 2.7 %collective-permute-start.28 = (bf16[64,2048]{1,0:T(8,128)(2,1)}, bf16[64,2048]{1,0:T(8,128)(2,1)}, u32[]{:S(2)}, u32[]{:S(2)}) collective-permute-start(bf16[64,2048]{1,0:T(8,128)(2,1)} %slice.9), channel_id=1, source_target_pairs={{0,7},{1,0},{2,1},{3,2},{4,3},{5,4},{6,5},{7,6},{8,15},{9,8},{10,9... | collective-permute-start | bytes 786440 | tf_op jit(solution)/shard_map/ppermute | solution.py:380
  198.3 5.6 %all-to-all-done.4.mix_ref = bf16[16,2,32,256]{3,2,1,0:T(8,128)(2,1)S(1)} async-done(((bf16[16,2,32,256]{3,2,1,0:T(8,128)(2,1)}), bf16[16,2,32,256]{3,2,1,0:T(8,128)(2,1)S(1)}, u32[]{:S(2)}, u32[]{:S(2)}) %all-to-all-start.4) | async-done | bytes 524320 | tf_op jit(solution)/shard_map/all_to_all | solution.py:456
  205.2 2.9 %shard_map.91 = (f32[128,2048]{1,0:T(8,128)S(1)}, bf16[128,2048]{1,0:T(8,128)(2,1)S(1)}) custom-call(s32[2]{0:T(128)S(1)} %pad_add_fusion.place_ref, bf16[16,2,32,256]{3,2,1,0:T(8,128)(2,1)S(1)} %all-to-all-done.4.mix_ref, bf16[128,2048]{1,0:T(8,128)(2,1)S(1)} %constant_dynamic-slice_fusion.refs_0_, bf16[128,2048]{1,0:T(8,128)(2,1)S(1)} %copy-done.9, ...), custom_call_target="tpu_custom_call" | custom-call | flops 1073741824 | bytes 8388608 | tf_op jit(solution)/shard_map/pallas_call | solution.py:335
  (99 shorter events, 47.2 us)
Async XLA Ops:
  6.5 105.4 %all-gather.5.cloned.1.call-start = ((), (), s32[]{:S(2)}) async-start(), calls=%async_computation.5 | async-start | bytes 8650752 | tf_op jit(solution)/shard_map/all_gather | solution.py:413
  7.5 18.1 %collective-permute-start = (bf16[128,256]{1,0:T(8,128)(2,1)S(1)}, bf16[128,256]{1,0:T(8,128)(2,1)S(1)}, u32[]{:S(2)}, u32[]{:S(2)}) collective-permute-start(bf16[128,256]{1,0:T(8,128)(2,1)S(1)} %dynamic_slice.10), channel_id=1, source_target_pairs={{0,0},{1,1},{2,2},{3,3},{4,12},{5,13},{6,14},{7,15},{8,4},{9,5},{1... | collective-permute-start | bytes 196616 | tf_op jit(solution)/shard_map/ppermute | solution.py:410
  26.3 147.2 %all-gather.7.cloned.1.call-start = ((), (), s32[]{:S(2)}) async-start(), calls=%async_computation.6 | async-start | bytes 7077888 | tf_op jit(solution)/shard_map/all_gather | solution.py:428
  26.4 11.4 %collective-permute-start.4 = (bf16[80,2048]{1,0:T(8,128)(2,1)S(1)}, bf16[80,2048]{1,0:T(8,128)(2,1)S(1)}, u32[]{:S(2)}, u32[]{:S(2)}) collective-permute-start(bf16[80,2048]{1,0:T(8,128)(2,1)S(1)} %get-tuple-element.54.refs_0_), channel_id=1, source_target_pairs={{0,1},{1,2},{2,3},{3,4},{4,5},{5,6},{6,7},{7,0},{8,9},{9,10},{10,1... | collective-permute-start | bytes 983048 | tf_op jit(solution)/shard_map/ppermute | solution.py:380
  30.0 9.3 %collective-permute-start.12 = (bf16[80,2048]{1,0:T(8,128)(2,1)S(1)}, bf16[80,2048]{1,0:T(8,128)(2,1)S(1)}, u32[]{:S(2)}, u32[]{:S(2)}) collective-permute-start(bf16[80,2048]{1,0:T(8,128)(2,1)S(1)} %get-tuple-element.63.refs_0_.refs_1_), channel_id=1, source_target_pairs={{0,7},{1,0},{2,1},{3,2},{4,3},{5,4},{6,5},{7,6},{8,15},{9,8},{10,9... | collective-permute-start | bytes 983048 | tf_op jit(solution)/shard_map/ppermute | solution.py:380
  30.0 14.8 %collective-permute-start.11 = (bf16[80,2048]{1,0:T(8,128)(2,1)S(1)}, bf16[80,2048]{1,0:T(8,128)(2,1)S(1)}, u32[]{:S(2)}, u32[]{:S(2)}) collective-permute-start(bf16[80,2048]{1,0:T(8,128)(2,1)S(1)} %get-tuple-element.63.refs_0_.refs_1_), channel_id=1, source_target_pairs={{0,1},{1,2},{2,3},{3,4},{4,5},{5,6},{6,7},{7,0},{8,9},{9,10},{10,1... | collective-permute-start | bytes 983048 | tf_op jit(solution)/shard_map/ppermute | solution.py:380
  31.5 14.9 %collective-permute-start.5 = (bf16[80,2048]{1,0:T(8,128)(2,1)S(1)}, bf16[80,2048]{1,0:T(8,128)(2,1)S(1)}, u32[]{:S(2)}, u32[]{:S(2)}) collective-permute-start(bf16[80,2048]{1,0:T(8,128)(2,1)S(1)} %get-tuple-element.54.refs_0_), channel_id=1, source_target_pairs={{0,7},{1,0},{2,1},{3,2},{4,3},{5,4},{6,5},{7,6},{8,15},{9,8},{10,9... | collective-permute-start | bytes 983048 | tf_op jit(solution)/shard_map/ppermute | solution.py:380
  37.8 14.0 %collective-permute-start.6 = (bf16[80,2048]{1,0:T(8,128)(2,1)S(1)}, bf16[80,2048]{1,0:T(8,128)(2,1)S(1)}, u32[]{:S(2)}, u32[]{:S(2)}) collective-permute-start(bf16[80,2048]{1,0:T(8,128)(2,1)S(1)} %collective-permute-done.4.refs_1_.refs_2_), channel_id=1, source_target_pairs={{0,1},{1,2},{2,3},{3,4},{4,5},{5,6},{6,7},{7,0},{8,9},{9,10},{10,1... | collective-permute-start | bytes 983048 | tf_op jit(solution)/shard_map/ppermute | solution.py:380
  39.3 14.0 %collective-permute-start.14 = (bf16[80,2048]{1,0:T(8,128)(2,1)S(1)}, bf16[80,2048]{1,0:T(8,128)(2,1)S(1)}, u32[]{:S(2)}, u32[]{:S(2)}) collective-permute-start(bf16[80,2048]{1,0:T(8,128)(2,1)S(1)} %collective-permute-done.12.refs_2_.refs_5_), channel_id=1, source_target_pairs={{0,7},{1,0},{2,1},{3,2},{4,3},{5,4},{6,5},{7,6},{8,15},{9,8},{10,9... | collective-permute-start | bytes 983048 | tf_op jit(solution)/shard_map/ppermute | solution.py:380
  44.8 14.0 %collective-permute-start.13 = (bf16[80,2048]{1,0:T(8,128)(2,1)S(1)}, bf16[80,2048]{1,0:T(8,128)(2,1)S(1)}, u32[]{:S(2)}, u32[]{:S(2)}) collective-permute-start(bf16[80,2048]{1,0:T(8,128)(2,1)S(1)} %collective-permute-done.11.refs_1_.refs_3_), channel_id=1, source_target_pairs={{0,1},{1,2},{2,3},{3,4},{4,5},{5,6},{6,7},{7,0},{8,9},{9,10},{10,1... | collective-permute-start | bytes 983048 | tf_op jit(solution)/shard_map/ppermute | solution.py:380
  46.4 13.9 %collective-permute-start.7 = (bf16[80,2048]{1,0:T(8,128)(2,1)S(1)}, bf16[80,2048]{1,0:T(8,128)(2,1)S(1)}, u32[]{:S(2)}, u32[]{:S(2)}) collective-permute-start(bf16[80,2048]{1,0:T(8,128)(2,1)S(1)} %collective-permute-done.5.refs_2_.refs_4_), channel_id=1, source_target_pairs={{0,7},{1,0},{2,1},{3,2},{4,3},{5,4},{6,5},{7,6},{8,15},{9,8},{10,9... | collective-permute-start | bytes 983048 | tf_op jit(solution)/shard_map/ppermute | solution.py:380
  51.8 14.0 %collective-permute-start.8 = (bf16[80,2048]{1,0:T(8,128)(2,1)S(1)}, bf16[80,2048]{1,0:T(8,128)(2,1)S(1)}, u32[]{:S(2)}, u32[]{:S(2)}) collective-permute-start(bf16[80,2048]{1,0:T(8,128)(2,1)S(1)} %collective-permute-done.6.refs_3_.refs_6_), channel_id=1, source_target_pairs={{0,1},{1,2},{2,3},{3,4},{4,5},{5,6},{6,7},{7,0},{8,9},{9,10},{10,1... | collective-permute-start | bytes 983048 | tf_op jit(solution)/shard_map/ppermute | solution.py:380
  53.3 14.0 %collective-permute-start.16 = (bf16[80,2048]{1,0:T(8,128)(2,1)S(1)}, bf16[80,2048]{1,0:T(8,128)(2,1)S(1)}, u32[]{:S(2)}, u32[]{:S(2)}) collective-permute-start(bf16[80,2048]{1,0:T(8,128)(2,1)S(1)} %collective-permute-done.14.refs_4_.refs_9_), channel_id=1, source_target_pairs={{0,7},{1,0},{2,1},{3,2},{4,3},{5,4},{6,5},{7,6},{8,15},{9,8},{10,9... | collective-permute-start | bytes 983048 | tf_op jit(solution)/shard_map/ppermute | solution.py:380
  58.8 14.1 %collective-permute-start.15 = (bf16[80,2048]{1,0:T(8,128)(2,1)S(1)}, bf16[80,2048]{1,0:T(8,128)(2,1)S(1)}, u32[]{:S(2)}, u32[]{:S(2)}) collective-permute-start(bf16[80,2048]{1,0:T(8,128)(2,1)S(1)} %collective-permute-done.13.refs_3_.refs_7_), channel_id=1, source_target_pairs={{0,1},{1,2},{2,3},{3,4},{4,5},{5,6},{6,7},{7,0},{8,9},{9,10},{10,1... | collective-permute-start | bytes 983048 | tf_op jit(solution)/shard_map/ppermute | solution.py:380
  60.3 13.8 %collective-permute-start.9 = (bf16[80,2048]{1,0:T(8,128)(2,1)S(1)}, bf16[80,2048]{1,0:T(8,128)(2,1)S(1)}, u32[]{:S(2)}, u32[]{:S(2)}) collective-permute-start(bf16[80,2048]{1,0:T(8,128)(2,1)S(1)} %collective-permute-done.7.refs_4_.refs_8_), channel_id=1, source_target_pairs={{0,7},{1,0},{2,1},{3,2},{4,3},{5,4},{6,5},{7,6},{8,15},{9,8},{10,9... | collective-permute-start | bytes 983048 | tf_op jit(solution)/shard_map/ppermute | solution.py:380
  65.9 14.1 %collective-permute-start.10 = (bf16[80,2048]{1,0:T(8,128)(2,1)S(1)}, bf16[80,2048]{1,0:T(8,128)(2,1)S(1)}, u32[]{:S(2)}, u32[]{:S(2)}) collective-permute-start(bf16[80,2048]{1,0:T(8,128)(2,1)S(1)} %collective-permute-done.8.refs_5_.refs_10_), channel_id=1, source_target_pairs={{0,1},{1,2},{2,3},{3,4},{4,5},{5,6},{6,7},{7,0},{8,9},{9,10},{10,1... | collective-permute-start | bytes 983048 | tf_op jit(solution)/shard_map/ppermute | solution.py:380
  67.3 13.8 %collective-permute-start.17 = (bf16[80,2048]{1,0:T(8,128)(2,1)S(1)}, bf16[80,2048]{1,0:T(8,128)(2,1)S(1)}, u32[]{:S(2)}, u32[]{:S(2)}) collective-permute-start(bf16[80,2048]{1,0:T(8,128)(2,1)S(1)} %collective-permute-done.16.refs_6_.refs_13_), channel_id=1, source_target_pairs={{0,7},{1,0},{2,1},{3,2},{4,3},{5,4},{6,5},{7,6},{8,15},{9,8},{10,9... | collective-permute-start | bytes 983048 | tf_op jit(solution)/shard_map/ppermute | solution.py:380
  82.0 12.5 %collective-permute-start.18 = (bf16[2,3,64,256]{3,2,1,0:T(8,128)(2,1)S(1)}, bf16[2,3,64,256]{3,2,1,0:T(8,128)(2,1)S(1)}, u32[]{:S(2)}, u32[]{:S(2)}) collective-permute-start(bf16[2,3,64,256]{3,2,1,0:T(8,128)(2,1)S(1)} %get-tuple-element.72), channel_id=1, source_target_pairs={{0,16},{16,32},{32,48},{48,0},{1,17},{17,33},{33,49},{49,1},{2,18}... | collective-permute-start | bytes 589832 | tf_op jit(solution)/shard_map/ppermute | solution.py:380
  83.4 11.1 %collective-permute-start.19 = (bf16[2,3,64,256]{3,2,1,0:T(8,128)(2,1)S(1)}, bf16[2,3,64,256]{3,2,1,0:T(8,128)(2,1)S(1)}, u32[]{:S(2)}, u32[]{:S(2)}) collective-permute-start(bf16[2,3,64,256]{3,2,1,0:T(8,128)(2,1)S(1)} %get-tuple-element.73), channel_id=1, source_target_pairs={{0,32},{16,48},{32,0},{48,16},{1,33},{17,49},{33,1},{49,17},{2,34}... | collective-permute-start | bytes 589832 | tf_op jit(solution)/shard_map/ppermute | solution.py:380
  86.0 8.5 %collective-permute-start.20 = (bf16[2,3,64,256]{3,2,1,0:T(8,128)(2,1)S(1)}, bf16[2,3,64,256]{3,2,1,0:T(8,128)(2,1)S(1)}, u32[]{:S(2)}, u32[]{:S(2)}) collective-permute-start(bf16[2,3,64,256]{3,2,1,0:T(8,128)(2,1)S(1)} %get-tuple-element.74), channel_id=1, source_target_pairs={{0,48},{16,0},{32,16},{48,32},{1,49},{17,1},{33,17},{49,33},{2,50}... | collective-permute-start | bytes 589832 | tf_op jit(solution)/shard_map/ppermute | solution.py:380
  108.5 12.8 %all-to-all-start.2 = ((bf16[8,64,256]{2,1,0:T(8,128)(2,1)}), bf16[8,64,256]{2,1,0:T(8,128)(2,1)S(1)}, u32[]{:S(2)}, u32[]{:S(2)}) async-start(bf16[8,64,256]{2,1,0:T(8,128)(2,1)} %shard_map.86), calls=%async_computation.2 | async-start | bytes 524288 | tf_op jit(solution)/shard_map/all_to_all | solution.py:434
  128.3 24.4 %all-to-all-start.3 = ((bf16[16,16,2048]{2,1,0:T(8,128)(2,1)}), bf16[16,16,2048]{2,1,0:T(8,128)(2,1)S(1)}, u32[]{:S(2)}, u32[]{:S(2)}) async-start(bf16[16,16,2048]{2,1,0:T(8,128)(2,1)} %copy-done.7), calls=%async_computation.3 | async-start | bytes 2097152 | tf_op jit(solution)/shard_map/all_to_all | solution.py:440
  136.8 20.8 %collective-permute-start.21 = (bf16[128,2048]{1,0:T(8,128)(2,1)S(1)}, bf16[128,2048]{1,0:T(8,128)(2,1)S(1)}, u32[]{:S(2)}, u32[]{:S(2)}) collective-permute-start(bf16[128,2048]{1,0:T(8,128)(2,1)S(1)} %constant_dynamic-slice_fusion.refs_0_), channel_id=1, source_target_pairs={{0,1},{1,2},{2,3},{3,4},{4,5},{5,6},{6,7},{7,0},{8,9},{9,10},{10,1... | collective-permute-start | bytes 1572872 | tf_op jit(solution)/shard_map/ppermute | solution.py:380
  137.1 20.4 %collective-permute-start.22 = (bf16[128,2048]{1,0:T(8,128)(2,1)S(1)}, bf16[128,2048]{1,0:T(8,128)(2,1)}, u32[]{:S(2)}, u32[]{:S(2)}) collective-permute-start(bf16[128,2048]{1,0:T(8,128)(2,1)S(1)} %constant_dynamic-slice_fusion.refs_0_), channel_id=1, source_target_pairs={{0,7},{1,0},{2,1},{3,2},{4,3},{5,4},{6,5},{7,6},{8,15},{9,8},{10,9... | collective-permute-start | bytes 1572872 | tf_op jit(solution)/shard_map/ppermute | solution.py:380
  152.6 20.9 %all-to-all-start.1 = ((bf16[16,16,2048]{2,1,0:T(8,128)(2,1)}), bf16[16,16,2048]{2,1,0:T(8,128)(2,1)}, u32[]{:S(2)}, u32[]{:S(2)}) async-start(bf16[16,16,2048]{2,1,0:T(8,128)(2,1)} %copy-done.6), calls=%async_computation.1 | async-start | bytes 2097152 | tf_op jit(solution)/shard_map/all_to_all | solution.py:440
  157.6 16.0 %collective-permute-start.23 = (bf16[128,2048]{1,0:T(8,128)(2,1)S(1)}, bf16[128,2048]{1,0:T(8,128)(2,1)}, u32[]{:S(2)}, u32[]{:S(2)}) collective-permute-start(bf16[128,2048]{1,0:T(8,128)(2,1)S(1)} %collective-permute-done.21.refs_1_), channel_id=1, source_target_pairs={{0,1},{1,2},{2,3},{3,4},{4,5},{5,6},{6,7},{7,0},{8,9},{9,10},{10,1... | collective-permute-start | bytes 1572872 | tf_op jit(solution)/shard_map/ppermute | solution.py:380
  158.0 15.6 %collective-permute-start.24 = (bf16[128,2048]{1,0:T(8,128)(2,1)}, bf16[128,2048]{1,0:T(8,128)(2,1)}, u32[]{:S(2)}, u32[]{:S(2)}) collective-permute-start(bf16[128,2048]{1,0:T(8,128)(2,1)} %collective-permute-done.22.refs_2_), channel_id=1, source_target_pairs={{0,7},{1,0},{2,1},{3,2},{4,3},{5,4},{6,5},{7,6},{8,15},{9,8},{10,9... | collective-permute-start | bytes 1572872 | tf_op jit(solution)/shard_map/ppermute | solution.py:380
  173.6 20.4 %collective-permute-start.25 = (bf16[128,2048]{1,0:T(8,128)(2,1)}, bf16[128,2048]{1,0:T(8,128)(2,1)S(1)}, u32[]{:S(2)}, u32[]{:S(2)}) collective-permute-start(bf16[128,2048]{1,0:T(8,128)(2,1)} %collective-permute-done.23.refs_3_), channel_id=1, source_target_pairs={{0,1},{1,2},{2,3},{3,4},{4,5},{5,6},{6,7},{7,0},{8,9},{9,10},{10,1... | collective-permute-start | bytes 1572872 | tf_op jit(solution)/shard_map/ppermute | solution.py:380
  174.0 20.8 %collective-permute-start.26 = (bf16[128,2048]{1,0:T(8,128)(2,1)}, bf16[128,2048]{1,0:T(8,128)(2,1)S(1)}, u32[]{:S(2)}, u32[]{:S(2)}) collective-permute-start(bf16[128,2048]{1,0:T(8,128)(2,1)} %collective-permute-done.24.refs_4_), channel_id=1, source_target_pairs={{0,7},{1,0},{2,1},{3,2},{4,3},{5,4},{6,5},{7,6},{8,15},{9,8},{10,9... | collective-permute-start | bytes 1572872 | tf_op jit(solution)/shard_map/ppermute | solution.py:380
  188.4 15.4 %all-to-all-start.4 = ((bf16[16,2,32,256]{3,2,1,0:T(8,128)(2,1)}), bf16[16,2,32,256]{3,2,1,0:T(8,128)(2,1)S(1)}, u32[]{:S(2)}, u32[]{:S(2)}) async-start(bf16[16,2,32,256]{3,2,1,0:T(8,128)(2,1)} %copy-done.10), calls=%async_computation.4 | async-start | bytes 1048576 | tf_op jit(solution)/shard_map/all_to_all | solution.py:456
  194.8 9.4 %collective-permute-start.27 = (bf16[64,2048]{1,0:T(8,128)(2,1)}, bf16[64,2048]{1,0:T(8,128)(2,1)}, u32[]{:S(2)}, u32[]{:S(2)}) collective-permute-start(bf16[64,2048]{1,0:T(8,128)(2,1)} %slice.8), channel_id=1, source_target_pairs={{0,1},{1,2},{2,3},{3,4},{4,5},{5,6},{6,7},{7,0},{8,9},{9,10},{10,1... | collective-permute-start | bytes 786440 | tf_op jit(solution)/shard_map/ppermute | solution.py:380
  195.5 8.7 %collective-permute-start.28 = (bf16[64,2048]{1,0:T(8,128)(2,1)}, bf16[64,2048]{1,0:T(8,128)(2,1)}, u32[]{:S(2)}, u32[]{:S(2)}) collective-permute-start(bf16[64,2048]{1,0:T(8,128)(2,1)} %slice.9), channel_id=1, source_target_pairs={{0,7},{1,0},{2,1},{3,2},{4,3},{5,4},{6,5},{7,6},{8,15},{9,8},{10,9... | collective-permute-start | bytes 786440 | tf_op jit(solution)/shard_map/ppermute | solution.py:380
  (23 other events, 260.6 us)
Sparse Core Ops, SparseCore 0:
  26.5 59.9 all-gather.4
  95.6 42.0 all-gather.6

commit v9 on v7

--- a/solution.py
+++ b/solution.py
@@ -416,9 +416,8 @@
 
     weight = jnp.transpose(spatial_qkv, (1, 0, 2))
     mix = spatial_attend(z.reshape(1), weight, pieces)
-    mix, *got = lax.optimization_barrier((mix, *got))
+    mix, whole_out = lax.optimization_barrier((mix, whole_out))
     quarter = join_shares(y.reshape(1), got)
-    mix, quarter, whole_out = lax.optimization_barrier((mix, quarter, whole_out))
     quarter = lax.all_gather(quarter[None], ("w", "xl", "c"), axis=0, tiled=True)
     mix = lax.all_to_all(mix, "z", 0, 0, tiled=True)
 
@@ -434,7 +433,7 @@
     halves += [shifted(up[:64], "z", 1), shifted(down[64:], "z", -1)]
 
     window = lax.all_to_all(send, ("xl", "y", "c"), 0, 0, tiled=True)
-    window, *halves[1:5] = lax.optimization_barrier((window, *halves[1:5]))
+    window, *halves[1:3] = lax.optimization_barrier((window, *halves[1:3]))
     start = lax.dynamic_slice(starts, (w,), (1,))
     mix = temporal_attend(start, window.reshape(512, width), quarter)
     mix = lax.all_to_all(mix, ("xl", "y", "c"), 0, 0, tiled=True)

time: 206 us -> 226 us (1.097)
  waiting for transfers between devices: 81.5 us -> 96.7 us
  local copies, waits for them, and re-layouts: 19 us -> 32.5 us
  starting transfers between devices: 70 us -> 60.7 us
    unnamed x38 -> x82, local copies, waits for them, and re-layouts: 17.4 us -> 30.9 us
    ppermute x26, waiting for transfers between devices: 65.8 us -> 76.5 us  [shifted(): lax.ppermute(value, axis, [(i, (i + step) % count) for i in range(count)])]
    ppermute x26, starting transfers between devices: 36.9 us -> 31 us  [shifted(): lax.ppermute(value, axis, [(i, (i + step) % count) for i in range(count)])]
    all_to_all x1, waiting for transfers between devices: 15.6 us -> 17.9 us  [local(): mix = lax.all_to_all(mix, 'z', 0, 0, tiled=True)]
  transfers between devices with their start and end apart: 35 -> 35, of which waited for: 15 -> 19; matrix products, arithmetic and copies ran while one was open for 0% -> 0% of each run, Pallas kernels for 8% -> 7%
where the time goes in v9:
time: 226 us; the launch traced here: 225 us
  waiting for transfers between devices  96.7 us (43%)
  starting transfers between devices  60.7 us (27%)
  local copies, waits for them, and re-layouts  32.5 us (14%)
  Pallas kernels  21.3 us (9%)
  between operations  13.7 us (6%)
    ppermute x26, waiting for transfers between devices, shifted(): lax.ppermute(value, axis, [(i, (i + step) % count) for i in range(count)])  76.5 us
    ppermute x26, starting transfers between devices, shifted(): lax.ppermute(value, axis, [(i, (i + step) % count) for i in range(count)])  31 us
    unnamed x82, local copies, waits for them, and re-layouts  30.9 us
    all_to_all x1, waiting for transfers between devices, local(): mix = lax.all_to_all(mix, 'z', 0, 0, tiled=True)  17.9 us
    ppermute x4, starting transfers between devices, local(): parts.append(lax.ppermute(block, ('c', 'z'), pairs))  11.8 us
    pallas_call x1, Pallas kernels, temporal_attend(): pl.pallas_call(temporal_kernel, out_shape=jax.ShapeDtypeStruct((16, 2, 32...  7.6 us
    all_to_all x1, starting transfers between devices, local(): mix = lax.all_to_all(mix, ('xl', 'y', 'c'), 0, 0, tiled=True)  6.88 us
    all_to_all x1, starting transfers between devices, local(): mix = lax.all_to_all(mix, 'z', 0, 0, tiled=True)  5.82 us
  transfers between devices with their start and end apart: 35, of which 19 were waited for; matrix products, arithmetic and copies ran while one was open for 0% of the time, Pallas kernels for 7%

profile of v9, /device:TPU:1, one launch (start us, length us, event | category | flops | bytes accessed | tf_op | source)
XLA Modules:
  0.0 225.1 jit_solution(6133487327715466805)
XLA Ops:
  7.5 7.0 %collective-permute-start.3 = (bf16[128,256]{1,0:T(8,128)(2,1)S(1)}, bf16[128,256]{1,0:T(8,128)(2,1)S(1)}, u32[]{:S(2)}, u32[]{:S(2)}) collective-permute-start(bf16[128,256]{1,0:T(8,128)(2,1)S(1)} %dynamic_slice.10), channel_id=1, source_target_pairs={{0,3},{1,4},{2,5},{3,6},{4,15},{5,8},{6,9},{7,10},{8,7},{9,0},{10,... | collective-permute-start | bytes 196616 | tf_op jit(solution)/shard_map/ppermute | solution.py:406
  17.0 2.3 %collective-permute-start = (bf16[128,256]{1,0:T(8,128)(2,1)S(1)}, bf16[128,256]{1,0:T(8,128)(2,1)S(1)}, u32[]{:S(2)}, u32[]{:S(2)}) collective-permute-start(bf16[128,256]{1,0:T(8,128)(2,1)S(1)} %dynamic_slice.10), channel_id=1, source_target_pairs={{0,0},{1,1},{2,2},{3,3},{4,12},{5,13},{6,14},{7,15},{8,4},{9,5},{1... | collective-permute-start | bytes 196616 | tf_op jit(solution)/shard_map/ppermute | solution.py:406
  26.7 2.7 %collective-permute-start.4 = (bf16[80,2048]{1,0:T(8,128)(2,1)S(1)}, bf16[80,2048]{1,0:T(8,128)(2,1)S(1)}, u32[]{:S(2)}, u32[]{:S(2)}) collective-permute-start(bf16[80,2048]{1,0:T(8,128)(2,1)S(1)} %get-tuple-element.31.refs_0_), channel_id=1, source_target_pairs={{0,1},{1,2},{2,3},{3,4},{4,5},{5,6},{6,7},{7,0},{8,9},{9,10},{10,1... | collective-permute-start | bytes 983048 | tf_op jit(solution)/shard_map/ppermute | solution.py:376
  31.4 6.8 %collective-permute-done.4.refs_2_ = bf16[80,2048]{1,0:T(8,128)(2,1)S(1)} collective-permute-done((bf16[80,2048]{1,0:T(8,128)(2,1)S(1)}, bf16[80,2048]{1,0:T(8,128)(2,1)S(1)}, u32[]{:S(2)}, u32[]{:S(2)}) %collective-permute-start.4) | collective-permute-done | bytes 327712 | tf_op jit(solution)/shard_map/ppermute | solution.py:376
  40.9 4.9 %collective-permute-done.6.refs_4_ = bf16[80,2048]{1,0:T(8,128)(2,1)S(1)} collective-permute-done((bf16[80,2048]{1,0:T(8,128)(2,1)S(1)}, bf16[80,2048]{1,0:T(8,128)(2,1)S(1)}, u32[]{:S(2)}, u32[]{:S(2)}) %collective-permute-start.6) | collective-permute-done | bytes 327712 | tf_op jit(solution)/shard_map/ppermute | solution.py:376
  47.9 2.6 %collective-permute-done.8.refs_6_ = bf16[80,2048]{1,0:T(8,128)(2,1)S(1)} collective-permute-done((bf16[80,2048]{1,0:T(8,128)(2,1)S(1)}, bf16[80,2048]{1,0:T(8,128)(2,1)S(1)}, u32[]{:S(2)}, u32[]{:S(2)}) %collective-permute-start.8) | collective-permute-done | bytes 327712 | tf_op jit(solution)/shard_map/ppermute | solution.py:376
  50.5 2.3 %collective-permute-done.11.refs_9_ = bf16[80,2048]{1,0:T(8,128)(2,1)S(1)} collective-permute-done((bf16[80,2048]{1,0:T(8,128)(2,1)S(1)}, bf16[80,2048]{1,0:T(8,128)(2,1)S(1)}, u32[]{:S(2)}, u32[]{:S(2)}) %collective-permute-start.11) | collective-permute-done | bytes 327712 | tf_op jit(solution)/shard_map/ppermute | solution.py:376
  52.8 2.2 collective-permute-start.15
  55.0 4.7 %collective-permute-done.10.refs_8_ = bf16[80,2048]{1,0:T(8,128)(2,1)S(1)} collective-permute-done((bf16[80,2048]{1,0:T(8,128)(2,1)S(1)}, bf16[80,2048]{1,0:T(8,128)(2,1)S(1)}, u32[]{:S(2)}, u32[]{:S(2)}) %collective-permute-start.10) | collective-permute-done | bytes 327712 | tf_op jit(solution)/shard_map/ppermute | solution.py:376
  59.7 2.2 collective-permute-start.14
  62.0 2.6 %collective-permute-done.12.refs_10_ = bf16[80,2048]{1,0:T(8,128)(2,1)S(1)} collective-permute-done((bf16[80,2048]{1,0:T(8,128)(2,1)S(1)}, bf16[80,2048]{1,0:T(8,128)(2,1)S(1)}, u32[]{:S(2)}, u32[]{:S(2)}) %collective-permute-start.12) | collective-permute-done | bytes 327712 | tf_op jit(solution)/shard_map/ppermute | solution.py:376
  64.6 2.3 %collective-permute-done.15.refs_13_ = bf16[80,2048]{1,0:T(8,128)(2,1)S(1)} collective-permute-done((bf16[80,2048]{1,0:T(8,128)(2,1)S(1)}, bf16[80,2048]{1,0:T(8,128)(2,1)S(1)}, u32[]{:S(2)}, u32[]{:S(2)}) %collective-permute-start.15) | collective-permute-done | bytes 327712 | tf_op jit(solution)/shard_map/ppermute | solution.py:376
  69.1 4.5 %collective-permute-done.14.refs_12_ = bf16[80,2048]{1,0:T(8,128)(2,1)S(1)} collective-permute-done((bf16[80,2048]{1,0:T(8,128)(2,1)S(1)}, bf16[80,2048]{1,0:T(8,128)(2,1)S(1)}, u32[]{:S(2)}, u32[]{:S(2)}) %collective-permute-start.14) | collective-permute-done | bytes 327712 | tf_op jit(solution)/shard_map/ppermute | solution.py:376
  73.5 5.5 %collective-permute-done.16.refs_14_ = bf16[80,2048]{1,0:T(8,128)(2,1)S(1)} collective-permute-done((bf16[80,2048]{1,0:T(8,128)(2,1)S(1)}, bf16[80,2048]{1,0:T(8,128)(2,1)S(1)}, u32[]{:S(2)}, u32[]{:S(2)}) %collective-permute-start.16) | collective-permute-done | bytes 327712 | tf_op jit(solution)/shard_map/ppermute | solution.py:376
  81.9 2.6 %collective-permute-start.21 = (bf16[2,3,64,256]{3,2,1,0:T(8,128)(2,1)S(1)}, bf16[2,3,64,256]{3,2,1,0:T(8,128)(2,1)S(1)}, u32[]{:S(2)}, u32[]{:S(2)}) collective-permute-start(bf16[2,3,64,256]{3,2,1,0:T(8,128)(2,1)S(1)} %get-tuple-element.46), channel_id=1, source_target_pairs={{0,32},{16,48},{32,0},{48,16},{1,33},{17,49},{33,1},{49,17},{2,34}... | collective-permute-start | bytes 589832 | tf_op jit(solution)/shard_map/ppermute | solution.py:376
  85.6 2.6 %collective-permute-done.20.refs_1_ = bf16[2,3,64,256]{3,2,1,0:T(8,128)(2,1)S(1)} collective-permute-done((bf16[2,3,64,256]{3,2,1,0:T(8,128)(2,1)S(1)}, bf16[2,3,64,256]{3,2,1,0:T(8,128)(2,1)S(1)}, u32[]{:S(2)}, u32[]{:S(2)}) %collective-permute-start.20) | collective-permute-done | bytes 196640 | tf_op jit(solution)/shard_map/ppermute | solution.py:376
  88.2 5.4 %collective-permute-done.21.refs_2_ = bf16[2,3,64,256]{3,2,1,0:T(8,128)(2,1)S(1)} collective-permute-done((bf16[2,3,64,256]{3,2,1,0:T(8,128)(2,1)S(1)}, bf16[2,3,64,256]{3,2,1,0:T(8,128)(2,1)S(1)}, u32[]{:S(2)}, u32[]{:S(2)}) %collective-permute-start.21) | collective-permute-done | bytes 196640 | tf_op jit(solution)/shard_map/ppermute | solution.py:376
  107.4 5.2 %shard_map.83 = bf16[8,128,256]{2,1,0:T(8,128)(2,1)} custom-call(s32[1]{0:T(128)} %bitcast.place_ref.z_ref, bf16[3,2048,256]{2,1,0:T(8,128)(2,1)S(1)} %bitcast.16, bf16[80,2048]{1,0:T(8,128)(2,1)S(1)} %get-tuple-element.31.refs_0_, bf16[80,2048]{1,0:T(8,128)(2,1)S(1)} %get-tuple-element.32.refs_1_, bf16[80,2048]{1,0:T(8,128)(2,1)S(1)} %collective-permute-done.4.refs_2_, ...), custom_call_target="tpu_custom_call" | custom-call | flops 6442450944 | bytes 8388608 | tf_op jit(solution)/shard_map/pallas_call | solution.py:184
  112.7 5.8 %all-to-all-start = ((bf16[8,128,256]{2,1,0:T(8,128)(2,1)}), bf16[8,128,256]{2,1,0:T(8,128)(2,1)S(1)}, u32[]{:S(2)}, u32[]{:S(2)}) async-start(bf16[8,128,256]{2,1,0:T(8,128)(2,1)} %shard_map.83), calls=%async_computation | async-start | bytes 1048576 | tf_op jit(solution)/shard_map/all_to_all | solution.py:422
  118.5 17.9 %all-to-all-done.mix_ref = bf16[8,128,256]{2,1,0:T(8,128)(2,1)S(1)} async-done(((bf16[8,128,256]{2,1,0:T(8,128)(2,1)}), bf16[8,128,256]{2,1,0:T(8,128)(2,1)S(1)}, u32[]{:S(2)}, u32[]{:S(2)}) %all-to-all-start) | async-done | bytes 524320 | tf_op jit(solution)/shard_map/all_to_all | solution.py:422
  136.4 3.4 %copy-done.1 = bf16[128,128,256]{2,1,0:T(8,128)(2,1)S(1)} copy-done((bf16[128,128,256]{2,1,0:T(8,128)(2,1)S(1)}, bf16[128,128,256]{2,1,0:T(8,128)(2,1)}, u32[]{:S(2)}) %copy-start.1) | copy-done | bytes 8388632
  143.5 5.1 %all-to-all-start.1 = ((bf16[16,32,2048]{2,1,0:T(8,128)(2,1)}), bf16[16,32,2048]{2,1,0:T(8,128)(2,1)}, u32[]{:S(2)}, u32[]{:S(2)}) async-start(bf16[16,32,2048]{2,1,0:T(8,128)(2,1)} %copy-done.3), calls=%async_computation.1 | async-start | bytes 4194304 | tf_op jit(solution)/shard_map/all_to_all | solution.py:435
  150.1 11.9 %collective-permute-done.19.refs_2_ = bf16[128,2048]{1,0:T(8,128)(2,1)S(1)} collective-permute-done((bf16[128,2048]{1,0:T(8,128)(2,1)S(1)}, bf16[128,2048]{1,0:T(8,128)(2,1)S(1)}, u32[]{:S(2)}, u32[]{:S(2)}) %collective-permute-start.19) | collective-permute-done | bytes 524320 | tf_op jit(solution)/shard_map/ppermute | solution.py:376
  165.0 9.7 %collective-permute-done.24.refs_4_ = bf16[128,2048]{1,0:T(8,128)(2,1)} collective-permute-done((bf16[128,2048]{1,0:T(8,128)(2,1)S(1)}, bf16[128,2048]{1,0:T(8,128)(2,1)}, u32[]{:S(2)}, u32[]{:S(2)}) %collective-permute-start.24) | collective-permute-done | bytes 524320 | tf_op jit(solution)/shard_map/ppermute | solution.py:376
  174.7 3.1 %collective-permute-start.26 = (bf16[128,2048]{1,0:T(8,128)(2,1)}, bf16[128,2048]{1,0:T(8,128)(2,1)S(1)}, u32[]{:S(2)}, u32[]{:S(2)}) collective-permute-start(bf16[128,2048]{1,0:T(8,128)(2,1)} %collective-permute-done.24.refs_4_), channel_id=1, source_target_pairs={{0,7},{1,0},{2,1},{3,2},{4,3},{5,4},{6,5},{7,6},{8,15},{9,8},{10,9... | collective-permute-start | bytes 1572872 | tf_op jit(solution)/shard_map/ppermute | solution.py:376
  177.8 2.8 %copy-done.38 = bf16[48,256,256]{2,1,0:T(8,128)(2,1)S(1)} copy-done((bf16[48,256,256]{2,1,0:T(8,128)(2,1)S(1)}, bf16[48,256,256]{2,1,0:T(8,128)(2,1)}, u32[]{:S(2)}) %copy-start.38) | copy-done | bytes 6291480
  180.6 7.6 %shard_map.88 = bf16[16,2,32,256]{3,2,1,0:T(8,128)(2,1)S(1)} custom-call(s32[1]{0:T(128)} %dynamic_slice.9.start_ref, bf16[512,2048]{1,0:T(8,128)(2,1)} %bitcast.8.rows_ref, bf16[8,6,256,256]{3,2,1,0:T(8,128)(2,1)S(1)} %bitcast.15), custom_call_target="tpu_custom_call" | custom-call | flops 3221225472 | bytes 9437184 | tf_op jit(solution)/shard_map/pallas_call | solution.py:288
  189.0 6.9 %all-to-all-start.2 = ((bf16[16,2,32,256]{3,2,1,0:T(8,128)(2,1)}), bf16[16,2,32,256]{3,2,1,0:T(8,128)(2,1)S(1)}, u32[]{:S(2)}, u32[]{:S(2)}) async-start(bf16[16,2,32,256]{3,2,1,0:T(8,128)(2,1)} %copy-done.10), calls=%async_computation.2 | async-start | bytes 1048576 | tf_op jit(solution)/shard_map/all_to_all | solution.py:439
  195.9 3.0 %collective-permute-start.28 = (bf16[64,2048]{1,0:T(8,128)(2,1)S(1)}, bf16[64,2048]{1,0:T(8,128)(2,1)S(1)}, u32[]{:S(2)}, u32[]{:S(2)}) collective-permute-start(bf16[64,2048]{1,0:T(8,128)(2,1)S(1)} %slice.9), channel_id=1, source_target_pairs={{0,7},{1,0},{2,1},{3,2},{4,3},{5,4},{6,5},{7,6},{8,15},{9,8},{10,9... | collective-permute-start | bytes 786440 | tf_op jit(solution)/shard_map/ppermute | solution.py:376
  199.1 5.5 %collective-permute-done.28.refs_8_ = bf16[64,2048]{1,0:T(8,128)(2,1)S(1)} collective-permute-done((bf16[64,2048]{1,0:T(8,128)(2,1)S(1)}, bf16[64,2048]{1,0:T(8,128)(2,1)S(1)}, u32[]{:S(2)}, u32[]{:S(2)}) %collective-permute-start.28) | collective-permute-done | bytes 262176 | tf_op jit(solution)/shard_map/ppermute | solution.py:376
  204.6 3.2 %collective-permute-done.27.refs_7_ = bf16[64,2048]{1,0:T(8,128)(2,1)S(1)} collective-permute-done((bf16[64,2048]{1,0:T(8,128)(2,1)S(1)}, bf16[64,2048]{1,0:T(8,128)(2,1)S(1)}, u32[]{:S(2)}, u32[]{:S(2)}) %collective-permute-start.27) | collective-permute-done | bytes 262176 | tf_op jit(solution)/shard_map/ppermute | solution.py:376
  211.5 2.6 %shard_map.89 = (f32[128,2048]{1,0:T(8,128)S(1)}, bf16[128,2048]{1,0:T(8,128)(2,1)S(1)}) custom-call(s32[2]{0:T(128)S(1)} %pad_add_fusion.place_ref, bf16[16,2,32,256]{3,2,1,0:T(8,128)(2,1)S(1)} %all-to-all-done.2.mix_ref, bf16[128,2048]{1,0:T(8,128)(2,1)S(1)} %constant_dynamic-slice_fusion.refs_0_, bf16[128,2048]{1,0:T(8,128)(2,1)S(1)} %copy-done.9, ...), custom_call_target="tpu_custom_call" | custom-call | flops 1073741824 | bytes 8388608 | tf_op jit(solution)/shard_map/pallas_call | solution.py:332
  (138 shorter events, 54.5 us)
Async XLA Ops:
  6.5 106.1 %all-gather.5.cloned.1.call-start = ((), (), s32[]{:S(2)}) async-start(), calls=%async_computation.3 | async-start | bytes 8650752 | tf_op jit(solution)/shard_map/all_gather | solution.py:409
  7.5 16.2 %collective-permute-start.3 = (bf16[128,256]{1,0:T(8,128)(2,1)S(1)}, bf16[128,256]{1,0:T(8,128)(2,1)S(1)}, u32[]{:S(2)}, u32[]{:S(2)}) collective-permute-start(bf16[128,256]{1,0:T(8,128)(2,1)S(1)} %dynamic_slice.10), channel_id=1, source_target_pairs={{0,3},{1,4},{2,5},{3,6},{4,15},{5,8},{6,9},{7,10},{8,7},{9,0},{10,... | collective-permute-start | bytes 196616 | tf_op jit(solution)/shard_map/ppermute | solution.py:406
  14.4 9.2 %collective-permute-start.2 = (bf16[128,256]{1,0:T(8,128)(2,1)S(1)}, bf16[128,256]{1,0:T(8,128)(2,1)S(1)}, u32[]{:S(2)}, u32[]{:S(2)}) collective-permute-start(bf16[128,256]{1,0:T(8,128)(2,1)S(1)} %dynamic_slice.10), channel_id=1, source_target_pairs={{0,2},{1,3},{2,4},{3,5},{4,14},{5,15},{6,8},{7,9},{8,6},{9,7},{10,... | collective-permute-start | bytes 196616 | tf_op jit(solution)/shard_map/ppermute | solution.py:406
  14.9 8.8 %collective-permute-start.1 = (bf16[128,256]{1,0:T(8,128)(2,1)S(1)}, bf16[128,256]{1,0:T(8,128)(2,1)S(1)}, u32[]{:S(2)}, u32[]{:S(2)}) collective-permute-start(bf16[128,256]{1,0:T(8,128)(2,1)S(1)} %dynamic_slice.10), channel_id=1, source_target_pairs={{0,1},{1,2},{2,3},{3,4},{4,13},{5,14},{6,15},{7,8},{8,5},{9,6},{10... | collective-permute-start | bytes 196616 | tf_op jit(solution)/shard_map/ppermute | solution.py:406
  17.0 8.9 %collective-permute-start = (bf16[128,256]{1,0:T(8,128)(2,1)S(1)}, bf16[128,256]{1,0:T(8,128)(2,1)S(1)}, u32[]{:S(2)}, u32[]{:S(2)}) collective-permute-start(bf16[128,256]{1,0:T(8,128)(2,1)S(1)} %dynamic_slice.10), channel_id=1, source_target_pairs={{0,0},{1,1},{2,2},{3,3},{4,12},{5,13},{6,14},{7,15},{8,4},{9,5},{1... | collective-permute-start | bytes 196616 | tf_op jit(solution)/shard_map/ppermute | solution.py:406
  26.6 151.2 %all-gather.7.cloned.1.call-start = ((), (), s32[]{:S(2)}) async-start(), calls=%async_computation.4 | async-start | bytes 7077888 | tf_op jit(solution)/shard_map/all_gather | solution.py:421
  26.7 11.5 %collective-permute-start.4 = (bf16[80,2048]{1,0:T(8,128)(2,1)S(1)}, bf16[80,2048]{1,0:T(8,128)(2,1)S(1)}, u32[]{:S(2)}, u32[]{:S(2)}) collective-permute-start(bf16[80,2048]{1,0:T(8,128)(2,1)S(1)} %get-tuple-element.31.refs_0_), channel_id=1, source_target_pairs={{0,1},{1,2},{2,3},{3,4},{4,5},{5,6},{6,7},{7,0},{8,9},{9,10},{10,1... | collective-permute-start | bytes 983048 | tf_op jit(solution)/shard_map/ppermute | solution.py:376
  29.4 9.5 %collective-permute-start.7 = (bf16[80,2048]{1,0:T(8,128)(2,1)S(1)}, bf16[80,2048]{1,0:T(8,128)(2,1)S(1)}, u32[]{:S(2)}, u32[]{:S(2)}) collective-permute-start(bf16[80,2048]{1,0:T(8,128)(2,1)S(1)} %get-tuple-element.32.refs_1_), channel_id=1, source_target_pairs={{0,7},{1,0},{2,1},{3,2},{4,3},{5,4},{6,5},{7,6},{8,15},{9,8},{10,9... | collective-permute-start | bytes 983048 | tf_op jit(solution)/shard_map/ppermute | solution.py:376
  29.9 15.8 %collective-permute-start.6 = (bf16[80,2048]{1,0:T(8,128)(2,1)S(1)}, bf16[80,2048]{1,0:T(8,128)(2,1)S(1)}, u32[]{:S(2)}, u32[]{:S(2)}) collective-permute-start(bf16[80,2048]{1,0:T(8,128)(2,1)S(1)} %get-tuple-element.31.refs_0_), channel_id=1, source_target_pairs={{0,7},{1,0},{2,1},{3,2},{4,3},{5,4},{6,5},{7,6},{8,15},{9,8},{10,9... | collective-permute-start | bytes 983048 | tf_op jit(solution)/shard_map/ppermute | solution.py:376
  31.3 16.6 %collective-permute-start.5 = (bf16[80,2048]{1,0:T(8,128)(2,1)S(1)}, bf16[80,2048]{1,0:T(8,128)(2,1)S(1)}, u32[]{:S(2)}, u32[]{:S(2)}) collective-permute-start(bf16[80,2048]{1,0:T(8,128)(2,1)S(1)} %get-tuple-element.32.refs_1_), channel_id=1, source_target_pairs={{0,1},{1,2},{2,3},{3,4},{4,5},{5,6},{6,7},{7,0},{8,9},{9,10},{10,1... | collective-permute-start | bytes 983048 | tf_op jit(solution)/shard_map/ppermute | solution.py:376
  38.2 12.3 %collective-permute-start.8 = (bf16[80,2048]{1,0:T(8,128)(2,1)S(1)}, bf16[80,2048]{1,0:T(8,128)(2,1)S(1)}, u32[]{:S(2)}, u32[]{:S(2)}) collective-permute-start(bf16[80,2048]{1,0:T(8,128)(2,1)S(1)} %collective-permute-done.4.refs_2_), channel_id=1, source_target_pairs={{0,1},{1,2},{2,3},{3,4},{4,5},{5,6},{6,7},{7,0},{8,9},{9,10},{10,1... | collective-permute-start | bytes 983048 | tf_op jit(solution)/shard_map/ppermute | solution.py:376
  38.9 13.9 %collective-permute-start.11 = (bf16[80,2048]{1,0:T(8,128)(2,1)S(1)}, bf16[80,2048]{1,0:T(8,128)(2,1)S(1)}, u32[]{:S(2)}, u32[]{:S(2)}) collective-permute-start(bf16[80,2048]{1,0:T(8,128)(2,1)S(1)} %collective-permute-done.7.refs_5_), channel_id=1, source_target_pairs={{0,7},{1,0},{2,1},{3,2},{4,3},{5,4},{6,5},{7,6},{8,15},{9,8},{10,9... | collective-permute-start | bytes 983048 | tf_op jit(solution)/shard_map/ppermute | solution.py:376
  45.8 14.0 %collective-permute-start.10 = (bf16[80,2048]{1,0:T(8,128)(2,1)S(1)}, bf16[80,2048]{1,0:T(8,128)(2,1)S(1)}, u32[]{:S(2)}, u32[]{:S(2)}) collective-permute-start(bf16[80,2048]{1,0:T(8,128)(2,1)S(1)} %collective-permute-done.6.refs_4_), channel_id=1, source_target_pairs={{0,7},{1,0},{2,1},{3,2},{4,3},{5,4},{6,5},{7,6},{8,15},{9,8},{10,9... | collective-permute-start | bytes 983048 | tf_op jit(solution)/shard_map/ppermute | solution.py:376
  47.9 14.0 %collective-permute-start.9 = (bf16[80,2048]{1,0:T(8,128)(2,1)S(1)}, bf16[80,2048]{1,0:T(8,128)(2,1)S(1)}, u32[]{:S(2)}, u32[]{:S(2)}) collective-permute-start(bf16[80,2048]{1,0:T(8,128)(2,1)S(1)} %collective-permute-done.5.refs_3_), channel_id=1, source_target_pairs={{0,1},{1,2},{2,3},{3,4},{4,5},{5,6},{6,7},{7,0},{8,9},{9,10},{10,1... | collective-permute-start | bytes 983048 | tf_op jit(solution)/shard_map/ppermute | solution.py:376
  50.5 14.0 %collective-permute-start.12 = (bf16[80,2048]{1,0:T(8,128)(2,1)S(1)}, bf16[80,2048]{1,0:T(8,128)(2,1)S(1)}, u32[]{:S(2)}, u32[]{:S(2)}) collective-permute-start(bf16[80,2048]{1,0:T(8,128)(2,1)S(1)} %collective-permute-done.8.refs_6_), channel_id=1, source_target_pairs={{0,1},{1,2},{2,3},{3,4},{4,5},{5,6},{6,7},{7,0},{8,9},{9,10},{10,1... | collective-permute-start | bytes 983048 | tf_op jit(solution)/shard_map/ppermute | solution.py:376
  52.8 14.1 %collective-permute-start.15 = (bf16[80,2048]{1,0:T(8,128)(2,1)S(1)}, bf16[80,2048]{1,0:T(8,128)(2,1)S(1)}, u32[]{:S(2)}, u32[]{:S(2)}) collective-permute-start(bf16[80,2048]{1,0:T(8,128)(2,1)S(1)} %collective-permute-done.11.refs_9_), channel_id=1, source_target_pairs={{0,7},{1,0},{2,1},{3,2},{4,3},{5,4},{6,5},{7,6},{8,15},{9,8},{10,9... | collective-permute-start | bytes 983048 | tf_op jit(solution)/shard_map/ppermute | solution.py:376
  59.7 13.8 %collective-permute-start.14 = (bf16[80,2048]{1,0:T(8,128)(2,1)S(1)}, bf16[80,2048]{1,0:T(8,128)(2,1)S(1)}, u32[]{:S(2)}, u32[]{:S(2)}) collective-permute-start(bf16[80,2048]{1,0:T(8,128)(2,1)S(1)} %collective-permute-done.10.refs_8_), channel_id=1, source_target_pairs={{0,7},{1,0},{2,1},{3,2},{4,3},{5,4},{6,5},{7,6},{8,15},{9,8},{10,9... | collective-permute-start | bytes 983048 | tf_op jit(solution)/shard_map/ppermute | solution.py:376
  62.0 11.5 %collective-permute-start.13 = (bf16[80,2048]{1,0:T(8,128)(2,1)S(1)}, bf16[80,2048]{1,0:T(8,128)(2,1)S(1)}, u32[]{:S(2)}, u32[]{:S(2)}) collective-permute-start(bf16[80,2048]{1,0:T(8,128)(2,1)S(1)} %collective-permute-done.9.refs_7_), channel_id=1, source_target_pairs={{0,1},{1,2},{2,3},{3,4},{4,5},{5,6},{6,7},{7,0},{8,9},{9,10},{10,1... | collective-permute-start | bytes 983048 | tf_op jit(solution)/shard_map/ppermute | solution.py:376
  64.6 14.4 %collective-permute-start.16 = (bf16[80,2048]{1,0:T(8,128)(2,1)S(1)}, bf16[80,2048]{1,0:T(8,128)(2,1)S(1)}, u32[]{:S(2)}, u32[]{:S(2)}) collective-permute-start(bf16[80,2048]{1,0:T(8,128)(2,1)S(1)} %collective-permute-done.12.refs_10_), channel_id=1, source_target_pairs={{0,1},{1,2},{2,3},{3,4},{4,5},{5,6},{6,7},{7,0},{8,9},{9,10},{10,1... | collective-permute-start | bytes 983048 | tf_op jit(solution)/shard_map/ppermute | solution.py:376
  66.9 12.1 %collective-permute-start.17 = (bf16[80,2048]{1,0:T(8,128)(2,1)S(1)}, bf16[80,2048]{1,0:T(8,128)(2,1)S(1)}, u32[]{:S(2)}, u32[]{:S(2)}) collective-permute-start(bf16[80,2048]{1,0:T(8,128)(2,1)S(1)} %collective-permute-done.15.refs_13_), channel_id=1, source_target_pairs={{0,7},{1,0},{2,1},{3,2},{4,3},{5,4},{6,5},{7,6},{8,15},{9,8},{10,9... | collective-permute-start | bytes 983048 | tf_op jit(solution)/shard_map/ppermute | solution.py:376
  81.9 11.7 %collective-permute-start.21 = (bf16[2,3,64,256]{3,2,1,0:T(8,128)(2,1)S(1)}, bf16[2,3,64,256]{3,2,1,0:T(8,128)(2,1)S(1)}, u32[]{:S(2)}, u32[]{:S(2)}) collective-permute-start(bf16[2,3,64,256]{3,2,1,0:T(8,128)(2,1)S(1)} %get-tuple-element.46), channel_id=1, source_target_pairs={{0,32},{16,48},{32,0},{48,16},{1,33},{17,49},{33,1},{49,17},{2,34}... | collective-permute-start | bytes 589832 | tf_op jit(solution)/shard_map/ppermute | solution.py:376
  84.5 9.1 %collective-permute-start.22 = (bf16[2,3,64,256]{3,2,1,0:T(8,128)(2,1)S(1)}, bf16[2,3,64,256]{3,2,1,0:T(8,128)(2,1)S(1)}, u32[]{:S(2)}, u32[]{:S(2)}) collective-permute-start(bf16[2,3,64,256]{3,2,1,0:T(8,128)(2,1)S(1)} %get-tuple-element.47), channel_id=1, source_target_pairs={{0,48},{16,0},{32,16},{48,32},{1,49},{17,1},{33,17},{49,33},{2,50}... | collective-permute-start | bytes 589832 | tf_op jit(solution)/shard_map/ppermute | solution.py:376
  112.7 23.8 %all-to-all-start = ((bf16[8,128,256]{2,1,0:T(8,128)(2,1)}), bf16[8,128,256]{2,1,0:T(8,128)(2,1)S(1)}, u32[]{:S(2)}, u32[]{:S(2)}) async-start(bf16[8,128,256]{2,1,0:T(8,128)(2,1)} %shard_map.83), calls=%async_computation | async-start | bytes 1048576 | tf_op jit(solution)/shard_map/all_to_all | solution.py:422
  143.5 34.2 %all-to-all-start.1 = ((bf16[16,32,2048]{2,1,0:T(8,128)(2,1)}), bf16[16,32,2048]{2,1,0:T(8,128)(2,1)}, u32[]{:S(2)}, u32[]{:S(2)}) async-start(bf16[16,32,2048]{2,1,0:T(8,128)(2,1)} %copy-done.3), calls=%async_computation.1 | async-start | bytes 4194304 | tf_op jit(solution)/shard_map/all_to_all | solution.py:435
  148.7 13.4 %collective-permute-start.19 = (bf16[128,2048]{1,0:T(8,128)(2,1)S(1)}, bf16[128,2048]{1,0:T(8,128)(2,1)S(1)}, u32[]{:S(2)}, u32[]{:S(2)}) collective-permute-start(bf16[128,2048]{1,0:T(8,128)(2,1)S(1)} %constant_dynamic-slice_fusion.refs_0_), channel_id=1, source_target_pairs={{0,7},{1,0},{2,1},{3,2},{4,3},{5,4},{6,5},{7,6},{8,15},{9,8},{10,9... | collective-permute-start | bytes 1572872 | tf_op jit(solution)/shard_map/ppermute | solution.py:376
  148.7 14.9 %collective-permute-start.18 = (bf16[128,2048]{1,0:T(8,128)(2,1)S(1)}, bf16[128,2048]{1,0:T(8,128)(2,1)S(1)}, u32[]{:S(2)}, u32[]{:S(2)}) collective-permute-start(bf16[128,2048]{1,0:T(8,128)(2,1)S(1)} %constant_dynamic-slice_fusion.refs_0_), channel_id=1, source_target_pairs={{0,1},{1,2},{2,3},{3,4},{4,5},{5,6},{6,7},{7,0},{8,9},{9,10},{10,1... | collective-permute-start | bytes 1572872 | tf_op jit(solution)/shard_map/ppermute | solution.py:376
  162.1 12.6 %collective-permute-start.24 = (bf16[128,2048]{1,0:T(8,128)(2,1)S(1)}, bf16[128,2048]{1,0:T(8,128)(2,1)}, u32[]{:S(2)}, u32[]{:S(2)}) collective-permute-start(bf16[128,2048]{1,0:T(8,128)(2,1)S(1)} %collective-permute-done.19.refs_2_), channel_id=1, source_target_pairs={{0,7},{1,0},{2,1},{3,2},{4,3},{5,4},{6,5},{7,6},{8,15},{9,8},{10,9... | collective-permute-start | bytes 1572872 | tf_op jit(solution)/shard_map/ppermute | solution.py:376
  163.6 14.2 %collective-permute-start.23 = (bf16[128,2048]{1,0:T(8,128)(2,1)S(1)}, bf16[128,2048]{1,0:T(8,128)(2,1)}, u32[]{:S(2)}, u32[]{:S(2)}) collective-permute-start(bf16[128,2048]{1,0:T(8,128)(2,1)S(1)} %collective-permute-done.18.refs_1_), channel_id=1, source_target_pairs={{0,1},{1,2},{2,3},{3,4},{4,5},{5,6},{6,7},{7,0},{8,9},{9,10},{10,1... | collective-permute-start | bytes 1572872 | tf_op jit(solution)/shard_map/ppermute | solution.py:376
  174.7 21.2 %collective-permute-start.26 = (bf16[128,2048]{1,0:T(8,128)(2,1)}, bf16[128,2048]{1,0:T(8,128)(2,1)S(1)}, u32[]{:S(2)}, u32[]{:S(2)}) collective-permute-start(bf16[128,2048]{1,0:T(8,128)(2,1)} %collective-permute-done.24.refs_4_), channel_id=1, source_target_pairs={{0,7},{1,0},{2,1},{3,2},{4,3},{5,4},{6,5},{7,6},{8,15},{9,8},{10,9... | collective-permute-start | bytes 1572872 | tf_op jit(solution)/shard_map/ppermute | solution.py:376
  177.8 21.2 %collective-permute-start.25 = (bf16[128,2048]{1,0:T(8,128)(2,1)}, bf16[128,2048]{1,0:T(8,128)(2,1)S(1)}, u32[]{:S(2)}, u32[]{:S(2)}) collective-permute-start(bf16[128,2048]{1,0:T(8,128)(2,1)} %collective-permute-done.23.refs_3_), channel_id=1, source_target_pairs={{0,1},{1,2},{2,3},{3,4},{4,5},{5,6},{6,7},{7,0},{8,9},{9,10},{10,1... | collective-permute-start | bytes 1572872 | tf_op jit(solution)/shard_map/ppermute | solution.py:376
  189.0 19.5 %all-to-all-start.2 = ((bf16[16,2,32,256]{3,2,1,0:T(8,128)(2,1)}), bf16[16,2,32,256]{3,2,1,0:T(8,128)(2,1)S(1)}, u32[]{:S(2)}, u32[]{:S(2)}) async-start(bf16[16,2,32,256]{3,2,1,0:T(8,128)(2,1)} %copy-done.10), calls=%async_computation.2 | async-start | bytes 1048576 | tf_op jit(solution)/shard_map/all_to_all | solution.py:439
  199.0 8.8 %collective-permute-start.27 = (bf16[64,2048]{1,0:T(8,128)(2,1)S(1)}, bf16[64,2048]{1,0:T(8,128)(2,1)S(1)}, u32[]{:S(2)}, u32[]{:S(2)}) collective-permute-start(bf16[64,2048]{1,0:T(8,128)(2,1)S(1)} %slice.8), channel_id=1, source_target_pairs={{0,1},{1,2},{2,3},{3,4},{4,5},{5,6},{6,7},{7,0},{8,9},{9,10},{10,1... | collective-permute-start | bytes 786440 | tf_op jit(solution)/shard_map/ppermute | solution.py:376
  (44 other events, 436.3 us)
Sparse Core Ops, SparseCore 0:
  26.7 57.9 all-gather.4
  94.7 43.8 all-gather.6

commit v10 on v7

--- a/solution.py
+++ b/solution.py
@@ -15,7 +15,7 @@
 BF = jnp.bfloat16
 F32 = jnp.float32
 NZ = 8
-VMEM_LIMIT = 28 * 1024 * 1024
+VMEM_LIMIT = 20 * 1024 * 1024
 OFFSETS = (0, -1, 1, -2, 2, -3, 3, 4)
 
 
@@ -415,10 +415,10 @@
     got = [sends[0]] + [shifted(sends[k], "y", k) for k in range(1, 4)]
 
     weight = jnp.transpose(spatial_qkv, (1, 0, 2))
+    pieces, whole_out = lax.optimization_barrier((pieces, whole_out))
     mix = spatial_attend(z.reshape(1), weight, pieces)
-    mix, *got = lax.optimization_barrier((mix, *got))
+    _, *got = lax.optimization_barrier((mix, *got))
     quarter = join_shares(y.reshape(1), got)
-    mix, quarter, whole_out = lax.optimization_barrier((mix, quarter, whole_out))
     quarter = lax.all_gather(quarter[None], ("w", "xl", "c"), axis=0, tiled=True)
     mix = lax.all_to_all(mix, "z", 0, 0, tiled=True)
 

time: 206 us -> 224 us (1.087)
  local copies, waits for them, and re-layouts: 19 us -> 32.4 us
    unnamed x38 -> x82, local copies, waits for them, and re-layouts: 17.4 us -> 30.8 us
    all_to_all x1, starting transfers between devices: 4.35 us -> 7.94 us  [local(): mix = lax.all_to_all(mix, 'z', 0, 0, tiled=True)]
    all_to_all x1, starting transfers between devices: 7.14 us -> 4.71 us  [local(): window = lax.all_to_all(send, ('xl', 'y', 'c'), 0, 0, tiled=True)]
    all_to_all x1, waiting for transfers between devices: 15.6 us -> 17.9 us  [local(): mix = lax.all_to_all(mix, 'z', 0, 0, tiled=True)]
  transfers between devices with their start and end apart: 35 -> 35, of which waited for: 15 -> 14; matrix products, arithmetic and copies ran while one was open for 0% -> 0% of each run, Pallas kernels for 8% -> 7%
where the time goes in v10:
time: 224 us; the launch traced here: 223 us
  waiting for transfers between devices  82 us (37%)
  starting transfers between devices  71.2 us (32%)
  local copies, waits for them, and re-layouts  32.4 us (14%)
  Pallas kernels  23.3 us (10%)
  between operations  13.7 us (6%)
    ppermute x26, waiting for transfers between devices, shifted(): lax.ppermute(value, axis, [(i, (i + step) % count) for i in range(count)])  64 us
    ppermute x26, starting transfers between devices, shifted(): lax.ppermute(value, axis, [(i, (i + step) % count) for i in range(count)])  36.9 us
    unnamed x82, local copies, waits for them, and re-layouts  30.8 us
    all_to_all x1, waiting for transfers between devices, local(): mix = lax.all_to_all(mix, 'z', 0, 0, tiled=True)  17.9 us
    ppermute x4, starting transfers between devices, local(): parts.append(lax.ppermute(block, ('c', 'z'), pairs))  13.8 us
    all_to_all x1, starting transfers between devices, local(): mix = lax.all_to_all(mix, 'z', 0, 0, tiled=True)  7.94 us
    all_to_all x1, starting transfers between devices, local(): mix = lax.all_to_all(mix, ('xl', 'y', 'c'), 0, 0, tiled=True)  7.85 us
    pallas_call x1, Pallas kernels, temporal_attend(): pl.pallas_call(temporal_kernel, out_shape=jax.ShapeDtypeStruct((16, 2, 32...  7.61 us
  transfers between devices with their start and end apart: 35, of which 14 were waited for; matrix products, arithmetic and copies ran while one was open for 0% of the time, Pallas kernels for 7%

profile of v10, /device:TPU:1, one launch (start us, length us, event | category | flops | bytes accessed | tf_op | source)
XLA Modules:
  0.0 222.7 jit_solution(4652349851441977341)
XLA Ops:
  7.5 10.2 %collective-permute-start = (bf16[128,256]{1,0:T(8,128)(2,1)S(1)}, bf16[128,256]{1,0:T(8,128)(2,1)S(1)}, u32[]{:S(2)}, u32[]{:S(2)}) collective-permute-start(bf16[128,256]{1,0:T(8,128)(2,1)S(1)} %dynamic_slice.10), channel_id=1, source_target_pairs={{0,0},{1,1},{2,2},{3,3},{4,12},{5,13},{6,14},{7,15},{8,4},{9,5},{1... | collective-permute-start | bytes 196616 | tf_op jit(solution)/shard_map/ppermute | solution.py:406
  18.5 2.8 %collective-permute-start.3 = (bf16[128,256]{1,0:T(8,128)(2,1)S(1)}, bf16[128,256]{1,0:T(8,128)(2,1)S(1)}, u32[]{:S(2)}, u32[]{:S(2)}) collective-permute-start(bf16[128,256]{1,0:T(8,128)(2,1)S(1)} %dynamic_slice.10), channel_id=1, source_target_pairs={{0,3},{1,4},{2,5},{3,6},{4,15},{5,8},{6,9},{7,10},{8,7},{9,0},{10,... | collective-permute-start | bytes 196616 | tf_op jit(solution)/shard_map/ppermute | solution.py:406
  21.3 1.9 copy-done.2
  26.4 3.6 %collective-permute-start.4 = (bf16[80,2048]{1,0:T(8,128)(2,1)S(1)}, bf16[80,2048]{1,0:T(8,128)(2,1)S(1)}, u32[]{:S(2)}, u32[]{:S(2)}) collective-permute-start(bf16[80,2048]{1,0:T(8,128)(2,1)S(1)} %get-tuple-element.58.refs_0_), channel_id=1, source_target_pairs={{0,1},{1,2},{2,3},{3,4},{4,5},{5,6},{6,7},{7,0},{8,9},{9,10},{10,1... | collective-permute-start | bytes 983048 | tf_op jit(solution)/shard_map/ppermute | solution.py:376
  32.7 5.1 %collective-permute-done.4.refs_2_ = bf16[80,2048]{1,0:T(8,128)(2,1)S(1)} collective-permute-done((bf16[80,2048]{1,0:T(8,128)(2,1)S(1)}, bf16[80,2048]{1,0:T(8,128)(2,1)S(1)}, u32[]{:S(2)}, u32[]{:S(2)}) %collective-permute-start.4) | collective-permute-done | bytes 327712 | tf_op jit(solution)/shard_map/ppermute | solution.py:376
  40.5 4.3 %collective-permute-done.5.refs_3_ = bf16[80,2048]{1,0:T(8,128)(2,1)S(1)} collective-permute-done((bf16[80,2048]{1,0:T(8,128)(2,1)S(1)}, bf16[80,2048]{1,0:T(8,128)(2,1)S(1)}, u32[]{:S(2)}, u32[]{:S(2)}) %collective-permute-start.5) | collective-permute-done | bytes 327712 | tf_op jit(solution)/shard_map/ppermute | solution.py:376
  44.8 1.6 collective-permute-start.9
  47.5 4.3 %collective-permute-done.8.refs_6_ = bf16[80,2048]{1,0:T(8,128)(2,1)S(1)} collective-permute-done((bf16[80,2048]{1,0:T(8,128)(2,1)S(1)}, bf16[80,2048]{1,0:T(8,128)(2,1)S(1)}, u32[]{:S(2)}, u32[]{:S(2)}) %collective-permute-start.8) | collective-permute-done | bytes 327712 | tf_op jit(solution)/shard_map/ppermute | solution.py:376
  54.5 4.3 %collective-permute-done.9.refs_7_ = bf16[80,2048]{1,0:T(8,128)(2,1)S(1)} collective-permute-done((bf16[80,2048]{1,0:T(8,128)(2,1)S(1)}, bf16[80,2048]{1,0:T(8,128)(2,1)S(1)}, u32[]{:S(2)}, u32[]{:S(2)}) %collective-permute-start.9) | collective-permute-done | bytes 327712 | tf_op jit(solution)/shard_map/ppermute | solution.py:376
  61.6 4.3 %collective-permute-done.12.refs_10_ = bf16[80,2048]{1,0:T(8,128)(2,1)S(1)} collective-permute-done((bf16[80,2048]{1,0:T(8,128)(2,1)S(1)}, bf16[80,2048]{1,0:T(8,128)(2,1)S(1)}, u32[]{:S(2)}, u32[]{:S(2)}) %collective-permute-start.12) | collective-permute-done | bytes 327712 | tf_op jit(solution)/shard_map/ppermute | solution.py:376
  68.7 4.3 %collective-permute-done.13.refs_11_ = bf16[80,2048]{1,0:T(8,128)(2,1)S(1)} collective-permute-done((bf16[80,2048]{1,0:T(8,128)(2,1)S(1)}, bf16[80,2048]{1,0:T(8,128)(2,1)S(1)}, u32[]{:S(2)}, u32[]{:S(2)}) %collective-permute-start.13) | collective-permute-done | bytes 327712 | tf_op jit(solution)/shard_map/ppermute | solution.py:376
  74.2 5.8 %collective-permute-done.16.refs_14_ = bf16[80,2048]{1,0:T(8,128)(2,1)S(1)} collective-permute-done((bf16[80,2048]{1,0:T(8,128)(2,1)S(1)}, bf16[80,2048]{1,0:T(8,128)(2,1)S(1)}, u32[]{:S(2)}, u32[]{:S(2)}) %collective-permute-start.16) | collective-permute-done | bytes 327712 | tf_op jit(solution)/shard_map/ppermute | solution.py:376
  81.2 1.7 shard_map.86
  84.9 2.6 %collective-permute-start.23 = (bf16[2,3,64,256]{3,2,1,0:T(8,128)(2,1)}, bf16[2,3,64,256]{3,2,1,0:T(8,128)(2,1)}, u32[]{:S(2)}, u32[]{:S(2)}) collective-permute-start(bf16[2,3,64,256]{3,2,1,0:T(8,128)(2,1)} %get-tuple-element.82), channel_id=1, source_target_pairs={{0,32},{16,48},{32,0},{48,16},{1,33},{17,49},{33,1},{49,17},{2,34}... | collective-permute-start | bytes 589832 | tf_op jit(solution)/shard_map/ppermute | solution.py:376
  99.4 1.9 copy-done.39
  101.3 5.2 %shard_map.84 = bf16[8,128,256]{2,1,0:T(8,128)(2,1)} custom-call(s32[1]{0:T(128)} %bitcast.z_ref.place_ref, bf16[3,2048,256]{2,1,0:T(8,128)(2,1)S(1)} %bitcast.16, bf16[80,2048]{1,0:T(8,128)(2,1)S(1)} %get-tuple-element.58.refs_0_, bf16[80,2048]{1,0:T(8,128)(2,1)S(1)} %get-tuple-element.59.refs_1_, bf16[80,2048]{1,0:T(8,128)(2,1)S(1)} %collective-permute-done.4.refs_2_, ...), custom_call_target="tpu_custom_call" | custom-call | flops 6442450944 | bytes 8388608 | tf_op jit(solution)/shard_map/pallas_call | solution.py:184
  106.5 2.1 shard_map.87
  108.6 7.9 %all-to-all-start = ((bf16[8,128,256]{2,1,0:T(8,128)(2,1)}), bf16[8,128,256]{2,1,0:T(8,128)(2,1)S(1)}, u32[]{:S(2)}, u32[]{:S(2)}) async-start(bf16[8,128,256]{2,1,0:T(8,128)(2,1)} %shard_map.84), calls=%async_computation | async-start | bytes 1048576 | tf_op jit(solution)/shard_map/all_to_all | solution.py:423
  116.6 17.9 %all-to-all-done.mix_ref = bf16[8,128,256]{2,1,0:T(8,128)(2,1)S(1)} async-done(((bf16[8,128,256]{2,1,0:T(8,128)(2,1)}), bf16[8,128,256]{2,1,0:T(8,128)(2,1)S(1)}, u32[]{:S(2)}, u32[]{:S(2)}) %all-to-all-start) | async-done | bytes 524320 | tf_op jit(solution)/shard_map/all_to_all | solution.py:423
  134.5 3.6 %copy-done.1 = bf16[128,128,256]{2,1,0:T(8,128)(2,1)S(1)} copy-done((bf16[128,128,256]{2,1,0:T(8,128)(2,1)S(1)}, bf16[128,128,256]{2,1,0:T(8,128)(2,1)}, u32[]{:S(2)}) %copy-start.1) | copy-done | bytes 8388632
  141.8 4.7 %all-to-all-start.1 = ((bf16[16,32,2048]{2,1,0:T(8,128)(2,1)}), bf16[16,32,2048]{2,1,0:T(8,128)(2,1)}, u32[]{:S(2)}, u32[]{:S(2)}) async-start(bf16[16,32,2048]{2,1,0:T(8,128)(2,1)} %copy-done.3), calls=%async_computation.1 | async-start | bytes 4194304 | tf_op jit(solution)/shard_map/all_to_all | solution.py:436
  146.8 2.4 %collective-permute-start.19 = (bf16[128,2048]{1,0:T(8,128)(2,1)S(1)}, bf16[128,2048]{1,0:T(8,128)(2,1)S(1)}, u32[]{:S(2)}, u32[]{:S(2)}) collective-permute-start(bf16[128,2048]{1,0:T(8,128)(2,1)S(1)} %constant_dynamic-slice_fusion.refs_0_), channel_id=1, source_target_pairs={{0,7},{1,0},{2,1},{3,2},{4,3},{5,4},{6,5},{7,6},{8,15},{9,8},{10,9... | collective-permute-start | bytes 1572872 | tf_op jit(solution)/shard_map/ppermute | solution.py:376
  149.2 11.8 %collective-permute-done.18.refs_1_ = bf16[128,2048]{1,0:T(8,128)(2,1)S(1)} collective-permute-done((bf16[128,2048]{1,0:T(8,128)(2,1)S(1)}, bf16[128,2048]{1,0:T(8,128)(2,1)S(1)}, u32[]{:S(2)}, u32[]{:S(2)}) %collective-permute-start.18) | collective-permute-done | bytes 524320 | tf_op jit(solution)/shard_map/ppermute | solution.py:376
  161.0 2.7 %collective-permute-start.21 = (bf16[128,2048]{1,0:T(8,128)(2,1)S(1)}, bf16[128,2048]{1,0:T(8,128)(2,1)}, u32[]{:S(2)}, u32[]{:S(2)}) collective-permute-start(bf16[128,2048]{1,0:T(8,128)(2,1)S(1)} %collective-permute-done.19.refs_2_), channel_id=1, source_target_pairs={{0,7},{1,0},{2,1},{3,2},{4,3},{5,4},{6,5},{7,6},{8,15},{9,8},{10,9... | collective-permute-start | bytes 1572872 | tf_op jit(solution)/shard_map/ppermute | solution.py:376
  165.0 9.6 %collective-permute-done.20.refs_3_ = bf16[128,2048]{1,0:T(8,128)(2,1)} collective-permute-done((bf16[128,2048]{1,0:T(8,128)(2,1)S(1)}, bf16[128,2048]{1,0:T(8,128)(2,1)}, u32[]{:S(2)}, u32[]{:S(2)}) %collective-permute-start.20) | collective-permute-done | bytes 524320 | tf_op jit(solution)/shard_map/ppermute | solution.py:376
  174.7 2.7 %collective-permute-start.26 = (bf16[128,2048]{1,0:T(8,128)(2,1)}, bf16[128,2048]{1,0:T(8,128)(2,1)S(1)}, u32[]{:S(2)}, u32[]{:S(2)}) collective-permute-start(bf16[128,2048]{1,0:T(8,128)(2,1)} %collective-permute-done.21.refs_4_), channel_id=1, source_target_pairs={{0,7},{1,0},{2,1},{3,2},{4,3},{5,4},{6,5},{7,6},{8,15},{9,8},{10,9... | collective-permute-start | bytes 1572872 | tf_op jit(solution)/shard_map/ppermute | solution.py:376
  177.3 2.8 %copy-done.38 = bf16[48,256,256]{2,1,0:T(8,128)(2,1)S(1)} copy-done((bf16[48,256,256]{2,1,0:T(8,128)(2,1)S(1)}, bf16[48,256,256]{2,1,0:T(8,128)(2,1)}, u32[]{:S(2)}) %copy-start.38) | copy-done | bytes 6291480
  180.1 7.6 %shard_map.88 = bf16[16,2,32,256]{3,2,1,0:T(8,128)(2,1)S(1)} custom-call(s32[1]{0:T(128)} %dynamic_slice.9.start_ref, bf16[512,2048]{1,0:T(8,128)(2,1)} %bitcast.8.rows_ref, bf16[8,6,256,256]{3,2,1,0:T(8,128)(2,1)S(1)} %bitcast.15), custom_call_target="tpu_custom_call" | custom-call | flops 3221225472 | bytes 9437184 | tf_op jit(solution)/shard_map/pallas_call | solution.py:288
  188.5 7.8 %all-to-all-start.2 = ((bf16[16,2,32,256]{3,2,1,0:T(8,128)(2,1)}), bf16[16,2,32,256]{3,2,1,0:T(8,128)(2,1)S(1)}, u32[]{:S(2)}, u32[]{:S(2)}) async-start(bf16[16,2,32,256]{3,2,1,0:T(8,128)(2,1)} %copy-done.10), calls=%async_computation.2 | async-start | bytes 1048576 | tf_op jit(solution)/shard_map/all_to_all | solution.py:440
  196.6 2.8 %collective-permute-start.28 = (bf16[64,2048]{1,0:T(8,128)(2,1)S(1)}, bf16[64,2048]{1,0:T(8,128)(2,1)S(1)}, u32[]{:S(2)}, u32[]{:S(2)}) collective-permute-start(bf16[64,2048]{1,0:T(8,128)(2,1)S(1)} %slice.9), channel_id=1, source_target_pairs={{0,7},{1,0},{2,1},{3,2},{4,3},{5,4},{6,5},{7,6},{8,15},{9,8},{10,9... | collective-permute-start | bytes 786440 | tf_op jit(solution)/shard_map/ppermute | solution.py:376
  199.4 6.2 %collective-permute-done.27.refs_7_ = bf16[64,2048]{1,0:T(8,128)(2,1)S(1)} collective-permute-done((bf16[64,2048]{1,0:T(8,128)(2,1)S(1)}, bf16[64,2048]{1,0:T(8,128)(2,1)S(1)}, u32[]{:S(2)}, u32[]{:S(2)}) %collective-permute-start.27) | collective-permute-done | bytes 262176 | tf_op jit(solution)/shard_map/ppermute | solution.py:376
  209.3 2.6 %shard_map.89 = (f32[128,2048]{1,0:T(8,128)S(1)}, bf16[128,2048]{1,0:T(8,128)(2,1)S(1)}) custom-call(s32[2]{0:T(128)S(1)} %pad_add_fusion.place_ref, bf16[16,2,32,256]{3,2,1,0:T(8,128)(2,1)S(1)} %all-to-all-done.2.mix_ref, bf16[128,2048]{1,0:T(8,128)(2,1)S(1)} %constant_dynamic-slice_fusion.refs_0_, bf16[128,2048]{1,0:T(8,128)(2,1)S(1)} %copy-done.7, ...), custom_call_target="tpu_custom_call" | custom-call | flops 1073741824 | bytes 8388608 | tf_op jit(solution)/shard_map/pallas_call | solution.py:332
  (138 shorter events, 49.9 us)
Async XLA Ops:
  6.5 82.2 %all-gather.5.cloned.1.call-start = ((), (), s32[]{:S(2)}) async-start(), calls=%async_computation.3 | async-start | bytes 8650752 | tf_op jit(solution)/shard_map/all_gather | solution.py:409
  7.5 18.1 %collective-permute-start = (bf16[128,256]{1,0:T(8,128)(2,1)S(1)}, bf16[128,256]{1,0:T(8,128)(2,1)S(1)}, u32[]{:S(2)}, u32[]{:S(2)}) collective-permute-start(bf16[128,256]{1,0:T(8,128)(2,1)S(1)} %dynamic_slice.10), channel_id=1, source_target_pairs={{0,0},{1,1},{2,2},{3,3},{4,12},{5,13},{6,14},{7,15},{8,4},{9,5},{1... | collective-permute-start | bytes 196616 | tf_op jit(solution)/shard_map/ppermute | solution.py:406
  17.7 7.9 %collective-permute-start.1 = (bf16[128,256]{1,0:T(8,128)(2,1)S(1)}, bf16[128,256]{1,0:T(8,128)(2,1)S(1)}, u32[]{:S(2)}, u32[]{:S(2)}) collective-permute-start(bf16[128,256]{1,0:T(8,128)(2,1)S(1)} %dynamic_slice.10), channel_id=1, source_target_pairs={{0,1},{1,2},{2,3},{3,4},{4,13},{5,14},{6,15},{7,8},{8,5},{9,6},{10... | collective-permute-start | bytes 196616 | tf_op jit(solution)/shard_map/ppermute | solution.py:406
  26.4 151.0 %all-gather.7.cloned.1.call-start = ((), (), s32[]{:S(2)}) async-start(), calls=%async_computation.4 | async-start | bytes 7077888 | tf_op jit(solution)/shard_map/all_gather | solution.py:422
  26.4 11.4 %collective-permute-start.4 = (bf16[80,2048]{1,0:T(8,128)(2,1)S(1)}, bf16[80,2048]{1,0:T(8,128)(2,1)S(1)}, u32[]{:S(2)}, u32[]{:S(2)}) collective-permute-start(bf16[80,2048]{1,0:T(8,128)(2,1)S(1)} %get-tuple-element.58.refs_0_), channel_id=1, source_target_pairs={{0,1},{1,2},{2,3},{3,4},{4,5},{5,6},{6,7},{7,0},{8,9},{9,10},{10,1... | collective-permute-start | bytes 983048 | tf_op jit(solution)/shard_map/ppermute | solution.py:376
  30.0 9.3 %collective-permute-start.7 = (bf16[80,2048]{1,0:T(8,128)(2,1)S(1)}, bf16[80,2048]{1,0:T(8,128)(2,1)S(1)}, u32[]{:S(2)}, u32[]{:S(2)}) collective-permute-start(bf16[80,2048]{1,0:T(8,128)(2,1)S(1)} %get-tuple-element.59.refs_1_), channel_id=1, source_target_pairs={{0,7},{1,0},{2,1},{3,2},{4,3},{5,4},{6,5},{7,6},{8,15},{9,8},{10,9... | collective-permute-start | bytes 983048 | tf_op jit(solution)/shard_map/ppermute | solution.py:376
  30.0 14.8 %collective-permute-start.5 = (bf16[80,2048]{1,0:T(8,128)(2,1)S(1)}, bf16[80,2048]{1,0:T(8,128)(2,1)S(1)}, u32[]{:S(2)}, u32[]{:S(2)}) collective-permute-start(bf16[80,2048]{1,0:T(8,128)(2,1)S(1)} %get-tuple-element.59.refs_1_), channel_id=1, source_target_pairs={{0,1},{1,2},{2,3},{3,4},{4,5},{5,6},{6,7},{7,0},{8,9},{9,10},{10,1... | collective-permute-start | bytes 983048 | tf_op jit(solution)/shard_map/ppermute | solution.py:376
  31.5 14.9 %collective-permute-start.6 = (bf16[80,2048]{1,0:T(8,128)(2,1)S(1)}, bf16[80,2048]{1,0:T(8,128)(2,1)S(1)}, u32[]{:S(2)}, u32[]{:S(2)}) collective-permute-start(bf16[80,2048]{1,0:T(8,128)(2,1)S(1)} %get-tuple-element.58.refs_0_), channel_id=1, source_target_pairs={{0,7},{1,0},{2,1},{3,2},{4,3},{5,4},{6,5},{7,6},{8,15},{9,8},{10,9... | collective-permute-start | bytes 983048 | tf_op jit(solution)/shard_map/ppermute | solution.py:376
  37.8 14.0 %collective-permute-start.8 = (bf16[80,2048]{1,0:T(8,128)(2,1)S(1)}, bf16[80,2048]{1,0:T(8,128)(2,1)S(1)}, u32[]{:S(2)}, u32[]{:S(2)}) collective-permute-start(bf16[80,2048]{1,0:T(8,128)(2,1)S(1)} %collective-permute-done.4.refs_2_), channel_id=1, source_target_pairs={{0,1},{1,2},{2,3},{3,4},{4,5},{5,6},{6,7},{7,0},{8,9},{9,10},{10,1... | collective-permute-start | bytes 983048 | tf_op jit(solution)/shard_map/ppermute | solution.py:376
  39.3 14.0 %collective-permute-start.11 = (bf16[80,2048]{1,0:T(8,128)(2,1)S(1)}, bf16[80,2048]{1,0:T(8,128)(2,1)S(1)}, u32[]{:S(2)}, u32[]{:S(2)}) collective-permute-start(bf16[80,2048]{1,0:T(8,128)(2,1)S(1)} %collective-permute-done.7.refs_5_), channel_id=1, source_target_pairs={{0,7},{1,0},{2,1},{3,2},{4,3},{5,4},{6,5},{7,6},{8,15},{9,8},{10,9... | collective-permute-start | bytes 983048 | tf_op jit(solution)/shard_map/ppermute | solution.py:376
  44.8 14.0 %collective-permute-start.9 = (bf16[80,2048]{1,0:T(8,128)(2,1)S(1)}, bf16[80,2048]{1,0:T(8,128)(2,1)S(1)}, u32[]{:S(2)}, u32[]{:S(2)}) collective-permute-start(bf16[80,2048]{1,0:T(8,128)(2,1)S(1)} %collective-permute-done.5.refs_3_), channel_id=1, source_target_pairs={{0,1},{1,2},{2,3},{3,4},{4,5},{5,6},{6,7},{7,0},{8,9},{9,10},{10,1... | collective-permute-start | bytes 983048 | tf_op jit(solution)/shard_map/ppermute | solution.py:376
  46.4 13.9 %collective-permute-start.10 = (bf16[80,2048]{1,0:T(8,128)(2,1)S(1)}, bf16[80,2048]{1,0:T(8,128)(2,1)S(1)}, u32[]{:S(2)}, u32[]{:S(2)}) collective-permute-start(bf16[80,2048]{1,0:T(8,128)(2,1)S(1)} %collective-permute-done.6.refs_4_), channel_id=1, source_target_pairs={{0,7},{1,0},{2,1},{3,2},{4,3},{5,4},{6,5},{7,6},{8,15},{9,8},{10,9... | collective-permute-start | bytes 983048 | tf_op jit(solution)/shard_map/ppermute | solution.py:376
  51.8 14.0 %collective-permute-start.12 = (bf16[80,2048]{1,0:T(8,128)(2,1)S(1)}, bf16[80,2048]{1,0:T(8,128)(2,1)S(1)}, u32[]{:S(2)}, u32[]{:S(2)}) collective-permute-start(bf16[80,2048]{1,0:T(8,128)(2,1)S(1)} %collective-permute-done.8.refs_6_), channel_id=1, source_target_pairs={{0,1},{1,2},{2,3},{3,4},{4,5},{5,6},{6,7},{7,0},{8,9},{9,10},{10,1... | collective-permute-start | bytes 983048 | tf_op jit(solution)/shard_map/ppermute | solution.py:376
  53.3 14.0 %collective-permute-start.15 = (bf16[80,2048]{1,0:T(8,128)(2,1)S(1)}, bf16[80,2048]{1,0:T(8,128)(2,1)S(1)}, u32[]{:S(2)}, u32[]{:S(2)}) collective-permute-start(bf16[80,2048]{1,0:T(8,128)(2,1)S(1)} %collective-permute-done.11.refs_9_), channel_id=1, source_target_pairs={{0,7},{1,0},{2,1},{3,2},{4,3},{5,4},{6,5},{7,6},{8,15},{9,8},{10,9... | collective-permute-start | bytes 983048 | tf_op jit(solution)/shard_map/ppermute | solution.py:376
  58.8 14.1 %collective-permute-start.13 = (bf16[80,2048]{1,0:T(8,128)(2,1)S(1)}, bf16[80,2048]{1,0:T(8,128)(2,1)S(1)}, u32[]{:S(2)}, u32[]{:S(2)}) collective-permute-start(bf16[80,2048]{1,0:T(8,128)(2,1)S(1)} %collective-permute-done.9.refs_7_), channel_id=1, source_target_pairs={{0,1},{1,2},{2,3},{3,4},{4,5},{5,6},{6,7},{7,0},{8,9},{9,10},{10,1... | collective-permute-start | bytes 983048 | tf_op jit(solution)/shard_map/ppermute | solution.py:376
  60.4 13.8 %collective-permute-start.14 = (bf16[80,2048]{1,0:T(8,128)(2,1)S(1)}, bf16[80,2048]{1,0:T(8,128)(2,1)S(1)}, u32[]{:S(2)}, u32[]{:S(2)}) collective-permute-start(bf16[80,2048]{1,0:T(8,128)(2,1)S(1)} %collective-permute-done.10.refs_8_), channel_id=1, source_target_pairs={{0,7},{1,0},{2,1},{3,2},{4,3},{5,4},{6,5},{7,6},{8,15},{9,8},{10,9... | collective-permute-start | bytes 983048 | tf_op jit(solution)/shard_map/ppermute | solution.py:376
  65.9 14.1 %collective-permute-start.16 = (bf16[80,2048]{1,0:T(8,128)(2,1)S(1)}, bf16[80,2048]{1,0:T(8,128)(2,1)S(1)}, u32[]{:S(2)}, u32[]{:S(2)}) collective-permute-start(bf16[80,2048]{1,0:T(8,128)(2,1)S(1)} %collective-permute-done.12.refs_10_), channel_id=1, source_target_pairs={{0,1},{1,2},{2,3},{3,4},{4,5},{5,6},{6,7},{7,0},{8,9},{9,10},{10,1... | collective-permute-start | bytes 983048 | tf_op jit(solution)/shard_map/ppermute | solution.py:376
  67.4 13.8 %collective-permute-start.17 = (bf16[80,2048]{1,0:T(8,128)(2,1)S(1)}, bf16[80,2048]{1,0:T(8,128)(2,1)S(1)}, u32[]{:S(2)}, u32[]{:S(2)}) collective-permute-start(bf16[80,2048]{1,0:T(8,128)(2,1)S(1)} %collective-permute-done.15.refs_13_), channel_id=1, source_target_pairs={{0,7},{1,0},{2,1},{3,2},{4,3},{5,4},{6,5},{7,6},{8,15},{9,8},{10,9... | collective-permute-start | bytes 983048 | tf_op jit(solution)/shard_map/ppermute | solution.py:376
  83.6 22.9 %collective-permute-start.22 = (bf16[2,3,64,256]{3,2,1,0:T(8,128)(2,1)}, bf16[2,3,64,256]{3,2,1,0:T(8,128)(2,1)}, u32[]{:S(2)}, u32[]{:S(2)}) collective-permute-start(bf16[2,3,64,256]{3,2,1,0:T(8,128)(2,1)} %get-tuple-element.81), channel_id=1, source_target_pairs={{0,16},{16,32},{32,48},{48,0},{1,17},{17,33},{33,49},{49,1},{2,18}... | collective-permute-start | bytes 589832 | tf_op jit(solution)/shard_map/ppermute | solution.py:376
  84.9 21.6 %collective-permute-start.23 = (bf16[2,3,64,256]{3,2,1,0:T(8,128)(2,1)}, bf16[2,3,64,256]{3,2,1,0:T(8,128)(2,1)}, u32[]{:S(2)}, u32[]{:S(2)}) collective-permute-start(bf16[2,3,64,256]{3,2,1,0:T(8,128)(2,1)} %get-tuple-element.82), channel_id=1, source_target_pairs={{0,32},{16,48},{32,0},{48,16},{1,33},{17,49},{33,1},{49,17},{2,34}... | collective-permute-start | bytes 589832 | tf_op jit(solution)/shard_map/ppermute | solution.py:376
  87.6 19.0 %collective-permute-start.24 = (bf16[2,3,64,256]{3,2,1,0:T(8,128)(2,1)}, bf16[2,3,64,256]{3,2,1,0:T(8,128)(2,1)}, u32[]{:S(2)}, u32[]{:S(2)}) collective-permute-start(bf16[2,3,64,256]{3,2,1,0:T(8,128)(2,1)} %get-tuple-element.83), channel_id=1, source_target_pairs={{0,48},{16,0},{32,16},{48,32},{1,49},{17,1},{33,17},{49,33},{2,50}... | collective-permute-start | bytes 589832 | tf_op jit(solution)/shard_map/ppermute | solution.py:376
  108.6 25.9 %all-to-all-start = ((bf16[8,128,256]{2,1,0:T(8,128)(2,1)}), bf16[8,128,256]{2,1,0:T(8,128)(2,1)S(1)}, u32[]{:S(2)}, u32[]{:S(2)}) async-start(bf16[8,128,256]{2,1,0:T(8,128)(2,1)} %shard_map.84), calls=%async_computation | async-start | bytes 1048576 | tf_op jit(solution)/shard_map/all_to_all | solution.py:423
  141.8 35.6 %all-to-all-start.1 = ((bf16[16,32,2048]{2,1,0:T(8,128)(2,1)}), bf16[16,32,2048]{2,1,0:T(8,128)(2,1)}, u32[]{:S(2)}, u32[]{:S(2)}) async-start(bf16[16,32,2048]{2,1,0:T(8,128)(2,1)} %copy-done.3), calls=%async_computation.1 | async-start | bytes 4194304 | tf_op jit(solution)/shard_map/all_to_all | solution.py:436
  146.5 14.5 %collective-permute-start.18 = (bf16[128,2048]{1,0:T(8,128)(2,1)S(1)}, bf16[128,2048]{1,0:T(8,128)(2,1)S(1)}, u32[]{:S(2)}, u32[]{:S(2)}) collective-permute-start(bf16[128,2048]{1,0:T(8,128)(2,1)S(1)} %constant_dynamic-slice_fusion.refs_0_), channel_id=1, source_target_pairs={{0,1},{1,2},{2,3},{3,4},{4,5},{5,6},{6,7},{7,0},{8,9},{9,10},{10,1... | collective-permute-start | bytes 1572872 | tf_op jit(solution)/shard_map/ppermute | solution.py:376
  146.8 14.2 %collective-permute-start.19 = (bf16[128,2048]{1,0:T(8,128)(2,1)S(1)}, bf16[128,2048]{1,0:T(8,128)(2,1)S(1)}, u32[]{:S(2)}, u32[]{:S(2)}) collective-permute-start(bf16[128,2048]{1,0:T(8,128)(2,1)S(1)} %constant_dynamic-slice_fusion.refs_0_), channel_id=1, source_target_pairs={{0,7},{1,0},{2,1},{3,2},{4,3},{5,4},{6,5},{7,6},{8,15},{9,8},{10,9... | collective-permute-start | bytes 1572872 | tf_op jit(solution)/shard_map/ppermute | solution.py:376
  161.0 13.7 %collective-permute-start.20 = (bf16[128,2048]{1,0:T(8,128)(2,1)S(1)}, bf16[128,2048]{1,0:T(8,128)(2,1)}, u32[]{:S(2)}, u32[]{:S(2)}) collective-permute-start(bf16[128,2048]{1,0:T(8,128)(2,1)S(1)} %collective-permute-done.18.refs_1_), channel_id=1, source_target_pairs={{0,1},{1,2},{2,3},{3,4},{4,5},{5,6},{6,7},{7,0},{8,9},{9,10},{10,1... | collective-permute-start | bytes 1572872 | tf_op jit(solution)/shard_map/ppermute | solution.py:376
  161.0 13.7 %collective-permute-start.21 = (bf16[128,2048]{1,0:T(8,128)(2,1)S(1)}, bf16[128,2048]{1,0:T(8,128)(2,1)}, u32[]{:S(2)}, u32[]{:S(2)}) collective-permute-start(bf16[128,2048]{1,0:T(8,128)(2,1)S(1)} %collective-permute-done.19.refs_2_), channel_id=1, source_target_pairs={{0,7},{1,0},{2,1},{3,2},{4,3},{5,4},{6,5},{7,6},{8,15},{9,8},{10,9... | collective-permute-start | bytes 1572872 | tf_op jit(solution)/shard_map/ppermute | solution.py:376
  174.7 21.7 %collective-permute-start.25 = (bf16[128,2048]{1,0:T(8,128)(2,1)}, bf16[128,2048]{1,0:T(8,128)(2,1)S(1)}, u32[]{:S(2)}, u32[]{:S(2)}) collective-permute-start(bf16[128,2048]{1,0:T(8,128)(2,1)} %collective-permute-done.20.refs_3_), channel_id=1, source_target_pairs={{0,1},{1,2},{2,3},{3,4},{4,5},{5,6},{6,7},{7,0},{8,9},{9,10},{10,1... | collective-permute-start | bytes 1572872 | tf_op jit(solution)/shard_map/ppermute | solution.py:376
  174.7 21.9 %collective-permute-start.26 = (bf16[128,2048]{1,0:T(8,128)(2,1)}, bf16[128,2048]{1,0:T(8,128)(2,1)S(1)}, u32[]{:S(2)}, u32[]{:S(2)}) collective-permute-start(bf16[128,2048]{1,0:T(8,128)(2,1)} %collective-permute-done.21.refs_4_), channel_id=1, source_target_pairs={{0,7},{1,0},{2,1},{3,2},{4,3},{5,4},{6,5},{7,6},{8,15},{9,8},{10,9... | collective-permute-start | bytes 1572872 | tf_op jit(solution)/shard_map/ppermute | solution.py:376
  188.5 17.7 %all-to-all-start.2 = ((bf16[16,2,32,256]{3,2,1,0:T(8,128)(2,1)}), bf16[16,2,32,256]{3,2,1,0:T(8,128)(2,1)S(1)}, u32[]{:S(2)}, u32[]{:S(2)}) async-start(bf16[16,2,32,256]{3,2,1,0:T(8,128)(2,1)} %copy-done.10), calls=%async_computation.2 | async-start | bytes 1048576 | tf_op jit(solution)/shard_map/all_to_all | solution.py:440
  196.4 9.2 %collective-permute-start.27 = (bf16[64,2048]{1,0:T(8,128)(2,1)S(1)}, bf16[64,2048]{1,0:T(8,128)(2,1)S(1)}, u32[]{:S(2)}, u32[]{:S(2)}) collective-permute-start(bf16[64,2048]{1,0:T(8,128)(2,1)S(1)} %slice.8), channel_id=1, source_target_pairs={{0,1},{1,2},{2,3},{3,4},{4,5},{5,6},{6,7},{7,0},{8,9},{9,10},{10,1... | collective-permute-start | bytes 786440 | tf_op jit(solution)/shard_map/ppermute | solution.py:376
  196.6 9.0 %collective-permute-start.28 = (bf16[64,2048]{1,0:T(8,128)(2,1)S(1)}, bf16[64,2048]{1,0:T(8,128)(2,1)S(1)}, u32[]{:S(2)}, u32[]{:S(2)}) collective-permute-start(bf16[64,2048]{1,0:T(8,128)(2,1)S(1)} %slice.9), channel_id=1, source_target_pairs={{0,7},{1,0},{2,1},{3,2},{4,3},{5,4},{6,5},{7,6},{8,15},{9,8},{10,9... | collective-permute-start | bytes 786440 | tf_op jit(solution)/shard_map/ppermute | solution.py:376
  (44 other events, 436.7 us)
Sparse Core Ops, SparseCore 0:
  26.5 59.9 all-gather.4
  108.7 44.9 all-gather.6

commit v11 on v7

--- a/solution.py
+++ b/solution.py
@@ -302,8 +302,14 @@
 
 
 def last_kernel(place_ref, mix_ref, *refs):
-    pieces, (keep_ref, give_ref, total) = refs[: NZ + 1], refs[NZ + 1 :]
+    pieces, (keep_ref, give_ref, total, weight, sems) = refs[: NZ + 1], refs[NZ + 1 :]
     z, c = place_ref[0], place_ref[1]
+    copies = []
+    for index, piece in enumerate(pieces):
+        low = E * index if index < NZ else E * NZ - E // 2
+        rows = weight.at[pl.ds(low, piece.shape[0])]
+        copies.append(pltpu.make_async_copy(piece, rows, sems.at[index]))
+        copies[-1].start()
     blocks = []
     for k in range(NZ):
         source = lax.rem(z + (OFFSETS[k] + NZ), NZ)
@@ -320,9 +326,10 @@
             )
         )
     mix = jnp.concatenate(blocks, axis=1)
+    for copy in copies:
+        copy.wait()
     for low in range(0, 2048, 512):
-        part = jnp.concatenate([piece[:, low : low + 512] for piece in pieces], axis=0)
-        total[:, :, low : low + 512] = dot(mix, part).reshape(2, 128, 512)
+        total[:, :, low : low + 512] = dot(mix, weight[:, low : low + 512]).reshape(2, 128, 512)
     keep_ref[...] = total[c]
     give_ref[...] = total[1 - c].astype(BF)
 
@@ -335,9 +342,13 @@
             jax.ShapeDtypeStruct((128, width), F32),
             jax.ShapeDtypeStruct((128, width), BF),
         ),
-        in_specs=[smem()] + [vmem()] * (NZ + 2),
+        in_specs=[smem(), vmem()] + [pl.BlockSpec(memory_space=pltpu.HBM)] * (NZ + 1),
         out_specs=(vmem(), vmem()),
-        scratch_shapes=[pltpu.VMEM((2, 128, width), F32)],
+        scratch_shapes=[
+            pltpu.VMEM((2, 128, width), F32),
+            pltpu.VMEM((E * NZ, width), BF),
+            pltpu.SemaphoreType.DMA((NZ + 1,)),
+        ],
         compiler_params=params(),
         cost_estimate=pl.CostEstimate(
             flops=2 * 128 * 2048 * 2048, bytes_accessed=8 << 20, transcendentals=0

time: 206 us -> 207 us (level)
  no operation moved by 1% of the time
where the time goes in v11:
time: 207 us; the launch traced here: 206 us
  waiting for transfers between devices  81.5 us (39%)
  starting transfers between devices  70 us (34%)
  Pallas kernels  22.1 us (11%)
  local copies, waits for them, and re-layouts  19 us (9%)
  between operations  13.6 us (7%)
    ppermute x26, waiting for transfers between devices, shifted(): lax.ppermute(value, axis, [(i, (i + step) % count) for i in range(count)])  65.8 us
    ppermute x26, starting transfers between devices, shifted(): lax.ppermute(value, axis, [(i, (i + step) % count) for i in range(count)])  36.9 us
    unnamed x38, local copies, waits for them, and re-layouts  17.4 us
    all_to_all x1, waiting for transfers between devices, local(): mix = lax.all_to_all(mix, 'z', 0, 0, tiled=True)  15.6 us
    ppermute x4, starting transfers between devices, local(): parts.append(lax.ppermute(block, ('c', 'z'), pairs))  13.8 us
    all_to_all x1, starting transfers between devices, local(): mix = lax.all_to_all(mix, ('xl', 'y', 'c'), 0, 0, tiled=True)  7.78 us
    pallas_call x1, Pallas kernels, temporal_attend(): pl.pallas_call(temporal_kernel, out_shape=jax.ShapeDtypeStruct((16, 2, 32...  7.6 us
    all_to_all x1, starting transfers between devices, local(): window = lax.all_to_all(send, ('xl', 'y', 'c'), 0, 0, tiled=True)  7.14 us
  transfers between devices with their start and end apart: 35, of which 15 were waited for; matrix products, arithmetic and copies ran while one was open for 0% of the time, Pallas kernels for 8%

profile of v11, /device:TPU:1, one launch (start us, length us, event | category | flops | bytes accessed | tf_op | source)
XLA Modules:
  0.0 206.4 jit_solution(13114635880397063653)
XLA Ops:
  7.5 10.2 %collective-permute-start = (bf16[128,256]{1,0:T(8,128)(2,1)S(1)}, bf16[128,256]{1,0:T(8,128)(2,1)S(1)}, u32[]{:S(2)}, u32[]{:S(2)}) collective-permute-start(bf16[128,256]{1,0:T(8,128)(2,1)S(1)} %dynamic_slice.10), channel_id=1, source_target_pairs={{0,0},{1,1},{2,2},{3,3},{4,12},{5,13},{6,14},{7,15},{8,4},{9,5},{1... | collective-permute-start | bytes 196616 | tf_op jit(solution)/shard_map/ppermute | solution.py:417
  18.5 2.8 %collective-permute-start.3 = (bf16[128,256]{1,0:T(8,128)(2,1)S(1)}, bf16[128,256]{1,0:T(8,128)(2,1)S(1)}, u32[]{:S(2)}, u32[]{:S(2)}) collective-permute-start(bf16[128,256]{1,0:T(8,128)(2,1)S(1)} %dynamic_slice.10), channel_id=1, source_target_pairs={{0,3},{1,4},{2,5},{3,6},{4,15},{5,8},{6,9},{7,10},{8,7},{9,0},{10,... | collective-permute-start | bytes 196616 | tf_op jit(solution)/shard_map/ppermute | solution.py:417
  21.3 1.9 copy-done.2
  26.4 3.6 %collective-permute-start.4 = (bf16[80,2048]{1,0:T(8,128)(2,1)S(1)}, bf16[80,2048]{1,0:T(8,128)(2,1)S(1)}, u32[]{:S(2)}, u32[]{:S(2)}) collective-permute-start(bf16[80,2048]{1,0:T(8,128)(2,1)S(1)} %get-tuple-element.39.refs_0_), channel_id=1, source_target_pairs={{0,1},{1,2},{2,3},{3,4},{4,5},{5,6},{6,7},{7,0},{8,9},{9,10},{10,1... | collective-permute-start | bytes 983048 | tf_op jit(solution)/shard_map/ppermute | solution.py:387
  32.7 5.1 %collective-permute-done.4.refs_2_ = bf16[80,2048]{1,0:T(8,128)(2,1)S(1)} collective-permute-done((bf16[80,2048]{1,0:T(8,128)(2,1)S(1)}, bf16[80,2048]{1,0:T(8,128)(2,1)S(1)}, u32[]{:S(2)}, u32[]{:S(2)}) %collective-permute-start.4) | collective-permute-done | bytes 327712 | tf_op jit(solution)/shard_map/ppermute | solution.py:387
  37.8 1.5 collective-permute-start.8
  40.5 4.3 %collective-permute-done.5.refs_3_ = bf16[80,2048]{1,0:T(8,128)(2,1)S(1)} collective-permute-done((bf16[80,2048]{1,0:T(8,128)(2,1)S(1)}, bf16[80,2048]{1,0:T(8,128)(2,1)S(1)}, u32[]{:S(2)}, u32[]{:S(2)}) %collective-permute-start.5) | collective-permute-done | bytes 327712 | tf_op jit(solution)/shard_map/ppermute | solution.py:387
  44.8 1.6 collective-permute-start.9
  47.5 4.3 %collective-permute-done.8.refs_6_ = bf16[80,2048]{1,0:T(8,128)(2,1)S(1)} collective-permute-done((bf16[80,2048]{1,0:T(8,128)(2,1)S(1)}, bf16[80,2048]{1,0:T(8,128)(2,1)S(1)}, u32[]{:S(2)}, u32[]{:S(2)}) %collective-permute-start.8) | collective-permute-done | bytes 327712 | tf_op jit(solution)/shard_map/ppermute | solution.py:387
  54.5 4.3 %collective-permute-done.9.refs_7_ = bf16[80,2048]{1,0:T(8,128)(2,1)S(1)} collective-permute-done((bf16[80,2048]{1,0:T(8,128)(2,1)S(1)}, bf16[80,2048]{1,0:T(8,128)(2,1)S(1)}, u32[]{:S(2)}, u32[]{:S(2)}) %collective-permute-start.9) | collective-permute-done | bytes 327712 | tf_op jit(solution)/shard_map/ppermute | solution.py:387
  61.6 4.3 %collective-permute-done.12.refs_10_ = bf16[80,2048]{1,0:T(8,128)(2,1)S(1)} collective-permute-done((bf16[80,2048]{1,0:T(8,128)(2,1)S(1)}, bf16[80,2048]{1,0:T(8,128)(2,1)S(1)}, u32[]{:S(2)}, u32[]{:S(2)}) %collective-permute-start.12) | collective-permute-done | bytes 327712 | tf_op jit(solution)/shard_map/ppermute | solution.py:387
  68.7 4.3 %collective-permute-done.13.refs_11_ = bf16[80,2048]{1,0:T(8,128)(2,1)S(1)} collective-permute-done((bf16[80,2048]{1,0:T(8,128)(2,1)S(1)}, bf16[80,2048]{1,0:T(8,128)(2,1)S(1)}, u32[]{:S(2)}, u32[]{:S(2)}) %collective-permute-start.13) | collective-permute-done | bytes 327712 | tf_op jit(solution)/shard_map/ppermute | solution.py:387
  74.2 5.8 %collective-permute-done.16.refs_14_ = bf16[80,2048]{1,0:T(8,128)(2,1)S(1)} collective-permute-done((bf16[80,2048]{1,0:T(8,128)(2,1)S(1)}, bf16[80,2048]{1,0:T(8,128)(2,1)S(1)}, u32[]{:S(2)}, u32[]{:S(2)}) %collective-permute-start.16) | collective-permute-done | bytes 327712 | tf_op jit(solution)/shard_map/ppermute | solution.py:387
  83.4 2.6 %collective-permute-start.19 = (bf16[2,3,64,256]{3,2,1,0:T(8,128)(2,1)S(1)}, bf16[2,3,64,256]{3,2,1,0:T(8,128)(2,1)S(1)}, u32[]{:S(2)}, u32[]{:S(2)}) collective-permute-start(bf16[2,3,64,256]{3,2,1,0:T(8,128)(2,1)S(1)} %get-tuple-element.43), channel_id=1, source_target_pairs={{0,32},{16,48},{32,0},{48,16},{1,33},{17,49},{33,1},{49,17},{2,34}... | collective-permute-start | bytes 589832 | tf_op jit(solution)/shard_map/ppermute | solution.py:387
  87.1 5.3 %shard_map.83 = bf16[8,128,256]{2,1,0:T(8,128)(2,1)} custom-call(s32[1]{0:T(128)} %bitcast.place_ref.z_ref, bf16[3,2048,256]{2,1,0:T(8,128)(2,1)S(1)} %bitcast.16, bf16[80,2048]{1,0:T(8,128)(2,1)S(1)} %get-tuple-element.39.refs_0_, bf16[80,2048]{1,0:T(8,128)(2,1)S(1)} %get-tuple-element.40.refs_1_, bf16[80,2048]{1,0:T(8,128)(2,1)S(1)} %collective-permute-done.4.refs_2_, ...), custom_call_target="tpu_custom_call" | custom-call | flops 6442450944 | bytes 8388608 | tf_op jit(solution)/shard_map/pallas_call | solution.py:184
  92.4 1.7 collective-permute-done.19.refs_2_
  95.1 4.4 %all-to-all-start = ((bf16[8,128,256]{2,1,0:T(8,128)(2,1)}), bf16[8,128,256]{2,1,0:T(8,128)(2,1)S(1)}, u32[]{:S(2)}, u32[]{:S(2)}) async-start(bf16[8,128,256]{2,1,0:T(8,128)(2,1)} %shard_map.83), calls=%async_computation | async-start | bytes 1048576 | tf_op jit(solution)/shard_map/all_to_all | solution.py:434
  99.5 15.6 %all-to-all-done.mix_ref = bf16[8,128,256]{2,1,0:T(8,128)(2,1)S(1)} async-done(((bf16[8,128,256]{2,1,0:T(8,128)(2,1)}), bf16[8,128,256]{2,1,0:T(8,128)(2,1)S(1)}, u32[]{:S(2)}, u32[]{:S(2)}) %all-to-all-start) | async-done | bytes 524320 | tf_op jit(solution)/shard_map/all_to_all | solution.py:434
  115.2 3.5 %copy-done.1 = bf16[128,128,256]{2,1,0:T(8,128)(2,1)S(1)} copy-done((bf16[128,128,256]{2,1,0:T(8,128)(2,1)S(1)}, bf16[128,128,256]{2,1,0:T(8,128)(2,1)}, u32[]{:S(2)}) %copy-start.1) | copy-done | bytes 8388632
  122.4 7.1 %all-to-all-start.1 = ((bf16[16,32,2048]{2,1,0:T(8,128)(2,1)}), bf16[16,32,2048]{2,1,0:T(8,128)(2,1)}, u32[]{:S(2)}, u32[]{:S(2)}) async-start(bf16[16,32,2048]{2,1,0:T(8,128)(2,1)} %copy-done.3), calls=%async_computation.1 | async-start | bytes 4194304 | tf_op jit(solution)/shard_map/all_to_all | solution.py:447
  129.8 2.4 %collective-permute-start.22 = (bf16[128,2048]{1,0:T(8,128)(2,1)S(1)}, bf16[128,2048]{1,0:T(8,128)(2,1)S(1)}, u32[]{:S(2)}, u32[]{:S(2)}) collective-permute-start(bf16[128,2048]{1,0:T(8,128)(2,1)S(1)} %constant_dynamic-slice_fusion.refs_0_), channel_id=1, source_target_pairs={{0,7},{1,0},{2,1},{3,2},{4,3},{5,4},{6,5},{7,6},{8,15},{9,8},{10,9... | collective-permute-start | bytes 1572872 | tf_op jit(solution)/shard_map/ppermute | solution.py:387
  132.2 11.8 %collective-permute-done.21.refs_1_ = bf16[128,2048]{1,0:T(8,128)(2,1)S(1)} collective-permute-done((bf16[128,2048]{1,0:T(8,128)(2,1)S(1)}, bf16[128,2048]{1,0:T(8,128)(2,1)S(1)}, u32[]{:S(2)}, u32[]{:S(2)}) %collective-permute-start.21) | collective-permute-done | bytes 524320 | tf_op jit(solution)/shard_map/ppermute | solution.py:387
  144.0 2.7 %collective-permute-start.24 = (bf16[128,2048]{1,0:T(8,128)(2,1)S(1)}, bf16[128,2048]{1,0:T(8,128)(2,1)}, u32[]{:S(2)}, u32[]{:S(2)}) collective-permute-start(bf16[128,2048]{1,0:T(8,128)(2,1)S(1)} %collective-permute-done.22.refs_2_), channel_id=1, source_target_pairs={{0,7},{1,0},{2,1},{3,2},{4,3},{5,4},{6,5},{7,6},{8,15},{9,8},{10,9... | collective-permute-start | bytes 1572872 | tf_op jit(solution)/shard_map/ppermute | solution.py:387
  148.1 9.6 %collective-permute-done.23.refs_3_ = bf16[128,2048]{1,0:T(8,128)(2,1)} collective-permute-done((bf16[128,2048]{1,0:T(8,128)(2,1)S(1)}, bf16[128,2048]{1,0:T(8,128)(2,1)}, u32[]{:S(2)}, u32[]{:S(2)}) %collective-permute-start.23) | collective-permute-done | bytes 524320 | tf_op jit(solution)/shard_map/ppermute | solution.py:387
  157.7 2.7 %collective-permute-start.26 = (bf16[128,2048]{1,0:T(8,128)(2,1)}, bf16[128,2048]{1,0:T(8,128)(2,1)S(1)}, u32[]{:S(2)}, u32[]{:S(2)}) collective-permute-start(bf16[128,2048]{1,0:T(8,128)(2,1)} %collective-permute-done.24.refs_4_), channel_id=1, source_target_pairs={{0,7},{1,0},{2,1},{3,2},{4,3},{5,4},{6,5},{7,6},{8,15},{9,8},{10,9... | collective-permute-start | bytes 1572872 | tf_op jit(solution)/shard_map/ppermute | solution.py:387
  160.4 2.8 %copy-done.16 = bf16[48,256,256]{2,1,0:T(8,128)(2,1)S(1)} copy-done((bf16[48,256,256]{2,1,0:T(8,128)(2,1)S(1)}, bf16[48,256,256]{2,1,0:T(8,128)(2,1)}, u32[]{:S(2)}) %copy-start.16) | copy-done | bytes 6291480
  163.2 7.6 %shard_map.88 = bf16[16,2,32,256]{3,2,1,0:T(8,128)(2,1)S(1)} custom-call(s32[1]{0:T(128)} %dynamic_slice.9.start_ref, bf16[512,2048]{1,0:T(8,128)(2,1)} %bitcast.9.rows_ref, bf16[8,6,256,256]{3,2,1,0:T(8,128)(2,1)S(1)} %bitcast.15), custom_call_target="tpu_custom_call" | custom-call | flops 3221225472 | bytes 9437184 | tf_op jit(solution)/shard_map/pallas_call | solution.py:288
  171.6 7.8 %all-to-all-start.2 = ((bf16[16,2,32,256]{3,2,1,0:T(8,128)(2,1)}), bf16[16,2,32,256]{3,2,1,0:T(8,128)(2,1)S(1)}, u32[]{:S(2)}, u32[]{:S(2)}) async-start(bf16[16,2,32,256]{3,2,1,0:T(8,128)(2,1)} %copy-done.10), calls=%async_computation.2 | async-start | bytes 1048576 | tf_op jit(solution)/shard_map/all_to_all | solution.py:451
  179.5 2.8 %collective-permute-start.28 = (bf16[64,2048]{1,0:T(8,128)(2,1)S(1)}, bf16[64,2048]{1,0:T(8,128)(2,1)S(1)}, u32[]{:S(2)}, u32[]{:S(2)}) collective-permute-start(bf16[64,2048]{1,0:T(8,128)(2,1)S(1)} %slice.9), channel_id=1, source_target_pairs={{0,7},{1,0},{2,1},{3,2},{4,3},{5,4},{6,5},{7,6},{8,15},{9,8},{10,9... | collective-permute-start | bytes 786440 | tf_op jit(solution)/shard_map/ppermute | solution.py:387
  182.4 6.2 %collective-permute-done.27.refs_7_ = bf16[64,2048]{1,0:T(8,128)(2,1)S(1)} collective-permute-done((bf16[64,2048]{1,0:T(8,128)(2,1)S(1)}, bf16[64,2048]{1,0:T(8,128)(2,1)S(1)}, u32[]{:S(2)}, u32[]{:S(2)}) %collective-permute-start.27) | collective-permute-done | bytes 262176 | tf_op jit(solution)/shard_map/ppermute | solution.py:387
  192.3 3.3 %shard_map.89 = (f32[128,2048]{1,0:T(8,128)S(1)}, bf16[128,2048]{1,0:T(8,128)(2,1)S(1)}) custom-call(s32[2]{0:T(128)S(1)} %pad_add_fusion.place_ref, bf16[16,2,32,256]{3,2,1,0:T(8,128)(2,1)S(1)} %all-to-all-done.2.mix_ref, bf16[128,2048]{1,0:T(8,128)(2,1)S(1)} %constant_dynamic-slice_fusion.refs_0_, bf16[128,2048]{1,0:T(8,128)(2,1)S(1)} %copy-done.7, ...), custom_call_target="tpu_custom_call" | custom-call | flops 1073741824 | bytes 8388608 | tf_op jit(solution)/shard_map/pallas_call | solution.py:339
  196.8 1.5 collective-permute-done.29.got_ref
  (94 shorter events, 37.3 us)
Async XLA Ops:
  6.5 88.5 %all-gather.5.cloned.1.call-start = ((), (), s32[]{:S(2)}) async-start(), calls=%async_computation.3 | async-start | bytes 8650752 | tf_op jit(solution)/shard_map/all_gather | solution.py:420
  7.5 18.1 %collective-permute-start = (bf16[128,256]{1,0:T(8,128)(2,1)S(1)}, bf16[128,256]{1,0:T(8,128)(2,1)S(1)}, u32[]{:S(2)}, u32[]{:S(2)}) collective-permute-start(bf16[128,256]{1,0:T(8,128)(2,1)S(1)} %dynamic_slice.10), channel_id=1, source_target_pairs={{0,0},{1,1},{2,2},{3,3},{4,12},{5,13},{6,14},{7,15},{8,4},{9,5},{1... | collective-permute-start | bytes 196616 | tf_op jit(solution)/shard_map/ppermute | solution.py:417
  17.7 7.9 %collective-permute-start.1 = (bf16[128,256]{1,0:T(8,128)(2,1)S(1)}, bf16[128,256]{1,0:T(8,128)(2,1)S(1)}, u32[]{:S(2)}, u32[]{:S(2)}) collective-permute-start(bf16[128,256]{1,0:T(8,128)(2,1)S(1)} %dynamic_slice.10), channel_id=1, source_target_pairs={{0,1},{1,2},{2,3},{3,4},{4,13},{5,14},{6,15},{7,8},{8,5},{9,6},{10... | collective-permute-start | bytes 196616 | tf_op jit(solution)/shard_map/ppermute | solution.py:417
  26.4 134.0 %all-gather.7.cloned.1.call-start = ((), (), s32[]{:S(2)}) async-start(), calls=%async_computation.4 | async-start | bytes 7077888 | tf_op jit(solution)/shard_map/all_gather | solution.py:433
  26.4 11.4 %collective-permute-start.4 = (bf16[80,2048]{1,0:T(8,128)(2,1)S(1)}, bf16[80,2048]{1,0:T(8,128)(2,1)S(1)}, u32[]{:S(2)}, u32[]{:S(2)}) collective-permute-start(bf16[80,2048]{1,0:T(8,128)(2,1)S(1)} %get-tuple-element.39.refs_0_), channel_id=1, source_target_pairs={{0,1},{1,2},{2,3},{3,4},{4,5},{5,6},{6,7},{7,0},{8,9},{9,10},{10,1... | collective-permute-start | bytes 983048 | tf_op jit(solution)/shard_map/ppermute | solution.py:387
  30.0 9.3 %collective-permute-start.7 = (bf16[80,2048]{1,0:T(8,128)(2,1)S(1)}, bf16[80,2048]{1,0:T(8,128)(2,1)S(1)}, u32[]{:S(2)}, u32[]{:S(2)}) collective-permute-start(bf16[80,2048]{1,0:T(8,128)(2,1)S(1)} %get-tuple-element.40.refs_1_), channel_id=1, source_target_pairs={{0,7},{1,0},{2,1},{3,2},{4,3},{5,4},{6,5},{7,6},{8,15},{9,8},{10,9... | collective-permute-start | bytes 983048 | tf_op jit(solution)/shard_map/ppermute | solution.py:387
  30.0 14.8 %collective-permute-start.5 = (bf16[80,2048]{1,0:T(8,128)(2,1)S(1)}, bf16[80,2048]{1,0:T(8,128)(2,1)S(1)}, u32[]{:S(2)}, u32[]{:S(2)}) collective-permute-start(bf16[80,2048]{1,0:T(8,128)(2,1)S(1)} %get-tuple-element.40.refs_1_), channel_id=1, source_target_pairs={{0,1},{1,2},{2,3},{3,4},{4,5},{5,6},{6,7},{7,0},{8,9},{9,10},{10,1... | collective-permute-start | bytes 983048 | tf_op jit(solution)/shard_map/ppermute | solution.py:387
  31.5 14.9 %collective-permute-start.6 = (bf16[80,2048]{1,0:T(8,128)(2,1)S(1)}, bf16[80,2048]{1,0:T(8,128)(2,1)S(1)}, u32[]{:S(2)}, u32[]{:S(2)}) collective-permute-start(bf16[80,2048]{1,0:T(8,128)(2,1)S(1)} %get-tuple-element.39.refs_0_), channel_id=1, source_target_pairs={{0,7},{1,0},{2,1},{3,2},{4,3},{5,4},{6,5},{7,6},{8,15},{9,8},{10,9... | collective-permute-start | bytes 983048 | tf_op jit(solution)/shard_map/ppermute | solution.py:387
  37.8 14.0 %collective-permute-start.8 = (bf16[80,2048]{1,0:T(8,128)(2,1)S(1)}, bf16[80,2048]{1,0:T(8,128)(2,1)S(1)}, u32[]{:S(2)}, u32[]{:S(2)}) collective-permute-start(bf16[80,2048]{1,0:T(8,128)(2,1)S(1)} %collective-permute-done.4.refs_2_), channel_id=1, source_target_pairs={{0,1},{1,2},{2,3},{3,4},{4,5},{5,6},{6,7},{7,0},{8,9},{9,10},{10,1... | collective-permute-start | bytes 983048 | tf_op jit(solution)/shard_map/ppermute | solution.py:387
  39.3 14.0 %collective-permute-start.11 = (bf16[80,2048]{1,0:T(8,128)(2,1)S(1)}, bf16[80,2048]{1,0:T(8,128)(2,1)S(1)}, u32[]{:S(2)}, u32[]{:S(2)}) collective-permute-start(bf16[80,2048]{1,0:T(8,128)(2,1)S(1)} %collective-permute-done.7.refs_5_), channel_id=1, source_target_pairs={{0,7},{1,0},{2,1},{3,2},{4,3},{5,4},{6,5},{7,6},{8,15},{9,8},{10,9... | collective-permute-start | bytes 983048 | tf_op jit(solution)/shard_map/ppermute | solution.py:387
  44.8 14.0 %collective-permute-start.9 = (bf16[80,2048]{1,0:T(8,128)(2,1)S(1)}, bf16[80,2048]{1,0:T(8,128)(2,1)S(1)}, u32[]{:S(2)}, u32[]{:S(2)}) collective-permute-start(bf16[80,2048]{1,0:T(8,128)(2,1)S(1)} %collective-permute-done.5.refs_3_), channel_id=1, source_target_pairs={{0,1},{1,2},{2,3},{3,4},{4,5},{5,6},{6,7},{7,0},{8,9},{9,10},{10,1... | collective-permute-start | bytes 983048 | tf_op jit(solution)/shard_map/ppermute | solution.py:387
  46.4 13.9 %collective-permute-start.10 = (bf16[80,2048]{1,0:T(8,128)(2,1)S(1)}, bf16[80,2048]{1,0:T(8,128)(2,1)S(1)}, u32[]{:S(2)}, u32[]{:S(2)}) collective-permute-start(bf16[80,2048]{1,0:T(8,128)(2,1)S(1)} %collective-permute-done.6.refs_4_), channel_id=1, source_target_pairs={{0,7},{1,0},{2,1},{3,2},{4,3},{5,4},{6,5},{7,6},{8,15},{9,8},{10,9... | collective-permute-start | bytes 983048 | tf_op jit(solution)/shard_map/ppermute | solution.py:387
  51.8 14.0 %collective-permute-start.12 = (bf16[80,2048]{1,0:T(8,128)(2,1)S(1)}, bf16[80,2048]{1,0:T(8,128)(2,1)S(1)}, u32[]{:S(2)}, u32[]{:S(2)}) collective-permute-start(bf16[80,2048]{1,0:T(8,128)(2,1)S(1)} %collective-permute-done.8.refs_6_), channel_id=1, source_target_pairs={{0,1},{1,2},{2,3},{3,4},{4,5},{5,6},{6,7},{7,0},{8,9},{9,10},{10,1... | collective-permute-start | bytes 983048 | tf_op jit(solution)/shard_map/ppermute | solution.py:387
  53.3 14.0 %collective-permute-start.15 = (bf16[80,2048]{1,0:T(8,128)(2,1)S(1)}, bf16[80,2048]{1,0:T(8,128)(2,1)S(1)}, u32[]{:S(2)}, u32[]{:S(2)}) collective-permute-start(bf16[80,2048]{1,0:T(8,128)(2,1)S(1)} %collective-permute-done.11.refs_9_), channel_id=1, source_target_pairs={{0,7},{1,0},{2,1},{3,2},{4,3},{5,4},{6,5},{7,6},{8,15},{9,8},{10,9... | collective-permute-start | bytes 983048 | tf_op jit(solution)/shard_map/ppermute | solution.py:387
  58.8 14.1 %collective-permute-start.13 = (bf16[80,2048]{1,0:T(8,128)(2,1)S(1)}, bf16[80,2048]{1,0:T(8,128)(2,1)S(1)}, u32[]{:S(2)}, u32[]{:S(2)}) collective-permute-start(bf16[80,2048]{1,0:T(8,128)(2,1)S(1)} %collective-permute-done.9.refs_7_), channel_id=1, source_target_pairs={{0,1},{1,2},{2,3},{3,4},{4,5},{5,6},{6,7},{7,0},{8,9},{9,10},{10,1... | collective-permute-start | bytes 983048 | tf_op jit(solution)/shard_map/ppermute | solution.py:387
  60.4 13.8 %collective-permute-start.14 = (bf16[80,2048]{1,0:T(8,128)(2,1)S(1)}, bf16[80,2048]{1,0:T(8,128)(2,1)S(1)}, u32[]{:S(2)}, u32[]{:S(2)}) collective-permute-start(bf16[80,2048]{1,0:T(8,128)(2,1)S(1)} %collective-permute-done.10.refs_8_), channel_id=1, source_target_pairs={{0,7},{1,0},{2,1},{3,2},{4,3},{5,4},{6,5},{7,6},{8,15},{9,8},{10,9... | collective-permute-start | bytes 983048 | tf_op jit(solution)/shard_map/ppermute | solution.py:387
  65.9 14.1 %collective-permute-start.16 = (bf16[80,2048]{1,0:T(8,128)(2,1)S(1)}, bf16[80,2048]{1,0:T(8,128)(2,1)S(1)}, u32[]{:S(2)}, u32[]{:S(2)}) collective-permute-start(bf16[80,2048]{1,0:T(8,128)(2,1)S(1)} %collective-permute-done.12.refs_10_), channel_id=1, source_target_pairs={{0,1},{1,2},{2,3},{3,4},{4,5},{5,6},{6,7},{7,0},{8,9},{9,10},{10,1... | collective-permute-start | bytes 983048 | tf_op jit(solution)/shard_map/ppermute | solution.py:387
  67.4 13.8 %collective-permute-start.17 = (bf16[80,2048]{1,0:T(8,128)(2,1)S(1)}, bf16[80,2048]{1,0:T(8,128)(2,1)S(1)}, u32[]{:S(2)}, u32[]{:S(2)}) collective-permute-start(bf16[80,2048]{1,0:T(8,128)(2,1)S(1)} %collective-permute-done.15.refs_13_), channel_id=1, source_target_pairs={{0,7},{1,0},{2,1},{3,2},{4,3},{5,4},{6,5},{7,6},{8,15},{9,8},{10,9... | collective-permute-start | bytes 983048 | tf_op jit(solution)/shard_map/ppermute | solution.py:387
  82.1 10.3 %collective-permute-start.18 = (bf16[2,3,64,256]{3,2,1,0:T(8,128)(2,1)S(1)}, bf16[2,3,64,256]{3,2,1,0:T(8,128)(2,1)S(1)}, u32[]{:S(2)}, u32[]{:S(2)}) collective-permute-start(bf16[2,3,64,256]{3,2,1,0:T(8,128)(2,1)S(1)} %get-tuple-element.42), channel_id=1, source_target_pairs={{0,16},{16,32},{32,48},{48,0},{1,17},{17,33},{33,49},{49,1},{2,18}... | collective-permute-start | bytes 589832 | tf_op jit(solution)/shard_map/ppermute | solution.py:387
  83.4 10.7 %collective-permute-start.19 = (bf16[2,3,64,256]{3,2,1,0:T(8,128)(2,1)S(1)}, bf16[2,3,64,256]{3,2,1,0:T(8,128)(2,1)S(1)}, u32[]{:S(2)}, u32[]{:S(2)}) collective-permute-start(bf16[2,3,64,256]{3,2,1,0:T(8,128)(2,1)S(1)} %get-tuple-element.43), channel_id=1, source_target_pairs={{0,32},{16,48},{32,0},{48,16},{1,33},{17,49},{33,1},{49,17},{2,34}... | collective-permute-start | bytes 589832 | tf_op jit(solution)/shard_map/ppermute | solution.py:387
  86.0 8.1 %collective-permute-start.20 = (bf16[2,3,64,256]{3,2,1,0:T(8,128)(2,1)S(1)}, bf16[2,3,64,256]{3,2,1,0:T(8,128)(2,1)S(1)}, u32[]{:S(2)}, u32[]{:S(2)}) collective-permute-start(bf16[2,3,64,256]{3,2,1,0:T(8,128)(2,1)S(1)} %get-tuple-element.44), channel_id=1, source_target_pairs={{0,48},{16,0},{32,16},{48,32},{1,49},{17,1},{33,17},{49,33},{2,50}... | collective-permute-start | bytes 589832 | tf_op jit(solution)/shard_map/ppermute | solution.py:387
  95.1 20.0 %all-to-all-start = ((bf16[8,128,256]{2,1,0:T(8,128)(2,1)}), bf16[8,128,256]{2,1,0:T(8,128)(2,1)S(1)}, u32[]{:S(2)}, u32[]{:S(2)}) async-start(bf16[8,128,256]{2,1,0:T(8,128)(2,1)} %shard_map.83), calls=%async_computation | async-start | bytes 1048576 | tf_op jit(solution)/shard_map/all_to_all | solution.py:434
  122.4 38.0 %all-to-all-start.1 = ((bf16[16,32,2048]{2,1,0:T(8,128)(2,1)}), bf16[16,32,2048]{2,1,0:T(8,128)(2,1)}, u32[]{:S(2)}, u32[]{:S(2)}) async-start(bf16[16,32,2048]{2,1,0:T(8,128)(2,1)} %copy-done.3), calls=%async_computation.1 | async-start | bytes 4194304 | tf_op jit(solution)/shard_map/all_to_all | solution.py:447
  129.5 14.5 %collective-permute-start.21 = (bf16[128,2048]{1,0:T(8,128)(2,1)S(1)}, bf16[128,2048]{1,0:T(8,128)(2,1)S(1)}, u32[]{:S(2)}, u32[]{:S(2)}) collective-permute-start(bf16[128,2048]{1,0:T(8,128)(2,1)S(1)} %constant_dynamic-slice_fusion.refs_0_), channel_id=1, source_target_pairs={{0,1},{1,2},{2,3},{3,4},{4,5},{5,6},{6,7},{7,0},{8,9},{9,10},{10,1... | collective-permute-start | bytes 1572872 | tf_op jit(solution)/shard_map/ppermute | solution.py:387
  129.8 14.2 %collective-permute-start.22 = (bf16[128,2048]{1,0:T(8,128)(2,1)S(1)}, bf16[128,2048]{1,0:T(8,128)(2,1)S(1)}, u32[]{:S(2)}, u32[]{:S(2)}) collective-permute-start(bf16[128,2048]{1,0:T(8,128)(2,1)S(1)} %constant_dynamic-slice_fusion.refs_0_), channel_id=1, source_target_pairs={{0,7},{1,0},{2,1},{3,2},{4,3},{5,4},{6,5},{7,6},{8,15},{9,8},{10,9... | collective-permute-start | bytes 1572872 | tf_op jit(solution)/shard_map/ppermute | solution.py:387
  144.0 13.7 %collective-permute-start.23 = (bf16[128,2048]{1,0:T(8,128)(2,1)S(1)}, bf16[128,2048]{1,0:T(8,128)(2,1)}, u32[]{:S(2)}, u32[]{:S(2)}) collective-permute-start(bf16[128,2048]{1,0:T(8,128)(2,1)S(1)} %collective-permute-done.21.refs_1_), channel_id=1, source_target_pairs={{0,1},{1,2},{2,3},{3,4},{4,5},{5,6},{6,7},{7,0},{8,9},{9,10},{10,1... | collective-permute-start | bytes 1572872 | tf_op jit(solution)/shard_map/ppermute | solution.py:387
  144.0 13.7 %collective-permute-start.24 = (bf16[128,2048]{1,0:T(8,128)(2,1)S(1)}, bf16[128,2048]{1,0:T(8,128)(2,1)}, u32[]{:S(2)}, u32[]{:S(2)}) collective-permute-start(bf16[128,2048]{1,0:T(8,128)(2,1)S(1)} %collective-permute-done.22.refs_2_), channel_id=1, source_target_pairs={{0,7},{1,0},{2,1},{3,2},{4,3},{5,4},{6,5},{7,6},{8,15},{9,8},{10,9... | collective-permute-start | bytes 1572872 | tf_op jit(solution)/shard_map/ppermute | solution.py:387
  157.7 21.7 %collective-permute-start.25 = (bf16[128,2048]{1,0:T(8,128)(2,1)}, bf16[128,2048]{1,0:T(8,128)(2,1)S(1)}, u32[]{:S(2)}, u32[]{:S(2)}) collective-permute-start(bf16[128,2048]{1,0:T(8,128)(2,1)} %collective-permute-done.23.refs_3_), channel_id=1, source_target_pairs={{0,1},{1,2},{2,3},{3,4},{4,5},{5,6},{6,7},{7,0},{8,9},{9,10},{10,1... | collective-permute-start | bytes 1572872 | tf_op jit(solution)/shard_map/ppermute | solution.py:387
  157.7 21.8 %collective-permute-start.26 = (bf16[128,2048]{1,0:T(8,128)(2,1)}, bf16[128,2048]{1,0:T(8,128)(2,1)S(1)}, u32[]{:S(2)}, u32[]{:S(2)}) collective-permute-start(bf16[128,2048]{1,0:T(8,128)(2,1)} %collective-permute-done.24.refs_4_), channel_id=1, source_target_pairs={{0,7},{1,0},{2,1},{3,2},{4,3},{5,4},{6,5},{7,6},{8,15},{9,8},{10,9... | collective-permute-start | bytes 1572872 | tf_op jit(solution)/shard_map/ppermute | solution.py:387
  171.6 17.7 %all-to-all-start.2 = ((bf16[16,2,32,256]{3,2,1,0:T(8,128)(2,1)}), bf16[16,2,32,256]{3,2,1,0:T(8,128)(2,1)S(1)}, u32[]{:S(2)}, u32[]{:S(2)}) async-start(bf16[16,2,32,256]{3,2,1,0:T(8,128)(2,1)} %copy-done.10), calls=%async_computation.2 | async-start | bytes 1048576 | tf_op jit(solution)/shard_map/all_to_all | solution.py:451
  179.4 9.2 %collective-permute-start.27 = (bf16[64,2048]{1,0:T(8,128)(2,1)S(1)}, bf16[64,2048]{1,0:T(8,128)(2,1)S(1)}, u32[]{:S(2)}, u32[]{:S(2)}) collective-permute-start(bf16[64,2048]{1,0:T(8,128)(2,1)S(1)} %slice.8), channel_id=1, source_target_pairs={{0,1},{1,2},{2,3},{3,4},{4,5},{5,6},{6,7},{7,0},{8,9},{9,10},{10,1... | collective-permute-start | bytes 786440 | tf_op jit(solution)/shard_map/ppermute | solution.py:387
  179.5 9.0 %collective-permute-start.28 = (bf16[64,2048]{1,0:T(8,128)(2,1)S(1)}, bf16[64,2048]{1,0:T(8,128)(2,1)S(1)}, u32[]{:S(2)}, u32[]{:S(2)}) collective-permute-start(bf16[64,2048]{1,0:T(8,128)(2,1)S(1)} %slice.9), channel_id=1, source_target_pairs={{0,7},{1,0},{2,1},{3,2},{4,3},{5,4},{6,5},{7,6},{8,15},{9,8},{10,9... | collective-permute-start | bytes 786440 | tf_op jit(solution)/shard_map/ppermute | solution.py:387
  (22 other events, 269.3 us)
Sparse Core Ops, SparseCore 0:
  26.5 59.9 all-gather.4
  95.2 44.2 all-gather.6

commit v12 on v7

--- a/solution.py
+++ b/solution.py
@@ -430,6 +430,8 @@
     halves = [half]
     for step in (1, 2, 3):
         up, down = shifted(up, "z", 1), shifted(down, "z", -1)
+        if step == 1:
+            up, down, quarter = lax.optimization_barrier((up, down, quarter))
         halves += [up, down]
     halves += [shifted(up[:64], "z", 1), shifted(down[64:], "z", -1)]
 

time: 206 us -> 210 us (1.019)
    ppermute x26, waiting for transfers between devices: 65.8 us -> 50.2 us  [shifted(): lax.ppermute(value, axis, [(i, (i + step) % count) for i in range(count)])]
    all_to_all x1, waiting for transfers between devices: 0.01 us -> 10.8 us  [local(): window = lax.all_to_all(send, ('xl', 'y', 'c'), 0, 0, tiled=True)]
    all_to_all x1, waiting for transfers between devices: 0.01 us -> 5.58 us  [local(): mix = lax.all_to_all(mix, ('xl', 'y', 'c'), 0, 0, tiled=True)]
  transfers between devices with their start and end apart: 35 -> 35, of which waited for: 15 -> 16; matrix products, arithmetic and copies ran while one was open for 0% -> 1% of each run, Pallas kernels for 8% -> 8%
where the time goes in v12:
time: 210 us; the launch traced here: 208 us
  waiting for transfers between devices  82.3 us (39%)
  starting transfers between devices  70.3 us (33%)
  Pallas kernels  21.2 us (10%)
  local copies, waits for them, and re-layouts  20.6 us (10%)
  between operations  13.6 us (6%)
    ppermute x26, waiting for transfers between devices, shifted(): lax.ppermute(value, axis, [(i, (i + step) % count) for i in range(count)])  50.2 us
    ppermute x26, starting transfers between devices, shifted(): lax.ppermute(value, axis, [(i, (i + step) % count) for i in range(count)])  37.7 us
    unnamed x38, local copies, waits for them, and re-layouts  17.7 us
    all_to_all x1, waiting for transfers between devices, local(): mix = lax.all_to_all(mix, 'z', 0, 0, tiled=True)  15.6 us
    ppermute x4, starting transfers between devices, local(): parts.append(lax.ppermute(block, ('c', 'z'), pairs))  13.8 us
    all_to_all x1, waiting for transfers between devices, local(): window = lax.all_to_all(send, ('xl', 'y', 'c'), 0, 0, tiled=True)  10.8 us
    pallas_call x1, Pallas kernels, temporal_attend(): pl.pallas_call(temporal_kernel, out_shape=jax.ShapeDtypeStruct((16, 2, 32...  7.61 us
    all_to_all x1, starting transfers between devices, local(): mix = lax.all_to_all(mix, ('xl', 'y', 'c'), 0, 0, tiled=True)  7.25 us
  transfers between devices with their start and end apart: 35, of which 16 were waited for; matrix products, arithmetic and copies ran while one was open for 1% of the time, Pallas kernels for 8%

profile of v12, /device:TPU:1, one launch (start us, length us, event | category | flops | bytes accessed | tf_op | source)
XLA Modules:
  0.0 208.2 jit_solution(7976464119442888743)
XLA Ops:
  7.5 10.2 %collective-permute-start = (bf16[128,256]{1,0:T(8,128)(2,1)S(1)}, bf16[128,256]{1,0:T(8,128)(2,1)S(1)}, u32[]{:S(2)}, u32[]{:S(2)}) collective-permute-start(bf16[128,256]{1,0:T(8,128)(2,1)S(1)} %dynamic_slice.10), channel_id=1, source_target_pairs={{0,0},{1,1},{2,2},{3,3},{4,12},{5,13},{6,14},{7,15},{8,4},{9,5},{1... | collective-permute-start | bytes 196616 | tf_op jit(solution)/shard_map/ppermute | solution.py:406
  18.5 2.8 %collective-permute-start.3 = (bf16[128,256]{1,0:T(8,128)(2,1)S(1)}, bf16[128,256]{1,0:T(8,128)(2,1)S(1)}, u32[]{:S(2)}, u32[]{:S(2)}) collective-permute-start(bf16[128,256]{1,0:T(8,128)(2,1)S(1)} %dynamic_slice.10), channel_id=1, source_target_pairs={{0,3},{1,4},{2,5},{3,6},{4,15},{5,8},{6,9},{7,10},{8,7},{9,0},{10,... | collective-permute-start | bytes 196616 | tf_op jit(solution)/shard_map/ppermute | solution.py:406
  21.3 1.9 copy-done.2
  26.4 3.6 %collective-permute-start.4 = (bf16[80,2048]{1,0:T(8,128)(2,1)S(1)}, bf16[80,2048]{1,0:T(8,128)(2,1)S(1)}, u32[]{:S(2)}, u32[]{:S(2)}) collective-permute-start(bf16[80,2048]{1,0:T(8,128)(2,1)S(1)} %get-tuple-element.42.refs_0_), channel_id=1, source_target_pairs={{0,1},{1,2},{2,3},{3,4},{4,5},{5,6},{6,7},{7,0},{8,9},{9,10},{10,1... | collective-permute-start | bytes 983048 | tf_op jit(solution)/shard_map/ppermute | solution.py:376
  32.7 5.1 %collective-permute-done.4.refs_2_ = bf16[80,2048]{1,0:T(8,128)(2,1)S(1)} collective-permute-done((bf16[80,2048]{1,0:T(8,128)(2,1)S(1)}, bf16[80,2048]{1,0:T(8,128)(2,1)S(1)}, u32[]{:S(2)}, u32[]{:S(2)}) %collective-permute-start.4) | collective-permute-done | bytes 327712 | tf_op jit(solution)/shard_map/ppermute | solution.py:376
  37.8 1.5 collective-permute-start.8
  40.5 4.3 %collective-permute-done.5.refs_3_ = bf16[80,2048]{1,0:T(8,128)(2,1)S(1)} collective-permute-done((bf16[80,2048]{1,0:T(8,128)(2,1)S(1)}, bf16[80,2048]{1,0:T(8,128)(2,1)S(1)}, u32[]{:S(2)}, u32[]{:S(2)}) %collective-permute-start.5) | collective-permute-done | bytes 327712 | tf_op jit(solution)/shard_map/ppermute | solution.py:376
  44.8 1.6 collective-permute-start.9
  47.5 4.3 %collective-permute-done.8.refs_6_ = bf16[80,2048]{1,0:T(8,128)(2,1)S(1)} collective-permute-done((bf16[80,2048]{1,0:T(8,128)(2,1)S(1)}, bf16[80,2048]{1,0:T(8,128)(2,1)S(1)}, u32[]{:S(2)}, u32[]{:S(2)}) %collective-permute-start.8) | collective-permute-done | bytes 327712 | tf_op jit(solution)/shard_map/ppermute | solution.py:376
  54.5 4.3 %collective-permute-done.9.refs_7_ = bf16[80,2048]{1,0:T(8,128)(2,1)S(1)} collective-permute-done((bf16[80,2048]{1,0:T(8,128)(2,1)S(1)}, bf16[80,2048]{1,0:T(8,128)(2,1)S(1)}, u32[]{:S(2)}, u32[]{:S(2)}) %collective-permute-start.9) | collective-permute-done | bytes 327712 | tf_op jit(solution)/shard_map/ppermute | solution.py:376
  61.6 4.3 %collective-permute-done.12.refs_10_ = bf16[80,2048]{1,0:T(8,128)(2,1)S(1)} collective-permute-done((bf16[80,2048]{1,0:T(8,128)(2,1)S(1)}, bf16[80,2048]{1,0:T(8,128)(2,1)S(1)}, u32[]{:S(2)}, u32[]{:S(2)}) %collective-permute-start.12) | collective-permute-done | bytes 327712 | tf_op jit(solution)/shard_map/ppermute | solution.py:376
  68.7 4.3 %collective-permute-done.13.refs_11_ = bf16[80,2048]{1,0:T(8,128)(2,1)S(1)} collective-permute-done((bf16[80,2048]{1,0:T(8,128)(2,1)S(1)}, bf16[80,2048]{1,0:T(8,128)(2,1)S(1)}, u32[]{:S(2)}, u32[]{:S(2)}) %collective-permute-start.13) | collective-permute-done | bytes 327712 | tf_op jit(solution)/shard_map/ppermute | solution.py:376
  74.2 5.8 %collective-permute-done.16.refs_14_ = bf16[80,2048]{1,0:T(8,128)(2,1)S(1)} collective-permute-done((bf16[80,2048]{1,0:T(8,128)(2,1)S(1)}, bf16[80,2048]{1,0:T(8,128)(2,1)S(1)}, u32[]{:S(2)}, u32[]{:S(2)}) %collective-permute-start.16) | collective-permute-done | bytes 327712 | tf_op jit(solution)/shard_map/ppermute | solution.py:376
  83.4 2.6 %collective-permute-start.19 = (bf16[2,3,64,256]{3,2,1,0:T(8,128)(2,1)S(1)}, bf16[2,3,64,256]{3,2,1,0:T(8,128)(2,1)S(1)}, u32[]{:S(2)}, u32[]{:S(2)}) collective-permute-start(bf16[2,3,64,256]{3,2,1,0:T(8,128)(2,1)S(1)} %get-tuple-element.46), channel_id=1, source_target_pairs={{0,32},{16,48},{32,0},{48,16},{1,33},{17,49},{33,1},{49,17},{2,34}... | collective-permute-start | bytes 589832 | tf_op jit(solution)/shard_map/ppermute | solution.py:376
  87.1 5.3 %shard_map.83 = bf16[8,128,256]{2,1,0:T(8,128)(2,1)} custom-call(s32[1]{0:T(128)} %bitcast.place_ref.z_ref, bf16[3,2048,256]{2,1,0:T(8,128)(2,1)S(1)} %bitcast.16, bf16[80,2048]{1,0:T(8,128)(2,1)S(1)} %get-tuple-element.42.refs_0_, bf16[80,2048]{1,0:T(8,128)(2,1)S(1)} %get-tuple-element.43.refs_1_, bf16[80,2048]{1,0:T(8,128)(2,1)S(1)} %collective-permute-done.4.refs_2_, ...), custom_call_target="tpu_custom_call" | custom-call | flops 6442450944 | bytes 8388608 | tf_op jit(solution)/shard_map/pallas_call | solution.py:184
  92.4 1.7 collective-permute-done.19.refs_2_
  95.1 4.4 %all-to-all-start = ((bf16[8,128,256]{2,1,0:T(8,128)(2,1)}), bf16[8,128,256]{2,1,0:T(8,128)(2,1)S(1)}, u32[]{:S(2)}, u32[]{:S(2)}) async-start(bf16[8,128,256]{2,1,0:T(8,128)(2,1)} %shard_map.83), calls=%async_computation | async-start | bytes 1048576 | tf_op jit(solution)/shard_map/all_to_all | solution.py:423
  99.5 15.6 %all-to-all-done.mix_ref = bf16[8,128,256]{2,1,0:T(8,128)(2,1)S(1)} async-done(((bf16[8,128,256]{2,1,0:T(8,128)(2,1)}), bf16[8,128,256]{2,1,0:T(8,128)(2,1)S(1)}, u32[]{:S(2)}, u32[]{:S(2)}) %all-to-all-start) | async-done | bytes 524320 | tf_op jit(solution)/shard_map/all_to_all | solution.py:423
  115.2 3.5 %copy-done.1 = bf16[128,128,256]{2,1,0:T(8,128)(2,1)S(1)} copy-done((bf16[128,128,256]{2,1,0:T(8,128)(2,1)S(1)}, bf16[128,128,256]{2,1,0:T(8,128)(2,1)}, u32[]{:S(2)}) %copy-start.1) | copy-done | bytes 8388632
  122.4 7.1 %all-to-all-start.1 = ((bf16[16,32,2048]{2,1,0:T(8,128)(2,1)}), bf16[16,32,2048]{2,1,0:T(8,128)(2,1)}, u32[]{:S(2)}, u32[]{:S(2)}) async-start(bf16[16,32,2048]{2,1,0:T(8,128)(2,1)} %copy-done.3), calls=%async_computation.1 | async-start | bytes 4194304 | tf_op jit(solution)/shard_map/all_to_all | solution.py:438
  129.8 2.4 %collective-permute-start.22 = (bf16[128,2048]{1,0:T(8,128)(2,1)S(1)}, bf16[128,2048]{1,0:T(8,128)(2,1)S(1)}, u32[]{:S(2)}, u32[]{:S(2)}) collective-permute-start(bf16[128,2048]{1,0:T(8,128)(2,1)S(1)} %constant_dynamic-slice_fusion.refs_0_), channel_id=1, source_target_pairs={{0,7},{1,0},{2,1},{3,2},{4,3},{5,4},{6,5},{7,6},{8,15},{9,8},{10,9... | collective-permute-start | bytes 1572872 | tf_op jit(solution)/shard_map/ppermute | solution.py:376
  132.2 11.8 %collective-permute-done.21.refs_1_ = bf16[128,2048]{1,0:T(8,128)(2,1)S(1)} collective-permute-done((bf16[128,2048]{1,0:T(8,128)(2,1)S(1)}, bf16[128,2048]{1,0:T(8,128)(2,1)S(1)}, u32[]{:S(2)}, u32[]{:S(2)}) %collective-permute-start.21) | collective-permute-done | bytes 524320 | tf_op jit(solution)/shard_map/ppermute | solution.py:376
  144.3 3.1 %collective-permute-start.24 = (bf16[128,2048]{1,0:T(8,128)(2,1)S(1)}, bf16[128,2048]{1,0:T(8,128)(2,1)S(1)}, u32[]{:S(2)}, u32[]{:S(2)}) collective-permute-start(bf16[128,2048]{1,0:T(8,128)(2,1)S(1)} %collective-permute-done.22.refs_2_), channel_id=1, source_target_pairs={{0,7},{1,0},{2,1},{3,2},{4,3},{5,4},{6,5},{7,6},{8,15},{9,8},{10,9... | collective-permute-start | bytes 1572872 | tf_op jit(solution)/shard_map/ppermute | solution.py:376
  148.8 10.8 %all-to-all-done.1 = bf16[16,32,2048]{2,1,0:T(8,128)(2,1)} async-done(((bf16[16,32,2048]{2,1,0:T(8,128)(2,1)}), bf16[16,32,2048]{2,1,0:T(8,128)(2,1)}, u32[]{:S(2)}, u32[]{:S(2)}) %all-to-all-start.1) | async-done | bytes 2097184 | tf_op jit(solution)/shard_map/all_to_all | solution.py:438
  161.7 1.7 collective-permute-start.26
  163.4 2.8 %copy-done.16 = bf16[48,256,256]{2,1,0:T(8,128)(2,1)S(1)} copy-done((bf16[48,256,256]{2,1,0:T(8,128)(2,1)S(1)}, bf16[48,256,256]{2,1,0:T(8,128)(2,1)}, u32[]{:S(2)}) %copy-start.16) | copy-done | bytes 6291480
  166.2 7.6 %shard_map.88 = bf16[16,2,32,256]{3,2,1,0:T(8,128)(2,1)S(1)} custom-call(s32[1]{0:T(128)} %dynamic_slice.9.start_ref, bf16[512,2048]{1,0:T(8,128)(2,1)} %bitcast.10.rows_ref, bf16[8,6,256,256]{3,2,1,0:T(8,128)(2,1)S(1)} %bitcast.15), custom_call_target="tpu_custom_call" | custom-call | flops 3221225472 | bytes 9437184 | tf_op jit(solution)/shard_map/pallas_call | solution.py:288
  174.6 7.2 %all-to-all-start.2 = ((bf16[16,2,32,256]{3,2,1,0:T(8,128)(2,1)}), bf16[16,2,32,256]{3,2,1,0:T(8,128)(2,1)S(1)}, u32[]{:S(2)}, u32[]{:S(2)}) async-start(bf16[16,2,32,256]{3,2,1,0:T(8,128)(2,1)} %copy-done.12), calls=%async_computation.2 | async-start | bytes 1048576 | tf_op jit(solution)/shard_map/all_to_all | solution.py:442
  183.3 2.7 %collective-permute-start.28 = (bf16[64,2048]{1,0:T(8,128)(2,1)}, bf16[64,2048]{1,0:T(8,128)(2,1)}, u32[]{:S(2)}, u32[]{:S(2)}) collective-permute-start(bf16[64,2048]{1,0:T(8,128)(2,1)} %slice.9), channel_id=1, source_target_pairs={{0,7},{1,0},{2,1},{3,2},{4,3},{5,4},{6,5},{7,6},{8,15},{9,8},{10,9... | collective-permute-start | bytes 786440 | tf_op jit(solution)/shard_map/ppermute | solution.py:376
  186.1 5.6 %all-to-all-done.2.mix_ref = bf16[16,2,32,256]{3,2,1,0:T(8,128)(2,1)S(1)} async-done(((bf16[16,2,32,256]{3,2,1,0:T(8,128)(2,1)}), bf16[16,2,32,256]{3,2,1,0:T(8,128)(2,1)S(1)}, u32[]{:S(2)}, u32[]{:S(2)}) %all-to-all-start.2) | async-done | bytes 524320 | tf_op jit(solution)/shard_map/all_to_all | solution.py:442
  195.0 2.5 %shard_map.89 = (f32[128,2048]{1,0:T(8,128)S(1)}, bf16[128,2048]{1,0:T(8,128)(2,1)S(1)}) custom-call(s32[2]{0:T(128)S(1)} %pad_add_fusion.place_ref, bf16[16,2,32,256]{3,2,1,0:T(8,128)(2,1)S(1)} %all-to-all-done.2.mix_ref, bf16[128,2048]{1,0:T(8,128)(2,1)S(1)} %constant_dynamic-slice_fusion.refs_0_, bf16[128,2048]{1,0:T(8,128)(2,1)S(1)} %copy-done.7, ...), custom_call_target="tpu_custom_call" | custom-call | flops 1073741824 | bytes 8388608 | tf_op jit(solution)/shard_map/pallas_call | solution.py:332
  198.6 1.5 collective-permute-done.29.got_ref
  (94 shorter events, 40.5 us)
Async XLA Ops:
  6.5 88.5 %all-gather.5.cloned.1.call-start = ((), (), s32[]{:S(2)}) async-start(), calls=%async_computation.3 | async-start | bytes 8650752 | tf_op jit(solution)/shard_map/all_gather | solution.py:409
  7.5 18.1 %collective-permute-start = (bf16[128,256]{1,0:T(8,128)(2,1)S(1)}, bf16[128,256]{1,0:T(8,128)(2,1)S(1)}, u32[]{:S(2)}, u32[]{:S(2)}) collective-permute-start(bf16[128,256]{1,0:T(8,128)(2,1)S(1)} %dynamic_slice.10), channel_id=1, source_target_pairs={{0,0},{1,1},{2,2},{3,3},{4,12},{5,13},{6,14},{7,15},{8,4},{9,5},{1... | collective-permute-start | bytes 196616 | tf_op jit(solution)/shard_map/ppermute | solution.py:406
  17.7 7.9 %collective-permute-start.1 = (bf16[128,256]{1,0:T(8,128)(2,1)S(1)}, bf16[128,256]{1,0:T(8,128)(2,1)S(1)}, u32[]{:S(2)}, u32[]{:S(2)}) collective-permute-start(bf16[128,256]{1,0:T(8,128)(2,1)S(1)} %dynamic_slice.10), channel_id=1, source_target_pairs={{0,1},{1,2},{2,3},{3,4},{4,13},{5,14},{6,15},{7,8},{8,5},{9,6},{10... | collective-permute-start | bytes 196616 | tf_op jit(solution)/shard_map/ppermute | solution.py:406
  26.4 117.7 %all-gather.7.cloned.1.call-start = ((), (), s32[]{:S(2)}) async-start(), calls=%async_computation.4 | async-start | bytes 7077888 | tf_op jit(solution)/shard_map/all_gather | solution.py:422
  26.4 11.4 %collective-permute-start.4 = (bf16[80,2048]{1,0:T(8,128)(2,1)S(1)}, bf16[80,2048]{1,0:T(8,128)(2,1)S(1)}, u32[]{:S(2)}, u32[]{:S(2)}) collective-permute-start(bf16[80,2048]{1,0:T(8,128)(2,1)S(1)} %get-tuple-element.42.refs_0_), channel_id=1, source_target_pairs={{0,1},{1,2},{2,3},{3,4},{4,5},{5,6},{6,7},{7,0},{8,9},{9,10},{10,1... | collective-permute-start | bytes 983048 | tf_op jit(solution)/shard_map/ppermute | solution.py:376
  30.0 9.3 %collective-permute-start.7 = (bf16[80,2048]{1,0:T(8,128)(2,1)S(1)}, bf16[80,2048]{1,0:T(8,128)(2,1)S(1)}, u32[]{:S(2)}, u32[]{:S(2)}) collective-permute-start(bf16[80,2048]{1,0:T(8,128)(2,1)S(1)} %get-tuple-element.43.refs_1_), channel_id=1, source_target_pairs={{0,7},{1,0},{2,1},{3,2},{4,3},{5,4},{6,5},{7,6},{8,15},{9,8},{10,9... | collective-permute-start | bytes 983048 | tf_op jit(solution)/shard_map/ppermute | solution.py:376
  30.0 14.8 %collective-permute-start.5 = (bf16[80,2048]{1,0:T(8,128)(2,1)S(1)}, bf16[80,2048]{1,0:T(8,128)(2,1)S(1)}, u32[]{:S(2)}, u32[]{:S(2)}) collective-permute-start(bf16[80,2048]{1,0:T(8,128)(2,1)S(1)} %get-tuple-element.43.refs_1_), channel_id=1, source_target_pairs={{0,1},{1,2},{2,3},{3,4},{4,5},{5,6},{6,7},{7,0},{8,9},{9,10},{10,1... | collective-permute-start | bytes 983048 | tf_op jit(solution)/shard_map/ppermute | solution.py:376
  31.5 14.9 %collective-permute-start.6 = (bf16[80,2048]{1,0:T(8,128)(2,1)S(1)}, bf16[80,2048]{1,0:T(8,128)(2,1)S(1)}, u32[]{:S(2)}, u32[]{:S(2)}) collective-permute-start(bf16[80,2048]{1,0:T(8,128)(2,1)S(1)} %get-tuple-element.42.refs_0_), channel_id=1, source_target_pairs={{0,7},{1,0},{2,1},{3,2},{4,3},{5,4},{6,5},{7,6},{8,15},{9,8},{10,9... | collective-permute-start | bytes 983048 | tf_op jit(solution)/shard_map/ppermute | solution.py:376
  37.8 14.0 %collective-permute-start.8 = (bf16[80,2048]{1,0:T(8,128)(2,1)S(1)}, bf16[80,2048]{1,0:T(8,128)(2,1)S(1)}, u32[]{:S(2)}, u32[]{:S(2)}) collective-permute-start(bf16[80,2048]{1,0:T(8,128)(2,1)S(1)} %collective-permute-done.4.refs_2_), channel_id=1, source_target_pairs={{0,1},{1,2},{2,3},{3,4},{4,5},{5,6},{6,7},{7,0},{8,9},{9,10},{10,1... | collective-permute-start | bytes 983048 | tf_op jit(solution)/shard_map/ppermute | solution.py:376
  39.3 14.0 %collective-permute-start.11 = (bf16[80,2048]{1,0:T(8,128)(2,1)S(1)}, bf16[80,2048]{1,0:T(8,128)(2,1)S(1)}, u32[]{:S(2)}, u32[]{:S(2)}) collective-permute-start(bf16[80,2048]{1,0:T(8,128)(2,1)S(1)} %collective-permute-done.7.refs_5_), channel_id=1, source_target_pairs={{0,7},{1,0},{2,1},{3,2},{4,3},{5,4},{6,5},{7,6},{8,15},{9,8},{10,9... | collective-permute-start | bytes 983048 | tf_op jit(solution)/shard_map/ppermute | solution.py:376
  44.8 14.0 %collective-permute-start.9 = (bf16[80,2048]{1,0:T(8,128)(2,1)S(1)}, bf16[80,2048]{1,0:T(8,128)(2,1)S(1)}, u32[]{:S(2)}, u32[]{:S(2)}) collective-permute-start(bf16[80,2048]{1,0:T(8,128)(2,1)S(1)} %collective-permute-done.5.refs_3_), channel_id=1, source_target_pairs={{0,1},{1,2},{2,3},{3,4},{4,5},{5,6},{6,7},{7,0},{8,9},{9,10},{10,1... | collective-permute-start | bytes 983048 | tf_op jit(solution)/shard_map/ppermute | solution.py:376
  46.4 13.9 %collective-permute-start.10 = (bf16[80,2048]{1,0:T(8,128)(2,1)S(1)}, bf16[80,2048]{1,0:T(8,128)(2,1)S(1)}, u32[]{:S(2)}, u32[]{:S(2)}) collective-permute-start(bf16[80,2048]{1,0:T(8,128)(2,1)S(1)} %collective-permute-done.6.refs_4_), channel_id=1, source_target_pairs={{0,7},{1,0},{2,1},{3,2},{4,3},{5,4},{6,5},{7,6},{8,15},{9,8},{10,9... | collective-permute-start | bytes 983048 | tf_op jit(solution)/shard_map/ppermute | solution.py:376
  51.8 14.0 %collective-permute-start.12 = (bf16[80,2048]{1,0:T(8,128)(2,1)S(1)}, bf16[80,2048]{1,0:T(8,128)(2,1)S(1)}, u32[]{:S(2)}, u32[]{:S(2)}) collective-permute-start(bf16[80,2048]{1,0:T(8,128)(2,1)S(1)} %collective-permute-done.8.refs_6_), channel_id=1, source_target_pairs={{0,1},{1,2},{2,3},{3,4},{4,5},{5,6},{6,7},{7,0},{8,9},{9,10},{10,1... | collective-permute-start | bytes 983048 | tf_op jit(solution)/shard_map/ppermute | solution.py:376
  53.3 14.0 %collective-permute-start.15 = (bf16[80,2048]{1,0:T(8,128)(2,1)S(1)}, bf16[80,2048]{1,0:T(8,128)(2,1)S(1)}, u32[]{:S(2)}, u32[]{:S(2)}) collective-permute-start(bf16[80,2048]{1,0:T(8,128)(2,1)S(1)} %collective-permute-done.11.refs_9_), channel_id=1, source_target_pairs={{0,7},{1,0},{2,1},{3,2},{4,3},{5,4},{6,5},{7,6},{8,15},{9,8},{10,9... | collective-permute-start | bytes 983048 | tf_op jit(solution)/shard_map/ppermute | solution.py:376
  58.8 14.1 %collective-permute-start.13 = (bf16[80,2048]{1,0:T(8,128)(2,1)S(1)}, bf16[80,2048]{1,0:T(8,128)(2,1)S(1)}, u32[]{:S(2)}, u32[]{:S(2)}) collective-permute-start(bf16[80,2048]{1,0:T(8,128)(2,1)S(1)} %collective-permute-done.9.refs_7_), channel_id=1, source_target_pairs={{0,1},{1,2},{2,3},{3,4},{4,5},{5,6},{6,7},{7,0},{8,9},{9,10},{10,1... | collective-permute-start | bytes 983048 | tf_op jit(solution)/shard_map/ppermute | solution.py:376
  60.4 13.8 %collective-permute-start.14 = (bf16[80,2048]{1,0:T(8,128)(2,1)S(1)}, bf16[80,2048]{1,0:T(8,128)(2,1)S(1)}, u32[]{:S(2)}, u32[]{:S(2)}) collective-permute-start(bf16[80,2048]{1,0:T(8,128)(2,1)S(1)} %collective-permute-done.10.refs_8_), channel_id=1, source_target_pairs={{0,7},{1,0},{2,1},{3,2},{4,3},{5,4},{6,5},{7,6},{8,15},{9,8},{10,9... | collective-permute-start | bytes 983048 | tf_op jit(solution)/shard_map/ppermute | solution.py:376
  65.9 14.1 %collective-permute-start.16 = (bf16[80,2048]{1,0:T(8,128)(2,1)S(1)}, bf16[80,2048]{1,0:T(8,128)(2,1)S(1)}, u32[]{:S(2)}, u32[]{:S(2)}) collective-permute-start(bf16[80,2048]{1,0:T(8,128)(2,1)S(1)} %collective-permute-done.12.refs_10_), channel_id=1, source_target_pairs={{0,1},{1,2},{2,3},{3,4},{4,5},{5,6},{6,7},{7,0},{8,9},{9,10},{10,1... | collective-permute-start | bytes 983048 | tf_op jit(solution)/shard_map/ppermute | solution.py:376
  67.4 13.8 %collective-permute-start.17 = (bf16[80,2048]{1,0:T(8,128)(2,1)S(1)}, bf16[80,2048]{1,0:T(8,128)(2,1)S(1)}, u32[]{:S(2)}, u32[]{:S(2)}) collective-permute-start(bf16[80,2048]{1,0:T(8,128)(2,1)S(1)} %collective-permute-done.15.refs_13_), channel_id=1, source_target_pairs={{0,7},{1,0},{2,1},{3,2},{4,3},{5,4},{6,5},{7,6},{8,15},{9,8},{10,9... | collective-permute-start | bytes 983048 | tf_op jit(solution)/shard_map/ppermute | solution.py:376
  82.1 10.3 %collective-permute-start.18 = (bf16[2,3,64,256]{3,2,1,0:T(8,128)(2,1)S(1)}, bf16[2,3,64,256]{3,2,1,0:T(8,128)(2,1)S(1)}, u32[]{:S(2)}, u32[]{:S(2)}) collective-permute-start(bf16[2,3,64,256]{3,2,1,0:T(8,128)(2,1)S(1)} %get-tuple-element.45), channel_id=1, source_target_pairs={{0,16},{16,32},{32,48},{48,0},{1,17},{17,33},{33,49},{49,1},{2,18}... | collective-permute-start | bytes 589832 | tf_op jit(solution)/shard_map/ppermute | solution.py:376
  83.4 10.7 %collective-permute-start.19 = (bf16[2,3,64,256]{3,2,1,0:T(8,128)(2,1)S(1)}, bf16[2,3,64,256]{3,2,1,0:T(8,128)(2,1)S(1)}, u32[]{:S(2)}, u32[]{:S(2)}) collective-permute-start(bf16[2,3,64,256]{3,2,1,0:T(8,128)(2,1)S(1)} %get-tuple-element.46), channel_id=1, source_target_pairs={{0,32},{16,48},{32,0},{48,16},{1,33},{17,49},{33,1},{49,17},{2,34}... | collective-permute-start | bytes 589832 | tf_op jit(solution)/shard_map/ppermute | solution.py:376
  86.0 8.1 %collective-permute-start.20 = (bf16[2,3,64,256]{3,2,1,0:T(8,128)(2,1)S(1)}, bf16[2,3,64,256]{3,2,1,0:T(8,128)(2,1)S(1)}, u32[]{:S(2)}, u32[]{:S(2)}) collective-permute-start(bf16[2,3,64,256]{3,2,1,0:T(8,128)(2,1)S(1)} %get-tuple-element.47), channel_id=1, source_target_pairs={{0,48},{16,0},{32,16},{48,32},{1,49},{17,1},{33,17},{49,33},{2,50}... | collective-permute-start | bytes 589832 | tf_op jit(solution)/shard_map/ppermute | solution.py:376
  95.1 20.0 %all-to-all-start = ((bf16[8,128,256]{2,1,0:T(8,128)(2,1)}), bf16[8,128,256]{2,1,0:T(8,128)(2,1)S(1)}, u32[]{:S(2)}, u32[]{:S(2)}) async-start(bf16[8,128,256]{2,1,0:T(8,128)(2,1)} %shard_map.83), calls=%async_computation | async-start | bytes 1048576 | tf_op jit(solution)/shard_map/all_to_all | solution.py:423
  122.4 37.3 %all-to-all-start.1 = ((bf16[16,32,2048]{2,1,0:T(8,128)(2,1)}), bf16[16,32,2048]{2,1,0:T(8,128)(2,1)}, u32[]{:S(2)}, u32[]{:S(2)}) async-start(bf16[16,32,2048]{2,1,0:T(8,128)(2,1)} %copy-done.3), calls=%async_computation.1 | async-start | bytes 4194304 | tf_op jit(solution)/shard_map/all_to_all | solution.py:438
  129.5 14.5 %collective-permute-start.21 = (bf16[128,2048]{1,0:T(8,128)(2,1)S(1)}, bf16[128,2048]{1,0:T(8,128)(2,1)S(1)}, u32[]{:S(2)}, u32[]{:S(2)}) collective-permute-start(bf16[128,2048]{1,0:T(8,128)(2,1)S(1)} %constant_dynamic-slice_fusion.refs_0_), channel_id=1, source_target_pairs={{0,1},{1,2},{2,3},{3,4},{4,5},{5,6},{6,7},{7,0},{8,9},{9,10},{10,1... | collective-permute-start | bytes 1572872 | tf_op jit(solution)/shard_map/ppermute | solution.py:376
  129.8 14.2 %collective-permute-start.22 = (bf16[128,2048]{1,0:T(8,128)(2,1)S(1)}, bf16[128,2048]{1,0:T(8,128)(2,1)S(1)}, u32[]{:S(2)}, u32[]{:S(2)}) collective-permute-start(bf16[128,2048]{1,0:T(8,128)(2,1)S(1)} %constant_dynamic-slice_fusion.refs_0_), channel_id=1, source_target_pairs={{0,7},{1,0},{2,1},{3,2},{4,3},{5,4},{6,5},{7,6},{8,15},{9,8},{10,9... | collective-permute-start | bytes 1572872 | tf_op jit(solution)/shard_map/ppermute | solution.py:376
  144.0 15.6 %collective-permute-start.23 = (bf16[128,2048]{1,0:T(8,128)(2,1)S(1)}, bf16[128,2048]{1,0:T(8,128)(2,1)}, u32[]{:S(2)}, u32[]{:S(2)}) collective-permute-start(bf16[128,2048]{1,0:T(8,128)(2,1)S(1)} %collective-permute-done.21.refs_1_), channel_id=1, source_target_pairs={{0,1},{1,2},{2,3},{3,4},{4,5},{5,6},{6,7},{7,0},{8,9},{9,10},{10,1... | collective-permute-start | bytes 1572872 | tf_op jit(solution)/shard_map/ppermute | solution.py:376
  144.3 15.3 %collective-permute-start.24 = (bf16[128,2048]{1,0:T(8,128)(2,1)S(1)}, bf16[128,2048]{1,0:T(8,128)(2,1)S(1)}, u32[]{:S(2)}, u32[]{:S(2)}) collective-permute-start(bf16[128,2048]{1,0:T(8,128)(2,1)S(1)} %collective-permute-done.22.refs_2_), channel_id=1, source_target_pairs={{0,7},{1,0},{2,1},{3,2},{4,3},{5,4},{6,5},{7,6},{8,15},{9,8},{10,9... | collective-permute-start | bytes 1572872 | tf_op jit(solution)/shard_map/ppermute | solution.py:376
  160.4 21.4 %collective-permute-start.25 = (bf16[128,2048]{1,0:T(8,128)(2,1)}, bf16[128,2048]{1,0:T(8,128)(2,1)S(1)}, u32[]{:S(2)}, u32[]{:S(2)}) collective-permute-start(bf16[128,2048]{1,0:T(8,128)(2,1)} %collective-permute-done.23.refs_3_), channel_id=1, source_target_pairs={{0,1},{1,2},{2,3},{3,4},{4,5},{5,6},{6,7},{7,0},{8,9},{9,10},{10,1... | collective-permute-start | bytes 1572872 | tf_op jit(solution)/shard_map/ppermute | solution.py:376
  161.7 20.9 %collective-permute-start.26 = (bf16[128,2048]{1,0:T(8,128)(2,1)}, bf16[128,2048]{1,0:T(8,128)(2,1)S(1)}, u32[]{:S(2)}, u32[]{:S(2)}) collective-permute-start(bf16[128,2048]{1,0:T(8,128)(2,1)} %copy-done.10), channel_id=1, source_target_pairs={{0,7},{1,0},{2,1},{3,2},{4,3},{5,4},{6,5},{7,6},{8,15},{9,8},{10,9... | collective-permute-start | bytes 1572872 | tf_op jit(solution)/shard_map/ppermute | solution.py:376
  174.6 17.0 %all-to-all-start.2 = ((bf16[16,2,32,256]{3,2,1,0:T(8,128)(2,1)}), bf16[16,2,32,256]{3,2,1,0:T(8,128)(2,1)S(1)}, u32[]{:S(2)}, u32[]{:S(2)}) async-start(bf16[16,2,32,256]{3,2,1,0:T(8,128)(2,1)} %copy-done.12), calls=%async_computation.2 | async-start | bytes 1048576 | tf_op jit(solution)/shard_map/all_to_all | solution.py:442
  182.6 9.3 %collective-permute-start.27 = (bf16[64,2048]{1,0:T(8,128)(2,1)}, bf16[64,2048]{1,0:T(8,128)(2,1)S(1)}, u32[]{:S(2)}, u32[]{:S(2)}) collective-permute-start(bf16[64,2048]{1,0:T(8,128)(2,1)} %slice.8), channel_id=1, source_target_pairs={{0,1},{1,2},{2,3},{3,4},{4,5},{5,6},{6,7},{7,0},{8,9},{9,10},{10,1... | collective-permute-start | bytes 786440 | tf_op jit(solution)/shard_map/ppermute | solution.py:376
  183.3 8.6 %collective-permute-start.28 = (bf16[64,2048]{1,0:T(8,128)(2,1)}, bf16[64,2048]{1,0:T(8,128)(2,1)}, u32[]{:S(2)}, u32[]{:S(2)}) collective-permute-start(bf16[64,2048]{1,0:T(8,128)(2,1)} %slice.9), channel_id=1, source_target_pairs={{0,7},{1,0},{2,1},{3,2},{4,3},{5,4},{6,5},{7,6},{8,15},{9,8},{10,9... | collective-permute-start | bytes 786440 | tf_op jit(solution)/shard_map/ppermute | solution.py:376
  (22 other events, 275.8 us)
Sparse Core Ops, SparseCore 0:
  26.5 59.9 all-gather.4
  95.2 44.2 all-gather.6

commit v13 on v12

--- a/solution.py
+++ b/solution.py
@@ -251,14 +251,29 @@
     )(mix, weight, rows, gain)
 
 
-def temporal_kernel(start_ref, rows_ref, weight_ref, out_ref, qkv, bias):
-    count = rows_ref.shape[0]
+def mask_kernel(start_ref, bias):
+    count = bias.shape[0]
     start = start_ref[0]
     late = lax.broadcasted_iota(jnp.int32, (count, count), 0)
     early = lax.broadcasted_iota(jnp.int32, (count, count), 1)
     same = (late & 7) == (early & 7)
     allowed = same & (early <= late) & ((early >= 8 * start) == (late >= 8 * start))
     bias[...] = jnp.where(allowed, 0.0, -1e30)
+
+
+def frame_mask(start, count):
+    return pl.pallas_call(
+        mask_kernel,
+        out_shape=jax.ShapeDtypeStruct((count, count), F32),
+        in_specs=[smem()],
+        out_specs=vmem(),
+        compiler_params=params(),
+        cost_estimate=pl.CostEstimate(flops=16 << 20, bytes_accessed=16 << 20, transcendentals=0),
+    )(start)
+
+
+def temporal_kernel(rows_ref, weight_ref, bias, out_ref, qkv):
+    count = rows_ref.shape[0]
     for block in range(6):
         qkv[block] = dot(rows_ref[...], weight_ref[:, block].reshape(2048, 256)).astype(BF)
     size = 256
@@ -283,22 +298,21 @@
                     out_ref[at] = rows
 
 
-def temporal_attend(start, rows, weight):
+def temporal_attend(rows, weight, bias):
     count, width = rows.shape
     return pl.pallas_call(
         temporal_kernel,
         out_shape=jax.ShapeDtypeStruct((16, 2, 32, 256), BF),
-        in_specs=[smem(), vmem(), vmem()],
+        in_specs=[vmem()] * 3,
         out_specs=vmem(),
         scratch_shapes=[
             pltpu.VMEM((6, count, 256), BF),
-            pltpu.VMEM((count, count), F32),
         ],
         compiler_params=params(),
         cost_estimate=pl.CostEstimate(
             flops=2 * 512 * 2048 * 1536, bytes_accessed=9 << 20, transcendentals=131072
         ),
-    )(start, rows, weight)
+    )(rows, weight, bias)
 
 
 def last_kernel(place_ref, mix_ref, *refs):
@@ -424,6 +438,7 @@
 
     middle, send = middle_rows(mix, whole_out, rows, temporal_gain.reshape(1, width))
 
+    start = lax.dynamic_slice(starts, (w,), (1,))
     half = lax.dynamic_slice(temporal_out, (c * E, 0), (E, width))
     send, half = lax.optimization_barrier((send, half))
     up, down = half, half
@@ -431,14 +446,15 @@
     for step in (1, 2, 3):
         up, down = shifted(up, "z", 1), shifted(down, "z", -1)
         if step == 1:
-            up, down, quarter = lax.optimization_barrier((up, down, quarter))
+            up, down, quarter, start = lax.optimization_barrier((up, down, quarter, start))
+            bias = frame_mask(start, 512)
+            up, down, bias = lax.optimization_barrier((up, down, bias))
         halves += [up, down]
     halves += [shifted(up[:64], "z", 1), shifted(down[64:], "z", -1)]
 
     window = lax.all_to_all(send, ("xl", "y", "c"), 0, 0, tiled=True)
-    window, *halves[1:5] = lax.optimization_barrier((window, *halves[1:5]))
-    start = lax.dynamic_slice(starts, (w,), (1,))
-    mix = temporal_attend(start, window.reshape(512, width), quarter)
+    window, bias, *halves[1:5] = lax.optimization_barrier((window, bias, *halves[1:5]))
+    mix = temporal_attend(window.reshape(512, width), quarter, bias)
     mix = lax.all_to_all(mix, ("xl", "y", "c"), 0, 0, tiled=True)
     keep, give = last_sums(jnp.stack([z, c]).astype(jnp.int32), mix, halves)
     return end_rows(keep, shifted(give, "c", 1), middle)

time: 210 us -> 211 us (level)
    unnamed x38 -> x42, local copies, waits for them, and re-layouts: 17.7 us -> 19.1 us
  transfers between devices with their start and end apart: 35 -> 35, of which waited for: 16 -> 18; matrix products, arithmetic and copies ran while one was open for 1% -> 1% of each run, Pallas kernels for 8% -> 8%
where the time goes in v13:
time: 211 us; the launch traced here: 210 us
  waiting for transfers between devices  83.7 us (40%)
  starting transfers between devices  69 us (33%)
  local copies, waits for them, and re-layouts  22.1 us (10%)
  Pallas kernels  21.5 us (10%)
  between operations  13.6 us (6%)
    ppermute x26, waiting for transfers between devices, shifted(): lax.ppermute(value, axis, [(i, (i + step) % count) for i in range(count)])  52 us
    ppermute x26, starting transfers between devices, shifted(): lax.ppermute(value, axis, [(i, (i + step) % count) for i in range(count)])  37.2 us
    unnamed x42, local copies, waits for them, and re-layouts  19.1 us
    all_to_all x1, waiting for transfers between devices, local(): mix = lax.all_to_all(mix, 'z', 0, 0, tiled=True)  15.7 us
    ppermute x4, starting transfers between devices, local(): parts.append(lax.ppermute(block, ('c', 'z'), pairs))  13.8 us
    all_to_all x1, waiting for transfers between devices, local(): window = lax.all_to_all(send, ('xl', 'y', 'c'), 0, 0, tiled=True)  10.4 us
    all_to_all x1, starting transfers between devices, local(): window = lax.all_to_all(send, ('xl', 'y', 'c'), 0, 0, tiled=True)  7.07 us
    pallas_call x1, Pallas kernels, temporal_attend(): pl.pallas_call(temporal_kernel, out_shape=jax.ShapeDtypeStruct((16, 2, 32...  6.97 us
  transfers between devices with their start and end apart: 35, of which 18 were waited for; matrix products, arithmetic and copies ran while one was open for 1% of the time, Pallas kernels for 8%

profile of v13, /device:TPU:1, one launch (start us, length us, event | category | flops | bytes accessed | tf_op | source)
XLA Modules:
  0.0 210.0 jit_solution(349706846979024630)
XLA Ops:
  7.5 10.2 %collective-permute-start = (bf16[128,256]{1,0:T(8,128)(2,1)S(1)}, bf16[128,256]{1,0:T(8,128)(2,1)S(1)}, u32[]{:S(2)}, u32[]{:S(2)}) collective-permute-start(bf16[128,256]{1,0:T(8,128)(2,1)S(1)} %dynamic_slice.9), channel_id=1, source_target_pairs={{0,0},{1,1},{2,2},{3,3},{4,12},{5,13},{6,14},{7,15},{8,4},{9,5},{1... | collective-permute-start | bytes 196616 | tf_op jit(solution)/shard_map/ppermute | solution.py:420
  18.5 2.8 %collective-permute-start.3 = (bf16[128,256]{1,0:T(8,128)(2,1)S(1)}, bf16[128,256]{1,0:T(8,128)(2,1)S(1)}, u32[]{:S(2)}, u32[]{:S(2)}) collective-permute-start(bf16[128,256]{1,0:T(8,128)(2,1)S(1)} %dynamic_slice.9), channel_id=1, source_target_pairs={{0,3},{1,4},{2,5},{3,6},{4,15},{5,8},{6,9},{7,10},{8,7},{9,0},{10,... | collective-permute-start | bytes 196616 | tf_op jit(solution)/shard_map/ppermute | solution.py:420
  21.3 1.9 copy-done.2
  26.4 3.6 %collective-permute-start.4 = (bf16[80,2048]{1,0:T(8,128)(2,1)S(1)}, bf16[80,2048]{1,0:T(8,128)(2,1)S(1)}, u32[]{:S(2)}, u32[]{:S(2)}) collective-permute-start(bf16[80,2048]{1,0:T(8,128)(2,1)S(1)} %get-tuple-element.47.refs_0_), channel_id=1, source_target_pairs={{0,1},{1,2},{2,3},{3,4},{4,5},{5,6},{6,7},{7,0},{8,9},{9,10},{10,1... | collective-permute-start | bytes 983048 | tf_op jit(solution)/shard_map/ppermute | solution.py:390
  32.7 5.1 %collective-permute-done.4.refs_2_ = bf16[80,2048]{1,0:T(8,128)(2,1)S(1)} collective-permute-done((bf16[80,2048]{1,0:T(8,128)(2,1)S(1)}, bf16[80,2048]{1,0:T(8,128)(2,1)S(1)}, u32[]{:S(2)}, u32[]{:S(2)}) %collective-permute-start.4) | collective-permute-done | bytes 327712 | tf_op jit(solution)/shard_map/ppermute | solution.py:390
  37.8 1.5 collective-permute-start.8
  40.5 4.3 %collective-permute-done.5.refs_3_ = bf16[80,2048]{1,0:T(8,128)(2,1)S(1)} collective-permute-done((bf16[80,2048]{1,0:T(8,128)(2,1)S(1)}, bf16[80,2048]{1,0:T(8,128)(2,1)S(1)}, u32[]{:S(2)}, u32[]{:S(2)}) %collective-permute-start.5) | collective-permute-done | bytes 327712 | tf_op jit(solution)/shard_map/ppermute | solution.py:390
  44.8 1.6 collective-permute-start.9
  47.5 4.3 %collective-permute-done.8.refs_6_ = bf16[80,2048]{1,0:T(8,128)(2,1)S(1)} collective-permute-done((bf16[80,2048]{1,0:T(8,128)(2,1)S(1)}, bf16[80,2048]{1,0:T(8,128)(2,1)S(1)}, u32[]{:S(2)}, u32[]{:S(2)}) %collective-permute-start.8) | collective-permute-done | bytes 327712 | tf_op jit(solution)/shard_map/ppermute | solution.py:390
  54.5 4.3 %collective-permute-done.9.refs_7_ = bf16[80,2048]{1,0:T(8,128)(2,1)S(1)} collective-permute-done((bf16[80,2048]{1,0:T(8,128)(2,1)S(1)}, bf16[80,2048]{1,0:T(8,128)(2,1)S(1)}, u32[]{:S(2)}, u32[]{:S(2)}) %collective-permute-start.9) | collective-permute-done | bytes 327712 | tf_op jit(solution)/shard_map/ppermute | solution.py:390
  61.5 4.3 %collective-permute-done.12.refs_10_ = bf16[80,2048]{1,0:T(8,128)(2,1)S(1)} collective-permute-done((bf16[80,2048]{1,0:T(8,128)(2,1)S(1)}, bf16[80,2048]{1,0:T(8,128)(2,1)S(1)}, u32[]{:S(2)}, u32[]{:S(2)}) %collective-permute-start.12) | collective-permute-done | bytes 327712 | tf_op jit(solution)/shard_map/ppermute | solution.py:390
  68.6 4.3 %collective-permute-done.13.refs_11_ = bf16[80,2048]{1,0:T(8,128)(2,1)S(1)} collective-permute-done((bf16[80,2048]{1,0:T(8,128)(2,1)S(1)}, bf16[80,2048]{1,0:T(8,128)(2,1)S(1)}, u32[]{:S(2)}, u32[]{:S(2)}) %collective-permute-start.13) | collective-permute-done | bytes 327712 | tf_op jit(solution)/shard_map/ppermute | solution.py:390
  74.2 5.8 %collective-permute-done.16.refs_14_ = bf16[80,2048]{1,0:T(8,128)(2,1)S(1)} collective-permute-done((bf16[80,2048]{1,0:T(8,128)(2,1)S(1)}, bf16[80,2048]{1,0:T(8,128)(2,1)S(1)}, u32[]{:S(2)}, u32[]{:S(2)}) %collective-permute-start.16) | collective-permute-done | bytes 327712 | tf_op jit(solution)/shard_map/ppermute | solution.py:390
  83.4 2.6 %collective-permute-start.19 = (bf16[2,3,64,256]{3,2,1,0:T(8,128)(2,1)S(1)}, bf16[2,3,64,256]{3,2,1,0:T(8,128)(2,1)S(1)}, u32[]{:S(2)}, u32[]{:S(2)}) collective-permute-start(bf16[2,3,64,256]{3,2,1,0:T(8,128)(2,1)S(1)} %get-tuple-element.51), channel_id=1, source_target_pairs={{0,32},{16,48},{32,0},{48,16},{1,33},{17,49},{33,1},{49,17},{2,34}... | collective-permute-start | bytes 589832 | tf_op jit(solution)/shard_map/ppermute | solution.py:390
  87.1 5.3 %shard_map.83 = bf16[8,128,256]{2,1,0:T(8,128)(2,1)} custom-call(s32[1]{0:T(128)} %bitcast.place_ref.z_ref, bf16[3,2048,256]{2,1,0:T(8,128)(2,1)S(1)} %bitcast.16, bf16[80,2048]{1,0:T(8,128)(2,1)S(1)} %get-tuple-element.47.refs_0_, bf16[80,2048]{1,0:T(8,128)(2,1)S(1)} %get-tuple-element.48.refs_1_, bf16[80,2048]{1,0:T(8,128)(2,1)S(1)} %collective-permute-done.4.refs_2_, ...), custom_call_target="tpu_custom_call" | custom-call | flops 6442450944 | bytes 8388608 | tf_op jit(solution)/shard_map/pallas_call | solution.py:184
  92.4 1.7 collective-permute-done.19.refs_2_
  95.1 4.4 %all-to-all-start = ((bf16[8,128,256]{2,1,0:T(8,128)(2,1)}), bf16[8,128,256]{2,1,0:T(8,128)(2,1)S(1)}, u32[]{:S(2)}, u32[]{:S(2)}) async-start(bf16[8,128,256]{2,1,0:T(8,128)(2,1)} %shard_map.83), calls=%async_computation | async-start | bytes 1048576 | tf_op jit(solution)/shard_map/all_to_all | solution.py:437
  99.5 15.7 %all-to-all-done.mix_ref = bf16[8,128,256]{2,1,0:T(8,128)(2,1)S(1)} async-done(((bf16[8,128,256]{2,1,0:T(8,128)(2,1)}), bf16[8,128,256]{2,1,0:T(8,128)(2,1)S(1)}, u32[]{:S(2)}, u32[]{:S(2)}) %all-to-all-start) | async-done | bytes 524320 | tf_op jit(solution)/shard_map/all_to_all | solution.py:437
  115.2 3.5 %copy-done.1 = bf16[128,128,256]{2,1,0:T(8,128)(2,1)S(1)} copy-done((bf16[128,128,256]{2,1,0:T(8,128)(2,1)S(1)}, bf16[128,128,256]{2,1,0:T(8,128)(2,1)}, u32[]{:S(2)}) %copy-start.1) | copy-done | bytes 8388632
  122.4 7.1 %all-to-all-start.1 = ((bf16[16,32,2048]{2,1,0:T(8,128)(2,1)}), bf16[16,32,2048]{2,1,0:T(8,128)(2,1)}, u32[]{:S(2)}, u32[]{:S(2)}) async-start(bf16[16,32,2048]{2,1,0:T(8,128)(2,1)} %copy-done.3), calls=%async_computation.1 | async-start | bytes 4194304 | tf_op jit(solution)/shard_map/all_to_all | solution.py:455
  129.8 2.4 %collective-permute-start.22 = (bf16[128,2048]{1,0:T(8,128)(2,1)S(1)}, bf16[128,2048]{1,0:T(8,128)(2,1)S(1)}, u32[]{:S(2)}, u32[]{:S(2)}) collective-permute-start(bf16[128,2048]{1,0:T(8,128)(2,1)S(1)} %constant_dynamic-slice_fusion.refs_0_), channel_id=1, source_target_pairs={{0,7},{1,0},{2,1},{3,2},{4,3},{5,4},{6,5},{7,6},{8,15},{9,8},{10,9... | collective-permute-start | bytes 1572872 | tf_op jit(solution)/shard_map/ppermute | solution.py:390
  132.7 11.2 %collective-permute-done.21.refs_1_ = bf16[128,2048]{1,0:T(8,128)(2,1)S(1)} collective-permute-done((bf16[128,2048]{1,0:T(8,128)(2,1)S(1)}, bf16[128,2048]{1,0:T(8,128)(2,1)S(1)}, u32[]{:S(2)}, u32[]{:S(2)}) %collective-permute-start.21) | collective-permute-done | bytes 524320 | tf_op jit(solution)/shard_map/ppermute | solution.py:390
  145.9 3.3 %collective-permute-start.24 = (bf16[128,2048]{1,0:T(8,128)(2,1)S(1)}, bf16[128,2048]{1,0:T(8,128)(2,1)S(1)}, u32[]{:S(2)}, u32[]{:S(2)}) collective-permute-start(bf16[128,2048]{1,0:T(8,128)(2,1)S(1)} %collective-permute-done.22.refs_2_), channel_id=1, source_target_pairs={{0,7},{1,0},{2,1},{3,2},{4,3},{5,4},{6,5},{7,6},{8,15},{9,8},{10,9... | collective-permute-start | bytes 1572872 | tf_op jit(solution)/shard_map/ppermute | solution.py:390
  149.2 10.4 %all-to-all-done.1 = bf16[16,32,2048]{2,1,0:T(8,128)(2,1)} async-done(((bf16[16,32,2048]{2,1,0:T(8,128)(2,1)}), bf16[16,32,2048]{2,1,0:T(8,128)(2,1)}, u32[]{:S(2)}, u32[]{:S(2)}) %all-to-all-start.1) | async-done | bytes 2097184 | tf_op jit(solution)/shard_map/all_to_all | solution.py:455
  161.8 2.7 %collective-permute-start.26 = (bf16[128,2048]{1,0:T(8,128)(2,1)}, bf16[128,2048]{1,0:T(8,128)(2,1)S(1)}, u32[]{:S(2)}, u32[]{:S(2)}) collective-permute-start(bf16[128,2048]{1,0:T(8,128)(2,1)} %copy-done.12), channel_id=1, source_target_pairs={{0,7},{1,0},{2,1},{3,2},{4,3},{5,4},{6,5},{7,6},{8,15},{9,8},{10,9... | collective-permute-start | bytes 1572872 | tf_op jit(solution)/shard_map/ppermute | solution.py:390
  165.7 2.8 %copy-done.18 = bf16[48,256,256]{2,1,0:T(8,128)(2,1)S(1)} copy-done((bf16[48,256,256]{2,1,0:T(8,128)(2,1)S(1)}, bf16[48,256,256]{2,1,0:T(8,128)(2,1)}, u32[]{:S(2)}) %copy-start.18) | copy-done | bytes 6291480
  168.5 7.0 %shard_map.89 = bf16[16,2,32,256]{3,2,1,0:T(8,128)(2,1)S(1)} custom-call(bf16[512,2048]{1,0:T(8,128)(2,1)} %bitcast.10.rows_ref, bf16[8,6,256,256]{3,2,1,0:T(8,128)(2,1)S(1)} %bitcast.15, f32[512,512]{1,0:T(8,128)S(1)} %copy-done.5), custom_call_target="tpu_custom_call" | custom-call | flops 3221225472 | bytes 9437184 | tf_op jit(solution)/shard_map/pallas_call | solution.py:303
  176.2 6.5 %all-to-all-start.2 = ((bf16[16,2,32,256]{3,2,1,0:T(8,128)(2,1)}), bf16[16,2,32,256]{3,2,1,0:T(8,128)(2,1)S(1)}, u32[]{:S(2)}, u32[]{:S(2)}) async-start(bf16[16,2,32,256]{3,2,1,0:T(8,128)(2,1)} %copy-done.14), calls=%async_computation.2 | async-start | bytes 1048576 | tf_op jit(solution)/shard_map/all_to_all | solution.py:458
  184.4 2.5 %collective-permute-start.28 = (bf16[64,2048]{1,0:T(8,128)(2,1)}, bf16[64,2048]{1,0:T(8,128)(2,1)}, u32[]{:S(2)}, u32[]{:S(2)}) collective-permute-start(bf16[64,2048]{1,0:T(8,128)(2,1)} %slice.9), channel_id=1, source_target_pairs={{0,7},{1,0},{2,1},{3,2},{4,3},{5,4},{6,5},{7,6},{8,15},{9,8},{10,9... | collective-permute-start | bytes 786440 | tf_op jit(solution)/shard_map/ppermute | solution.py:390
  187.0 5.6 %all-to-all-done.2.mix_ref = bf16[16,2,32,256]{3,2,1,0:T(8,128)(2,1)S(1)} async-done(((bf16[16,2,32,256]{3,2,1,0:T(8,128)(2,1)}), bf16[16,2,32,256]{3,2,1,0:T(8,128)(2,1)S(1)}, u32[]{:S(2)}, u32[]{:S(2)}) %all-to-all-start.2) | async-done | bytes 524320 | tf_op jit(solution)/shard_map/all_to_all | solution.py:458
  196.9 2.5 %shard_map.90 = (f32[128,2048]{1,0:T(8,128)S(1)}, bf16[128,2048]{1,0:T(8,128)(2,1)S(1)}) custom-call(s32[2]{0:T(128)S(1)} %pad_add_fusion.place_ref, bf16[16,2,32,256]{3,2,1,0:T(8,128)(2,1)S(1)} %all-to-all-done.2.mix_ref, bf16[128,2048]{1,0:T(8,128)(2,1)S(1)} %constant_dynamic-slice_fusion.refs_0_, bf16[128,2048]{1,0:T(8,128)(2,1)S(1)} %copy-done.9, ...), custom_call_target="tpu_custom_call" | custom-call | flops 1073741824 | bytes 8388608 | tf_op jit(solution)/shard_map/pallas_call | solution.py:346
  200.4 1.5 collective-permute-done.29.got_ref
  (99 shorter events, 43.7 us)
Async XLA Ops:
  6.5 88.5 %all-gather.5.cloned.1.call-start = ((), (), s32[]{:S(2)}) async-start(), calls=%async_computation.3 | async-start | bytes 8650752 | tf_op jit(solution)/shard_map/all_gather | solution.py:423
  7.5 18.1 %collective-permute-start = (bf16[128,256]{1,0:T(8,128)(2,1)S(1)}, bf16[128,256]{1,0:T(8,128)(2,1)S(1)}, u32[]{:S(2)}, u32[]{:S(2)}) collective-permute-start(bf16[128,256]{1,0:T(8,128)(2,1)S(1)} %dynamic_slice.9), channel_id=1, source_target_pairs={{0,0},{1,1},{2,2},{3,3},{4,12},{5,13},{6,14},{7,15},{8,4},{9,5},{1... | collective-permute-start | bytes 196616 | tf_op jit(solution)/shard_map/ppermute | solution.py:420
  17.7 7.9 %collective-permute-start.1 = (bf16[128,256]{1,0:T(8,128)(2,1)S(1)}, bf16[128,256]{1,0:T(8,128)(2,1)S(1)}, u32[]{:S(2)}, u32[]{:S(2)}) collective-permute-start(bf16[128,256]{1,0:T(8,128)(2,1)S(1)} %dynamic_slice.9), channel_id=1, source_target_pairs={{0,1},{1,2},{2,3},{3,4},{4,13},{5,14},{6,15},{7,8},{8,5},{9,6},{10... | collective-permute-start | bytes 196616 | tf_op jit(solution)/shard_map/ppermute | solution.py:420
  26.3 117.7 %all-gather.7.cloned.1.call-start = ((), (), s32[]{:S(2)}) async-start(), calls=%async_computation.4 | async-start | bytes 7077888 | tf_op jit(solution)/shard_map/all_gather | solution.py:436
  26.4 11.4 %collective-permute-start.4 = (bf16[80,2048]{1,0:T(8,128)(2,1)S(1)}, bf16[80,2048]{1,0:T(8,128)(2,1)S(1)}, u32[]{:S(2)}, u32[]{:S(2)}) collective-permute-start(bf16[80,2048]{1,0:T(8,128)(2,1)S(1)} %get-tuple-element.47.refs_0_), channel_id=1, source_target_pairs={{0,1},{1,2},{2,3},{3,4},{4,5},{5,6},{6,7},{7,0},{8,9},{9,10},{10,1... | collective-permute-start | bytes 983048 | tf_op jit(solution)/shard_map/ppermute | solution.py:390
  30.0 9.3 %collective-permute-start.7 = (bf16[80,2048]{1,0:T(8,128)(2,1)S(1)}, bf16[80,2048]{1,0:T(8,128)(2,1)S(1)}, u32[]{:S(2)}, u32[]{:S(2)}) collective-permute-start(bf16[80,2048]{1,0:T(8,128)(2,1)S(1)} %get-tuple-element.48.refs_1_), channel_id=1, source_target_pairs={{0,7},{1,0},{2,1},{3,2},{4,3},{5,4},{6,5},{7,6},{8,15},{9,8},{10,9... | collective-permute-start | bytes 983048 | tf_op jit(solution)/shard_map/ppermute | solution.py:390
  30.0 14.8 %collective-permute-start.5 = (bf16[80,2048]{1,0:T(8,128)(2,1)S(1)}, bf16[80,2048]{1,0:T(8,128)(2,1)S(1)}, u32[]{:S(2)}, u32[]{:S(2)}) collective-permute-start(bf16[80,2048]{1,0:T(8,128)(2,1)S(1)} %get-tuple-element.48.refs_1_), channel_id=1, source_target_pairs={{0,1},{1,2},{2,3},{3,4},{4,5},{5,6},{6,7},{7,0},{8,9},{9,10},{10,1... | collective-permute-start | bytes 983048 | tf_op jit(solution)/shard_map/ppermute | solution.py:390
  31.5 14.9 %collective-permute-start.6 = (bf16[80,2048]{1,0:T(8,128)(2,1)S(1)}, bf16[80,2048]{1,0:T(8,128)(2,1)S(1)}, u32[]{:S(2)}, u32[]{:S(2)}) collective-permute-start(bf16[80,2048]{1,0:T(8,128)(2,1)S(1)} %get-tuple-element.47.refs_0_), channel_id=1, source_target_pairs={{0,7},{1,0},{2,1},{3,2},{4,3},{5,4},{6,5},{7,6},{8,15},{9,8},{10,9... | collective-permute-start | bytes 983048 | tf_op jit(solution)/shard_map/ppermute | solution.py:390
  37.8 14.0 %collective-permute-start.8 = (bf16[80,2048]{1,0:T(8,128)(2,1)S(1)}, bf16[80,2048]{1,0:T(8,128)(2,1)S(1)}, u32[]{:S(2)}, u32[]{:S(2)}) collective-permute-start(bf16[80,2048]{1,0:T(8,128)(2,1)S(1)} %collective-permute-done.4.refs_2_), channel_id=1, source_target_pairs={{0,1},{1,2},{2,3},{3,4},{4,5},{5,6},{6,7},{7,0},{8,9},{9,10},{10,1... | collective-permute-start | bytes 983048 | tf_op jit(solution)/shard_map/ppermute | solution.py:390
  39.3 14.0 %collective-permute-start.11 = (bf16[80,2048]{1,0:T(8,128)(2,1)S(1)}, bf16[80,2048]{1,0:T(8,128)(2,1)S(1)}, u32[]{:S(2)}, u32[]{:S(2)}) collective-permute-start(bf16[80,2048]{1,0:T(8,128)(2,1)S(1)} %collective-permute-done.7.refs_5_), channel_id=1, source_target_pairs={{0,7},{1,0},{2,1},{3,2},{4,3},{5,4},{6,5},{7,6},{8,15},{9,8},{10,9... | collective-permute-start | bytes 983048 | tf_op jit(solution)/shard_map/ppermute | solution.py:390
  44.8 14.0 %collective-permute-start.9 = (bf16[80,2048]{1,0:T(8,128)(2,1)S(1)}, bf16[80,2048]{1,0:T(8,128)(2,1)S(1)}, u32[]{:S(2)}, u32[]{:S(2)}) collective-permute-start(bf16[80,2048]{1,0:T(8,128)(2,1)S(1)} %collective-permute-done.5.refs_3_), channel_id=1, source_target_pairs={{0,1},{1,2},{2,3},{3,4},{4,5},{5,6},{6,7},{7,0},{8,9},{9,10},{10,1... | collective-permute-start | bytes 983048 | tf_op jit(solution)/shard_map/ppermute | solution.py:390
  46.4 13.9 %collective-permute-start.10 = (bf16[80,2048]{1,0:T(8,128)(2,1)S(1)}, bf16[80,2048]{1,0:T(8,128)(2,1)S(1)}, u32[]{:S(2)}, u32[]{:S(2)}) collective-permute-start(bf16[80,2048]{1,0:T(8,128)(2,1)S(1)} %collective-permute-done.6.refs_4_), channel_id=1, source_target_pairs={{0,7},{1,0},{2,1},{3,2},{4,3},{5,4},{6,5},{7,6},{8,15},{9,8},{10,9... | collective-permute-start | bytes 983048 | tf_op jit(solution)/shard_map/ppermute | solution.py:390
  51.8 14.0 %collective-permute-start.12 = (bf16[80,2048]{1,0:T(8,128)(2,1)S(1)}, bf16[80,2048]{1,0:T(8,128)(2,1)S(1)}, u32[]{:S(2)}, u32[]{:S(2)}) collective-permute-start(bf16[80,2048]{1,0:T(8,128)(2,1)S(1)} %collective-permute-done.8.refs_6_), channel_id=1, source_target_pairs={{0,1},{1,2},{2,3},{3,4},{4,5},{5,6},{6,7},{7,0},{8,9},{9,10},{10,1... | collective-permute-start | bytes 983048 | tf_op jit(solution)/shard_map/ppermute | solution.py:390
  53.3 14.0 %collective-permute-start.15 = (bf16[80,2048]{1,0:T(8,128)(2,1)S(1)}, bf16[80,2048]{1,0:T(8,128)(2,1)S(1)}, u32[]{:S(2)}, u32[]{:S(2)}) collective-permute-start(bf16[80,2048]{1,0:T(8,128)(2,1)S(1)} %collective-permute-done.11.refs_9_), channel_id=1, source_target_pairs={{0,7},{1,0},{2,1},{3,2},{4,3},{5,4},{6,5},{7,6},{8,15},{9,8},{10,9... | collective-permute-start | bytes 983048 | tf_op jit(solution)/shard_map/ppermute | solution.py:390
  58.8 14.1 %collective-permute-start.13 = (bf16[80,2048]{1,0:T(8,128)(2,1)S(1)}, bf16[80,2048]{1,0:T(8,128)(2,1)S(1)}, u32[]{:S(2)}, u32[]{:S(2)}) collective-permute-start(bf16[80,2048]{1,0:T(8,128)(2,1)S(1)} %collective-permute-done.9.refs_7_), channel_id=1, source_target_pairs={{0,1},{1,2},{2,3},{3,4},{4,5},{5,6},{6,7},{7,0},{8,9},{9,10},{10,1... | collective-permute-start | bytes 983048 | tf_op jit(solution)/shard_map/ppermute | solution.py:390
  60.3 13.8 %collective-permute-start.14 = (bf16[80,2048]{1,0:T(8,128)(2,1)S(1)}, bf16[80,2048]{1,0:T(8,128)(2,1)S(1)}, u32[]{:S(2)}, u32[]{:S(2)}) collective-permute-start(bf16[80,2048]{1,0:T(8,128)(2,1)S(1)} %collective-permute-done.10.refs_8_), channel_id=1, source_target_pairs={{0,7},{1,0},{2,1},{3,2},{4,3},{5,4},{6,5},{7,6},{8,15},{9,8},{10,9... | collective-permute-start | bytes 983048 | tf_op jit(solution)/shard_map/ppermute | solution.py:390
  65.9 14.1 %collective-permute-start.16 = (bf16[80,2048]{1,0:T(8,128)(2,1)S(1)}, bf16[80,2048]{1,0:T(8,128)(2,1)S(1)}, u32[]{:S(2)}, u32[]{:S(2)}) collective-permute-start(bf16[80,2048]{1,0:T(8,128)(2,1)S(1)} %collective-permute-done.12.refs_10_), channel_id=1, source_target_pairs={{0,1},{1,2},{2,3},{3,4},{4,5},{5,6},{6,7},{7,0},{8,9},{9,10},{10,1... | collective-permute-start | bytes 983048 | tf_op jit(solution)/shard_map/ppermute | solution.py:390
  67.4 13.8 %collective-permute-start.17 = (bf16[80,2048]{1,0:T(8,128)(2,1)S(1)}, bf16[80,2048]{1,0:T(8,128)(2,1)S(1)}, u32[]{:S(2)}, u32[]{:S(2)}) collective-permute-start(bf16[80,2048]{1,0:T(8,128)(2,1)S(1)} %collective-permute-done.15.refs_13_), channel_id=1, source_target_pairs={{0,7},{1,0},{2,1},{3,2},{4,3},{5,4},{6,5},{7,6},{8,15},{9,8},{10,9... | collective-permute-start | bytes 983048 | tf_op jit(solution)/shard_map/ppermute | solution.py:390
  82.0 10.3 %collective-permute-start.18 = (bf16[2,3,64,256]{3,2,1,0:T(8,128)(2,1)S(1)}, bf16[2,3,64,256]{3,2,1,0:T(8,128)(2,1)S(1)}, u32[]{:S(2)}, u32[]{:S(2)}) collective-permute-start(bf16[2,3,64,256]{3,2,1,0:T(8,128)(2,1)S(1)} %get-tuple-element.50), channel_id=1, source_target_pairs={{0,16},{16,32},{32,48},{48,0},{1,17},{17,33},{33,49},{49,1},{2,18}... | collective-permute-start | bytes 589832 | tf_op jit(solution)/shard_map/ppermute | solution.py:390
  83.4 10.7 %collective-permute-start.19 = (bf16[2,3,64,256]{3,2,1,0:T(8,128)(2,1)S(1)}, bf16[2,3,64,256]{3,2,1,0:T(8,128)(2,1)S(1)}, u32[]{:S(2)}, u32[]{:S(2)}) collective-permute-start(bf16[2,3,64,256]{3,2,1,0:T(8,128)(2,1)S(1)} %get-tuple-element.51), channel_id=1, source_target_pairs={{0,32},{16,48},{32,0},{48,16},{1,33},{17,49},{33,1},{49,17},{2,34}... | collective-permute-start | bytes 589832 | tf_op jit(solution)/shard_map/ppermute | solution.py:390
  86.0 8.1 %collective-permute-start.20 = (bf16[2,3,64,256]{3,2,1,0:T(8,128)(2,1)S(1)}, bf16[2,3,64,256]{3,2,1,0:T(8,128)(2,1)S(1)}, u32[]{:S(2)}, u32[]{:S(2)}) collective-permute-start(bf16[2,3,64,256]{3,2,1,0:T(8,128)(2,1)S(1)} %get-tuple-element.52), channel_id=1, source_target_pairs={{0,48},{16,0},{32,16},{48,32},{1,49},{17,1},{33,17},{49,33},{2,50}... | collective-permute-start | bytes 589832 | tf_op jit(solution)/shard_map/ppermute | solution.py:390
  95.1 20.1 %all-to-all-start = ((bf16[8,128,256]{2,1,0:T(8,128)(2,1)}), bf16[8,128,256]{2,1,0:T(8,128)(2,1)S(1)}, u32[]{:S(2)}, u32[]{:S(2)}) async-start(bf16[8,128,256]{2,1,0:T(8,128)(2,1)} %shard_map.83), calls=%async_computation | async-start | bytes 1048576 | tf_op jit(solution)/shard_map/all_to_all | solution.py:437
  122.4 37.2 %all-to-all-start.1 = ((bf16[16,32,2048]{2,1,0:T(8,128)(2,1)}), bf16[16,32,2048]{2,1,0:T(8,128)(2,1)}, u32[]{:S(2)}, u32[]{:S(2)}) async-start(bf16[16,32,2048]{2,1,0:T(8,128)(2,1)} %copy-done.3), calls=%async_computation.1 | async-start | bytes 4194304 | tf_op jit(solution)/shard_map/all_to_all | solution.py:455
  129.5 14.5 %collective-permute-start.21 = (bf16[128,2048]{1,0:T(8,128)(2,1)S(1)}, bf16[128,2048]{1,0:T(8,128)(2,1)S(1)}, u32[]{:S(2)}, u32[]{:S(2)}) collective-permute-start(bf16[128,2048]{1,0:T(8,128)(2,1)S(1)} %constant_dynamic-slice_fusion.refs_0_), channel_id=1, source_target_pairs={{0,1},{1,2},{2,3},{3,4},{4,5},{5,6},{6,7},{7,0},{8,9},{9,10},{10,1... | collective-permute-start | bytes 1572872 | tf_op jit(solution)/shard_map/ppermute | solution.py:390
  129.8 14.2 %collective-permute-start.22 = (bf16[128,2048]{1,0:T(8,128)(2,1)S(1)}, bf16[128,2048]{1,0:T(8,128)(2,1)S(1)}, u32[]{:S(2)}, u32[]{:S(2)}) collective-permute-start(bf16[128,2048]{1,0:T(8,128)(2,1)S(1)} %constant_dynamic-slice_fusion.refs_0_), channel_id=1, source_target_pairs={{0,7},{1,0},{2,1},{3,2},{4,3},{5,4},{6,5},{7,6},{8,15},{9,8},{10,9... | collective-permute-start | bytes 1572872 | tf_op jit(solution)/shard_map/ppermute | solution.py:390
  145.9 15.0 %collective-permute-start.23 = (bf16[128,2048]{1,0:T(8,128)(2,1)S(1)}, bf16[128,2048]{1,0:T(8,128)(2,1)}, u32[]{:S(2)}, u32[]{:S(2)}) collective-permute-start(bf16[128,2048]{1,0:T(8,128)(2,1)S(1)} %collective-permute-done.21.refs_1_), channel_id=1, source_target_pairs={{0,1},{1,2},{2,3},{3,4},{4,5},{5,6},{6,7},{7,0},{8,9},{9,10},{10,1... | collective-permute-start | bytes 1572872 | tf_op jit(solution)/shard_map/ppermute | solution.py:390
  145.9 15.0 %collective-permute-start.24 = (bf16[128,2048]{1,0:T(8,128)(2,1)S(1)}, bf16[128,2048]{1,0:T(8,128)(2,1)S(1)}, u32[]{:S(2)}, u32[]{:S(2)}) collective-permute-start(bf16[128,2048]{1,0:T(8,128)(2,1)S(1)} %collective-permute-done.22.refs_2_), channel_id=1, source_target_pairs={{0,7},{1,0},{2,1},{3,2},{4,3},{5,4},{6,5},{7,6},{8,15},{9,8},{10,9... | collective-permute-start | bytes 1572872 | tf_op jit(solution)/shard_map/ppermute | solution.py:390
  161.8 21.0 %collective-permute-start.25 = (bf16[128,2048]{1,0:T(8,128)(2,1)}, bf16[128,2048]{1,0:T(8,128)(2,1)S(1)}, u32[]{:S(2)}, u32[]{:S(2)}) collective-permute-start(bf16[128,2048]{1,0:T(8,128)(2,1)} %collective-permute-done.23.refs_3_), channel_id=1, source_target_pairs={{0,1},{1,2},{2,3},{3,4},{4,5},{5,6},{6,7},{7,0},{8,9},{9,10},{10,1... | collective-permute-start | bytes 1572872 | tf_op jit(solution)/shard_map/ppermute | solution.py:390
  161.8 21.9 %collective-permute-start.26 = (bf16[128,2048]{1,0:T(8,128)(2,1)}, bf16[128,2048]{1,0:T(8,128)(2,1)S(1)}, u32[]{:S(2)}, u32[]{:S(2)}) collective-permute-start(bf16[128,2048]{1,0:T(8,128)(2,1)} %copy-done.12), channel_id=1, source_target_pairs={{0,7},{1,0},{2,1},{3,2},{4,3},{5,4},{6,5},{7,6},{8,15},{9,8},{10,9... | collective-permute-start | bytes 1572872 | tf_op jit(solution)/shard_map/ppermute | solution.py:390
  176.2 16.3 %all-to-all-start.2 = ((bf16[16,2,32,256]{3,2,1,0:T(8,128)(2,1)}), bf16[16,2,32,256]{3,2,1,0:T(8,128)(2,1)S(1)}, u32[]{:S(2)}, u32[]{:S(2)}) async-start(bf16[16,2,32,256]{3,2,1,0:T(8,128)(2,1)} %copy-done.14), calls=%async_computation.2 | async-start | bytes 1048576 | tf_op jit(solution)/shard_map/all_to_all | solution.py:458
  183.5 9.3 %collective-permute-start.27 = (bf16[64,2048]{1,0:T(8,128)(2,1)}, bf16[64,2048]{1,0:T(8,128)(2,1)S(1)}, u32[]{:S(2)}, u32[]{:S(2)}) collective-permute-start(bf16[64,2048]{1,0:T(8,128)(2,1)} %slice.8), channel_id=1, source_target_pairs={{0,1},{1,2},{2,3},{3,4},{4,5},{5,6},{6,7},{7,0},{8,9},{9,10},{10,1... | collective-permute-start | bytes 786440 | tf_op jit(solution)/shard_map/ppermute | solution.py:390
  184.4 9.4 %collective-permute-start.28 = (bf16[64,2048]{1,0:T(8,128)(2,1)}, bf16[64,2048]{1,0:T(8,128)(2,1)}, u32[]{:S(2)}, u32[]{:S(2)}) collective-permute-start(bf16[64,2048]{1,0:T(8,128)(2,1)} %slice.9), channel_id=1, source_target_pairs={{0,7},{1,0},{2,1},{3,2},{4,3},{5,4},{6,5},{7,6},{8,15},{9,8},{10,9... | collective-permute-start | bytes 786440 | tf_op jit(solution)/shard_map/ppermute | solution.py:390
  (24 other events, 280.6 us)
Sparse Core Ops, SparseCore 0:
  26.5 59.9 all-gather.4
  95.2 44.1 all-gather.6

commit v14 on v7

--- a/solution.py
+++ b/solution.py
@@ -15,7 +15,7 @@
 BF = jnp.bfloat16
 F32 = jnp.float32
 NZ = 8
-VMEM_LIMIT = 28 * 1024 * 1024
+VMEM_LIMIT = 18 * 1024 * 1024
 OFFSETS = (0, -1, 1, -2, 2, -3, 3, 4)
 
 

time: 206 us -> 206 us (level)
  no operation moved by 1% of the time
where the time goes in v14:
time: 206 us
  waiting for transfers between devices  81.5 us (40%)
  starting transfers between devices  70 us (34%)
  Pallas kernels  21.4 us (10%)
  local copies, waits for them, and re-layouts  19 us (9%)
  between operations  13.6 us (7%)
    ppermute x26, waiting for transfers between devices, shifted(): lax.ppermute(value, axis, [(i, (i + step) % count) for i in range(count)])  65.8 us
    ppermute x26, starting transfers between devices, shifted(): lax.ppermute(value, axis, [(i, (i + step) % count) for i in range(count)])  36.9 us
    unnamed x38, local copies, waits for them, and re-layouts  17.4 us
    all_to_all x1, waiting for transfers between devices, local(): mix = lax.all_to_all(mix, 'z', 0, 0, tiled=True)  15.6 us
    ppermute x4, starting transfers between devices, local(): parts.append(lax.ppermute(block, ('c', 'z'), pairs))  13.8 us
    all_to_all x1, starting transfers between devices, local(): mix = lax.all_to_all(mix, ('xl', 'y', 'c'), 0, 0, tiled=True)  7.78 us
    pallas_call x1, Pallas kernels, temporal_attend(): pl.pallas_call(temporal_kernel, out_shape=jax.ShapeDtypeStruct((16, 2, 32...  7.6 us
    all_to_all x1, starting transfers between devices, local(): window = lax.all_to_all(send, ('xl', 'y', 'c'), 0, 0, tiled=True)  7.14 us
  transfers between devices with their start and end apart: 35, of which 15 were waited for; matrix products, arithmetic and copies ran while one was open for 0% of the time, Pallas kernels for 8%

profile of v14, /device:TPU:1, one launch (start us, length us, event | category | flops | bytes accessed | tf_op | source)
XLA Modules:
  0.0 205.7 jit_solution(9801811352537905317)
XLA Ops:
  7.5 10.2 %collective-permute-start = (bf16[128,256]{1,0:T(8,128)(2,1)S(1)}, bf16[128,256]{1,0:T(8,128)(2,1)S(1)}, u32[]{:S(2)}, u32[]{:S(2)}) collective-permute-start(bf16[128,256]{1,0:T(8,128)(2,1)S(1)} %dynamic_slice.10), channel_id=1, source_target_pairs={{0,0},{1,1},{2,2},{3,3},{4,12},{5,13},{6,14},{7,15},{8,4},{9,5},{1... | collective-permute-start | bytes 196616 | tf_op jit(solution)/shard_map/ppermute | solution.py:406
  18.5 2.8 %collective-permute-start.3 = (bf16[128,256]{1,0:T(8,128)(2,1)S(1)}, bf16[128,256]{1,0:T(8,128)(2,1)S(1)}, u32[]{:S(2)}, u32[]{:S(2)}) collective-permute-start(bf16[128,256]{1,0:T(8,128)(2,1)S(1)} %dynamic_slice.10), channel_id=1, source_target_pairs={{0,3},{1,4},{2,5},{3,6},{4,15},{5,8},{6,9},{7,10},{8,7},{9,0},{10,... | collective-permute-start | bytes 196616 | tf_op jit(solution)/shard_map/ppermute | solution.py:406
  21.3 1.9 copy-done.2
  26.4 3.6 %collective-permute-start.4 = (bf16[80,2048]{1,0:T(8,128)(2,1)S(1)}, bf16[80,2048]{1,0:T(8,128)(2,1)S(1)}, u32[]{:S(2)}, u32[]{:S(2)}) collective-permute-start(bf16[80,2048]{1,0:T(8,128)(2,1)S(1)} %get-tuple-element.39.refs_0_), channel_id=1, source_target_pairs={{0,1},{1,2},{2,3},{3,4},{4,5},{5,6},{6,7},{7,0},{8,9},{9,10},{10,1... | collective-permute-start | bytes 983048 | tf_op jit(solution)/shard_map/ppermute | solution.py:376
  32.7 5.1 %collective-permute-done.4.refs_2_ = bf16[80,2048]{1,0:T(8,128)(2,1)S(1)} collective-permute-done((bf16[80,2048]{1,0:T(8,128)(2,1)S(1)}, bf16[80,2048]{1,0:T(8,128)(2,1)S(1)}, u32[]{:S(2)}, u32[]{:S(2)}) %collective-permute-start.4) | collective-permute-done | bytes 327712 | tf_op jit(solution)/shard_map/ppermute | solution.py:376
  37.8 1.5 collective-permute-start.8
  40.5 4.3 %collective-permute-done.5.refs_3_ = bf16[80,2048]{1,0:T(8,128)(2,1)S(1)} collective-permute-done((bf16[80,2048]{1,0:T(8,128)(2,1)S(1)}, bf16[80,2048]{1,0:T(8,128)(2,1)S(1)}, u32[]{:S(2)}, u32[]{:S(2)}) %collective-permute-start.5) | collective-permute-done | bytes 327712 | tf_op jit(solution)/shard_map/ppermute | solution.py:376
  44.8 1.6 collective-permute-start.9
  47.5 4.3 %collective-permute-done.8.refs_6_ = bf16[80,2048]{1,0:T(8,128)(2,1)S(1)} collective-permute-done((bf16[80,2048]{1,0:T(8,128)(2,1)S(1)}, bf16[80,2048]{1,0:T(8,128)(2,1)S(1)}, u32[]{:S(2)}, u32[]{:S(2)}) %collective-permute-start.8) | collective-permute-done | bytes 327712 | tf_op jit(solution)/shard_map/ppermute | solution.py:376
  54.5 4.3 %collective-permute-done.9.refs_7_ = bf16[80,2048]{1,0:T(8,128)(2,1)S(1)} collective-permute-done((bf16[80,2048]{1,0:T(8,128)(2,1)S(1)}, bf16[80,2048]{1,0:T(8,128)(2,1)S(1)}, u32[]{:S(2)}, u32[]{:S(2)}) %collective-permute-start.9) | collective-permute-done | bytes 327712 | tf_op jit(solution)/shard_map/ppermute | solution.py:376
  61.6 4.3 %collective-permute-done.12.refs_10_ = bf16[80,2048]{1,0:T(8,128)(2,1)S(1)} collective-permute-done((bf16[80,2048]{1,0:T(8,128)(2,1)S(1)}, bf16[80,2048]{1,0:T(8,128)(2,1)S(1)}, u32[]{:S(2)}, u32[]{:S(2)}) %collective-permute-start.12) | collective-permute-done | bytes 327712 | tf_op jit(solution)/shard_map/ppermute | solution.py:376
  68.7 4.3 %collective-permute-done.13.refs_11_ = bf16[80,2048]{1,0:T(8,128)(2,1)S(1)} collective-permute-done((bf16[80,2048]{1,0:T(8,128)(2,1)S(1)}, bf16[80,2048]{1,0:T(8,128)(2,1)S(1)}, u32[]{:S(2)}, u32[]{:S(2)}) %collective-permute-start.13) | collective-permute-done | bytes 327712 | tf_op jit(solution)/shard_map/ppermute | solution.py:376
  74.2 5.8 %collective-permute-done.16.refs_14_ = bf16[80,2048]{1,0:T(8,128)(2,1)S(1)} collective-permute-done((bf16[80,2048]{1,0:T(8,128)(2,1)S(1)}, bf16[80,2048]{1,0:T(8,128)(2,1)S(1)}, u32[]{:S(2)}, u32[]{:S(2)}) %collective-permute-start.16) | collective-permute-done | bytes 327712 | tf_op jit(solution)/shard_map/ppermute | solution.py:376
  83.4 2.6 %collective-permute-start.19 = (bf16[2,3,64,256]{3,2,1,0:T(8,128)(2,1)S(1)}, bf16[2,3,64,256]{3,2,1,0:T(8,128)(2,1)S(1)}, u32[]{:S(2)}, u32[]{:S(2)}) collective-permute-start(bf16[2,3,64,256]{3,2,1,0:T(8,128)(2,1)S(1)} %get-tuple-element.43), channel_id=1, source_target_pairs={{0,32},{16,48},{32,0},{48,16},{1,33},{17,49},{33,1},{49,17},{2,34}... | collective-permute-start | bytes 589832 | tf_op jit(solution)/shard_map/ppermute | solution.py:376
  87.1 5.3 %shard_map.83 = bf16[8,128,256]{2,1,0:T(8,128)(2,1)} custom-call(s32[1]{0:T(128)} %bitcast.place_ref.z_ref, bf16[3,2048,256]{2,1,0:T(8,128)(2,1)S(1)} %bitcast.16, bf16[80,2048]{1,0:T(8,128)(2,1)S(1)} %get-tuple-element.39.refs_0_, bf16[80,2048]{1,0:T(8,128)(2,1)S(1)} %get-tuple-element.40.refs_1_, bf16[80,2048]{1,0:T(8,128)(2,1)S(1)} %collective-permute-done.4.refs_2_, ...), custom_call_target="tpu_custom_call" | custom-call | flops 6442450944 | bytes 8388608 | tf_op jit(solution)/shard_map/pallas_call | solution.py:184
  92.4 1.7 collective-permute-done.19.refs_2_
  95.1 4.4 %all-to-all-start = ((bf16[8,128,256]{2,1,0:T(8,128)(2,1)}), bf16[8,128,256]{2,1,0:T(8,128)(2,1)S(1)}, u32[]{:S(2)}, u32[]{:S(2)}) async-start(bf16[8,128,256]{2,1,0:T(8,128)(2,1)} %shard_map.83), calls=%async_computation | async-start | bytes 1048576 | tf_op jit(solution)/shard_map/all_to_all | solution.py:423
  99.5 15.6 %all-to-all-done.mix_ref = bf16[8,128,256]{2,1,0:T(8,128)(2,1)S(1)} async-done(((bf16[8,128,256]{2,1,0:T(8,128)(2,1)}), bf16[8,128,256]{2,1,0:T(8,128)(2,1)S(1)}, u32[]{:S(2)}, u32[]{:S(2)}) %all-to-all-start) | async-done | bytes 524320 | tf_op jit(solution)/shard_map/all_to_all | solution.py:423
  115.2 3.5 %copy-done.1 = bf16[128,128,256]{2,1,0:T(8,128)(2,1)S(1)} copy-done((bf16[128,128,256]{2,1,0:T(8,128)(2,1)S(1)}, bf16[128,128,256]{2,1,0:T(8,128)(2,1)}, u32[]{:S(2)}) %copy-start.1) | copy-done | bytes 8388632
  122.4 7.1 %all-to-all-start.1 = ((bf16[16,32,2048]{2,1,0:T(8,128)(2,1)}), bf16[16,32,2048]{2,1,0:T(8,128)(2,1)}, u32[]{:S(2)}, u32[]{:S(2)}) async-start(bf16[16,32,2048]{2,1,0:T(8,128)(2,1)} %copy-done.3), calls=%async_computation.1 | async-start | bytes 4194304 | tf_op jit(solution)/shard_map/all_to_all | solution.py:436
  129.8 2.4 %collective-permute-start.22 = (bf16[128,2048]{1,0:T(8,128)(2,1)S(1)}, bf16[128,2048]{1,0:T(8,128)(2,1)S(1)}, u32[]{:S(2)}, u32[]{:S(2)}) collective-permute-start(bf16[128,2048]{1,0:T(8,128)(2,1)S(1)} %constant_dynamic-slice_fusion.refs_0_), channel_id=1, source_target_pairs={{0,7},{1,0},{2,1},{3,2},{4,3},{5,4},{6,5},{7,6},{8,15},{9,8},{10,9... | collective-permute-start | bytes 1572872 | tf_op jit(solution)/shard_map/ppermute | solution.py:376
  132.2 11.8 %collective-permute-done.21.refs_1_ = bf16[128,2048]{1,0:T(8,128)(2,1)S(1)} collective-permute-done((bf16[128,2048]{1,0:T(8,128)(2,1)S(1)}, bf16[128,2048]{1,0:T(8,128)(2,1)S(1)}, u32[]{:S(2)}, u32[]{:S(2)}) %collective-permute-start.21) | collective-permute-done | bytes 524320 | tf_op jit(solution)/shard_map/ppermute | solution.py:376
  144.0 2.7 %collective-permute-start.24 = (bf16[128,2048]{1,0:T(8,128)(2,1)S(1)}, bf16[128,2048]{1,0:T(8,128)(2,1)}, u32[]{:S(2)}, u32[]{:S(2)}) collective-permute-start(bf16[128,2048]{1,0:T(8,128)(2,1)S(1)} %collective-permute-done.22.refs_2_), channel_id=1, source_target_pairs={{0,7},{1,0},{2,1},{3,2},{4,3},{5,4},{6,5},{7,6},{8,15},{9,8},{10,9... | collective-permute-start | bytes 1572872 | tf_op jit(solution)/shard_map/ppermute | solution.py:376
  148.1 9.6 %collective-permute-done.23.refs_3_ = bf16[128,2048]{1,0:T(8,128)(2,1)} collective-permute-done((bf16[128,2048]{1,0:T(8,128)(2,1)S(1)}, bf16[128,2048]{1,0:T(8,128)(2,1)}, u32[]{:S(2)}, u32[]{:S(2)}) %collective-permute-start.23) | collective-permute-done | bytes 524320 | tf_op jit(solution)/shard_map/ppermute | solution.py:376
  157.7 2.7 %collective-permute-start.26 = (bf16[128,2048]{1,0:T(8,128)(2,1)}, bf16[128,2048]{1,0:T(8,128)(2,1)S(1)}, u32[]{:S(2)}, u32[]{:S(2)}) collective-permute-start(bf16[128,2048]{1,0:T(8,128)(2,1)} %collective-permute-done.24.refs_4_), channel_id=1, source_target_pairs={{0,7},{1,0},{2,1},{3,2},{4,3},{5,4},{6,5},{7,6},{8,15},{9,8},{10,9... | collective-permute-start | bytes 1572872 | tf_op jit(solution)/shard_map/ppermute | solution.py:376
  160.4 2.8 %copy-done.16 = bf16[48,256,256]{2,1,0:T(8,128)(2,1)S(1)} copy-done((bf16[48,256,256]{2,1,0:T(8,128)(2,1)S(1)}, bf16[48,256,256]{2,1,0:T(8,128)(2,1)}, u32[]{:S(2)}) %copy-start.16) | copy-done | bytes 6291480
  163.2 7.6 %shard_map.88 = bf16[16,2,32,256]{3,2,1,0:T(8,128)(2,1)S(1)} custom-call(s32[1]{0:T(128)} %dynamic_slice.9.start_ref, bf16[512,2048]{1,0:T(8,128)(2,1)} %bitcast.9.rows_ref, bf16[8,6,256,256]{3,2,1,0:T(8,128)(2,1)S(1)} %bitcast.15), custom_call_target="tpu_custom_call" | custom-call | flops 3221225472 | bytes 9437184 | tf_op jit(solution)/shard_map/pallas_call | solution.py:288
  171.6 7.8 %all-to-all-start.2 = ((bf16[16,2,32,256]{3,2,1,0:T(8,128)(2,1)}), bf16[16,2,32,256]{3,2,1,0:T(8,128)(2,1)S(1)}, u32[]{:S(2)}, u32[]{:S(2)}) async-start(bf16[16,2,32,256]{3,2,1,0:T(8,128)(2,1)} %copy-done.10), calls=%async_computation.2 | async-start | bytes 1048576 | tf_op jit(solution)/shard_map/all_to_all | solution.py:440
  179.5 2.8 %collective-permute-start.28 = (bf16[64,2048]{1,0:T(8,128)(2,1)S(1)}, bf16[64,2048]{1,0:T(8,128)(2,1)S(1)}, u32[]{:S(2)}, u32[]{:S(2)}) collective-permute-start(bf16[64,2048]{1,0:T(8,128)(2,1)S(1)} %slice.9), channel_id=1, source_target_pairs={{0,7},{1,0},{2,1},{3,2},{4,3},{5,4},{6,5},{7,6},{8,15},{9,8},{10,9... | collective-permute-start | bytes 786440 | tf_op jit(solution)/shard_map/ppermute | solution.py:376
  182.4 6.2 %collective-permute-done.27.refs_7_ = bf16[64,2048]{1,0:T(8,128)(2,1)S(1)} collective-permute-done((bf16[64,2048]{1,0:T(8,128)(2,1)S(1)}, bf16[64,2048]{1,0:T(8,128)(2,1)S(1)}, u32[]{:S(2)}, u32[]{:S(2)}) %collective-permute-start.27) | collective-permute-done | bytes 262176 | tf_op jit(solution)/shard_map/ppermute | solution.py:376
  192.3 2.6 %shard_map.89 = (f32[128,2048]{1,0:T(8,128)S(1)}, bf16[128,2048]{1,0:T(8,128)(2,1)S(1)}) custom-call(s32[2]{0:T(128)S(1)} %pad_add_fusion.place_ref, bf16[16,2,32,256]{3,2,1,0:T(8,128)(2,1)S(1)} %all-to-all-done.2.mix_ref, bf16[128,2048]{1,0:T(8,128)(2,1)S(1)} %constant_dynamic-slice_fusion.refs_0_, bf16[128,2048]{1,0:T(8,128)(2,1)S(1)} %copy-done.7, ...), custom_call_target="tpu_custom_call" | custom-call | flops 1073741824 | bytes 8388608 | tf_op jit(solution)/shard_map/pallas_call | solution.py:332
  196.1 1.5 collective-permute-done.29.got_ref
  (94 shorter events, 37.3 us)
Async XLA Ops:
  6.5 88.5 %all-gather.5.cloned.1.call-start = ((), (), s32[]{:S(2)}) async-start(), calls=%async_computation.3 | async-start | bytes 8650752 | tf_op jit(solution)/shard_map/all_gather | solution.py:409
  7.5 18.1 %collective-permute-start = (bf16[128,256]{1,0:T(8,128)(2,1)S(1)}, bf16[128,256]{1,0:T(8,128)(2,1)S(1)}, u32[]{:S(2)}, u32[]{:S(2)}) collective-permute-start(bf16[128,256]{1,0:T(8,128)(2,1)S(1)} %dynamic_slice.10), channel_id=1, source_target_pairs={{0,0},{1,1},{2,2},{3,3},{4,12},{5,13},{6,14},{7,15},{8,4},{9,5},{1... | collective-permute-start | bytes 196616 | tf_op jit(solution)/shard_map/ppermute | solution.py:406
  17.7 7.9 %collective-permute-start.1 = (bf16[128,256]{1,0:T(8,128)(2,1)S(1)}, bf16[128,256]{1,0:T(8,128)(2,1)S(1)}, u32[]{:S(2)}, u32[]{:S(2)}) collective-permute-start(bf16[128,256]{1,0:T(8,128)(2,1)S(1)} %dynamic_slice.10), channel_id=1, source_target_pairs={{0,1},{1,2},{2,3},{3,4},{4,13},{5,14},{6,15},{7,8},{8,5},{9,6},{10... | collective-permute-start | bytes 196616 | tf_op jit(solution)/shard_map/ppermute | solution.py:406
  26.4 134.0 %all-gather.7.cloned.1.call-start = ((), (), s32[]{:S(2)}) async-start(), calls=%async_computation.4 | async-start | bytes 7077888 | tf_op jit(solution)/shard_map/all_gather | solution.py:422
  26.4 11.4 %collective-permute-start.4 = (bf16[80,2048]{1,0:T(8,128)(2,1)S(1)}, bf16[80,2048]{1,0:T(8,128)(2,1)S(1)}, u32[]{:S(2)}, u32[]{:S(2)}) collective-permute-start(bf16[80,2048]{1,0:T(8,128)(2,1)S(1)} %get-tuple-element.39.refs_0_), channel_id=1, source_target_pairs={{0,1},{1,2},{2,3},{3,4},{4,5},{5,6},{6,7},{7,0},{8,9},{9,10},{10,1... | collective-permute-start | bytes 983048 | tf_op jit(solution)/shard_map/ppermute | solution.py:376
  30.0 9.3 %collective-permute-start.7 = (bf16[80,2048]{1,0:T(8,128)(2,1)S(1)}, bf16[80,2048]{1,0:T(8,128)(2,1)S(1)}, u32[]{:S(2)}, u32[]{:S(2)}) collective-permute-start(bf16[80,2048]{1,0:T(8,128)(2,1)S(1)} %get-tuple-element.40.refs_1_), channel_id=1, source_target_pairs={{0,7},{1,0},{2,1},{3,2},{4,3},{5,4},{6,5},{7,6},{8,15},{9,8},{10,9... | collective-permute-start | bytes 983048 | tf_op jit(solution)/shard_map/ppermute | solution.py:376
  30.0 14.8 %collective-permute-start.5 = (bf16[80,2048]{1,0:T(8,128)(2,1)S(1)}, bf16[80,2048]{1,0:T(8,128)(2,1)S(1)}, u32[]{:S(2)}, u32[]{:S(2)}) collective-permute-start(bf16[80,2048]{1,0:T(8,128)(2,1)S(1)} %get-tuple-element.40.refs_1_), channel_id=1, source_target_pairs={{0,1},{1,2},{2,3},{3,4},{4,5},{5,6},{6,7},{7,0},{8,9},{9,10},{10,1... | collective-permute-start | bytes 983048 | tf_op jit(solution)/shard_map/ppermute | solution.py:376
  31.5 14.9 %collective-permute-start.6 = (bf16[80,2048]{1,0:T(8,128)(2,1)S(1)}, bf16[80,2048]{1,0:T(8,128)(2,1)S(1)}, u32[]{:S(2)}, u32[]{:S(2)}) collective-permute-start(bf16[80,2048]{1,0:T(8,128)(2,1)S(1)} %get-tuple-element.39.refs_0_), channel_id=1, source_target_pairs={{0,7},{1,0},{2,1},{3,2},{4,3},{5,4},{6,5},{7,6},{8,15},{9,8},{10,9... | collective-permute-start | bytes 983048 | tf_op jit(solution)/shard_map/ppermute | solution.py:376
  37.8 14.0 %collective-permute-start.8 = (bf16[80,2048]{1,0:T(8,128)(2,1)S(1)}, bf16[80,2048]{1,0:T(8,128)(2,1)S(1)}, u32[]{:S(2)}, u32[]{:S(2)}) collective-permute-start(bf16[80,2048]{1,0:T(8,128)(2,1)S(1)} %collective-permute-done.4.refs_2_), channel_id=1, source_target_pairs={{0,1},{1,2},{2,3},{3,4},{4,5},{5,6},{6,7},{7,0},{8,9},{9,10},{10,1... | collective-permute-start | bytes 983048 | tf_op jit(solution)/shard_map/ppermute | solution.py:376
  39.3 14.0 %collective-permute-start.11 = (bf16[80,2048]{1,0:T(8,128)(2,1)S(1)}, bf16[80,2048]{1,0:T(8,128)(2,1)S(1)}, u32[]{:S(2)}, u32[]{:S(2)}) collective-permute-start(bf16[80,2048]{1,0:T(8,128)(2,1)S(1)} %collective-permute-done.7.refs_5_), channel_id=1, source_target_pairs={{0,7},{1,0},{2,1},{3,2},{4,3},{5,4},{6,5},{7,6},{8,15},{9,8},{10,9... | collective-permute-start | bytes 983048 | tf_op jit(solution)/shard_map/ppermute | solution.py:376
  44.8 14.0 %collective-permute-start.9 = (bf16[80,2048]{1,0:T(8,128)(2,1)S(1)}, bf16[80,2048]{1,0:T(8,128)(2,1)S(1)}, u32[]{:S(2)}, u32[]{:S(2)}) collective-permute-start(bf16[80,2048]{1,0:T(8,128)(2,1)S(1)} %collective-permute-done.5.refs_3_), channel_id=1, source_target_pairs={{0,1},{1,2},{2,3},{3,4},{4,5},{5,6},{6,7},{7,0},{8,9},{9,10},{10,1... | collective-permute-start | bytes 983048 | tf_op jit(solution)/shard_map/ppermute | solution.py:376
  46.4 13.9 %collective-permute-start.10 = (bf16[80,2048]{1,0:T(8,128)(2,1)S(1)}, bf16[80,2048]{1,0:T(8,128)(2,1)S(1)}, u32[]{:S(2)}, u32[]{:S(2)}) collective-permute-start(bf16[80,2048]{1,0:T(8,128)(2,1)S(1)} %collective-permute-done.6.refs_4_), channel_id=1, source_target_pairs={{0,7},{1,0},{2,1},{3,2},{4,3},{5,4},{6,5},{7,6},{8,15},{9,8},{10,9... | collective-permute-start | bytes 983048 | tf_op jit(solution)/shard_map/ppermute | solution.py:376
  51.8 14.0 %collective-permute-start.12 = (bf16[80,2048]{1,0:T(8,128)(2,1)S(1)}, bf16[80,2048]{1,0:T(8,128)(2,1)S(1)}, u32[]{:S(2)}, u32[]{:S(2)}) collective-permute-start(bf16[80,2048]{1,0:T(8,128)(2,1)S(1)} %collective-permute-done.8.refs_6_), channel_id=1, source_target_pairs={{0,1},{1,2},{2,3},{3,4},{4,5},{5,6},{6,7},{7,0},{8,9},{9,10},{10,1... | collective-permute-start | bytes 983048 | tf_op jit(solution)/shard_map/ppermute | solution.py:376
  53.3 14.0 %collective-permute-start.15 = (bf16[80,2048]{1,0:T(8,128)(2,1)S(1)}, bf16[80,2048]{1,0:T(8,128)(2,1)S(1)}, u32[]{:S(2)}, u32[]{:S(2)}) collective-permute-start(bf16[80,2048]{1,0:T(8,128)(2,1)S(1)} %collective-permute-done.11.refs_9_), channel_id=1, source_target_pairs={{0,7},{1,0},{2,1},{3,2},{4,3},{5,4},{6,5},{7,6},{8,15},{9,8},{10,9... | collective-permute-start | bytes 983048 | tf_op jit(solution)/shard_map/ppermute | solution.py:376
  58.8 14.1 %collective-permute-start.13 = (bf16[80,2048]{1,0:T(8,128)(2,1)S(1)}, bf16[80,2048]{1,0:T(8,128)(2,1)S(1)}, u32[]{:S(2)}, u32[]{:S(2)}) collective-permute-start(bf16[80,2048]{1,0:T(8,128)(2,1)S(1)} %collective-permute-done.9.refs_7_), channel_id=1, source_target_pairs={{0,1},{1,2},{2,3},{3,4},{4,5},{5,6},{6,7},{7,0},{8,9},{9,10},{10,1... | collective-permute-start | bytes 983048 | tf_op jit(solution)/shard_map/ppermute | solution.py:376
  60.4 13.8 %collective-permute-start.14 = (bf16[80,2048]{1,0:T(8,128)(2,1)S(1)}, bf16[80,2048]{1,0:T(8,128)(2,1)S(1)}, u32[]{:S(2)}, u32[]{:S(2)}) collective-permute-start(bf16[80,2048]{1,0:T(8,128)(2,1)S(1)} %collective-permute-done.10.refs_8_), channel_id=1, source_target_pairs={{0,7},{1,0},{2,1},{3,2},{4,3},{5,4},{6,5},{7,6},{8,15},{9,8},{10,9... | collective-permute-start | bytes 983048 | tf_op jit(solution)/shard_map/ppermute | solution.py:376
  65.9 14.1 %collective-permute-start.16 = (bf16[80,2048]{1,0:T(8,128)(2,1)S(1)}, bf16[80,2048]{1,0:T(8,128)(2,1)S(1)}, u32[]{:S(2)}, u32[]{:S(2)}) collective-permute-start(bf16[80,2048]{1,0:T(8,128)(2,1)S(1)} %collective-permute-done.12.refs_10_), channel_id=1, source_target_pairs={{0,1},{1,2},{2,3},{3,4},{4,5},{5,6},{6,7},{7,0},{8,9},{9,10},{10,1... | collective-permute-start | bytes 983048 | tf_op jit(solution)/shard_map/ppermute | solution.py:376
  67.4 13.8 %collective-permute-start.17 = (bf16[80,2048]{1,0:T(8,128)(2,1)S(1)}, bf16[80,2048]{1,0:T(8,128)(2,1)S(1)}, u32[]{:S(2)}, u32[]{:S(2)}) collective-permute-start(bf16[80,2048]{1,0:T(8,128)(2,1)S(1)} %collective-permute-done.15.refs_13_), channel_id=1, source_target_pairs={{0,7},{1,0},{2,1},{3,2},{4,3},{5,4},{6,5},{7,6},{8,15},{9,8},{10,9... | collective-permute-start | bytes 983048 | tf_op jit(solution)/shard_map/ppermute | solution.py:376
  82.1 10.3 %collective-permute-start.18 = (bf16[2,3,64,256]{3,2,1,0:T(8,128)(2,1)S(1)}, bf16[2,3,64,256]{3,2,1,0:T(8,128)(2,1)S(1)}, u32[]{:S(2)}, u32[]{:S(2)}) collective-permute-start(bf16[2,3,64,256]{3,2,1,0:T(8,128)(2,1)S(1)} %get-tuple-element.42), channel_id=1, source_target_pairs={{0,16},{16,32},{32,48},{48,0},{1,17},{17,33},{33,49},{49,1},{2,18}... | collective-permute-start | bytes 589832 | tf_op jit(solution)/shard_map/ppermute | solution.py:376
  83.4 10.7 %collective-permute-start.19 = (bf16[2,3,64,256]{3,2,1,0:T(8,128)(2,1)S(1)}, bf16[2,3,64,256]{3,2,1,0:T(8,128)(2,1)S(1)}, u32[]{:S(2)}, u32[]{:S(2)}) collective-permute-start(bf16[2,3,64,256]{3,2,1,0:T(8,128)(2,1)S(1)} %get-tuple-element.43), channel_id=1, source_target_pairs={{0,32},{16,48},{32,0},{48,16},{1,33},{17,49},{33,1},{49,17},{2,34}... | collective-permute-start | bytes 589832 | tf_op jit(solution)/shard_map/ppermute | solution.py:376
  86.0 8.1 %collective-permute-start.20 = (bf16[2,3,64,256]{3,2,1,0:T(8,128)(2,1)S(1)}, bf16[2,3,64,256]{3,2,1,0:T(8,128)(2,1)S(1)}, u32[]{:S(2)}, u32[]{:S(2)}) collective-permute-start(bf16[2,3,64,256]{3,2,1,0:T(8,128)(2,1)S(1)} %get-tuple-element.44), channel_id=1, source_target_pairs={{0,48},{16,0},{32,16},{48,32},{1,49},{17,1},{33,17},{49,33},{2,50}... | collective-permute-start | bytes 589832 | tf_op jit(solution)/shard_map/ppermute | solution.py:376
  95.1 20.0 %all-to-all-start = ((bf16[8,128,256]{2,1,0:T(8,128)(2,1)}), bf16[8,128,256]{2,1,0:T(8,128)(2,1)S(1)}, u32[]{:S(2)}, u32[]{:S(2)}) async-start(bf16[8,128,256]{2,1,0:T(8,128)(2,1)} %shard_map.83), calls=%async_computation | async-start | bytes 1048576 | tf_op jit(solution)/shard_map/all_to_all | solution.py:423
  122.4 38.0 %all-to-all-start.1 = ((bf16[16,32,2048]{2,1,0:T(8,128)(2,1)}), bf16[16,32,2048]{2,1,0:T(8,128)(2,1)}, u32[]{:S(2)}, u32[]{:S(2)}) async-start(bf16[16,32,2048]{2,1,0:T(8,128)(2,1)} %copy-done.3), calls=%async_computation.1 | async-start | bytes 4194304 | tf_op jit(solution)/shard_map/all_to_all | solution.py:436
  129.5 14.5 %collective-permute-start.21 = (bf16[128,2048]{1,0:T(8,128)(2,1)S(1)}, bf16[128,2048]{1,0:T(8,128)(2,1)S(1)}, u32[]{:S(2)}, u32[]{:S(2)}) collective-permute-start(bf16[128,2048]{1,0:T(8,128)(2,1)S(1)} %constant_dynamic-slice_fusion.refs_0_), channel_id=1, source_target_pairs={{0,1},{1,2},{2,3},{3,4},{4,5},{5,6},{6,7},{7,0},{8,9},{9,10},{10,1... | collective-permute-start | bytes 1572872 | tf_op jit(solution)/shard_map/ppermute | solution.py:376
  129.8 14.2 %collective-permute-start.22 = (bf16[128,2048]{1,0:T(8,128)(2,1)S(1)}, bf16[128,2048]{1,0:T(8,128)(2,1)S(1)}, u32[]{:S(2)}, u32[]{:S(2)}) collective-permute-start(bf16[128,2048]{1,0:T(8,128)(2,1)S(1)} %constant_dynamic-slice_fusion.refs_0_), channel_id=1, source_target_pairs={{0,7},{1,0},{2,1},{3,2},{4,3},{5,4},{6,5},{7,6},{8,15},{9,8},{10,9... | collective-permute-start | bytes 1572872 | tf_op jit(solution)/shard_map/ppermute | solution.py:376
  144.0 13.7 %collective-permute-start.23 = (bf16[128,2048]{1,0:T(8,128)(2,1)S(1)}, bf16[128,2048]{1,0:T(8,128)(2,1)}, u32[]{:S(2)}, u32[]{:S(2)}) collective-permute-start(bf16[128,2048]{1,0:T(8,128)(2,1)S(1)} %collective-permute-done.21.refs_1_), channel_id=1, source_target_pairs={{0,1},{1,2},{2,3},{3,4},{4,5},{5,6},{6,7},{7,0},{8,9},{9,10},{10,1... | collective-permute-start | bytes 1572872 | tf_op jit(solution)/shard_map/ppermute | solution.py:376
  144.0 13.7 %collective-permute-start.24 = (bf16[128,2048]{1,0:T(8,128)(2,1)S(1)}, bf16[128,2048]{1,0:T(8,128)(2,1)}, u32[]{:S(2)}, u32[]{:S(2)}) collective-permute-start(bf16[128,2048]{1,0:T(8,128)(2,1)S(1)} %collective-permute-done.22.refs_2_), channel_id=1, source_target_pairs={{0,7},{1,0},{2,1},{3,2},{4,3},{5,4},{6,5},{7,6},{8,15},{9,8},{10,9... | collective-permute-start | bytes 1572872 | tf_op jit(solution)/shard_map/ppermute | solution.py:376
  157.7 21.7 %collective-permute-start.25 = (bf16[128,2048]{1,0:T(8,128)(2,1)}, bf16[128,2048]{1,0:T(8,128)(2,1)S(1)}, u32[]{:S(2)}, u32[]{:S(2)}) collective-permute-start(bf16[128,2048]{1,0:T(8,128)(2,1)} %collective-permute-done.23.refs_3_), channel_id=1, source_target_pairs={{0,1},{1,2},{2,3},{3,4},{4,5},{5,6},{6,7},{7,0},{8,9},{9,10},{10,1... | collective-permute-start | bytes 1572872 | tf_op jit(solution)/shard_map/ppermute | solution.py:376
  157.7 21.8 %collective-permute-start.26 = (bf16[128,2048]{1,0:T(8,128)(2,1)}, bf16[128,2048]{1,0:T(8,128)(2,1)S(1)}, u32[]{:S(2)}, u32[]{:S(2)}) collective-permute-start(bf16[128,2048]{1,0:T(8,128)(2,1)} %collective-permute-done.24.refs_4_), channel_id=1, source_target_pairs={{0,7},{1,0},{2,1},{3,2},{4,3},{5,4},{6,5},{7,6},{8,15},{9,8},{10,9... | collective-permute-start | bytes 1572872 | tf_op jit(solution)/shard_map/ppermute | solution.py:376
  171.6 17.7 %all-to-all-start.2 = ((bf16[16,2,32,256]{3,2,1,0:T(8,128)(2,1)}), bf16[16,2,32,256]{3,2,1,0:T(8,128)(2,1)S(1)}, u32[]{:S(2)}, u32[]{:S(2)}) async-start(bf16[16,2,32,256]{3,2,1,0:T(8,128)(2,1)} %copy-done.10), calls=%async_computation.2 | async-start | bytes 1048576 | tf_op jit(solution)/shard_map/all_to_all | solution.py:440
  179.4 9.2 %collective-permute-start.27 = (bf16[64,2048]{1,0:T(8,128)(2,1)S(1)}, bf16[64,2048]{1,0:T(8,128)(2,1)S(1)}, u32[]{:S(2)}, u32[]{:S(2)}) collective-permute-start(bf16[64,2048]{1,0:T(8,128)(2,1)S(1)} %slice.8), channel_id=1, source_target_pairs={{0,1},{1,2},{2,3},{3,4},{4,5},{5,6},{6,7},{7,0},{8,9},{9,10},{10,1... | collective-permute-start | bytes 786440 | tf_op jit(solution)/shard_map/ppermute | solution.py:376
  179.5 9.0 %collective-permute-start.28 = (bf16[64,2048]{1,0:T(8,128)(2,1)S(1)}, bf16[64,2048]{1,0:T(8,128)(2,1)S(1)}, u32[]{:S(2)}, u32[]{:S(2)}) collective-permute-start(bf16[64,2048]{1,0:T(8,128)(2,1)S(1)} %slice.9), channel_id=1, source_target_pairs={{0,7},{1,0},{2,1},{3,2},{4,3},{5,4},{6,5},{7,6},{8,15},{9,8},{10,9... | collective-permute-start | bytes 786440 | tf_op jit(solution)/shard_map/ppermute | solution.py:376
  (22 other events, 268.7 us)
Sparse Core Ops, SparseCore 0:
  26.5 59.9 all-gather.4
  95.2 44.2 all-gather.6
